TPU v7x, 32 devices: a whole 2x2x4 slice. The times are simulated.
32 devices in a mesh: groups: 2 (over y), space: 4 (over z), chan: 4 (over x, core).
Axes of the slice: x: 2, y: 2, z: 4, core: 2. Of those that a mesh axis runs over, the one named last changes fastest.
Arguments:
- labels: int32 [32, 32, 512], P(('groups', 'space'), 'chan'), parts along dimension 0, may hold values from 0 to 1023
- table: bfloat16 [1024, 16], replicated, may hold values from -6 to 6
- fine_weight: bfloat16 [27, 16, 16], replicated, may hold values from -0.3125 to 0.3125
- fine_cot: bfloat16 [16, 32, 32, 512], P(None, ('groups', 'space'), 'chan'), parts along dimension 1, may hold values from -6 to 6
- bott_in: bfloat16 [512, 16, 128], P('chan', ('groups', 'space')), parts along dimension 1, may hold values from -6 to 6
- bott_weight: bfloat16 [512, 27, 512], P('chan'), may hold values from -0.0625 to 0.0625
- bott_cot: bfloat16 [512, 16, 128], P('chan', ('groups', 'space')), parts along dimension 1, may hold values from -6 to 6
Outputs:
- fine_out: bfloat16 [16, 32, 32, 512], P(None, ('groups', 'space'), 'chan'), parts along dimension 1
- fine_wgrad: float32 [54, 16, 16], P('groups'), parts along dimension 0
- bott_out: bfloat16 [512, 16, 128], P('chan', ('groups', 'space')), parts along dimension 1
- bott_dgrad: bfloat16 [512, 16, 128], P('chan', ('groups', 'space')), parts along dimension 1
- bott_wgrad: float32 [1024, 27, 512], P(('groups', 'chan')), parts along dimension 0
There are 2 independent parts, one for each index of `groups`. A program takes and returns all parts, laid end to end along the dimension named above; an argument that names none is the same for every part. Nothing has to cross between parts.
All inputs are finite; a program needn't handle non-finite values.
Results may differ from a plain program's by a relative error of at most 0.005.
Values may be sent and summed in bfloat16 or wider, within the bound.
No kernel may reach another device: no remote copies, remote signals or barrier semaphores. Data moves between devices by JAX's collectives and lax.ppermute only.
A program may use at most 128 MiB of HBM per device.

v0:
```python
import jax
import jax.numpy as jnp
from jax import lax
from jax.sharding import PartitionSpec as P

BW = 32


def with_halo(cells, sides, width):
    for axis, dim in sides:
        count = lax.axis_size(axis)
        ends = count - 1
        head = lax.slice_in_dim(cells, 0, width, axis=dim)
        tail = lax.slice_in_dim(cells, cells.shape[dim] - width, cells.shape[dim], axis=dim)
        cells = jnp.concatenate(
            [
                lax.ppermute(tail, axis, [(i, (i + 1) % count) for i in range(ends)]),
                cells,
                lax.ppermute(head, axis, [((i + 1) % count, i) for i in range(ends)]),
            ],
            axis=dim,
        )
    return cells


def shift_flat(block, step_y, step_w, width):
    total = block.shape[-1]
    reach = width + 1
    padded = jnp.pad(block, [(0, 0)] * (block.ndim - 1) + [(reach, reach)])
    offset = reach + step_y * width + step_w
    moved = lax.slice_in_dim(padded, offset, offset + total, axis=block.ndim - 1)
    column = jnp.arange(total, dtype=jnp.int32) % width + step_w
    inside = (column >= 0) & (column < width)
    return jnp.where(inside, moved, jnp.zeros_like(moved))


def offset_number(step_x, step_y, step_w):
    return 9 * (step_x + 1) + 3 * (step_y + 1) + (step_w + 1)


def silu_parts(pre_act):
    sigmoid_val = jax.nn.sigmoid(pre_act)
    return (pre_act * sigmoid_val, sigmoid_val * (1.0 + pre_act * (1.0 - sigmoid_val)))


def plane_stack(framed, step_x, depth, rows_y, cols_w):
    pieces = []
    for step_y in (-1, 0, 1):
        for step_w in (-1, 0, 1):
            pieces.append(
                framed[
                    :,
                    1 + step_x : 1 + step_x + depth,
                    1 + step_y : 1 + step_y + rows_y,
                    1 + step_w : 1 + step_w + cols_w,
                ]
            )
    return jnp.concatenate(pieces, axis=0)


def shards(labels, table, fine_weight, fine_cot, bott_in, bott_weight, bott_cot):
    depth, rows_y, cols_w = labels.shape
    fine_ch = fine_weight.shape[2]
    lookup = jnp.concatenate([jnp.zeros((1, table.shape[1]), table.dtype), table], axis=0).T
    shifted_ids = labels + 1
    features = jnp.take(lookup, shifted_ids, axis=1)
    framed = with_halo(features, (("space", 1), ("chan", 2)), 1)
    framed = jnp.pad(framed, ((0, 0), (0, 0), (0, 0), (1, 1)))
    fine_pre = jnp.zeros((fine_ch, depth, rows_y, cols_w), jnp.float32)
    for step_x in (-1, 0, 1):
        stacked = plane_stack(framed, step_x, depth, rows_y, cols_w)
        first = 9 * (step_x + 1)
        kernel_block = fine_weight[first : first + 9].reshape(9 * fine_weight.shape[1], fine_ch)
        fine_pre = fine_pre + jnp.einsum(
            "kxyw,ko->oxyw", stacked, kernel_block, preferred_element_type=jnp.float32
        )
    fine_act, fine_slope = silu_parts(fine_pre)
    fine_out = fine_act.astype(jnp.bfloat16)
    fine_delta = (fine_cot.astype(jnp.float32) * fine_slope).astype(jnp.bfloat16)
    fine_scale = (depth * lax.axis_size("space") * rows_y * lax.axis_size("chan") * cols_w) ** (
        -0.5
    )
    fine_blocks = []
    for step_x in (-1, 0, 1):
        stacked = plane_stack(framed, step_x, depth, rows_y, cols_w)
        block_grad = (
            jnp.einsum("kxyw,oxyw->ko", stacked, fine_delta, preferred_element_type=jnp.float32)
            * fine_scale
        )
        fine_blocks.append(block_grad.reshape(9, fine_weight.shape[1], fine_ch))
    fine_wgrad = lax.psum(jnp.concatenate(fine_blocks, axis=0), ("space", "chan"))
    planes = bott_in.shape[1]
    framed_in = with_halo(bott_in, (("space", 1),), 1)
    slabs = lax.all_gather(framed_in, "chan", axis=0, tiled=True)
    bott_pre = jnp.zeros(bott_in.shape, jnp.float32)
    for step_y in (-1, 0, 1):
        for step_w in (-1, 0, 1):
            moved = shift_flat(slabs, step_y, step_w, BW)
            for step_x in (-1, 0, 1):
                plane = moved[:, 1 + step_x : 1 + step_x + planes]
                bott_pre = bott_pre + jnp.einsum(
                    "cpv,oc->opv",
                    plane,
                    bott_weight[:, offset_number(step_x, step_y, step_w), :],
                    preferred_element_type=jnp.float32,
                )
    bott_act, bott_slope = silu_parts(bott_pre)
    bott_out = bott_act.astype(jnp.bfloat16)
    bott_delta = (bott_cot.astype(jnp.float32) * bott_slope).astype(jnp.bfloat16)
    delta_slabs = with_halo(bott_delta, (("space", 1),), 1)
    partial_value = jnp.zeros((slabs.shape[0], planes, bott_in.shape[2]), jnp.float32)
    for step_y in (-1, 0, 1):
        for step_w in (-1, 0, 1):
            back = shift_flat(delta_slabs, -step_y, -step_w, BW)
            for step_x in (-1, 0, 1):
                plane = back[:, 1 - step_x : 1 - step_x + planes]
                partial_value = partial_value + jnp.einsum(
                    "opv,oc->cpv",
                    plane,
                    bott_weight[:, offset_number(step_x, step_y, step_w), :],
                    preferred_element_type=jnp.float32,
                )
    bott_dgrad = lax.psum_scatter(partial_value, "chan", scatter_dimension=0, tiled=True).astype(
        jnp.bfloat16
    )
    bott_scale = (planes * lax.axis_size("space") * bott_in.shape[2]) ** (-0.5)
    terms = [None] * 27
    for step_y in (-1, 0, 1):
        for step_w in (-1, 0, 1):
            moved_rows = shift_flat(slabs, step_y, step_w, BW)
            for step_x in (-1, 0, 1):
                source = moved_rows[:, 1 + step_x : 1 + step_x + planes]
                terms[offset_number(step_x, step_y, step_w)] = (
                    jnp.einsum(
                        "cpv,opv->oc", source, bott_delta, preferred_element_type=jnp.float32
                    )
                    * bott_scale
                )
    bott_wgrad = lax.psum(jnp.stack(terms, axis=1), "space")
    return (fine_out, fine_wgrad, bott_out, bott_dgrad, bott_wgrad)


def solution(mesh):
    placed = (
        P(("groups", "space"), "chan", None),
        P(),
        P(),
        P(None, ("groups", "space"), "chan", None),
        P("chan", ("groups", "space"), None),
        P("chan", None, None),
        P("chan", ("groups", "space"), None),
    )
    return jax.shard_map(
        shards,
        mesh=mesh,
        in_specs=placed,
        out_specs=(
            P(None, ("groups", "space"), "chan", None),
            P("groups", None, None),
            P("chan", ("groups", "space"), None),
            P("chan", ("groups", "space"), None),
            P(("groups", "chan"), None, None),
        ),
        check_vma=False,
    )
```

profile of v0, /device:TPU:1, one launch (start us, length us, event | category | flops | bytes accessed | tf_op | source)
XLA Modules:
  0.0 327.2 jit_solution(8302414156131127589)
XLA Ops:
  8.0 1.0 copy.94
  9.0 1.3 collective-permute-start.5
  10.3 4.7 %collective-permute-start.4 = (bf16[128,1,128]{0,2,1:T(8,128)(2,1)S(1)}, bf16[128,1,128]{0,2,1:T(8,128)(2,1)S(1)}, u32[]{:S(2)}, u32[]{:S(2)}) collective-permute-start(bf16[128,1,128]{0,2,1:T(8,128)(2,1)S(1)} %get-tuple-element.69), channel_id=1, source_target_pairs={{0,4},{4,8},{8,12},{1,5},{5,9},{9,13},{2,6},{6,10},{10,14},{3,7},{... | collective-permute-start | bytes 98312 | tf_op jit(solution)/shard_map/ppermute | solution.py:17
  15.0 0.9 copy.81
  16.1 1.0 copy.97
  17.1 8.5 %all_gather.3 = bf16[512,4,128]{0,2,1:T(8,128)(2,1)S(1)} all-gather(bf16[128,4,128]{0,2,1:T(8,128)(2,1)S(1)} %pad_maximum_fusion.4), channel_id=1, replica_groups=mesh['groups'=2,'space'=4,'chan'=4] {'chan'}, dimensions={0}, use_global_device_ids=true | all-gather | bytes 655360 | tf_op jit(solution)/shard_map/all_gather | solution.py:94
  25.6 2.0 fusion.123
  34.2 1.3 collective-permute-start.7
  35.5 4.1 %collective-permute-start.6 = (bf16[128,1,128]{0,2,1:T(8,128)(2,1)S(1)}, bf16[128,1,128]{0,2,1:T(8,128)(2,1)S(1)}, u32[]{:S(2)}, u32[]{:S(2)}) collective-permute-start(bf16[128,1,128]{0,2,1:T(8,128)(2,1)S(1)} %get-tuple-element.67), channel_id=1, source_target_pairs={{0,4},{4,8},{8,12},{1,5},{5,9},{9,13},{2,6},{6,10},{10,14},{3,7},{... | collective-permute-start | bytes 98312 | tf_op jit(solution)/shard_map/ppermute | solution.py:17
  44.2 2.9 copy-done.3
  47.2 0.3 fusion.183
  47.5 0.3 fusion.216
  47.7 0.3 convolution_add_fusion.14
  48.0 0.3 convolution_add_fusion.13
  48.3 0.3 convolution_add_fusion.12
  48.6 0.3 convolution_add_fusion.11
  48.8 0.3 convolution_add_fusion.10
  49.1 0.3 convolution_add_fusion.9
  49.4 0.3 convolution_add_fusion.8
  49.6 0.3 convolution_add_fusion.7
  49.9 0.3 convolution_add_fusion.6
  50.2 0.3 convolution_add_fusion.5
  50.5 0.3 convolution_add_fusion.4
  50.7 0.3 fusion.186
  51.0 0.3 fusion.189
  51.3 0.3 fusion.15
  51.5 0.3 fusion.12
  51.8 0.3 fusion.11
  52.1 0.3 fusion.10
  52.4 0.3 fusion.9
  52.6 0.3 fusion.8
  54.2 1.0 fusion.2
  55.3 0.9 fusion.35
  56.2 0.9 fusion.32
  57.2 0.9 fusion.29
  58.1 0.9 fusion.26
  59.0 0.9 fusion.23
  60.0 57.4 %gather_fusion = bf16[16384,16]{1,0:T(8,128)(2,1)} fusion(bf16[16,1025]{0,1:T(8,128)(2,1)S(1)} %pad_bitcast_fusion, s32[16384]{0:T(1024)S(1)} %broadcast_clamp_fusion), kind=kCustom, calls=%fused_computation | custom fusion | bytes 1114112 | tf_op jit(solution)/shard_map/jit(_take)/gather | solution.py:66
  117.4 3.5 %copy.83 = bf16[4,8,512,16]{2,3,1,0:T(8,128)(2,1)S(1)} copy(bf16[4,8,512,16]{3,2,1,0:T(8,128)(2,1)} %bitcast.678) | data formatting | bytes 1048576 | tf_op jit(solution)/shard_map/jit(_take)/gather | solution.py:66
  121.1 1.3 collective-permute-start.1
  122.4 4.0 %collective-permute-start = (bf16[16,1,8,512]{3,0,2,1:T(8,128)(2,1)S(1)}, bf16[16,1,8,512]{3,0,2,1:T(8,128)(2,1)S(1)}, u32[]{:S(2)}, u32[]{:S(2)}) collective-permute-start(bf16[16,1,8,512]{3,0,2,1:T(8,128)(2,1)S(1)} %get-tuple-element.63), channel_id=1, source_target_pairs={{0,4},{4,8},{8,12},{1,5},{5,9},{9,13},{2,6},{6,10},{10,14},{3,7},{... | collective-permute-start | bytes 393224 | tf_op jit(solution)/shard_map/ppermute | solution.py:17
  126.4 7.5 %collective-permute-done.1 = bf16[16,1,8,512]{3,0,2,1:T(8,128)(2,1)S(1)} collective-permute-done((bf16[16,1,8,512]{3,0,2,1:T(8,128)(2,1)S(1)}, bf16[16,1,8,512]{3,0,2,1:T(8,128)(2,1)S(1)}, u32[]{:S(2)}, u32[]{:S(2)}) %collective-permute-start.1) | collective-permute-done | bytes 131104 | tf_op jit(solution)/shard_map/ppermute | solution.py:19
  133.9 2.3 collective-permute-start.3
  136.2 3.4 %collective-permute-start.2 = (bf16[16,6,1,512]{3,0,2,1:T(8,128)(2,1)S(1)}, bf16[16,6,1,512]{3,0,2,1:T(8,128)(2,1)S(1)}, u32[]{:S(2)}, u32[]{:S(2)}) collective-permute-start(bf16[16,6,1,512]{3,0,2,1:T(8,128)(2,1)S(1)} %get-tuple-element.43), channel_id=1, source_target_pairs={{0,1},{1,2},{2,3},{4,5},{5,6},{6,7},{8,9},{9,10},{10,11},{12,13},{... | collective-permute-start | bytes 294920 | tf_op jit(solution)/shard_map/ppermute | solution.py:17
  140.3 0.8 copy.154
  141.3 0.8 select_maximum_fusion
  142.4 0.6 slice_dynamic-update-slice_fusion.5
  143.4 0.6 slice_dynamic-update-slice_fusion.3
  144.5 0.6 slice_dynamic-update-slice_fusion
  145.1 0.8 fusion.303
  145.9 1.3 copy-done
  147.2 1.4 copy-done.1
  148.6 0.8 convolution_add_fusion.1
  149.4 1.2 multiply_convert_fusion
  150.6 1.1 copy.152
  151.7 1.3 fusion.113
  153.1 3.7 %fusion.114 = f32[144,16]{0,1:T(8,128)S(1)} fusion(bf16[144,4,8,512]{3,0,2,1:T(8,128)(2,1)} %copy-done.1, bf16[16,4,8,512]{3,0,2,1:T(8,128)(2,1)S(1)} %get-tuple-element.33), kind=kOutput, calls=%fused_computation.207 | convolution fusion | flops 75499776 | bytes 5252096 | tf_op jit(solution)/shard_map/kxyw,oxyw->ko/dot_general | solution.py:87
  156.9 3.8 %fusion.115 = f32[144,16]{0,1:T(8,128)S(1)} fusion(bf16[144,4,8,512]{3,0,2,1:T(8,128)(2,1)} %copy-done, bf16[16,4,8,512]{3,0,2,1:T(8,128)(2,1)S(1)} %get-tuple-element.33), kind=kOutput, calls=%fused_computation.209 | convolution fusion | flops 75499776 | bytes 5252096 | tf_op jit(solution)/shard_map/kxyw,oxyw->ko/dot_general | solution.py:87
  160.8 67.1 %psum.14 = f32[27,16,16]{2,1,0:T(8,128)S(1)} all-reduce(f32[27,16,16]{2,1,0:T(8,128)S(1)} %pad_maximum_fusion.3), channel_id=1, replica_groups=mesh['groups'=2,'space'=4,'chan'=4] {'space','chan'}, use_global_device_ids=true, to_apply=%region_0.1 | all-reduce | flops 6912 | bytes 55296 | tf_op jit(solution)/shard_map/psum | solution.py:91
  227.9 0.8 copy.153
  228.7 0.9 convert_element_type.58
  229.7 0.8 copy.155
  230.4 82.0 %all-reduce.6.cloned.1.call-done = f32[128,27,512]{2,0,1:T(8,128)} async-done(((f32[128,27,512]{2,0,1:T(8,128)}), f32[128,27,512]{2,0,1:T(8,128)}) %all-reduce.6.cloned.1.call-update) | async-done | bytes 7077904 | tf_op jit(solution)/shard_map/psum | solution.py:139
  312.4 7.3 %copy.274 = f32[128,27,512]{2,0,1:T(8,128)} copy(f32[128,27,512]{2,0,1:T(8,128)} %all-reduce.6.cloned.1.call-done) | data formatting | bytes 14155776
  (106 shorter events, 14.9 us)
Async XLA Ops:
  8.0 220.8 %reduce-scatter.2.cloned.1.call-start = ((), (), s32[]{:S(2)}) async-start(), calls=%async_computation.1 | async-start | bytes 655360 | tf_op jit(solution)/shard_map/reduce_scatter | solution.py:123
  9.0 8.0 %collective-permute-start.5 = (bf16[128,1,128]{0,2,1:T(8,128)(2,1)S(1)}, bf16[128,1,128]{0,2,1:T(8,128)(2,1)S(1)}, u32[]{:S(2)}, u32[]{:S(2)}) collective-permute-start(bf16[128,1,128]{0,2,1:T(8,128)(2,1)S(1)} %get-tuple-element.70), channel_id=1, source_target_pairs={{4,0},{8,4},{12,8},{5,1},{9,5},{13,9},{6,2},{10,6},{14,10},{7,3},{... | collective-permute-start | bytes 98312 | tf_op jit(solution)/shard_map/ppermute | solution.py:19
  10.3 6.7 %collective-permute-start.4 = (bf16[128,1,128]{0,2,1:T(8,128)(2,1)S(1)}, bf16[128,1,128]{0,2,1:T(8,128)(2,1)S(1)}, u32[]{:S(2)}, u32[]{:S(2)}) collective-permute-start(bf16[128,1,128]{0,2,1:T(8,128)(2,1)S(1)} %get-tuple-element.69), channel_id=1, source_target_pairs={{0,4},{4,8},{8,12},{1,5},{5,9},{9,13},{2,6},{6,10},{10,14},{3,7},{... | collective-permute-start | bytes 98312 | tf_op jit(solution)/shard_map/ppermute | solution.py:17
  17.0 10.6 %copy-start.2 = (bf16[128,27,512]{2,0,1:T(8,128)(2,1)S(1)}, bf16[128,27,512]{2,0,1:T(8,128)(2,1)}, u32[]{:S(2)}) copy-start(bf16[128,27,512]{2,0,1:T(8,128)(2,1)} %param.12) | copy-start | bytes 10616836
  34.2 10.0 %collective-permute-start.7 = (bf16[128,1,128]{0,2,1:T(8,128)(2,1)S(1)}, bf16[128,1,128]{0,2,1:T(8,128)(2,1)S(1)}, u32[]{:S(2)}, u32[]{:S(2)}) collective-permute-start(bf16[128,1,128]{0,2,1:T(8,128)(2,1)S(1)} %get-tuple-element.68), channel_id=1, source_target_pairs={{4,0},{8,4},{12,8},{5,1},{9,5},{13,9},{6,2},{10,6},{14,10},{7,3},{... | collective-permute-start | bytes 98312 | tf_op jit(solution)/shard_map/ppermute | solution.py:19
  35.5 11.6 %collective-permute-start.6 = (bf16[128,1,128]{0,2,1:T(8,128)(2,1)S(1)}, bf16[128,1,128]{0,2,1:T(8,128)(2,1)S(1)}, u32[]{:S(2)}, u32[]{:S(2)}) collective-permute-start(bf16[128,1,128]{0,2,1:T(8,128)(2,1)S(1)} %get-tuple-element.67), channel_id=1, source_target_pairs={{0,4},{4,8},{8,12},{1,5},{5,9},{9,13},{2,6},{6,10},{10,14},{3,7},{... | collective-permute-start | bytes 98312 | tf_op jit(solution)/shard_map/ppermute | solution.py:17
  44.2 3.0 copy-start.3
  55.3 257.1 %all-reduce.6.cloned.1.call-start = ((), (), s32[]{:S(2)}) async-start(), calls=%async_computation.2 | async-start | bytes 14155776 | tf_op jit(solution)/shard_map/psum | solution.py:139
  56.2 3.7 %copy-start.5 = (s32[4,8,512]{2,1,0:T(8,128)S(1)}, s32[4,8,512]{2,1,0:T(8,128)}, u32[]{:S(2)}) copy-start(s32[4,8,512]{2,1,0:T(8,128)} %param.7) | copy-start | bytes 196612
  117.4 22.3 %copy-start.4 = (bf16[27,16,16]{0,2,1:T(8,128)(2,1)S(1)}, bf16[27,16,16]{0,2,1:T(8,128)(2,1)}, u32[]{:S(2)}) copy-start(bf16[27,16,16]{0,2,1:T(8,128)(2,1)} %param.9) | copy-start | bytes 41476
  121.1 12.8 %collective-permute-start.1 = (bf16[16,1,8,512]{3,0,2,1:T(8,128)(2,1)S(1)}, bf16[16,1,8,512]{3,0,2,1:T(8,128)(2,1)S(1)}, u32[]{:S(2)}, u32[]{:S(2)}) collective-permute-start(bf16[16,1,8,512]{3,0,2,1:T(8,128)(2,1)S(1)} %get-tuple-element.64), channel_id=1, source_target_pairs={{4,0},{8,4},{12,8},{5,1},{9,5},{13,9},{6,2},{10,6},{14,10},{7,3},{... | collective-permute-start | bytes 393224 | tf_op jit(solution)/shard_map/ppermute | solution.py:19
  122.4 11.5 %collective-permute-start = (bf16[16,1,8,512]{3,0,2,1:T(8,128)(2,1)S(1)}, bf16[16,1,8,512]{3,0,2,1:T(8,128)(2,1)S(1)}, u32[]{:S(2)}, u32[]{:S(2)}) collective-permute-start(bf16[16,1,8,512]{3,0,2,1:T(8,128)(2,1)S(1)} %get-tuple-element.63), channel_id=1, source_target_pairs={{0,4},{4,8},{8,12},{1,5},{5,9},{9,13},{2,6},{6,10},{10,14},{3,7},{... | collective-permute-start | bytes 393224 | tf_op jit(solution)/shard_map/ppermute | solution.py:17
  133.9 7.2 %collective-permute-start.3 = (bf16[16,6,1,512]{3,0,2,1:T(8,128)(2,1)S(1)}, bf16[16,6,1,512]{3,0,2,1:T(8,128)(2,1)S(1)}, u32[]{:S(2)}, u32[]{:S(2)}) collective-permute-start(bf16[16,6,1,512]{3,0,2,1:T(8,128)(2,1)S(1)} %get-tuple-element.44), channel_id=1, source_target_pairs={{1,0},{2,1},{3,2},{5,4},{6,5},{7,6},{9,8},{10,9},{11,10},{13,12},{... | collective-permute-start | bytes 294920 | tf_op jit(solution)/shard_map/ppermute | solution.py:19
  136.2 4.9 %collective-permute-start.2 = (bf16[16,6,1,512]{3,0,2,1:T(8,128)(2,1)S(1)}, bf16[16,6,1,512]{3,0,2,1:T(8,128)(2,1)S(1)}, u32[]{:S(2)}, u32[]{:S(2)}) collective-permute-start(bf16[16,6,1,512]{3,0,2,1:T(8,128)(2,1)S(1)} %get-tuple-element.43), channel_id=1, source_target_pairs={{0,1},{1,2},{2,3},{4,5},{5,6},{6,7},{8,9},{9,10},{10,11},{12,13},{... | collective-permute-start | bytes 294920 | tf_op jit(solution)/shard_map/ppermute | solution.py:17
  145.0 2.2 copy-start
  145.1 3.6 %copy-start.1 = (bf16[144,4,8,512]{3,0,2,1:T(8,128)(2,1)}, bf16[144,4,8,512]{3,0,2,1:T(8,128)(2,1)S(1)}, u32[]{:S(2)}) copy-start(bf16[144,4,8,512]{3,0,2,1:T(8,128)(2,1)S(1)} %get-tuple-element.16) | copy-start | bytes 14155780
  147.2 2.2 copy-start.6
Sparse Core Ops, SparseCore 0:
  55.4 21.4 reduce-scatter.1
Sparse Core Ops, SparseCore 1:
  60.0 252.3 all-reduce.5
where the time goes:
time: 329 us; the launch traced here: 327 us
  waiting for transfers between devices  89.6 us (27%)
  local copies, waits for them, and re-layouts  84.1 us (26%)
  blocking collectives  75.6 us (23%)
  matrix products  34.8 us (11%)
  starting transfers between devices  22.5 us (7%)
  between operations  16.4 us (5%)
  other arithmetic  4.27 us (1%)
    psum x1, waiting for transfers between devices, shards(): bott_wgrad = lax.psum(jnp.stack(terms, axis=1), 'space')  82 us
    psum x1, blocking collectives, shards(): lax.psum(jnp.concatenate(fine_blocks, axis=0), ('space', 'chan'))  67.1 us
    gather x2, local copies, waits for them, and re-layouts, shards(): features = jnp.take(lookup, shifted_ids, axis=1)  60.9 us
    unnamed x30, local copies, waits for them, and re-layouts  21.5 us
    ppermute x4, starting transfers between devices, with_halo(): lax.ppermute(tail, axis, [(i, (i + 1) % count) for i in range(ends)])  16.2 us
    dot_general x27, matrix products, shards(): jnp.einsum('cpv,opv->oc', source, bott_delta, preferred_element_type=jnp....  9.18 us
    dot_general x3, matrix products, shards(): jnp.einsum('kxyw,oxyw->ko', stacked, fine_delta, preferred_element_type=j...  8.78 us
    all_gather x1, blocking collectives, shards(): slabs = lax.all_gather(framed_in, 'chan', axis=0, tiled=True)  8.54 us
  transfers between devices with their start and end apart: 10, of which 2 were waited for; matrix products, arithmetic and copies ran while one was open for 28% of the time, Pallas kernels for 0%

commit v1 on v0

v1 whole, which is shorter than its diff:
```python
import functools
import jax
import jax.numpy as jnp
import numpy as np
from jax import lax
from jax.experimental import pallas as pl
from jax.experimental.pallas import tpu as pltpu
from jax.sharding import PartitionSpec as P

BW = 32
F32 = jnp.float32
BF16 = jnp.bfloat16
VM = pl.BlockSpec(memory_space=pltpu.VMEM)
HB = pl.BlockSpec(memory_space=pl.ANY)


def silu_parts(pre):
    s = jax.nn.sigmoid(pre)
    return pre * s, s * (1.0 + pre * (1.0 - s))


def dot_nt(a, b):
    return lax.dot_general(a, b, (((1,), (1,)), ((), ())), preferred_element_type=F32)


def call(body, outs, specs, scratch, flops, nbytes, mb, out_specs=None):
    return pl.pallas_call(
        body,
        out_shape=outs,
        in_specs=specs,
        out_specs=out_specs if out_specs is not None else [VM] * len(outs),
        scratch_shapes=scratch,
        compiler_params=pltpu.CompilerParams(vmem_limit_bytes=mb << 20),
        cost_estimate=pl.CostEstimate(flops=int(flops), bytes_accessed=int(nbytes), transcendentals=0),
    )


def fine_body(scale, own, below, above, left, right, table, kernel, cot, out, part, feats, grads):
    depth, rows, cols = own.shape
    ch = table.shape[0] // 8
    place, count = lax.axis_index("space"), lax.axis_size("space")
    lane, lanes = lax.axis_index("chan"), lax.axis_size("chan")
    key = lax.broadcasted_iota(jnp.int32, (128, cols), 0)
    for x in range(depth + 2):
        for y in range(rows + 2):
            if y == 0:
                ids = left[x]
                ids = jnp.where(lane == 0, 1024, ids)
            elif y == rows + 1:
                ids = right[x]
                ids = jnp.where(lane == lanes - 1, 1024, ids)
            elif x == 0:
                ids = below[0, y - 1 : y]
            elif x == depth + 1:
                ids = above[0, y - 1 : y]
            else:
                ids = own[x - 1, y - 1 : y]
            if x == 0:
                ids = jnp.where(place == 0, 1024, ids)
            if x == depth + 1:
                ids = jnp.where(place == count - 1, 1024, ids)
            low = (ids & 127) | ((ids >> 3) & 128)
            hot = (key == low).astype(F32).astype(BF16)
            picked = jnp.dot(table[...], hot, preferred_element_type=F32)
            for bit in (9, 8, 7):
                half = picked.shape[0] // 2
                picked = jnp.where(((ids >> bit) & 1) == 1, picked[half:], picked[:half])
            at = (x * (rows + 2) + y) * ch
            feats[at : at + ch, :] = picked.astype(BF16)
    group = ch * rows
    step = (rows + 2) * ch
    w = lax.broadcasted_iota(jnp.int32, (1, cols), 1)
    first, last = w == 0, w == cols - 1
    for x in range(depth):
        window = feats[x * step : (x + 3) * step, :]
        q = jnp.dot(kernel[...], window, preferred_element_type=F32)
        pre = q[group : 2 * group]
        pre = pre + jnp.where(first, 0.0, pltpu.roll(q[:group], 1, 1))
        pre = pre + jnp.where(last, 0.0, pltpu.roll(q[2 * group :], cols - 1, 1))
        act, slope = silu_parts(pre)
        out[:, x] = act.reshape(ch, rows, cols).astype(BF16)
        delta = cot[:, x].astype(F32).reshape(group, cols) * slope
        shifted = jnp.concatenate(
            [
                jnp.where(last, 0.0, pltpu.roll(delta, cols - 1, 1)).astype(BF16),
                delta.astype(BF16),
                jnp.where(first, 0.0, pltpu.roll(delta, 1, 1)).astype(BF16),
            ],
            axis=0,
        )
        term = dot_nt(shifted, window)
        grads[...] = term if x == 0 else grads[...] + term
    total = grads[...]
    wide = total.shape[1]
    y_out = lax.broadcasted_iota(jnp.int32, total.shape, 0) % rows
    y_in = (lax.broadcasted_iota(jnp.int32, total.shape, 1) % step) // ch
    fold_from = lax.broadcasted_iota(jnp.int32, (wide, 3 * ch), 0)
    fold_to = lax.broadcasted_iota(jnp.int32, (wide, 3 * ch), 1)
    fold = ((fold_from // step == fold_to // ch) & (fold_from % ch == fold_to % ch)).astype(F32).astype(BF16)
    for b in range(3):
        kept = jnp.where(y_in - y_out == b, total, 0.0)
        kept = kept.reshape(3 * ch, rows, wide).sum(axis=1)
        high = kept.astype(BF16)
        rest = kept - high.astype(F32)
        middle = rest.astype(BF16)
        lowest = (rest - middle.astype(F32)).astype(BF16)
        folded = jnp.dot(high, fold, preferred_element_type=F32)
        folded = folded + jnp.dot(middle, fold, preferred_element_type=F32)
        folded = folded + jnp.dot(lowest, fold, preferred_element_type=F32)
        part[b] = folded * scale


def fine_call(scale, own, below, above, left, right, table, kernel, cot):
    depth, rows, cols = own.shape
    ch = table.shape[0] // 8
    body = functools.partial(fine_body, scale)
    macs = 3 * ch * rows * 3 * ch * (rows + 2) * cols * depth * 2
    return call(
        body,
        [
            jax.ShapeDtypeStruct((ch, depth, rows, cols), BF16),
            jax.ShapeDtypeStruct((3, 3 * ch, 3 * ch), F32),
        ],
        [VM] * 8,
        [
            pltpu.VMEM(((depth + 2) * (rows + 2) * ch, cols), BF16),
            pltpu.VMEM((3 * ch * rows, 3 * ch * (rows + 2)), F32),
        ],
        2 * macs,
        4 << 20,
        24,
    )(own, below, above, left, right, table, kernel, cot)


def shift_masks(width, sign):
    lane = lax.broadcasted_iota(jnp.int32, (1, width), 1)
    y, w = lane // BW, lane % BW
    masks = []
    for b in (-1, 0, 1):
        for e in (-1, 0, 1):
            yy, ww = y + sign * b, w + sign * e
            masks.append((yy >= 0) & (yy < width // BW) & (ww >= 0) & (ww < BW))
    return masks


def bott_body(pieces, *refs):
    weight, cots = refs[0], refs[1]
    ins = refs[2 : 2 + pieces]
    own_out, delta_out, full, share, mine, padded, deltas, rows_t, sums = refs[2 + pieces :]
    slabs, cb, lanes = ins[0].shape
    planes = own_out.shape[1]
    width = lanes // planes
    c_all = cb * pieces
    o_own = own_out.shape[0]
    total = slabs * planes
    place = lax.axis_index("space")
    chan = lax.axis_index("chan")
    padded[:, :width] = jnp.zeros((c_all, width), BF16)
    padded[:, (total + 1) * width :] = jnp.zeros((c_all, width), BF16)
    for j in range(pieces):
        row = pl.multiple_of((chan ^ j) * cb, cb)
        for r in range(slabs):
            slab = lax.rem(place - r + slabs, slabs)
            at = pl.multiple_of(slab * lanes + width, width)
            padded[pl.ds(row, cb), pl.ds(at, lanes)] = ins[j][r]
    full[...] = padded[:, width : (total + 1) * width]
    deltas[:, :width] = jnp.zeros((o_own, width), F32)
    deltas[:, (total + 1) * width :] = jnp.zeros((o_own, width), F32)
    masks = shift_masks(width, 1)
    for n in range(slabs):
        base = n * lanes
        for a in range(3):
            win = padded[:, base + a * width : base + a * width + lanes]
            term = jnp.dot(weight[a * 9 * o_own : (a + 1) * 9 * o_own, :], win, preferred_element_type=F32)
            sums[...] = term if a == 0 else sums[...] + term
        cot = cots[lax.rem(place - n + slabs, slabs)].astype(F32)
        for p in range(planes):
            pre = jnp.zeros((o_own, width), F32)
            for k, (b, e) in enumerate([(b, e) for b in (-1, 0, 1) for e in (-1, 0, 1)]):
                block = sums[k * o_own : (k + 1) * o_own, p * width : (p + 1) * width]
                turn = -(b * BW + e) % width
                if turn:
                    block = jnp.where(masks[k], pltpu.roll(block, turn, 1), 0.0)
                pre = pre + block
            act, slope = silu_parts(pre)

            @pl.when(n == place)
            def _():
                own_out[:, p, :] = act.astype(BF16)

            delta = (cot[:, p * width : (p + 1) * width] * slope).astype(BF16).astype(F32)
            at = base + (p + 1) * width
            deltas[:, at : at + width] = delta
    delta_out[...] = deltas[:, width : (total + 1) * width]
    near = (planes + 2) * width
    turned = deltas[:, pl.ds(pl.multiple_of(place * lanes, width), near)].T
    w = lax.broadcasted_iota(jnp.int32, (near, 1), 0) % BW
    gap = width + 2 * BW
    for e in (-1, 0, 1):
        moved = turned
        if e:
            moved = jnp.where((w - e >= 0) & (w - e < BW), pltpu.roll(turned, e % near, 0), 0.0)
        moved = moved.astype(BF16)
        for p in range(planes + 2):
            rows_t[e + 1, p * gap : p * gap + BW, :] = jnp.zeros((BW, o_own), BF16)
            rows_t[e + 1, p * gap + BW : p * gap + BW + width, :] = moved[p * width : (p + 1) * width]
            rows_t[e + 1, p * gap + BW + width : (p + 1) * gap, :] = jnp.zeros((BW, o_own), BF16)
    blocks = []
    for a in (-1, 0, 1):
        for b in (-1, 0, 1):
            for e in (-1, 0, 1):
                per_plane = []
                for p in range(planes):
                    start = (1 + p - a) * gap + BW - b * BW
                    per_plane.append(rows_t[e + 1, start : start + width, :])
                blocks.append(jnp.concatenate(per_plane, axis=0))
    left = jnp.concatenate(blocks, axis=1)
    back = jnp.dot(left, weight[...], preferred_element_type=F32)
    for j in range(pieces):
        block = back[:, j * cb : (j + 1) * cb]
        to = lax.rem(j - chan + pieces, pieces)
        share[to] = block.astype(BF16)

        @pl.when(chan == j)
        def _():
            mine[...] = block


def bott_call(weight, cots, ins, planes):
    slabs, cb, lanes = ins[0].shape
    pieces = len(ins)
    o_own = cots.shape[1]
    c_all = pieces * cb
    width = lanes // planes
    total = slabs * planes
    S = jax.ShapeDtypeStruct
    macs = 27 * o_own * c_all * (total + planes) * width
    return call(
        functools.partial(bott_body, pieces),
        [
            S((o_own, planes, width), BF16),
            S((o_own, total * width), F32),
            S((c_all, total * width), BF16),
            S((pieces, lanes, cb), BF16),
            S((lanes, cb), F32),
        ],
        [VM] * (2 + pieces),
        [
            pltpu.VMEM((c_all, (total + 2) * width), BF16),
            pltpu.VMEM((o_own, (total + 2) * width), F32),
            pltpu.VMEM((3, (planes + 2) * (width + 2 * BW), o_own), BF16),
            pltpu.VMEM((9 * o_own, lanes), F32),
        ],
        2 * macs,
        8 << 20,
        32,
    )(weight, cots, *ins)


def wgrad_body(scale, delta, full, out, shifted, stage, sems):
    o_own, length = delta.shape
    c_all = full.shape[0]
    width = 4 * BW
    total = length // width
    masks = shift_masks(width, -1)
    shifted[:, :width] = jnp.zeros((9 * o_own, width), BF16)
    shifted[:, (total + 1) * width :] = jnp.zeros((9 * o_own, width), BF16)
    for p in range(total):
        block = delta[:, p * width : (p + 1) * width]
        for k, (b, e) in enumerate([(b, e) for b in (-1, 0, 1) for e in (-1, 0, 1)]):
            turn = (b * BW + e) % width
            moved = jnp.where(masks[k], pltpu.roll(block, turn, 1), 0.0) if turn else block
            shifted[k * o_own : (k + 1) * o_own, (p + 1) * width : (p + 2) * width] = moved.astype(BF16)
    chunk = stage.shape[3]
    copies = []
    for n in range(c_all // chunk):
        slot = n % 2
        if n >= 2:
            copies[n - 2].wait()
        right = full[n * chunk : (n + 1) * chunk, :]
        for a in range(3):
            left = shifted[:, (2 - a) * width : (2 - a) * width + length]
            term = dot_nt(left, right) * scale
            for k in range(9):
                stage[slot, :, a * 9 + k, :] = term[k * o_own : (k + 1) * o_own, :]
        copy = pltpu.make_async_copy(stage.at[slot], out.at[:, :, pl.ds(n * chunk, chunk)], sems.at[slot])
        copy.start()
        copies.append(copy)
    for copy in copies[-2:]:
        copy.wait()


def wgrad_call(scale, delta, full, chunk=256):
    o_own, length = delta.shape
    c_all = full.shape[0]
    width = 4 * BW
    total = length // width
    return call(
        functools.partial(wgrad_body, scale),
        [jax.ShapeDtypeStruct((o_own, 27, c_all), F32)],
        [VM] * 2,
        [
            pltpu.VMEM((9 * o_own, (total + 2) * width), BF16),
            pltpu.VMEM((2, o_own, 27, chunk), F32),
            pltpu.SemaphoreType.DMA((2,)),
        ],
        2 * 27 * o_own * c_all * length,
        8 << 20,
        40,
        [HB],
    )(delta, full)[0]


def last_body(count, *refs):
    mine, others, out = refs[0], refs[1 : 1 + count], refs[1 + count]
    total = mine[...]
    for other in others:
        total = total + other[...].astype(F32)
    turned = total.T
    planes = out.shape[1]
    width = turned.shape[1] // planes
    for p in range(planes):
        out[:, p, :] = turned[:, p * width : (p + 1) * width].astype(BF16)


def last_call(mine, others, planes):
    lanes, cb = mine.shape
    return call(
        functools.partial(last_body, len(others)),
        [jax.ShapeDtypeStruct((cb, planes, lanes // planes), BF16)],
        [VM] * (1 + len(others)),
        [],
        lanes * cb * 4,
        lanes * cb * 12,
        16,
    )(mine, *others)[0]


def hop(x, axis, offset):
    count = lax.axis_size(axis)
    return lax.ppermute(x, axis, [(i, (i + offset) % count) for i in range(count)])


def swap(x, axis, bit):
    count = lax.axis_size(axis)
    return lax.ppermute(x, axis, [(i, i ^ bit) for i in range(count)])


def shards(labels, table, fine_weight, fine_cot, bott_in, bott_weight, bott_cot):
    depth, rows, cols = labels.shape
    ch = fine_weight.shape[2]
    spaces, chans = lax.axis_size("space"), lax.axis_size("chan")
    cb, planes, width = bott_in.shape
    lanes = planes * width
    o_own = bott_cot.shape[0]

    below = hop(labels[-1:], "space", 1)
    above = hop(labels[:1], "space", spaces - 1)
    slab = bott_in.reshape(cb, lanes)
    slabs = jnp.stack([slab] + [hop(slab, "space", r) for r in range(1, spaces)])
    framed = jnp.concatenate([below, labels, above], axis=0)
    left = hop(framed[:, -1:], "chan", 1)
    right = hop(framed[:, :1], "chan", chans - 1)
    pieces = {0: slabs}
    bits = [1 << i for i in range(chans.bit_length() - 1)]
    for bit in bits[1:] + bits[:1]:
        pieces.update({j ^ bit: swap(x, "chan", bit) for j, x in list(pieces.items())})
    ins = [pieces[j] for j in range(chans)]
    cot = bott_cot.reshape(o_own, lanes)
    cots = jnp.stack([cot] + [hop(cot, "space", r) for r in range(1, spaces)])

    lookup = table.reshape(8, 128, ch).transpose(0, 2, 1).reshape(8 * ch, 128)
    taps = fine_weight.reshape(3, 3, 3, ch, ch)
    band = np.zeros((3, rows, rows + 2), np.float32)
    for b in range(3):
        for y in range(rows):
            band[b, y, y + b] = 1
    kernel = sum(
        taps[:, b].transpose(1, 3, 0, 2)[:, :, None, :, None, :] * band[b][None, None, :, None, :, None].astype(BF16)
        for b in range(3)
    ).reshape(3 * ch * rows, 3 * (rows + 2) * ch)
    scale = (depth * spaces * rows * chans * cols) ** -0.5
    fine_out, part = fine_call(scale, labels, below, above, left, right, lookup, kernel, fine_cot)
    part = part + sum(hop(part, "chan", r) for r in range(1, chans))
    part = part + sum(hop(part, "space", r) for r in range(1, spaces))
    fine_wgrad = part.reshape(3, 3, ch, 3, ch).transpose(3, 0, 1, 4, 2).reshape(27, ch, ch)

    weight = bott_weight.transpose(1, 0, 2).reshape(27 * o_own, cb * chans)
    bott_out, delta, full, share, mine = bott_call(weight, cots, ins, planes)
    others = [hop(share[r], "chan", r) for r in range(1, chans)]
    bott_wgrad = wgrad_call((planes * spaces * width) ** -0.5, delta, full)
    bott_dgrad = last_call(mine, others, planes)
    return fine_out, fine_wgrad, bott_out, bott_dgrad, bott_wgrad


def solution(mesh):
    placed = (
        P(("groups", "space"), "chan", None),
        P(),
        P(),
        P(None, ("groups", "space"), "chan", None),
        P("chan", ("groups", "space"), None),
        P("chan", None, None),
        P("chan", ("groups", "space"), None),
    )
    return jax.shard_map(
        shards,
        mesh=mesh,
        in_specs=placed,
        out_specs=(
            P(None, ("groups", "space"), "chan", None),
            P("groups", None, None),
            P("chan", ("groups", "space"), None),
            P("chan", ("groups", "space"), None),
            P(("groups", "chan"), None, None),
        ),
        check_vma=False,
    )
```

time: 329 us -> 86.8 us (0.26)
  waiting for transfers between devices: 89.6 us -> 7.68 us
  blocking collectives: 75.6 us -> 0 us
  local copies, waits for them, and re-layouts: 84.1 us -> 18.7 us
  matrix products: 34.8 us -> 0 us
  Pallas kernels: 0 us -> 29.4 us
  between operations: 16.4 us -> 0.88 us
  starting transfers between devices: 22.5 us -> 25.8 us
    psum x1 -> x0, waiting for transfers between devices: 82 us -> none  [shards(): bott_wgrad = lax.psum(jnp.stack(terms, axis=1), 'space')]
    psum x1 -> x0, blocking collectives: 67.1 us -> none  [shards(): lax.psum(jnp.concatenate(fine_blocks, axis=0), ('space', 'chan'))]
    gather x2 -> x0, local copies, waits for them, and re-layouts: 60.9 us -> none  [shards(): features = jnp.take(lookup, shifted_ids, axis=1)]
    dot_general x87 -> x0, matrix products: 34.8 us -> none  [the longest x27 9.18 us: shards(): jnp.einsum('cpv,opv->oc', source, bott_delta, preferred_element_type=jnp....]
    pallas_call x0 -> x4, Pallas kernels: none -> 29.4 us  [the longest x1 11.3 us: bott_call(): call(functools.partial(bott_body, pieces), [S((o_own, planes, width), BF1...]
    unnamed x30 -> x19, local copies, waits for them, and re-layouts: 21.5 us -> 11.9 us
    all_gather x1 -> x0, blocking collectives: 8.54 us -> none  [shards(): slabs = lax.all_gather(framed_in, 'chan', axis=0, tiled=True)]
    add x0 -> x1, local copies, waits for them, and re-layouts: none -> 5.34 us  [shards(): sum((taps[:, b].transpose(1, 3, 0, 2)[:, :, None, :, None, :] * band[b][N...]
  transfers between devices with their start and end apart: 10 -> 22, of which waited for: 2 -> 4; matrix products, arithmetic and copies ran while one was open for 28% -> 23% of each run, Pallas kernels for 0% -> 20%
where the time goes in v1:
time: 86.8 us; the launch traced here: 86.4 us
  Pallas kernels  29.4 us (34%)
  starting transfers between devices  25.8 us (30%)
  local copies, waits for them, and re-layouts  18.7 us (22%)
  waiting for transfers between devices  7.68 us (9%)
  other arithmetic  4.02 us (5%)
  between operations  0.88 us (1%)
    ppermute x19, starting transfers between devices, hop(): lax.ppermute(x, axis, [(i, (i + offset) % count) for i in range(count)])  23.7 us
    unnamed x19, local copies, waits for them, and re-layouts  11.9 us
    pallas_call x1, Pallas kernels, bott_call(): call(functools.partial(bott_body, pieces), [S((o_own, planes, width), BF1...  11.3 us
    pallas_call x1, Pallas kernels, wgrad_call(): call(functools.partial(wgrad_body, scale), [jax.ShapeDtypeStruct((o_own,...  8.81 us
    pallas_call x1, Pallas kernels, fine_call(): call(body, [jax.ShapeDtypeStruct((ch, depth, rows, cols), BF16), jax.Shap...  8.38 us
    ppermute x19, waiting for transfers between devices, hop(): lax.ppermute(x, axis, [(i, (i + offset) % count) for i in range(count)])  7.67 us
    add x1, local copies, waits for them, and re-layouts, shards(): sum((taps[:, b].transpose(1, 3, 0, 2)[:, :, None, :, None, :] * band[b][N...  5.34 us
    add x1, other arithmetic, shards(): sum((taps[:, b].transpose(1, 3, 0, 2)[:, :, None, :, None, :] * band[b][N...  3.91 us
  transfers between devices with their start and end apart: 22, of which 4 were waited for; matrix products, arithmetic and copies ran while one was open for 23% of the time, Pallas kernels for 20%

profile of v1, /device:TPU:1, one launch (start us, length us, event | category | flops | bytes accessed | tf_op | source)
XLA Modules:
  0.0 86.4 jit_solution(9315482894378501341)
XLA Ops:
  0.6 0.0 copy-start
  0.7 0.9 %copy.35 = bf16[16,8,2,128]{3,1,2,0:T(8,128)(2,1)S(1)} copy(bf16[16,8,2,128]{3,2,1,0:T(2,128)(2,1)} %bitcast.51) | data formatting | bytes 131072
  1.6 4.2 %collective-permute-start.15 = (bf16[128,256]{1,0:T(8,128)(2,1)S(1)}, bf16[128,256]{1,0:T(8,128)(2,1)S(1)}, u32[]{:S(2)}, u32[]{:S(2)}) collective-permute-start(bf16[128,256]{1,0:T(8,128)(2,1)S(1)} %bitcast.53), channel_id=1, source_target_pairs={{0,12},{4,0},{8,4},{12,8},{1,13},{5,1},{9,5},{13,9},{2,14},{6,2},{... | collective-permute-start | bytes 196616 | tf_op jit(solution)/shard_map/ppermute | solution.py:341
  5.8 0.0 collective-permute-start.14
  5.8 0.5 collective-permute-start.13
  6.2 0.7 fusion.1
  7.0 2.8 %collective-permute-start.1 = (s32[1,8,512]{2,1,0:T(8,128)S(1)}, s32[1,8,512]{2,1,0:T(8,128)S(1)}, u32[]{:S(2)}, u32[]{:S(2)}) collective-permute-start(s32[1,8,512]{2,1,0:T(8,128)S(1)} %get-tuple-element.37), channel_id=1, source_target_pairs={{0,12},{4,0},{8,4},{12,8},{1,13},{5,1},{9,5},{13,9},{2,14},{6,2},{... | collective-permute-start | bytes 49160 | tf_op jit(solution)/shard_map/ppermute | solution.py:341
  9.8 0.0 collective-permute-start
  9.8 1.0 %copy.22 = bf16[27,16,16]{2,1,0:T(8,128)(2,1)S(1)} copy(bf16[27,16,16]{0,2,1:T(8,128)(2,1)} %param.12) | data formatting | bytes 27648 | tf_op args[2]
  10.8 0.1 copy.23
  10.9 0.1 copy.25
  11.0 0.1 copy.24
  11.2 0.0 copy-start.1
  11.2 0.0 copy-start.3
  11.2 3.9 %multiply_add_fusion = bf16[3,16,8,3,10,16]{5,4,3,2,1,0:T(8,128)(2,1)} fusion(bf16[8,10]{1,0:T(8,128)(2,1)} %constant.15, bf16[3,16,3,16]{3,2,1,0:T(4,128)(2,1)S(1)} %copy.25, bf16[8,10]{1,0:T(8,128)(2,1)} %constant.14, bf16[3,16,3,16]{3,2,1,0:T(4,128)(2,1)S(1)} %copy.24, bf16[8,10]{1,0:T(8,128)(2,1)} %constant.13, bf16[3,16,3,16]{3,2,1,0:T(4,128)(2,1)S(1)} %copy.23), kind=kLoop, calls=%fused_computation | loop fusion | flops 921600 | bytes 382944 | tf_op jit(solution)/shard_map/add | solution.py:378
  15.2 0.0 copy-start.5
  15.2 5.3 %add.32.kernel = bf16[384,480]{1,0:T(8,128)(2,1)S(1)} reshape(bf16[3,16,8,3,10,16]{5,4,3,2,1,0:T(8,128)(2,1)} %multiply_add_fusion) | data formatting | bytes 737280 | tf_op jit(solution)/shard_map/add | solution.py:378
  20.5 0.0 collective-permute-done.below
  20.6 0.0 collective-permute-done.1.above
  20.6 1.6 %collective-permute-start.3 = (s32[6,1,512]{2,1,0:T(1,128)S(1)}, s32[6,1,512]{2,1,0:T(1,128)S(1)}, u32[]{:S(2)}, u32[]{:S(2)}) collective-permute-start(s32[6,1,512]{2,1,0:T(1,128)S(1)} %get-tuple-element.35), channel_id=1, source_target_pairs={{0,3},{1,0},{2,1},{3,2},{4,7},{5,4},{6,5},{7,6},{8,11},{9,8},{10,9... | collective-permute-start | bytes 36872 | tf_op jit(solution)/shard_map/ppermute | solution.py:341
  22.2 1.2 %collective-permute-start.2 = (s32[6,1,512]{2,1,0:T(1,128)S(1)}, s32[6,1,512]{2,1,0:T(1,128)S(1)}, u32[]{:S(2)}, u32[]{:S(2)}) collective-permute-start(s32[6,1,512]{2,1,0:T(1,128)S(1)} %get-tuple-element.36), channel_id=1, source_target_pairs={{0,1},{1,2},{2,3},{3,0},{4,5},{5,6},{6,7},{7,4},{8,9},{9,10},{10,1... | collective-permute-start | bytes 36872 | tf_op jit(solution)/shard_map/ppermute | solution.py:341
  23.4 0.0 collective-permute-done.15
  23.4 0.0 collective-permute-done.14
  23.4 0.0 collective-permute-done.13
  23.4 0.3 collective-permute-start.17
  23.8 1.3 %collective-permute-done.3.right = s32[6,1,512]{2,1,0:T(1,128)S(1)} collective-permute-done((s32[6,1,512]{2,1,0:T(1,128)S(1)}, s32[6,1,512]{2,1,0:T(1,128)S(1)}, u32[]{:S(2)}, u32[]{:S(2)}) %collective-permute-start.3) | collective-permute-done | bytes 12320 | tf_op jit(solution)/shard_map/ppermute | solution.py:341
  25.0 0.0 collective-permute-done.2.left
  25.1 8.4 %shard_map.137 = (bf16[16,4,8,512]{3,2,1,0:T(8,128)(2,1)}, f32[3,48,48]{2,1,0:T(8,128)S(1)}) custom-call(s32[4,8,512]{2,1,0:T(8,128)S(1)} %copy-done.1, s32[1,8,512]{2,1,0:T(8,128)S(1)} %collective-permute-done.below, s32[1,8,512]{2,1,0:T(8,128)S(1)} %collective-permute-done.1.above, s32[6,1,512]{2,1,0:T(1,128)S(1)} %collective-permute-done.2.left, ...), custom_call_target="tpu_custom_call" | custom-call | flops 1509949440 | bytes 4194304 | tf_op jit(solution)/shard_map/pallas_call | solution.py:118
  33.4 0.5 collective-permute-start.6
  33.9 1.1 %collective-permute-start.5 = (f32[3,48,48]{2,1,0:T(8,128)S(1)}, f32[3,48,48]{2,1,0:T(8,128)S(1)}, u32[]{:S(2)}, u32[]{:S(2)}) collective-permute-start(f32[3,48,48]{2,1,0:T(8,128)S(1)} %get-tuple-element.13), channel_id=1, source_target_pairs={{0,2},{1,3},{2,0},{3,1},{4,6},{5,7},{6,4},{7,5},{8,10},{9,11},{10,... | collective-permute-start | bytes 82952 | tf_op jit(solution)/shard_map/ppermute | solution.py:341
  35.0 0.6 collective-permute-start.4
  35.6 3.6 %collective-permute-start.12 = (bf16[128,256]{1,0:T(8,128)(2,1)S(1)}, bf16[128,256]{1,0:T(8,128)(2,1)S(1)}, u32[]{:S(2)}, u32[]{:S(2)}) collective-permute-start(bf16[128,256]{1,0:T(8,128)(2,1)S(1)} %bitcast.56), channel_id=1, source_target_pairs={{0,12},{4,0},{8,4},{12,8},{1,13},{5,1},{9,5},{13,9},{2,14},{6,2},{... | collective-permute-start | bytes 196616 | tf_op jit(solution)/shard_map/ppermute | solution.py:341
  39.3 0.0 collective-permute-done.6
  39.3 0.1 collective-permute-start.11
  39.4 0.0 collective-permute-done.5
  39.4 2.4 %collective-permute-start.10 = (bf16[128,256]{1,0:T(8,128)(2,1)S(1)}, bf16[128,256]{1,0:T(8,128)(2,1)S(1)}, u32[]{:S(2)}, u32[]{:S(2)}) collective-permute-start(bf16[128,256]{1,0:T(8,128)(2,1)S(1)} %bitcast.58), channel_id=1, source_target_pairs={{0,4},{4,8},{8,12},{12,0},{1,5},{5,9},{9,13},{13,1},{2,6},{6,10},{... | collective-permute-start | bytes 196616 | tf_op jit(solution)/shard_map/ppermute | solution.py:341
  41.7 0.0 collective-permute-done.4
  41.8 1.0 %collective-permute-start.9 = (f32[3,48,48]{2,1,0:T(8,128)S(1)}, f32[3,48,48]{2,1,0:T(8,128)S(1)}, u32[]{:S(2)}, u32[]{:S(2)}) collective-permute-start(f32[3,48,48]{2,1,0:T(8,128)S(1)} %add_add_fusion.1), channel_id=1, source_target_pairs={{0,12},{4,0},{8,4},{12,8},{1,13},{5,1},{9,5},{13,9},{2,14},{6,2},{... | collective-permute-start | bytes 82952 | tf_op jit(solution)/shard_map/ppermute | solution.py:341
  42.8 0.0 collective-permute-done.12
  42.8 0.5 collective-permute-start.8
  43.3 2.0 %collective-permute-done.11 = bf16[128,256]{1,0:T(8,128)(2,1)S(1)} collective-permute-done((bf16[128,256]{1,0:T(8,128)(2,1)S(1)}, bf16[128,256]{1,0:T(8,128)(2,1)S(1)}, u32[]{:S(2)}, u32[]{:S(2)}) %collective-permute-start.11) | collective-permute-done | bytes 65568 | tf_op jit(solution)/shard_map/ppermute | solution.py:341
  45.2 0.0 collective-permute-start.7
  45.3 0.0 collective-permute-done.10
  45.3 1.7 %collective-permute-start.16 = (bf16[4,128,256]{2,1,0:T(8,128)(2,1)S(1)}, bf16[4,128,256]{2,1,0:T(8,128)(2,1)S(1)}, u32[]{:S(2)}, u32[]{:S(2)}) collective-permute-start(bf16[4,128,256]{2,1,0:T(8,128)(2,1)S(1)} %pad_maximum_fusion.1.refs_2_), channel_id=1, source_target_pairs={{0,1},{1,0},{2,3},{3,2},{4,5},{5,4},{6,7},{7,6},{8,9},{9,8},{10,11... | collective-permute-start | bytes 786440 | tf_op jit(solution)/shard_map/ppermute | solution.py:346
  46.9 0.1 collective-permute-start.18
  47.1 0.7 collective-permute-done.9
  47.7 3.7 %collective-permute-done.8 = f32[3,48,48]{2,1,0:T(8,128)S(1)} collective-permute-done((f32[3,48,48]{2,1,0:T(8,128)S(1)}, f32[3,48,48]{2,1,0:T(8,128)S(1)}, u32[]{:S(2)}, u32[]{:S(2)}) %collective-permute-start.8) | collective-permute-done | bytes 27680 | tf_op jit(solution)/shard_map/ppermute | solution.py:341
  51.4 0.0 collective-permute-done.7
  51.4 0.2 reshape.52
  51.6 0.1 copy.26
  51.7 0.8 copy.27
  52.6 0.0 collective-permute-done.16.refs_3_
  52.6 0.0 collective-permute-done.18.refs_5_
  52.6 2.0 %copy-done.2 = bf16[128,27,512]{2,0,1:T(8,128)(2,1)S(1)} copy-done((bf16[128,27,512]{2,0,1:T(8,128)(2,1)S(1)}, bf16[128,27,512]{2,0,1:T(8,128)(2,1)}, u32[]{:S(2)}) %copy-start.2) | copy-done | bytes 3538968
  54.6 11.3 %shard_map.138 = (bf16[128,2,128]{2,1,0:T(2,128)(2,1)}, f32[128,1024]{1,0:T(8,128)S(1)}, bf16[512,1024]{1,0:T(8,128)(2,1)S(1)}, bf16[4,256,128]{2,1,0:T(8,128)(2,1)S(1)}, f32[256,128]{1,0:T(8,128)S(1)}) custom-call(bf16[3456,512]{1,0:T(8,128)(2,1)S(1)} %bitcast.47, bf16[4,128,256]{2,1,0:T(8,128)(2,1)S(1)} %pad_maximum_fusion.refs_1_, ...), custom_call_target="tpu_custom_call" | custom-call | flops 4529848320 | bytes 8388608 | tf_op jit(solution)/shard_map/pallas_call | solution.py:238
  65.9 1.7 %collective-permute-start.21 = (bf16[256,128]{1,0:T(8,128)(2,1)S(1)}, bf16[256,128]{1,0:T(8,128)(2,1)S(1)}, u32[]{:S(2)}, u32[]{:S(2)}) collective-permute-start(bf16[256,128]{1,0:T(8,128)(2,1)S(1)} %get-tuple-element.29), channel_id=1, source_target_pairs={{0,3},{1,0},{2,1},{3,2},{4,7},{5,4},{6,5},{7,6},{8,11},{9,8},{10,9... | collective-permute-start | bytes 196616 | tf_op jit(solution)/shard_map/ppermute | solution.py:341
  67.6 0.5 collective-permute-start.20
  68.1 1.6 %collective-permute-start.19 = (bf16[256,128]{1,0:T(8,128)(2,1)S(1)}, bf16[256,128]{1,0:T(8,128)(2,1)S(1)}, u32[]{:S(2)}, u32[]{:S(2)}) collective-permute-start(bf16[256,128]{1,0:T(8,128)(2,1)S(1)} %get-tuple-element.31), channel_id=1, source_target_pairs={{0,1},{1,2},{2,3},{3,0},{4,5},{5,6},{6,7},{7,4},{8,9},{9,10},{10,1... | collective-permute-start | bytes 196616 | tf_op jit(solution)/shard_map/ppermute | solution.py:341
  69.7 8.8 %shard_map.140 = f32[128,27,512]{2,1,0:T(8,128)S(1)} custom-call(f32[128,1024]{1,0:T(8,128)S(1)} %get-tuple-element.17.delta, bf16[512,1024]{1,0:T(8,128)(2,1)S(1)} %get-tuple-element.18.full), custom_call_target="tpu_custom_call" | custom-call | flops 3623878656 | bytes 8388608 | tf_op jit(solution)/shard_map/pallas_call | solution.py:298
  78.5 7.1 %copy.28 = f32[128,27,512]{2,0,1:T(8,128)} copy(f32[128,27,512]{2,1,0:T(8,128)S(1)} %shard_map.140) | data formatting | bytes 14155776
  85.5 0.0 collective-permute-done.21.refs_3_
  85.5 0.0 collective-permute-done.20.refs_2_
  85.5 0.0 collective-permute-done.19.refs_1_
  85.6 0.9 shard_map.139
  (22 shorter events, 0.3 us)
Async XLA Ops:
  0.6 14.5 %copy-start = (bf16[1024,16]{0,1:T(8,128)(2,1)S(1)}, bf16[1024,16]{0,1:T(8,128)(2,1)}, u32[]{:S(2)}) copy-start(bf16[1024,16]{0,1:T(8,128)(2,1)} %param.11) | copy-start | bytes 98308
  0.6 14.5 %copy-start.4 = (bf16[128,2,128]{2,1,0:T(2,128)(2,1)S(1)}, bf16[128,2,128]{2,1,0:T(2,128)(2,1)}, u32[]{:S(2)}) copy-start(bf16[128,2,128]{2,1,0:T(2,128)(2,1)} %param.14) | copy-start | bytes 196612
  1.6 21.8 %collective-permute-start.15 = (bf16[128,256]{1,0:T(8,128)(2,1)S(1)}, bf16[128,256]{1,0:T(8,128)(2,1)S(1)}, u32[]{:S(2)}, u32[]{:S(2)}) collective-permute-start(bf16[128,256]{1,0:T(8,128)(2,1)S(1)} %bitcast.53), channel_id=1, source_target_pairs={{0,12},{4,0},{8,4},{12,8},{1,13},{5,1},{9,5},{13,9},{2,14},{6,2},{... | collective-permute-start | bytes 196616 | tf_op jit(solution)/shard_map/ppermute | solution.py:341
  5.8 17.6 %collective-permute-start.14 = (bf16[128,256]{1,0:T(8,128)(2,1)S(1)}, bf16[128,256]{1,0:T(8,128)(2,1)S(1)}, u32[]{:S(2)}, u32[]{:S(2)}) collective-permute-start(bf16[128,256]{1,0:T(8,128)(2,1)S(1)} %bitcast.54), channel_id=1, source_target_pairs={{0,8},{4,12},{8,0},{12,4},{1,9},{5,13},{9,1},{13,5},{2,10},{6,14},... | collective-permute-start | bytes 196616 | tf_op jit(solution)/shard_map/ppermute | solution.py:341
  5.8 17.6 %collective-permute-start.13 = (bf16[128,256]{1,0:T(8,128)(2,1)S(1)}, bf16[128,256]{1,0:T(8,128)(2,1)S(1)}, u32[]{:S(2)}, u32[]{:S(2)}) collective-permute-start(bf16[128,256]{1,0:T(8,128)(2,1)S(1)} %bitcast.55), channel_id=1, source_target_pairs={{0,4},{4,8},{8,12},{12,0},{1,5},{5,9},{9,13},{13,1},{2,6},{6,10},{... | collective-permute-start | bytes 196616 | tf_op jit(solution)/shard_map/ppermute | solution.py:341
  7.0 13.6 %collective-permute-start.1 = (s32[1,8,512]{2,1,0:T(8,128)S(1)}, s32[1,8,512]{2,1,0:T(8,128)S(1)}, u32[]{:S(2)}, u32[]{:S(2)}) collective-permute-start(s32[1,8,512]{2,1,0:T(8,128)S(1)} %get-tuple-element.37), channel_id=1, source_target_pairs={{0,12},{4,0},{8,4},{12,8},{1,13},{5,1},{9,5},{13,9},{2,14},{6,2},{... | collective-permute-start | bytes 49160 | tf_op jit(solution)/shard_map/ppermute | solution.py:341
  9.8 10.7 %collective-permute-start = (s32[1,8,512]{2,1,0:T(8,128)S(1)}, s32[1,8,512]{2,1,0:T(8,128)S(1)}, u32[]{:S(2)}, u32[]{:S(2)}) collective-permute-start(s32[1,8,512]{2,1,0:T(8,128)S(1)} %get-tuple-element.38), channel_id=1, source_target_pairs={{0,4},{4,8},{8,12},{12,0},{1,5},{5,9},{9,13},{13,1},{2,6},{6,10},{... | collective-permute-start | bytes 49160 | tf_op jit(solution)/shard_map/ppermute | solution.py:341
  11.2 9.4 %copy-start.1 = (s32[4,8,512]{2,1,0:T(8,128)S(1)}, s32[4,8,512]{2,1,0:T(8,128)}, u32[]{:S(2)}) copy-start(s32[4,8,512]{2,1,0:T(8,128)} %own.1) | copy-start | bytes 196612
  11.2 13.9 %copy-start.3 = (bf16[16,4,8,512]{3,2,1,0:T(8,128)(2,1)S(1)}, bf16[16,4,8,512]{3,2,1,0:T(8,128)(2,1)}, u32[]{:S(2)}) copy-start(bf16[16,4,8,512]{3,2,1,0:T(8,128)(2,1)} %cot.1) | copy-start | bytes 1572868
  15.2 20.4 %copy-start.5 = (bf16[128,2,128]{2,1,0:T(2,128)(2,1)S(1)}, bf16[128,2,128]{2,1,0:T(2,128)(2,1)}, u32[]{:S(2)}) copy-start(bf16[128,2,128]{2,1,0:T(2,128)(2,1)} %param.16) | copy-start | bytes 196612
  20.6 4.4 %collective-permute-start.3 = (s32[6,1,512]{2,1,0:T(1,128)S(1)}, s32[6,1,512]{2,1,0:T(1,128)S(1)}, u32[]{:S(2)}, u32[]{:S(2)}) collective-permute-start(s32[6,1,512]{2,1,0:T(1,128)S(1)} %get-tuple-element.35), channel_id=1, source_target_pairs={{0,3},{1,0},{2,1},{3,2},{4,7},{5,4},{6,5},{7,6},{8,11},{9,8},{10,9... | collective-permute-start | bytes 36872 | tf_op jit(solution)/shard_map/ppermute | solution.py:341
  22.2 2.9 %collective-permute-start.2 = (s32[6,1,512]{2,1,0:T(1,128)S(1)}, s32[6,1,512]{2,1,0:T(1,128)S(1)}, u32[]{:S(2)}, u32[]{:S(2)}) collective-permute-start(s32[6,1,512]{2,1,0:T(1,128)S(1)} %get-tuple-element.36), channel_id=1, source_target_pairs={{0,1},{1,2},{2,3},{3,0},{4,5},{5,6},{6,7},{7,4},{8,9},{9,10},{10,1... | collective-permute-start | bytes 36872 | tf_op jit(solution)/shard_map/ppermute | solution.py:341
  23.4 23.5 %collective-permute-start.17 = (bf16[4,128,256]{2,1,0:T(8,128)(2,1)S(1)}, bf16[4,128,256]{2,1,0:T(8,128)(2,1)S(1)}, u32[]{:S(2)}, u32[]{:S(2)}) collective-permute-start(bf16[4,128,256]{2,1,0:T(8,128)(2,1)S(1)} %pad_maximum_fusion.1.refs_2_), channel_id=1, source_target_pairs={{0,2},{1,3},{2,0},{3,1},{4,6},{5,7},{6,4},{7,5},{8,10},{9,11},{10,... | collective-permute-start | bytes 786440 | tf_op jit(solution)/shard_map/ppermute | solution.py:346
  33.4 5.8 %collective-permute-start.6 = (f32[3,48,48]{2,1,0:T(8,128)S(1)}, f32[3,48,48]{2,1,0:T(8,128)S(1)}, u32[]{:S(2)}, u32[]{:S(2)}) collective-permute-start(f32[3,48,48]{2,1,0:T(8,128)S(1)} %get-tuple-element.13), channel_id=1, source_target_pairs={{0,3},{1,0},{2,1},{3,2},{4,7},{5,4},{6,5},{7,6},{8,11},{9,8},{10,9... | collective-permute-start | bytes 82952 | tf_op jit(solution)/shard_map/ppermute | solution.py:341
  33.9 5.5 %collective-permute-start.5 = (f32[3,48,48]{2,1,0:T(8,128)S(1)}, f32[3,48,48]{2,1,0:T(8,128)S(1)}, u32[]{:S(2)}, u32[]{:S(2)}) collective-permute-start(f32[3,48,48]{2,1,0:T(8,128)S(1)} %get-tuple-element.13), channel_id=1, source_target_pairs={{0,2},{1,3},{2,0},{3,1},{4,6},{5,7},{6,4},{7,5},{8,10},{9,11},{10,... | collective-permute-start | bytes 82952 | tf_op jit(solution)/shard_map/ppermute | solution.py:341
  35.0 6.8 %collective-permute-start.4 = (f32[3,48,48]{2,1,0:T(8,128)S(1)}, f32[3,48,48]{2,1,0:T(8,128)S(1)}, u32[]{:S(2)}, u32[]{:S(2)}) collective-permute-start(f32[3,48,48]{2,1,0:T(8,128)S(1)} %get-tuple-element.13), channel_id=1, source_target_pairs={{0,1},{1,2},{2,3},{3,0},{4,5},{5,6},{6,7},{7,4},{8,9},{9,10},{10,1... | collective-permute-start | bytes 82952 | tf_op jit(solution)/shard_map/ppermute | solution.py:341
  35.6 7.1 %collective-permute-start.12 = (bf16[128,256]{1,0:T(8,128)(2,1)S(1)}, bf16[128,256]{1,0:T(8,128)(2,1)S(1)}, u32[]{:S(2)}, u32[]{:S(2)}) collective-permute-start(bf16[128,256]{1,0:T(8,128)(2,1)S(1)} %bitcast.56), channel_id=1, source_target_pairs={{0,12},{4,0},{8,4},{12,8},{1,13},{5,1},{9,5},{13,9},{2,14},{6,2},{... | collective-permute-start | bytes 196616 | tf_op jit(solution)/shard_map/ppermute | solution.py:341
  39.3 6.0 %collective-permute-start.11 = (bf16[128,256]{1,0:T(8,128)(2,1)S(1)}, bf16[128,256]{1,0:T(8,128)(2,1)S(1)}, u32[]{:S(2)}, u32[]{:S(2)}) collective-permute-start(bf16[128,256]{1,0:T(8,128)(2,1)S(1)} %bitcast.57), channel_id=1, source_target_pairs={{0,8},{4,12},{8,0},{12,4},{1,9},{5,13},{9,1},{13,5},{2,10},{6,14},... | collective-permute-start | bytes 196616 | tf_op jit(solution)/shard_map/ppermute | solution.py:341
  39.4 5.9 %collective-permute-start.10 = (bf16[128,256]{1,0:T(8,128)(2,1)S(1)}, bf16[128,256]{1,0:T(8,128)(2,1)S(1)}, u32[]{:S(2)}, u32[]{:S(2)}) collective-permute-start(bf16[128,256]{1,0:T(8,128)(2,1)S(1)} %bitcast.58), channel_id=1, source_target_pairs={{0,4},{4,8},{8,12},{12,0},{1,5},{5,9},{9,13},{13,1},{2,6},{6,10},{... | collective-permute-start | bytes 196616 | tf_op jit(solution)/shard_map/ppermute | solution.py:341
  41.8 6.0 %collective-permute-start.9 = (f32[3,48,48]{2,1,0:T(8,128)S(1)}, f32[3,48,48]{2,1,0:T(8,128)S(1)}, u32[]{:S(2)}, u32[]{:S(2)}) collective-permute-start(f32[3,48,48]{2,1,0:T(8,128)S(1)} %add_add_fusion.1), channel_id=1, source_target_pairs={{0,12},{4,0},{8,4},{12,8},{1,13},{5,1},{9,5},{13,9},{2,14},{6,2},{... | collective-permute-start | bytes 82952 | tf_op jit(solution)/shard_map/ppermute | solution.py:341
  42.8 8.6 %collective-permute-start.8 = (f32[3,48,48]{2,1,0:T(8,128)S(1)}, f32[3,48,48]{2,1,0:T(8,128)S(1)}, u32[]{:S(2)}, u32[]{:S(2)}) collective-permute-start(f32[3,48,48]{2,1,0:T(8,128)S(1)} %add_add_fusion.1), channel_id=1, source_target_pairs={{0,8},{4,12},{8,0},{12,4},{1,9},{5,13},{9,1},{13,5},{2,10},{6,14},... | collective-permute-start | bytes 82952 | tf_op jit(solution)/shard_map/ppermute | solution.py:341
  45.2 6.2 %collective-permute-start.7 = (f32[3,48,48]{2,1,0:T(8,128)S(1)}, f32[3,48,48]{2,1,0:T(8,128)S(1)}, u32[]{:S(2)}, u32[]{:S(2)}) collective-permute-start(f32[3,48,48]{2,1,0:T(8,128)S(1)} %add_add_fusion.1), channel_id=1, source_target_pairs={{0,4},{4,8},{8,12},{12,0},{1,5},{5,9},{9,13},{13,1},{2,6},{6,10},{... | collective-permute-start | bytes 82952 | tf_op jit(solution)/shard_map/ppermute | solution.py:341
  45.3 7.3 %collective-permute-start.16 = (bf16[4,128,256]{2,1,0:T(8,128)(2,1)S(1)}, bf16[4,128,256]{2,1,0:T(8,128)(2,1)S(1)}, u32[]{:S(2)}, u32[]{:S(2)}) collective-permute-start(bf16[4,128,256]{2,1,0:T(8,128)(2,1)S(1)} %pad_maximum_fusion.1.refs_2_), channel_id=1, source_target_pairs={{0,1},{1,0},{2,3},{3,2},{4,5},{5,4},{6,7},{7,6},{8,9},{9,8},{10,11... | collective-permute-start | bytes 786440 | tf_op jit(solution)/shard_map/ppermute | solution.py:346
  46.9 5.7 %collective-permute-start.18 = (bf16[4,128,256]{2,1,0:T(8,128)(2,1)S(1)}, bf16[4,128,256]{2,1,0:T(8,128)(2,1)S(1)}, u32[]{:S(2)}, u32[]{:S(2)}) collective-permute-start(bf16[4,128,256]{2,1,0:T(8,128)(2,1)S(1)} %collective-permute-done.17.refs_4_), channel_id=1, source_target_pairs={{0,1},{1,0},{2,3},{3,2},{4,5},{5,4},{6,7},{7,6},{8,9},{9,8},{10,11... | collective-permute-start | bytes 786440 | tf_op jit(solution)/shard_map/ppermute | solution.py:346
  52.6 2.0 %copy-start.2 = (bf16[128,27,512]{2,0,1:T(8,128)(2,1)S(1)}, bf16[128,27,512]{2,0,1:T(8,128)(2,1)}, u32[]{:S(2)}) copy-start(bf16[128,27,512]{2,0,1:T(8,128)(2,1)} %param.15) | copy-start | bytes 10616836
  65.9 19.6 %collective-permute-start.21 = (bf16[256,128]{1,0:T(8,128)(2,1)S(1)}, bf16[256,128]{1,0:T(8,128)(2,1)S(1)}, u32[]{:S(2)}, u32[]{:S(2)}) collective-permute-start(bf16[256,128]{1,0:T(8,128)(2,1)S(1)} %get-tuple-element.29), channel_id=1, source_target_pairs={{0,3},{1,0},{2,1},{3,2},{4,7},{5,4},{6,5},{7,6},{8,11},{9,8},{10,9... | collective-permute-start | bytes 196616 | tf_op jit(solution)/shard_map/ppermute | solution.py:341
  67.6 17.9 %collective-permute-start.20 = (bf16[256,128]{1,0:T(8,128)(2,1)S(1)}, bf16[256,128]{1,0:T(8,128)(2,1)S(1)}, u32[]{:S(2)}, u32[]{:S(2)}) collective-permute-start(bf16[256,128]{1,0:T(8,128)(2,1)S(1)} %get-tuple-element.30), channel_id=1, source_target_pairs={{0,2},{1,3},{2,0},{3,1},{4,6},{5,7},{6,4},{7,5},{8,10},{9,11},{10,... | collective-permute-start | bytes 196616 | tf_op jit(solution)/shard_map/ppermute | solution.py:341
  68.1 17.5 %collective-permute-start.19 = (bf16[256,128]{1,0:T(8,128)(2,1)S(1)}, bf16[256,128]{1,0:T(8,128)(2,1)S(1)}, u32[]{:S(2)}, u32[]{:S(2)}) collective-permute-start(bf16[256,128]{1,0:T(8,128)(2,1)S(1)} %get-tuple-element.31), channel_id=1, source_target_pairs={{0,1},{1,2},{2,3},{3,0},{4,5},{5,6},{6,7},{7,4},{8,9},{9,10},{10,1... | collective-permute-start | bytes 196616 | tf_op jit(solution)/shard_map/ppermute | solution.py:341

commit v2 on v1

--- a/solution.py
+++ b/solution.py
@@ -8,10 +8,12 @@
 from jax.sharding import PartitionSpec as P
 
 BW = 32
+LOW = 256
 F32 = jnp.float32
 BF16 = jnp.bfloat16
 VM = pl.BlockSpec(memory_space=pltpu.VMEM)
-HB = pl.BlockSpec(memory_space=pl.ANY)
+HB = pl.BlockSpec(memory_space=pltpu.HBM)
+STEPS = [(b, e) for b in (-1, 0, 1) for e in (-1, 0, 1)]
 
 
 def silu_parts(pre):
@@ -35,20 +37,59 @@
     )
 
 
+def iota(shape, dim):
+    return lax.broadcasted_iota(jnp.int32, shape, dim)
+
+
+def prep_body(rows, taps, table, kernel, lookup):
+    ch = table.shape[0]
+    shape = kernel.shape
+    step = (rows + 2) * ch
+    spread = (iota((shape[0], 3 * ch), 0) // rows == iota((shape[0], 3 * ch), 1)).astype(F32).astype(BF16)
+    m, n = iota((3 * ch, shape[1]), 0), iota((3 * ch, shape[1]), 1)
+    repeat = ((m // ch == n // step) & (m % ch == n % ch)).astype(F32).astype(BF16)
+    gap = (iota(shape, 1) % step) // ch - iota(shape, 0) % rows
+    total = jnp.zeros(shape, F32)
+    for b in range(3):
+        tall = jnp.dot(spread, taps[b], preferred_element_type=F32).astype(BF16)
+        total = jnp.where(gap == b, jnp.dot(tall, repeat, preferred_element_type=F32), total)
+    kernel[...] = total.astype(BF16)
+    low = lookup.shape[1]
+    for high in range(table.shape[1] // low):
+        lookup[high * ch : (high + 1) * ch, :] = table[:, high * low : (high + 1) * low]
+
+
+def prep_call(taps, table, rows):
+    ch, grains = table.shape
+    return call(
+        functools.partial(prep_body, rows),
+        [
+            jax.ShapeDtypeStruct((3 * ch * rows, 3 * (rows + 2) * ch), BF16),
+            jax.ShapeDtypeStruct((grains // LOW * ch, LOW), BF16),
+        ],
+        [VM] * 2,
+        [],
+        2e9,
+        1 << 20,
+        16,
+    )(taps, table)
+
+
 def fine_body(scale, own, below, above, left, right, table, kernel, cot, out, part, feats, grads):
     depth, rows, cols = own.shape
-    ch = table.shape[0] // 8
+    ch = out.shape[0]
     place, count = lax.axis_index("space"), lax.axis_size("space")
     lane, lanes = lax.axis_index("chan"), lax.axis_size("chan")
-    key = lax.broadcasted_iota(jnp.int32, (128, cols), 0)
+    key = iota((LOW, cols), 0).astype(F32).astype(BF16)
+    one, none = jnp.ones((), BF16), jnp.zeros((), BF16)
     for x in range(depth + 2):
         for y in range(rows + 2):
             if y == 0:
                 ids = left[x]
-                ids = jnp.where(lane == 0, 1024, ids)
+                ids = jnp.where(lane == 0, -1, ids)
             elif y == rows + 1:
                 ids = right[x]
-                ids = jnp.where(lane == lanes - 1, 1024, ids)
+                ids = jnp.where(lane == lanes - 1, -1, ids)
             elif x == 0:
                 ids = below[0, y - 1 : y]
             elif x == depth + 1:
@@ -56,15 +97,17 @@
             else:
                 ids = own[x - 1, y - 1 : y]
             if x == 0:
-                ids = jnp.where(place == 0, 1024, ids)
+                ids = jnp.where(place == 0, -1, ids)
             if x == depth + 1:
-                ids = jnp.where(place == count - 1, 1024, ids)
-            low = (ids & 127) | ((ids >> 3) & 128)
-            hot = (key == low).astype(F32).astype(BF16)
+                ids = jnp.where(place == count - 1, -1, ids)
+            low = jnp.where(ids < 0, -1, ids & (LOW - 1))
+            hot = jnp.where(key == low.astype(F32).astype(BF16), one, none)
             picked = jnp.dot(table[...], hot, preferred_element_type=F32)
-            for bit in (9, 8, 7):
+            bit = 9
+            while picked.shape[0] > ch:
                 half = picked.shape[0] // 2
                 picked = jnp.where(((ids >> bit) & 1) == 1, picked[half:], picked[:half])
+                bit -= 1
             at = (x * (rows + 2) + y) * ch
             feats[at : at + ch, :] = picked.astype(BF16)
     group = ch * rows
@@ -112,7 +155,7 @@
 
 def fine_call(scale, own, below, above, left, right, table, kernel, cot):
     depth, rows, cols = own.shape
-    ch = table.shape[0] // 8
+    ch = cot.shape[0]
     body = functools.partial(fine_body, scale)
     macs = 3 * ch * rows * 3 * ch * (rows + 2) * cols * depth * 2
     return call(
@@ -136,19 +179,17 @@
     lane = lax.broadcasted_iota(jnp.int32, (1, width), 1)
     y, w = lane // BW, lane % BW
     masks = []
-    for b in (-1, 0, 1):
-        for e in (-1, 0, 1):
-            yy, ww = y + sign * b, w + sign * e
-            masks.append((yy >= 0) & (yy < width // BW) & (ww >= 0) & (ww < BW))
+    for b, e in STEPS:
+        yy, ww = y + sign * b, w + sign * e
+        masks.append((yy >= 0) & (yy < width // BW) & (ww >= 0) & (ww < BW))
     return masks
 
 
-def bott_body(pieces, *refs):
+def bott_body(pieces, planes, *refs):
     weight, cots = refs[0], refs[1]
     ins = refs[2 : 2 + pieces]
-    own_out, delta_out, full, share, mine, padded, deltas, rows_t, sums = refs[2 + pieces :]
+    own_out, deltas, padded, share, mine, acts, rows_t = refs[2 + pieces :]
     slabs, cb, lanes = ins[0].shape
-    planes = own_out.shape[1]
     width = lanes // planes
     c_all = cb * pieces
     o_own = own_out.shape[0]
@@ -163,35 +204,30 @@
             slab = lax.rem(place - r + slabs, slabs)
             at = pl.multiple_of(slab * lanes + width, width)
             padded[pl.ds(row, cb), pl.ds(at, lanes)] = ins[j][r]
-    full[...] = padded[:, width : (total + 1) * width]
     deltas[:, :width] = jnp.zeros((o_own, width), F32)
     deltas[:, (total + 1) * width :] = jnp.zeros((o_own, width), F32)
     masks = shift_masks(width, 1)
     for n in range(slabs):
         base = n * lanes
-        for a in range(3):
-            win = padded[:, base + a * width : base + a * width + lanes]
-            term = jnp.dot(weight[a * 9 * o_own : (a + 1) * 9 * o_own, :], win, preferred_element_type=F32)
-            sums[...] = term if a == 0 else sums[...] + term
+        pre = [jnp.zeros((o_own, width), F32) for _ in range(planes)]
+        for k, (b, e) in enumerate(STEPS):
+            term = jnp.zeros((o_own, lanes), F32)
+            for a in range(3):
+                at = (a * 9 + k) * o_own
+                win = padded[:, base + a * width : base + a * width + lanes]
+                term = term + jnp.dot(weight[at : at + o_own, :], win, preferred_element_type=F32)
+            turn = -(b * BW + e) % width
+            for p in range(planes):
+                block = term[:, p * width : (p + 1) * width]
+                if turn:
+                    block = jnp.where(masks[k], pltpu.roll(block, turn, 1), 0.0)
+                pre[p] = pre[p] + block
         cot = cots[lax.rem(place - n + slabs, slabs)].astype(F32)
         for p in range(planes):
-            pre = jnp.zeros((o_own, width), F32)
-            for k, (b, e) in enumerate([(b, e) for b in (-1, 0, 1) for e in (-1, 0, 1)]):
-                block = sums[k * o_own : (k + 1) * o_own, p * width : (p + 1) * width]
-                turn = -(b * BW + e) % width
-                if turn:
-                    block = jnp.where(masks[k], pltpu.roll(block, turn, 1), 0.0)
-                pre = pre + block
-            act, slope = silu_parts(pre)
-
-            @pl.when(n == place)
-            def _():
-                own_out[:, p, :] = act.astype(BF16)
-
+            act, slope = silu_parts(pre[p])
+            acts[n, :, p * width : (p + 1) * width] = act
             delta = (cot[:, p * width : (p + 1) * width] * slope).astype(BF16).astype(F32)
-            at = base + (p + 1) * width
-            deltas[:, at : at + width] = delta
-    delta_out[...] = deltas[:, width : (total + 1) * width]
+            deltas[:, base + (p + 1) * width : base + (p + 2) * width] = delta
     near = (planes + 2) * width
     turned = deltas[:, pl.ds(pl.multiple_of(place * lanes, width), near)].T
     w = lax.broadcasted_iota(jnp.int32, (near, 1), 0) % BW
@@ -207,23 +243,18 @@
             rows_t[e + 1, p * gap + BW + width : (p + 1) * gap, :] = jnp.zeros((BW, o_own), BF16)
     blocks = []
     for a in (-1, 0, 1):
-        for b in (-1, 0, 1):
-            for e in (-1, 0, 1):
-                per_plane = []
-                for p in range(planes):
-                    start = (1 + p - a) * gap + BW - b * BW
-                    per_plane.append(rows_t[e + 1, start : start + width, :])
-                blocks.append(jnp.concatenate(per_plane, axis=0))
-    left = jnp.concatenate(blocks, axis=1)
-    back = jnp.dot(left, weight[...], preferred_element_type=F32)
+        for b, e in STEPS:
+            starts = [(1 + p - a) * gap + BW - b * BW for p in range(planes)]
+            blocks.append(jnp.concatenate([rows_t[e + 1, s : s + width, :] for s in starts], axis=0))
+    back = jnp.dot(jnp.concatenate(blocks, axis=1), weight[...], preferred_element_type=F32)
     for j in range(pieces):
         block = back[:, j * cb : (j + 1) * cb]
         to = lax.rem(j - chan + pieces, pieces)
+        mine[to] = block
         share[to] = block.astype(BF16)
-
-        @pl.when(chan == j)
-        def _():
-            mine[...] = block
+    act = acts[place]
+    for p in range(planes):
+        own_out[:, p, :] = act[:, p * width : (p + 1) * width].astype(BF16)
 
 
 def bott_call(weight, cots, ins, planes):
@@ -236,84 +267,74 @@
     S = jax.ShapeDtypeStruct
     macs = 27 * o_own * c_all * (total + planes) * width
     return call(
-        functools.partial(bott_body, pieces),
+        functools.partial(bott_body, pieces, planes),
         [
             S((o_own, planes, width), BF16),
-            S((o_own, total * width), F32),
-            S((c_all, total * width), BF16),
+            S((o_own, (total + 2) * width), F32),
+            S((c_all, (total + 2) * width), BF16),
             S((pieces, lanes, cb), BF16),
-            S((lanes, cb), F32),
+            S((pieces, lanes, cb), F32),
         ],
         [VM] * (2 + pieces),
         [
-            pltpu.VMEM((c_all, (total + 2) * width), BF16),
-            pltpu.VMEM((o_own, (total + 2) * width), F32),
+            pltpu.VMEM((slabs, o_own, lanes), F32),
             pltpu.VMEM((3, (planes + 2) * (width + 2 * BW), o_own), BF16),
-            pltpu.VMEM((9 * o_own, lanes), F32),
         ],
         2 * macs,
         8 << 20,
-        32,
+        24,
     )(weight, cots, *ins)
 
 
 def wgrad_body(scale, delta, full, out, shifted, stage, sems):
-    o_own, length = delta.shape
-    c_all = full.shape[0]
+    o_own, length = delta.shape[0], delta.shape[1] - 8 * BW
     width = 4 * BW
     total = length // width
     masks = shift_masks(width, -1)
     shifted[:, :width] = jnp.zeros((9 * o_own, width), BF16)
     shifted[:, (total + 1) * width :] = jnp.zeros((9 * o_own, width), BF16)
     for p in range(total):
-        block = delta[:, p * width : (p + 1) * width]
-        for k, (b, e) in enumerate([(b, e) for b in (-1, 0, 1) for e in (-1, 0, 1)]):
+        block = delta[:, (p + 1) * width : (p + 2) * width]
+        for k, (b, e) in enumerate(STEPS):
             turn = (b * BW + e) % width
             moved = jnp.where(masks[k], pltpu.roll(block, turn, 1), 0.0) if turn else block
             shifted[k * o_own : (k + 1) * o_own, (p + 1) * width : (p + 2) * width] = moved.astype(BF16)
-    chunk = stage.shape[3]
     copies = []
-    for n in range(c_all // chunk):
-        slot = n % 2
-        if n >= 2:
-            copies[n - 2].wait()
-        right = full[n * chunk : (n + 1) * chunk, :]
-        for a in range(3):
-            left = shifted[:, (2 - a) * width : (2 - a) * width + length]
-            term = dot_nt(left, right) * scale
-            for k in range(9):
-                stage[slot, :, a * 9 + k, :] = term[k * o_own : (k + 1) * o_own, :]
-        copy = pltpu.make_async_copy(stage.at[slot], out.at[:, :, pl.ds(n * chunk, chunk)], sems.at[slot])
+    for a in range(3):
+        if a >= 2:
+            copies[a - 2].wait()
+        left = shifted[:, (2 - a) * width : (2 - a) * width + length]
+        term = dot_nt(left, full[:, width : width + length]) * scale
+        stage[a % 2] = term.reshape(stage.shape[1:])
+        copy = pltpu.make_async_copy(stage.at[a % 2], out.at[a * 9 : (a + 1) * 9], sems.at[a % 2])
         copy.start()
         copies.append(copy)
-    for copy in copies[-2:]:
+    for copy in copies[1:]:
         copy.wait()
 
 
-def wgrad_call(scale, delta, full, chunk=256):
+def wgrad_call(scale, delta, full):
     o_own, length = delta.shape
     c_all = full.shape[0]
-    width = 4 * BW
-    total = length // width
     return call(
         functools.partial(wgrad_body, scale),
-        [jax.ShapeDtypeStruct((o_own, 27, c_all), F32)],
+        [jax.ShapeDtypeStruct((27, o_own, c_all), F32)],
         [VM] * 2,
         [
-            pltpu.VMEM((9 * o_own, (total + 2) * width), BF16),
-            pltpu.VMEM((2, o_own, 27, chunk), F32),
+            pltpu.VMEM((9 * o_own, length), BF16),
+            pltpu.VMEM((2, 9, o_own, c_all), F32),
             pltpu.SemaphoreType.DMA((2,)),
         ],
         2 * 27 * o_own * c_all * length,
         8 << 20,
-        40,
+        32,
         [HB],
     )(delta, full)[0]
 
 
 def last_body(count, *refs):
     mine, others, out = refs[0], refs[1 : 1 + count], refs[1 + count]
-    total = mine[...]
+    total = mine[0]
     for other in others:
         total = total + other[...].astype(F32)
     turned = total.T
@@ -324,7 +345,7 @@
 
 
 def last_call(mine, others, planes):
-    lanes, cb = mine.shape
+    lanes, cb = mine.shape[1:]
     return call(
         functools.partial(last_body, len(others)),
         [jax.ShapeDtypeStruct((cb, planes, lanes // planes), BF16)],
@@ -369,16 +390,8 @@
     cot = bott_cot.reshape(o_own, lanes)
     cots = jnp.stack([cot] + [hop(cot, "space", r) for r in range(1, spaces)])
 
-    lookup = table.reshape(8, 128, ch).transpose(0, 2, 1).reshape(8 * ch, 128)
-    taps = fine_weight.reshape(3, 3, 3, ch, ch)
-    band = np.zeros((3, rows, rows + 2), np.float32)
-    for b in range(3):
-        for y in range(rows):
-            band[b, y, y + b] = 1
-    kernel = sum(
-        taps[:, b].transpose(1, 3, 0, 2)[:, :, None, :, None, :] * band[b][None, None, :, None, :, None].astype(BF16)
-        for b in range(3)
-    ).reshape(3 * ch * rows, 3 * (rows + 2) * ch)
+    taps = fine_weight.reshape(3, 3, 3, ch, ch).transpose(1, 2, 4, 0, 3).reshape(3, 3 * ch, 3 * ch)
+    kernel, lookup = prep_call(taps, table.T, rows)
     scale = (depth * spaces * rows * chans * cols) ** -0.5
     fine_out, part = fine_call(scale, labels, below, above, left, right, lookup, kernel, fine_cot)
     part = part + sum(hop(part, "chan", r) for r in range(1, chans))
@@ -388,7 +401,7 @@
     weight = bott_weight.transpose(1, 0, 2).reshape(27 * o_own, cb * chans)
     bott_out, delta, full, share, mine = bott_call(weight, cots, ins, planes)
     others = [hop(share[r], "chan", r) for r in range(1, chans)]
-    bott_wgrad = wgrad_call((planes * spaces * width) ** -0.5, delta, full)
+    bott_wgrad = wgrad_call((planes * spaces * width) ** -0.5, delta, full).transpose(1, 0, 2)
     bott_dgrad = last_call(mine, others, planes)
     return fine_out, fine_wgrad, bott_out, bott_dgrad, bott_wgrad
 

time: 86.8 us -> 63.8 us (0.74)
  local copies, waits for them, and re-layouts: 18.7 us -> 6.93 us
  Pallas kernels: 29.4 us -> 21 us
  waiting for transfers between devices: 7.68 us -> 11.6 us
  other arithmetic: 4.02 us -> 0.11 us
  starting transfers between devices: 25.8 us -> 23 us
    pallas_call x2 -> x3, Pallas kernels: 20.1 us -> 12.3 us  [the longest x1 5.8 us: bott_call(): call(functools.partial(bott_body, pieces, planes), [S((o_own, planes, wid...]
    unnamed x19 -> x18, local copies, waits for them, and re-layouts: 11.9 us -> 5.5 us
    add x1 -> x0, local copies, waits for them, and re-layouts: 5.34 us -> none  [shards(): sum((taps[:, b].transpose(1, 3, 0, 2)[:, :, None, :, None, :] * band[b][N...]
    add x1 -> x0, other arithmetic: 3.91 us -> none  [shards(): sum((taps[:, b].transpose(1, 3, 0, 2)[:, :, None, :, None, :] * band[b][N...]
    ppermute x19, waiting for transfers between devices: 7.67 us -> 11.6 us  [hop(): lax.ppermute(x, axis, [(i, (i + offset) % count) for i in range(count)])]
    ppermute x19, starting transfers between devices: 23.7 us -> 21.1 us  [hop(): lax.ppermute(x, axis, [(i, (i + offset) % count) for i in range(count)])]
  transfers between devices with their start and end apart: 22 -> 22, of which waited for: 4 -> 5; matrix products, arithmetic and copies ran while one was open for 23% -> 5% of each run, Pallas kernels for 20% -> 23%
where the time goes in v2:
time: 63.8 us; the launch traced here: 63.4 us
  starting transfers between devices  23 us (36%)
  Pallas kernels  21 us (33%)
  waiting for transfers between devices  11.6 us (18%)
  local copies, waits for them, and re-layouts  6.93 us (11%)
  between operations  0.83 us (1%)
    ppermute x19, starting transfers between devices, hop(): lax.ppermute(x, axis, [(i, (i + offset) % count) for i in range(count)])  21.1 us
    ppermute x19, waiting for transfers between devices, hop(): lax.ppermute(x, axis, [(i, (i + offset) % count) for i in range(count)])  11.6 us
    pallas_call x1, Pallas kernels, fine_call(): call(body, [jax.ShapeDtypeStruct((ch, depth, rows, cols), BF16), jax.Shap...  7.83 us
    pallas_call x1, Pallas kernels, bott_call(): call(functools.partial(bott_body, pieces, planes), [S((o_own, planes, wid...  5.8 us
    pallas_call x1, Pallas kernels, wgrad_call(): call(functools.partial(wgrad_body, scale), [jax.ShapeDtypeStruct((27, o_o...  5.71 us
    unnamed x18, local copies, waits for them, and re-layouts  5.5 us
    ppermute x3, starting transfers between devices, swap(): return lax.ppermute(x, axis, [(i, i ^ bit) for i in range(count)])  1.87 us
  transfers between devices with their start and end apart: 22, of which 5 were waited for; matrix products, arithmetic and copies ran while one was open for 5% of the time, Pallas kernels for 23%

profile of v2, /device:TPU:1, one launch (start us, length us, event | category | flops | bytes accessed | tf_op | source)
XLA Modules:
  0.0 63.4 jit_solution(2834559635452008022)
XLA Ops:
  0.6 0.9 %copy.22 = bf16[16,8,2,128]{3,1,2,0:T(8,128)(2,1)S(1)} copy(bf16[16,8,2,128]{3,2,1,0:T(2,128)(2,1)} %bitcast.35) | data formatting | bytes 131072
  1.5 4.2 %collective-permute-start.15 = (bf16[128,256]{1,0:T(8,128)(2,1)S(1)}, bf16[128,256]{1,0:T(8,128)(2,1)S(1)}, u32[]{:S(2)}, u32[]{:S(2)}) collective-permute-start(bf16[128,256]{1,0:T(8,128)(2,1)S(1)} %bitcast.37), channel_id=1, source_target_pairs={{0,12},{4,0},{8,4},{12,8},{1,13},{5,1},{9,5},{13,9},{2,14},{6,2},{... | collective-permute-start | bytes 196616 | tf_op jit(solution)/shard_map/ppermute | solution.py:362
  5.7 0.0 collective-permute-start.14
  5.7 0.5 collective-permute-start.13
  6.1 0.7 %fusion.1 = (s32[1,8,512]{2,1,0:T(8,128)S(1)}, s32[1,8,512]{2,1,0:T(8,128)S(1)}) fusion(s32[4,8,512]{2,1,0:T(8,128)} %own.1), kind=kLoop, calls=%fused_computation.13 | loop fusion | bytes 65536 | tf_op jit(solution)/shard_map/slice | solution.py:379
  6.9 2.8 %collective-permute-start.1 = (s32[1,8,512]{2,1,0:T(8,128)S(1)}, s32[1,8,512]{2,1,0:T(8,128)S(1)}, u32[]{:S(2)}, u32[]{:S(2)}) collective-permute-start(s32[1,8,512]{2,1,0:T(8,128)S(1)} %get-tuple-element.33), channel_id=1, source_target_pairs={{0,12},{4,0},{8,4},{12,8},{1,13},{5,1},{9,5},{13,9},{2,14},{6,2},{... | collective-permute-start | bytes 49160 | tf_op jit(solution)/shard_map/ppermute | solution.py:362
  9.7 0.0 collective-permute-start
  9.7 1.0 %copy.14 = bf16[27,16,16]{2,1,0:T(8,128)(2,1)S(1)} copy(bf16[27,16,16]{0,2,1:T(8,128)(2,1)} %param.9) | data formatting | bytes 27648 | tf_op args[2]
  10.7 0.1 copy.15
  10.9 0.1 reshape.32.taps
  11.0 0.0 copy-start.3
  11.0 0.7 %copy-done.3 = bf16[1024,16]{0,1:T(8,128)(2,1)S(1)} copy-done((bf16[1024,16]{0,1:T(8,128)(2,1)S(1)}, bf16[1024,16]{0,1:T(8,128)(2,1)}, u32[]{:S(2)}) %copy-start.3) | copy-done | bytes 32792
  11.8 0.8 %shard_map.110 = (bf16[384,480]{1,0:T(8,128)(2,1)S(1)}, bf16[64,256]{1,0:T(8,128)(2,1)S(1)}) custom-call(bf16[3,48,48]{2,1,0:T(8,128)(2,1)S(1)} %reshape.32.taps, bf16[16,1024]{1,0:T(8,128)(2,1)S(1)} %bitcast.31), custom_call_target="tpu_custom_call" | custom-call | flops 2000000000 | bytes 1048576 | tf_op jit(solution)/shard_map/pallas_call | solution.py:64
  12.6 0.0 copy-done.4
  12.6 0.0 copy-start.5
  12.7 1.4 %collective-permute-done.below = s32[1,8,512]{2,1,0:T(8,128)S(1)} collective-permute-done((s32[1,8,512]{2,1,0:T(8,128)S(1)}, s32[1,8,512]{2,1,0:T(8,128)S(1)}, u32[]{:S(2)}, u32[]{:S(2)}) %collective-permute-start) | collective-permute-done | bytes 16416 | tf_op jit(solution)/shard_map/ppermute | solution.py:362
  14.1 0.0 copy-done
  14.1 0.0 collective-permute-done.1.above
  14.1 2.7 %collective-permute-start.3 = (s32[6,1,512]{2,1,0:T(1,128)S(1)}, s32[6,1,512]{2,1,0:T(1,128)S(1)}, u32[]{:S(2)}, u32[]{:S(2)}) collective-permute-start(s32[6,1,512]{2,1,0:T(1,128)S(1)} %get-tuple-element.31), channel_id=1, source_target_pairs={{0,3},{1,0},{2,1},{3,2},{4,7},{5,4},{6,5},{7,6},{8,11},{9,8},{10,9... | collective-permute-start | bytes 36872 | tf_op jit(solution)/shard_map/ppermute | solution.py:362
  16.9 1.2 %collective-permute-start.2 = (s32[6,1,512]{2,1,0:T(1,128)S(1)}, s32[6,1,512]{2,1,0:T(1,128)S(1)}, u32[]{:S(2)}, u32[]{:S(2)}) collective-permute-start(s32[6,1,512]{2,1,0:T(1,128)S(1)} %get-tuple-element.32), channel_id=1, source_target_pairs={{0,1},{1,2},{2,3},{3,0},{4,5},{5,6},{6,7},{7,4},{8,9},{9,10},{10,1... | collective-permute-start | bytes 36872 | tf_op jit(solution)/shard_map/ppermute | solution.py:362
  18.0 0.0 collective-permute-done.15
  18.0 0.0 collective-permute-done.14
  18.0 0.0 collective-permute-done.13
  18.1 0.3 collective-permute-start.17
  18.4 1.3 %collective-permute-done.3.right = s32[6,1,512]{2,1,0:T(1,128)S(1)} collective-permute-done((s32[6,1,512]{2,1,0:T(1,128)S(1)}, s32[6,1,512]{2,1,0:T(1,128)S(1)}, u32[]{:S(2)}, u32[]{:S(2)}) %collective-permute-start.3) | collective-permute-done | bytes 12320 | tf_op jit(solution)/shard_map/ppermute | solution.py:362
  19.7 0.0 collective-permute-done.2.left
  19.7 7.8 %shard_map.111 = (bf16[16,4,8,512]{3,2,1,0:T(8,128)(2,1)}, f32[3,48,48]{2,1,0:T(8,128)S(1)}) custom-call(s32[4,8,512]{2,1,0:T(8,128)S(1)} %copy-done, s32[1,8,512]{2,1,0:T(8,128)S(1)} %collective-permute-done.below, s32[1,8,512]{2,1,0:T(8,128)S(1)} %collective-permute-done.1.above, s32[6,1,512]{2,1,0:T(1,128)S(1)} %collective-permute-done.2.left, ...), custom_call_target="tpu_custom_call" | custom-call | flops 1509949440 | bytes 4194304 | tf_op jit(solution)/shard_map/pallas_call | solution.py:161
  27.6 0.5 collective-permute-start.6
  28.0 1.1 %collective-permute-start.5 = (f32[3,48,48]{2,1,0:T(8,128)S(1)}, f32[3,48,48]{2,1,0:T(8,128)S(1)}, u32[]{:S(2)}, u32[]{:S(2)}) collective-permute-start(f32[3,48,48]{2,1,0:T(8,128)S(1)} %get-tuple-element.17), channel_id=1, source_target_pairs={{0,2},{1,3},{2,0},{3,1},{4,6},{5,7},{6,4},{7,5},{8,10},{9,11},{10,... | collective-permute-start | bytes 82952 | tf_op jit(solution)/shard_map/ppermute | solution.py:362
  29.1 0.6 collective-permute-start.4
  29.8 0.0 copy-done.5
  29.8 1.1 %collective-permute-start.12 = (bf16[128,256]{1,0:T(8,128)(2,1)S(1)}, bf16[128,256]{1,0:T(8,128)(2,1)S(1)}, u32[]{:S(2)}, u32[]{:S(2)}) collective-permute-start(bf16[128,256]{1,0:T(8,128)(2,1)S(1)} %bitcast.40), channel_id=1, source_target_pairs={{0,12},{4,0},{8,4},{12,8},{1,13},{5,1},{9,5},{13,9},{2,14},{6,2},{... | collective-permute-start | bytes 196616 | tf_op jit(solution)/shard_map/ppermute | solution.py:362
  30.9 1.2 %collective-permute-done.6 = f32[3,48,48]{2,1,0:T(8,128)S(1)} collective-permute-done((f32[3,48,48]{2,1,0:T(8,128)S(1)}, f32[3,48,48]{2,1,0:T(8,128)S(1)}, u32[]{:S(2)}, u32[]{:S(2)}) %collective-permute-start.6) | collective-permute-done | bytes 27680 | tf_op jit(solution)/shard_map/ppermute | solution.py:362
  32.1 0.0 collective-permute-start.11
  32.1 0.0 collective-permute-done.5
  32.1 1.3 %collective-permute-start.10 = (bf16[128,256]{1,0:T(8,128)(2,1)S(1)}, bf16[128,256]{1,0:T(8,128)(2,1)S(1)}, u32[]{:S(2)}, u32[]{:S(2)}) collective-permute-start(bf16[128,256]{1,0:T(8,128)(2,1)S(1)} %bitcast.42), channel_id=1, source_target_pairs={{0,4},{4,8},{8,12},{12,0},{1,5},{5,9},{9,13},{13,1},{2,6},{6,10},{... | collective-permute-start | bytes 196616 | tf_op jit(solution)/shard_map/ppermute | solution.py:362
  33.4 0.0 collective-permute-done.4
  33.4 2.0 %collective-permute-start.9 = (f32[3,48,48]{2,1,0:T(8,128)S(1)}, f32[3,48,48]{2,1,0:T(8,128)S(1)}, u32[]{:S(2)}, u32[]{:S(2)}) collective-permute-start(f32[3,48,48]{2,1,0:T(8,128)S(1)} %add_add_fusion.1), channel_id=1, source_target_pairs={{0,12},{4,0},{8,4},{12,8},{1,13},{5,1},{9,5},{13,9},{2,14},{6,2},{... | collective-permute-start | bytes 82952 | tf_op jit(solution)/shard_map/ppermute | solution.py:362
  35.4 0.0 collective-permute-done.12
  35.4 0.6 collective-permute-start.8
  36.0 2.9 %collective-permute-done.11 = bf16[128,256]{1,0:T(8,128)(2,1)S(1)} collective-permute-done((bf16[128,256]{1,0:T(8,128)(2,1)S(1)}, bf16[128,256]{1,0:T(8,128)(2,1)S(1)}, u32[]{:S(2)}, u32[]{:S(2)}) %collective-permute-start.11) | collective-permute-done | bytes 65568 | tf_op jit(solution)/shard_map/ppermute | solution.py:362
  38.9 0.0 collective-permute-start.7
  38.9 0.0 collective-permute-done.10
  38.9 1.5 %collective-permute-start.16 = (bf16[4,128,256]{2,1,0:T(8,128)(2,1)S(1)}, bf16[4,128,256]{2,1,0:T(8,128)(2,1)S(1)}, u32[]{:S(2)}, u32[]{:S(2)}) collective-permute-start(bf16[4,128,256]{2,1,0:T(8,128)(2,1)S(1)} %pad_maximum_fusion.1.refs_2_), channel_id=1, source_target_pairs={{0,1},{1,0},{2,3},{3,2},{4,5},{5,4},{6,7},{7,6},{8,9},{9,8},{10,11... | collective-permute-start | bytes 786440 | tf_op jit(solution)/shard_map/ppermute | solution.py:367
  40.4 0.0 collective-permute-done.17.refs_4_
  40.4 0.0 collective-permute-start.18
  40.5 0.0 collective-permute-done.9
  40.5 4.7 %collective-permute-done.8 = f32[3,48,48]{2,1,0:T(8,128)S(1)} collective-permute-done((f32[3,48,48]{2,1,0:T(8,128)S(1)}, f32[3,48,48]{2,1,0:T(8,128)S(1)}, u32[]{:S(2)}, u32[]{:S(2)}) %collective-permute-start.8) | collective-permute-done | bytes 27680 | tf_op jit(solution)/shard_map/ppermute | solution.py:362
  45.2 0.0 collective-permute-done.7
  45.2 0.2 reshape.33
  45.4 0.1 copy.16
  45.5 0.8 %copy.17 = f32[27,16,16]{0,2,1:T(8,128)} copy(f32[27,16,16]{2,1,0:T(8,128)S(1)} %bitcast.33) | data formatting | bytes 55296
  46.4 0.0 collective-permute-done.16.refs_3_
  46.4 0.0 collective-permute-done.18.refs_5_
  46.4 2.0 %copy-done.1 = bf16[128,27,512]{2,0,1:T(8,128)(2,1)S(1)} copy-done((bf16[128,27,512]{2,0,1:T(8,128)(2,1)S(1)}, bf16[128,27,512]{2,0,1:T(8,128)(2,1)}, u32[]{:S(2)}) %copy-start.1) | copy-done | bytes 3538968
  48.4 5.8 %shard_map.112 = (bf16[128,2,128]{2,1,0:T(2,128)(2,1)}, f32[128,1280]{1,0:T(8,128)S(1)}, bf16[512,1280]{1,0:T(8,128)(2,1)S(1)}, bf16[4,256,128]{2,1,0:T(8,128)(2,1)S(1)}, f32[4,256,128]{2,1,0:T(8,128)S(1)}) custom-call(bf16[3456,512]{1,0:T(8,128)(2,1)S(1)} %bitcast.30, bf16[4,128,256]{2,1,0:T(8,128)(2,1)S(1)} %pad_maximum_fusion.refs_1_, ...), custom_call_target="tpu_custom_call" | custom-call | flops 4529848320 | bytes 8388608 | tf_op jit(solution)/shard_map/pallas_call | solution.py:269
  54.2 0.6 collective-permute-start.21
  54.8 1.6 %collective-permute-start.20 = (bf16[256,128]{1,0:T(8,128)(2,1)S(1)}, bf16[256,128]{1,0:T(8,128)(2,1)S(1)}, u32[]{:S(2)}, u32[]{:S(2)}) collective-permute-start(bf16[256,128]{1,0:T(8,128)(2,1)S(1)} %get-tuple-element.29), channel_id=1, source_target_pairs={{0,2},{1,3},{2,0},{3,1},{4,6},{5,7},{6,4},{7,5},{8,10},{9,11},{10,... | collective-permute-start | bytes 196616 | tf_op jit(solution)/shard_map/ppermute | solution.py:362
  56.4 0.4 collective-permute-start.19
  56.8 5.7 %shard_map.114 = f32[27,128,512]{2,1,0:T(8,128)} custom-call(f32[128,1280]{1,0:T(8,128)S(1)} %get-tuple-element.21.delta, bf16[512,1280]{1,0:T(8,128)(2,1)S(1)} %get-tuple-element.22.full), custom_call_target="tpu_custom_call" | custom-call | flops 4529848320 | bytes 8388608 | tf_op jit(solution)/shard_map/pallas_call | solution.py:319
  62.5 0.0 collective-permute-done.21.refs_3_
  62.5 0.0 collective-permute-done.20.refs_2_
  62.6 0.0 collective-permute-done.19.refs_1_
  62.6 0.9 %shard_map.113 = bf16[128,2,128]{2,1,0:T(2,128)(2,1)} custom-call(f32[4,256,128]{2,1,0:T(8,128)S(1)} %get-tuple-element.19.refs_0_, bf16[256,128]{1,0:T(8,128)(2,1)S(1)} %collective-permute-done.19.refs_1_, bf16[256,128]{1,0:T(8,128)(2,1)S(1)} %collective-permute-done.20.refs_2_, bf16[256,128]{1,0:T(8,128)(2,1)S(1)} %collective-permute-done.21.refs_3_), custom_call_target="tpu_custom_call" | custom-call | flops 131072 | bytes 393216 | tf_op jit(solution)/shard_map/pallas_call | solution.py:349
  (17 shorter events, 0.3 us)
Async XLA Ops:
  1.5 16.5 %collective-permute-start.15 = (bf16[128,256]{1,0:T(8,128)(2,1)S(1)}, bf16[128,256]{1,0:T(8,128)(2,1)S(1)}, u32[]{:S(2)}, u32[]{:S(2)}) collective-permute-start(bf16[128,256]{1,0:T(8,128)(2,1)S(1)} %bitcast.37), channel_id=1, source_target_pairs={{0,12},{4,0},{8,4},{12,8},{1,13},{5,1},{9,5},{13,9},{2,14},{6,2},{... | collective-permute-start | bytes 196616 | tf_op jit(solution)/shard_map/ppermute | solution.py:362
  5.7 12.3 %collective-permute-start.14 = (bf16[128,256]{1,0:T(8,128)(2,1)S(1)}, bf16[128,256]{1,0:T(8,128)(2,1)S(1)}, u32[]{:S(2)}, u32[]{:S(2)}) collective-permute-start(bf16[128,256]{1,0:T(8,128)(2,1)S(1)} %bitcast.38), channel_id=1, source_target_pairs={{0,8},{4,12},{8,0},{12,4},{1,9},{5,13},{9,1},{13,5},{2,10},{6,14},... | collective-permute-start | bytes 196616 | tf_op jit(solution)/shard_map/ppermute | solution.py:362
  5.7 12.3 %collective-permute-start.13 = (bf16[128,256]{1,0:T(8,128)(2,1)S(1)}, bf16[128,256]{1,0:T(8,128)(2,1)S(1)}, u32[]{:S(2)}, u32[]{:S(2)}) collective-permute-start(bf16[128,256]{1,0:T(8,128)(2,1)S(1)} %bitcast.39), channel_id=1, source_target_pairs={{0,4},{4,8},{8,12},{12,0},{1,5},{5,9},{9,13},{13,1},{2,6},{6,10},{... | collective-permute-start | bytes 196616 | tf_op jit(solution)/shard_map/ppermute | solution.py:362
  6.9 7.2 %collective-permute-start.1 = (s32[1,8,512]{2,1,0:T(8,128)S(1)}, s32[1,8,512]{2,1,0:T(8,128)S(1)}, u32[]{:S(2)}, u32[]{:S(2)}) collective-permute-start(s32[1,8,512]{2,1,0:T(8,128)S(1)} %get-tuple-element.33), channel_id=1, source_target_pairs={{0,12},{4,0},{8,4},{12,8},{1,13},{5,1},{9,5},{13,9},{2,14},{6,2},{... | collective-permute-start | bytes 49160 | tf_op jit(solution)/shard_map/ppermute | solution.py:362
  9.7 4.4 %collective-permute-start = (s32[1,8,512]{2,1,0:T(8,128)S(1)}, s32[1,8,512]{2,1,0:T(8,128)S(1)}, u32[]{:S(2)}, u32[]{:S(2)}) collective-permute-start(s32[1,8,512]{2,1,0:T(8,128)S(1)} %get-tuple-element.34), channel_id=1, source_target_pairs={{0,4},{4,8},{8,12},{12,0},{1,5},{5,9},{9,13},{13,1},{2,6},{6,10},{... | collective-permute-start | bytes 49160 | tf_op jit(solution)/shard_map/ppermute | solution.py:362
  11.0 0.8 %copy-start.3 = (bf16[1024,16]{0,1:T(8,128)(2,1)S(1)}, bf16[1024,16]{0,1:T(8,128)(2,1)}, u32[]{:S(2)}) copy-start(bf16[1024,16]{0,1:T(8,128)(2,1)} %param.8) | copy-start | bytes 98308
  11.8 0.8 %copy-start.4 = (bf16[128,2,128]{2,1,0:T(2,128)(2,1)S(1)}, bf16[128,2,128]{2,1,0:T(2,128)(2,1)}, u32[]{:S(2)}) copy-start(bf16[128,2,128]{2,1,0:T(2,128)(2,1)} %param.11) | copy-start | bytes 196612
  11.8 2.3 %copy-start = (s32[4,8,512]{2,1,0:T(8,128)S(1)}, s32[4,8,512]{2,1,0:T(8,128)}, u32[]{:S(2)}) copy-start(s32[4,8,512]{2,1,0:T(8,128)} %own.1) | copy-start | bytes 196612
  11.8 8.0 %copy-start.2 = (bf16[16,4,8,512]{3,2,1,0:T(8,128)(2,1)S(1)}, bf16[16,4,8,512]{3,2,1,0:T(8,128)(2,1)}, u32[]{:S(2)}) copy-start(bf16[16,4,8,512]{3,2,1,0:T(8,128)(2,1)} %cot.1) | copy-start | bytes 1572868
  12.6 17.1 %copy-start.5 = (bf16[128,2,128]{2,1,0:T(2,128)(2,1)S(1)}, bf16[128,2,128]{2,1,0:T(2,128)(2,1)}, u32[]{:S(2)}) copy-start(bf16[128,2,128]{2,1,0:T(2,128)(2,1)} %param.13) | copy-start | bytes 196612
  14.1 5.6 %collective-permute-start.3 = (s32[6,1,512]{2,1,0:T(1,128)S(1)}, s32[6,1,512]{2,1,0:T(1,128)S(1)}, u32[]{:S(2)}, u32[]{:S(2)}) collective-permute-start(s32[6,1,512]{2,1,0:T(1,128)S(1)} %get-tuple-element.31), channel_id=1, source_target_pairs={{0,3},{1,0},{2,1},{3,2},{4,7},{5,4},{6,5},{7,6},{8,11},{9,8},{10,9... | collective-permute-start | bytes 36872 | tf_op jit(solution)/shard_map/ppermute | solution.py:362
  16.9 2.9 %collective-permute-start.2 = (s32[6,1,512]{2,1,0:T(1,128)S(1)}, s32[6,1,512]{2,1,0:T(1,128)S(1)}, u32[]{:S(2)}, u32[]{:S(2)}) collective-permute-start(s32[6,1,512]{2,1,0:T(1,128)S(1)} %get-tuple-element.32), channel_id=1, source_target_pairs={{0,1},{1,2},{2,3},{3,0},{4,5},{5,6},{6,7},{7,4},{8,9},{9,10},{10,1... | collective-permute-start | bytes 36872 | tf_op jit(solution)/shard_map/ppermute | solution.py:362
  18.1 22.3 %collective-permute-start.17 = (bf16[4,128,256]{2,1,0:T(8,128)(2,1)S(1)}, bf16[4,128,256]{2,1,0:T(8,128)(2,1)S(1)}, u32[]{:S(2)}, u32[]{:S(2)}) collective-permute-start(bf16[4,128,256]{2,1,0:T(8,128)(2,1)S(1)} %pad_maximum_fusion.1.refs_2_), channel_id=1, source_target_pairs={{0,2},{1,3},{2,0},{3,1},{4,6},{5,7},{6,4},{7,5},{8,10},{9,11},{10,... | collective-permute-start | bytes 786440 | tf_op jit(solution)/shard_map/ppermute | solution.py:367
  27.6 4.5 %collective-permute-start.6 = (f32[3,48,48]{2,1,0:T(8,128)S(1)}, f32[3,48,48]{2,1,0:T(8,128)S(1)}, u32[]{:S(2)}, u32[]{:S(2)}) collective-permute-start(f32[3,48,48]{2,1,0:T(8,128)S(1)} %get-tuple-element.17), channel_id=1, source_target_pairs={{0,3},{1,0},{2,1},{3,2},{4,7},{5,4},{6,5},{7,6},{8,11},{9,8},{10,9... | collective-permute-start | bytes 82952 | tf_op jit(solution)/shard_map/ppermute | solution.py:362
  28.0 4.0 %collective-permute-start.5 = (f32[3,48,48]{2,1,0:T(8,128)S(1)}, f32[3,48,48]{2,1,0:T(8,128)S(1)}, u32[]{:S(2)}, u32[]{:S(2)}) collective-permute-start(f32[3,48,48]{2,1,0:T(8,128)S(1)} %get-tuple-element.17), channel_id=1, source_target_pairs={{0,2},{1,3},{2,0},{3,1},{4,6},{5,7},{6,4},{7,5},{8,10},{9,11},{10,... | collective-permute-start | bytes 82952 | tf_op jit(solution)/shard_map/ppermute | solution.py:362
  29.1 4.2 %collective-permute-start.4 = (f32[3,48,48]{2,1,0:T(8,128)S(1)}, f32[3,48,48]{2,1,0:T(8,128)S(1)}, u32[]{:S(2)}, u32[]{:S(2)}) collective-permute-start(f32[3,48,48]{2,1,0:T(8,128)S(1)} %get-tuple-element.17), channel_id=1, source_target_pairs={{0,1},{1,2},{2,3},{3,0},{4,5},{5,6},{6,7},{7,4},{8,9},{9,10},{10,1... | collective-permute-start | bytes 82952 | tf_op jit(solution)/shard_map/ppermute | solution.py:362
  29.8 5.6 %collective-permute-start.12 = (bf16[128,256]{1,0:T(8,128)(2,1)S(1)}, bf16[128,256]{1,0:T(8,128)(2,1)S(1)}, u32[]{:S(2)}, u32[]{:S(2)}) collective-permute-start(bf16[128,256]{1,0:T(8,128)(2,1)S(1)} %bitcast.40), channel_id=1, source_target_pairs={{0,12},{4,0},{8,4},{12,8},{1,13},{5,1},{9,5},{13,9},{2,14},{6,2},{... | collective-permute-start | bytes 196616 | tf_op jit(solution)/shard_map/ppermute | solution.py:362
  32.1 6.8 %collective-permute-start.11 = (bf16[128,256]{1,0:T(8,128)(2,1)S(1)}, bf16[128,256]{1,0:T(8,128)(2,1)S(1)}, u32[]{:S(2)}, u32[]{:S(2)}) collective-permute-start(bf16[128,256]{1,0:T(8,128)(2,1)S(1)} %bitcast.41), channel_id=1, source_target_pairs={{0,8},{4,12},{8,0},{12,4},{1,9},{5,13},{9,1},{13,5},{2,10},{6,14},... | collective-permute-start | bytes 196616 | tf_op jit(solution)/shard_map/ppermute | solution.py:362
  32.1 6.8 %collective-permute-start.10 = (bf16[128,256]{1,0:T(8,128)(2,1)S(1)}, bf16[128,256]{1,0:T(8,128)(2,1)S(1)}, u32[]{:S(2)}, u32[]{:S(2)}) collective-permute-start(bf16[128,256]{1,0:T(8,128)(2,1)S(1)} %bitcast.42), channel_id=1, source_target_pairs={{0,4},{4,8},{8,12},{12,0},{1,5},{5,9},{9,13},{13,1},{2,6},{6,10},{... | collective-permute-start | bytes 196616 | tf_op jit(solution)/shard_map/ppermute | solution.py:362
  33.4 7.1 %collective-permute-start.9 = (f32[3,48,48]{2,1,0:T(8,128)S(1)}, f32[3,48,48]{2,1,0:T(8,128)S(1)}, u32[]{:S(2)}, u32[]{:S(2)}) collective-permute-start(f32[3,48,48]{2,1,0:T(8,128)S(1)} %add_add_fusion.1), channel_id=1, source_target_pairs={{0,12},{4,0},{8,4},{12,8},{1,13},{5,1},{9,5},{13,9},{2,14},{6,2},{... | collective-permute-start | bytes 82952 | tf_op jit(solution)/shard_map/ppermute | solution.py:362
  35.4 9.8 %collective-permute-start.8 = (f32[3,48,48]{2,1,0:T(8,128)S(1)}, f32[3,48,48]{2,1,0:T(8,128)S(1)}, u32[]{:S(2)}, u32[]{:S(2)}) collective-permute-start(f32[3,48,48]{2,1,0:T(8,128)S(1)} %add_add_fusion.1), channel_id=1, source_target_pairs={{0,8},{4,12},{8,0},{12,4},{1,9},{5,13},{9,1},{13,5},{2,10},{6,14},... | collective-permute-start | bytes 82952 | tf_op jit(solution)/shard_map/ppermute | solution.py:362
  38.9 6.3 %collective-permute-start.7 = (f32[3,48,48]{2,1,0:T(8,128)S(1)}, f32[3,48,48]{2,1,0:T(8,128)S(1)}, u32[]{:S(2)}, u32[]{:S(2)}) collective-permute-start(f32[3,48,48]{2,1,0:T(8,128)S(1)} %add_add_fusion.1), channel_id=1, source_target_pairs={{0,4},{4,8},{8,12},{12,0},{1,5},{5,9},{9,13},{13,1},{2,6},{6,10},{... | collective-permute-start | bytes 82952 | tf_op jit(solution)/shard_map/ppermute | solution.py:362
  38.9 7.5 %collective-permute-start.16 = (bf16[4,128,256]{2,1,0:T(8,128)(2,1)S(1)}, bf16[4,128,256]{2,1,0:T(8,128)(2,1)S(1)}, u32[]{:S(2)}, u32[]{:S(2)}) collective-permute-start(bf16[4,128,256]{2,1,0:T(8,128)(2,1)S(1)} %pad_maximum_fusion.1.refs_2_), channel_id=1, source_target_pairs={{0,1},{1,0},{2,3},{3,2},{4,5},{5,4},{6,7},{7,6},{8,9},{9,8},{10,11... | collective-permute-start | bytes 786440 | tf_op jit(solution)/shard_map/ppermute | solution.py:367
  40.4 6.0 %collective-permute-start.18 = (bf16[4,128,256]{2,1,0:T(8,128)(2,1)S(1)}, bf16[4,128,256]{2,1,0:T(8,128)(2,1)S(1)}, u32[]{:S(2)}, u32[]{:S(2)}) collective-permute-start(bf16[4,128,256]{2,1,0:T(8,128)(2,1)S(1)} %collective-permute-done.17.refs_4_), channel_id=1, source_target_pairs={{0,1},{1,0},{2,3},{3,2},{4,5},{5,4},{6,7},{7,6},{8,9},{9,8},{10,11... | collective-permute-start | bytes 786440 | tf_op jit(solution)/shard_map/ppermute | solution.py:367
  46.4 2.0 %copy-start.1 = (bf16[128,27,512]{2,0,1:T(8,128)(2,1)S(1)}, bf16[128,27,512]{2,0,1:T(8,128)(2,1)}, u32[]{:S(2)}) copy-start(bf16[128,27,512]{2,0,1:T(8,128)(2,1)} %param.12) | copy-start | bytes 10616836
  54.2 8.3 %collective-permute-start.21 = (bf16[256,128]{1,0:T(8,128)(2,1)S(1)}, bf16[256,128]{1,0:T(8,128)(2,1)S(1)}, u32[]{:S(2)}, u32[]{:S(2)}) collective-permute-start(bf16[256,128]{1,0:T(8,128)(2,1)S(1)} %get-tuple-element.28), channel_id=1, source_target_pairs={{0,3},{1,0},{2,1},{3,2},{4,7},{5,4},{6,5},{7,6},{8,11},{9,8},{10,9... | collective-permute-start | bytes 196616 | tf_op jit(solution)/shard_map/ppermute | solution.py:362
  54.8 7.8 %collective-permute-start.20 = (bf16[256,128]{1,0:T(8,128)(2,1)S(1)}, bf16[256,128]{1,0:T(8,128)(2,1)S(1)}, u32[]{:S(2)}, u32[]{:S(2)}) collective-permute-start(bf16[256,128]{1,0:T(8,128)(2,1)S(1)} %get-tuple-element.29), channel_id=1, source_target_pairs={{0,2},{1,3},{2,0},{3,1},{4,6},{5,7},{6,4},{7,5},{8,10},{9,11},{10,... | collective-permute-start | bytes 196616 | tf_op jit(solution)/shard_map/ppermute | solution.py:362
  56.4 6.2 %collective-permute-start.19 = (bf16[256,128]{1,0:T(8,128)(2,1)S(1)}, bf16[256,128]{1,0:T(8,128)(2,1)S(1)}, u32[]{:S(2)}, u32[]{:S(2)}) collective-permute-start(bf16[256,128]{1,0:T(8,128)(2,1)S(1)} %get-tuple-element.30), channel_id=1, source_target_pairs={{0,1},{1,2},{2,3},{3,0},{4,5},{5,6},{6,7},{7,4},{8,9},{9,10},{10,1... | collective-permute-start | bytes 196616 | tf_op jit(solution)/shard_map/ppermute | solution.py:362

commit v3 on v2

--- a/solution.py
+++ b/solution.py
@@ -8,7 +8,8 @@
 from jax.sharding import PartitionSpec as P
 
 BW = 32
-LOW = 256
+TAPS = 32
+LOW = 128
 F32 = jnp.float32
 BF16 = jnp.bfloat16
 VM = pl.BlockSpec(memory_space=pltpu.VMEM)
@@ -41,22 +42,95 @@
     return lax.broadcasted_iota(jnp.int32, shape, dim)
 
 
+def hot(condition):
+    return condition.astype(F32).astype(BF16)
+
+
+def pack_body(labels, cells, cots, slab, first, last, cot, ids, raw_cells, raw_cots, sems):
+    copies = [
+        pltpu.make_async_copy(cells, raw_cells, sems.at[0]),
+        pltpu.make_async_copy(labels, ids, sems.at[1]),
+        pltpu.make_async_copy(cots, raw_cots, sems.at[2]),
+    ]
+    for copy in copies:
+        copy.start()
+    cb, planes, width = cells.shape
+    lanes = planes * width
+    cols = labels.shape[2]
+    copies[0].wait()
+    for p in range(planes):
+        block = raw_cells[:, p, :]
+        for to in (slab, first, last):
+            to[:cb, p * width : (p + 1) * width] = block
+    copies[1].wait()
+    for to, plane in ((first, ids[0]), (last, ids[labels.shape[0] - 1])):
+        parts = [plane & 255, plane >> 8]
+        rows = jnp.concatenate([part[:, i : i + lanes] for part in parts for i in range(0, cols, lanes)], axis=0)
+        to[cb:, :] = rows.astype(F32).astype(BF16)
+    copies[2].wait()
+    for p in range(planes):
+        cot[:, p * width : (p + 1) * width] = raw_cots[:, p, :]
+
+
+def pack_call(labels, cells, cots):
+    depth, rows, cols = labels.shape
+    cb, planes, width = cells.shape
+    lanes = planes * width
+    more = 2 * rows * cols // lanes
+    S = jax.ShapeDtypeStruct
+    outs = [S((cb, lanes), BF16), S((cb + more, lanes), BF16), S((cb + more, lanes), BF16)]
+    outs += [S((cb, lanes), BF16), S(labels.shape, jnp.int32)]
+    scratch = [pltpu.VMEM(cells.shape, BF16), pltpu.VMEM(cots.shape, BF16), pltpu.SemaphoreType.DMA((3,))]
+    return call(pack_body, outs, [HB] * 3, scratch, 1e9, 1 << 18, 56)(labels, cells, cots)
+
+
+def unpack_body(count, *refs):
+    labels, slab, got = refs[0], refs[1], refs[2 : 2 + count]
+    slabs, below, above, top, bottom = refs[3 + count :]
+    cb, lanes = slab.shape
+    depth, rows, cols = labels.shape
+    slabs[0] = slab[...]
+    for r in range(count):
+        slabs[r + 1] = got[r][:cb, :]
+    planes = []
+    for ref in (got[0], got[count - 1]):
+        rest = ref[cb:, :].astype(F32)
+        pieces = [rest[i * rows : (i + 1) * rows] for i in range(rest.shape[0] // rows)]
+        half = len(pieces) // 2
+        low, high = (jnp.concatenate(part, axis=1) for part in (pieces[:half], pieces[half:]))
+        planes.append((low + 256.0 * high).astype(jnp.int32))
+    below[...] = planes[0]
+    above[...] = planes[1]
+    all_planes = [planes[0]] + [labels[x] for x in range(depth)] + [planes[1]]
+    top[...] = jnp.concatenate([plane[:1] for plane in all_planes], axis=0)
+    bottom[...] = jnp.concatenate([plane[rows - 1 :] for plane in all_planes], axis=0)
+
+
+def unpack_call(labels, slab, got, after):
+    depth, rows, cols = labels.shape
+    cb, lanes = slab.shape
+    S = jax.ShapeDtypeStruct
+    outs = [S((len(got) + 1, cb, lanes), BF16)]
+    outs += [S((rows, cols), jnp.int32)] * 2 + [S((depth + 2, cols), jnp.int32)] * 2
+    body = functools.partial(unpack_body, len(got))
+    return call(body, outs, [VM] * (3 + len(got)), [], 2e8, 1 << 18, 12)(labels, slab, *got, after)
+
+
 def prep_body(rows, taps, table, kernel, lookup):
     ch = table.shape[0]
     shape = kernel.shape
     step = (rows + 2) * ch
-    spread = (iota((shape[0], 3 * ch), 0) // rows == iota((shape[0], 3 * ch), 1)).astype(F32).astype(BF16)
+    spread = hot(iota((shape[0], 3 * ch), 0) // rows == iota((shape[0], 3 * ch), 1))
     m, n = iota((3 * ch, shape[1]), 0), iota((3 * ch, shape[1]), 1)
-    repeat = ((m // ch == n // step) & (m % ch == n % ch)).astype(F32).astype(BF16)
+    repeat = hot((m // ch == n // step) & (m % ch == n % ch))
     gap = (iota(shape, 1) % step) // ch - iota(shape, 0) % rows
     total = jnp.zeros(shape, F32)
     for b in range(3):
         tall = jnp.dot(spread, taps[b], preferred_element_type=F32).astype(BF16)
         total = jnp.where(gap == b, jnp.dot(tall, repeat, preferred_element_type=F32), total)
     kernel[...] = total.astype(BF16)
-    low = lookup.shape[1]
-    for high in range(table.shape[1] // low):
-        lookup[high * ch : (high + 1) * ch, :] = table[:, high * low : (high + 1) * low]
+    for high in range(table.shape[1] // LOW):
+        lookup[high * ch : (high + 1) * ch, :] = table[:, high * LOW : (high + 1) * LOW]
 
 
 def prep_call(taps, table, rows):
@@ -69,10 +143,15 @@
         ],
         [VM] * 2,
         [],
-        2e9,
-        1 << 20,
+        1.2e9,
+        1 << 18,
         16,
     )(taps, table)
+
+
+def split(x):
+    high = x.astype(BF16)
+    return high, (x - high.astype(F32)).astype(BF16)
 
 
 def fine_body(scale, own, below, above, left, right, table, kernel, cot, out, part, feats, grads):
@@ -85,15 +164,13 @@
     for x in range(depth + 2):
         for y in range(rows + 2):
             if y == 0:
-                ids = left[x]
-                ids = jnp.where(lane == 0, -1, ids)
+                ids = jnp.where(lane == 0, -1, left[x : x + 1])
             elif y == rows + 1:
-                ids = right[x]
-                ids = jnp.where(lane == lanes - 1, -1, ids)
+                ids = jnp.where(lane == lanes - 1, -1, right[x : x + 1])
             elif x == 0:
-                ids = below[0, y - 1 : y]
+                ids = below[y - 1 : y]
             elif x == depth + 1:
-                ids = above[0, y - 1 : y]
+                ids = above[y - 1 : y]
             else:
                 ids = own[x - 1, y - 1 : y]
             if x == 0:
@@ -101,8 +178,8 @@
             if x == depth + 1:
                 ids = jnp.where(place == count - 1, -1, ids)
             low = jnp.where(ids < 0, -1, ids & (LOW - 1))
-            hot = jnp.where(key == low.astype(F32).astype(BF16), one, none)
-            picked = jnp.dot(table[...], hot, preferred_element_type=F32)
+            match = jnp.where(key == low.astype(F32).astype(BF16), one, none)
+            picked = jnp.dot(table[...], match, preferred_element_type=F32)
             bit = 9
             while picked.shape[0] > ch:
                 half = picked.shape[0] // 2
@@ -134,44 +211,50 @@
         term = dot_nt(shifted, window)
         grads[...] = term if x == 0 else grads[...] + term
     total = grads[...]
-    wide = total.shape[1]
-    y_out = lax.broadcasted_iota(jnp.int32, total.shape, 0) % rows
-    y_in = (lax.broadcasted_iota(jnp.int32, total.shape, 1) % step) // ch
-    fold_from = lax.broadcasted_iota(jnp.int32, (wide, 3 * ch), 0)
-    fold_to = lax.broadcasted_iota(jnp.int32, (wide, 3 * ch), 1)
-    fold = ((fold_from // step == fold_to // ch) & (fold_from % ch == fold_to % ch)).astype(F32).astype(BF16)
+    shape = total.shape
+    gap = (iota(shape, 1) % step) // ch - iota(shape, 0) % rows
+    gather = hot(iota((3 * ch, shape[0]), 0) == iota((3 * ch, shape[0]), 1) // rows)
+    m, n = iota((shape[1], 3 * ch), 0), iota((shape[1], 3 * ch), 1)
+    fold = hot((m // step == n // ch) & (m % ch == n % ch))
+    high, rest = split(total)
+    sums = []
     for b in range(3):
-        kept = jnp.where(y_in - y_out == b, total, 0.0)
-        kept = kept.reshape(3 * ch, rows, wide).sum(axis=1)
-        high = kept.astype(BF16)
-        rest = kept - high.astype(F32)
-        middle = rest.astype(BF16)
-        lowest = (rest - middle.astype(F32)).astype(BF16)
-        folded = jnp.dot(high, fold, preferred_element_type=F32)
-        folded = folded + jnp.dot(middle, fold, preferred_element_type=F32)
-        folded = folded + jnp.dot(lowest, fold, preferred_element_type=F32)
-        part[b] = folded * scale
+        keep = hot(gap == b)
+        kept = jnp.dot(gather, high * keep, preferred_element_type=F32)
+        kept = kept + jnp.dot(gather, rest * keep, preferred_element_type=F32)
+        sums.append(kept)
+    tall = jnp.concatenate([piece for b in range(3) for piece in split(sums[b])], axis=0)
+    tall = jnp.dot(tall, fold, preferred_element_type=F32)
+    m, n = iota((3 * ch, ch * TAPS), 0), iota((3 * ch, ch * TAPS), 1)
+    spot = jnp.where(m % ch == n // TAPS, n % TAPS - 9 * (m // ch), -1)
+    result = jnp.zeros((ch, ch * TAPS), F32)
+    for b in range(3):
+        block = tall[6 * b * ch : (6 * b + 3) * ch] + tall[(6 * b + 3) * ch : (6 * b + 6) * ch]
+        for e in range(3):
+            both = jnp.concatenate(split(block[e * ch : (e + 1) * ch]), axis=0)
+            moved = jnp.dot(both, hot(spot == 3 * b + e), preferred_element_type=F32)
+            result = result + (moved[:ch] + moved[ch:])
+    part[...] = result * scale
 
 
 def fine_call(scale, own, below, above, left, right, table, kernel, cot):
     depth, rows, cols = own.shape
     ch = cot.shape[0]
     body = functools.partial(fine_body, scale)
-    macs = 3 * ch * rows * 3 * ch * (rows + 2) * cols * depth * 2
     return call(
         body,
         [
             jax.ShapeDtypeStruct((ch, depth, rows, cols), BF16),
-            jax.ShapeDtypeStruct((3, 3 * ch, 3 * ch), F32),
+            jax.ShapeDtypeStruct((ch, ch * TAPS), F32),
         ],
         [VM] * 8,
         [
             pltpu.VMEM(((depth + 2) * (rows + 2) * ch, cols), BF16),
             pltpu.VMEM((3 * ch * rows, 3 * ch * (rows + 2)), F32),
         ],
-        2 * macs,
+        7.4e9,
         4 << 20,
-        24,
+        20,
     )(own, below, above, left, right, table, kernel, cot)
 
 
@@ -185,10 +268,12 @@
     return masks
 
 
-def bott_body(pieces, planes, *refs):
-    weight, cots = refs[0], refs[1]
-    ins = refs[2 : 2 + pieces]
-    own_out, deltas, padded, share, mine, acts, rows_t = refs[2 + pieces :]
+def bott_body(pieces, slabs, planes, *refs):
+    weight, refs = refs[0], refs[1:]
+    cots, refs = refs[:slabs], refs[slabs:]
+    ins, refs = refs[:pieces], refs[pieces:]
+    parts, refs = refs[:pieces], refs[pieces:]
+    own_out, deltas, padded, share, mine, part_sum, acts, rows_t, cot_at = refs
     slabs, cb, lanes = ins[0].shape
     width = lanes // planes
     c_all = cb * pieces
@@ -196,6 +281,9 @@
     total = slabs * planes
     place = lax.axis_index("space")
     chan = lax.axis_index("chan")
+    part_sum[...] = sum((part[...] for part in parts[1:]), parts[0][...])
+    for r in range(slabs):
+        cot_at[lax.rem(place - r + slabs, slabs)] = cots[r][...]
     padded[:, :width] = jnp.zeros((c_all, width), BF16)
     padded[:, (total + 1) * width :] = jnp.zeros((c_all, width), BF16)
     for j in range(pieces):
@@ -222,7 +310,7 @@
                 if turn:
                     block = jnp.where(masks[k], pltpu.roll(block, turn, 1), 0.0)
                 pre[p] = pre[p] + block
-        cot = cots[lax.rem(place - n + slabs, slabs)].astype(F32)
+        cot = cot_at[n].astype(F32)
         for p in range(planes):
             act, slope = silu_parts(pre[p])
             acts[n, :, p * width : (p + 1) * width] = act
@@ -257,33 +345,34 @@
         own_out[:, p, :] = act[:, p * width : (p + 1) * width].astype(BF16)
 
 
-def bott_call(weight, cots, ins, planes):
+def bott_call(weight, cots, ins, parts, planes):
     slabs, cb, lanes = ins[0].shape
     pieces = len(ins)
-    o_own = cots.shape[1]
+    o_own = cots[0].shape[0]
     c_all = pieces * cb
     width = lanes // planes
     total = slabs * planes
     S = jax.ShapeDtypeStruct
-    macs = 27 * o_own * c_all * (total + planes) * width
     return call(
-        functools.partial(bott_body, pieces, planes),
+        functools.partial(bott_body, pieces, slabs, planes),
         [
             S((o_own, planes, width), BF16),
             S((o_own, (total + 2) * width), F32),
             S((c_all, (total + 2) * width), BF16),
             S((pieces, lanes, cb), BF16),
             S((pieces, lanes, cb), F32),
-        ],
-        [VM] * (2 + pieces),
+            S(parts[0].shape, F32),
+        ],
+        [VM] * (1 + slabs + 2 * pieces),
         [
             pltpu.VMEM((slabs, o_own, lanes), F32),
             pltpu.VMEM((3, (planes + 2) * (width + 2 * BW), o_own), BF16),
-        ],
-        2 * macs,
+            pltpu.VMEM((slabs, o_own, lanes), BF16),
+        ],
+        6.6e9,
         8 << 20,
         24,
-    )(weight, cots, *ins)
+    )(weight, *cots, *ins, *parts)
 
 
 def wgrad_body(scale, delta, full, out, shifted, stage, sems):
@@ -325,15 +414,17 @@
             pltpu.VMEM((2, 9, o_own, c_all), F32),
             pltpu.SemaphoreType.DMA((2,)),
         ],
-        2 * 27 * o_own * c_all * length,
+        6.6e9,
         8 << 20,
         32,
         [HB],
     )(delta, full)[0]
 
 
-def last_body(count, *refs):
-    mine, others, out = refs[0], refs[1 : 1 + count], refs[1 + count]
+def last_body(count, spaces, *refs):
+    mine, refs = refs[0], refs[1:]
+    others, refs = refs[:count], refs[count:]
+    parts, (out, taps) = refs[:spaces], refs[spaces:]
     total = mine[0]
     for other in others:
         total = total + other[...].astype(F32)
@@ -342,19 +433,26 @@
     width = turned.shape[1] // planes
     for p in range(planes):
         out[:, p, :] = turned[:, p * width : (p + 1) * width].astype(BF16)
-
-
-def last_call(mine, others, planes):
+    grad = sum((part[...] for part in parts[1:]), parts[0][...])
+    for c in range(taps.shape[0]):
+        taps[c] = grad[:, c * TAPS : c * TAPS + taps.shape[2]]
+
+
+def last_call(mine, others, parts, planes):
     lanes, cb = mine.shape[1:]
+    ch = parts[0].shape[0]
     return call(
-        functools.partial(last_body, len(others)),
-        [jax.ShapeDtypeStruct((cb, planes, lanes // planes), BF16)],
-        [VM] * (1 + len(others)),
+        functools.partial(last_body, len(others), len(parts)),
+        [
+            jax.ShapeDtypeStruct((cb, planes, lanes // planes), BF16),
+            jax.ShapeDtypeStruct((ch, ch, 27), F32),
+        ],
+        [VM] * (1 + len(others) + len(parts)),
         [],
         lanes * cb * 4,
         lanes * cb * 12,
-        16,
-    )(mine, *others)[0]
+        12,
+    )(mine, *others, *parts)
 
 
 def hop(x, axis, offset):
@@ -375,35 +473,32 @@
     lanes = planes * width
     o_own = bott_cot.shape[0]
 
-    below = hop(labels[-1:], "space", 1)
-    above = hop(labels[:1], "space", spaces - 1)
-    slab = bott_in.reshape(cb, lanes)
-    slabs = jnp.stack([slab] + [hop(slab, "space", r) for r in range(1, spaces)])
-    framed = jnp.concatenate([below, labels, above], axis=0)
-    left = hop(framed[:, -1:], "chan", 1)
-    right = hop(framed[:, :1], "chan", chans - 1)
+    slab, first, last, cot, ids = pack_call(labels, bott_in, bott_cot)
+    taps = fine_weight.reshape(3, 3, 3, ch, ch).transpose(1, 2, 4, 0, 3).reshape(3, 3 * ch, 3 * ch)
+    kernel, lookup = prep_call(taps, table.T, rows)
+    sends = [last] + [slab] * (spaces - 3) + [first]
+    got = [hop(x, "space", r + 1) for r, x in enumerate(sends)]
+    slabs, below, above, top, bottom = unpack_call(ids, slab, got, kernel)
+    left = hop(bottom, "chan", 1)
+    right = hop(top, "chan", chans - 1)
     pieces = {0: slabs}
     bits = [1 << i for i in range(chans.bit_length() - 1)]
     for bit in bits[1:] + bits[:1]:
         pieces.update({j ^ bit: swap(x, "chan", bit) for j, x in list(pieces.items())})
     ins = [pieces[j] for j in range(chans)]
-    cot = bott_cot.reshape(o_own, lanes)
-    cots = jnp.stack([cot] + [hop(cot, "space", r) for r in range(1, spaces)])
-
-    taps = fine_weight.reshape(3, 3, 3, ch, ch).transpose(1, 2, 4, 0, 3).reshape(3, 3 * ch, 3 * ch)
-    kernel, lookup = prep_call(taps, table.T, rows)
+    cots = [cot] + [hop(cot, "space", r) for r in range(1, spaces)]
+
+    weight = bott_weight.transpose(1, 0, 2).reshape(27 * o_own, cb * chans)
     scale = (depth * spaces * rows * chans * cols) ** -0.5
-    fine_out, part = fine_call(scale, labels, below, above, left, right, lookup, kernel, fine_cot)
-    part = part + sum(hop(part, "chan", r) for r in range(1, chans))
-    part = part + sum(hop(part, "space", r) for r in range(1, spaces))
-    fine_wgrad = part.reshape(3, 3, ch, 3, ch).transpose(3, 0, 1, 4, 2).reshape(27, ch, ch)
-
-    weight = bott_weight.transpose(1, 0, 2).reshape(27 * o_own, cb * chans)
-    bott_out, delta, full, share, mine = bott_call(weight, cots, ins, planes)
+    fine_out, part = fine_call(scale, ids, below, above, left, right, lookup, kernel, fine_cot)
+    parts = [part] + [hop(part, "chan", r) for r in range(1, chans)]
+
+    bott_out, delta, full, share, mine, part = bott_call(weight, cots, ins, parts, planes)
     others = [hop(share[r], "chan", r) for r in range(1, chans)]
+    parts = [part] + [hop(part, "space", r) for r in range(1, spaces)]
     bott_wgrad = wgrad_call((planes * spaces * width) ** -0.5, delta, full).transpose(1, 0, 2)
-    bott_dgrad = last_call(mine, others, planes)
-    return fine_out, fine_wgrad, bott_out, bott_dgrad, bott_wgrad
+    bott_dgrad, fine_wgrad = last_call(mine, others, parts, planes)
+    return fine_out, fine_wgrad.transpose(2, 0, 1), bott_out, bott_dgrad, bott_wgrad
 
 
 def solution(mesh):

time: 63.8 us -> 53.1 us (0.83)
  waiting for transfers between devices: 11.6 us -> 2.99 us
  local copies, waits for them, and re-layouts: 6.93 us -> 0.51 us
  starting transfers between devices: 23 us -> 27.1 us
    ppermute x19 -> x17, waiting for transfers between devices: 11.6 us -> 2.98 us  [hop(): lax.ppermute(x, axis, [(i, (i + offset) % count) for i in range(count)])]
    unnamed x18 -> x15, local copies, waits for them, and re-layouts: 5.5 us -> 0.23 us
    ppermute x19 -> x17, starting transfers between devices: 21.1 us -> 24.1 us  [hop(): lax.ppermute(x, axis, [(i, (i + offset) % count) for i in range(count)])]
    pallas_call x2 -> x4, Pallas kernels: 6.66 us -> 8.67 us  [the longest x1 5.82 us: bott_call(): call(functools.partial(bott_body, pieces, slabs, planes), [S((o_own, plan...]
    pallas_call x1, Pallas kernels: 7.83 us -> 6.38 us  [fine_call(): call(body, [jax.ShapeDtypeStruct((ch, depth, rows, cols), BF16), jax.Shap...]
    ppermute x3, starting transfers between devices: 1.87 us -> 2.94 us  [swap(): return lax.ppermute(x, axis, [(i, i ^ bit) for i in range(count)])]
    slice x2 -> x0, local copies, waits for them, and re-layouts: 0.75 us -> none  [the longest x1 0.74 us: shards(): above = hop(labels[:1], 'space', spaces - 1)]
  transfers between devices with their start and end apart: 22 -> 20, of which waited for: 5 -> 5; matrix products, arithmetic and copies ran while one was open for 5% -> 1% of each run, Pallas kernels for 23% -> 24%
where the time goes in v3:
time: 53.1 us; the launch traced here: 53 us
  starting transfers between devices  27.1 us (51%)
  Pallas kernels  21.6 us (41%)
  waiting for transfers between devices  2.99 us (6%)
  between operations  0.82 us (2%)
    ppermute x17, starting transfers between devices, hop(): lax.ppermute(x, axis, [(i, (i + offset) % count) for i in range(count)])  24.1 us
    pallas_call x1, Pallas kernels, fine_call(): call(body, [jax.ShapeDtypeStruct((ch, depth, rows, cols), BF16), jax.Shap...  6.38 us
    pallas_call x1, Pallas kernels, bott_call(): call(functools.partial(bott_body, pieces, slabs, planes), [S((o_own, plan...  5.82 us
    pallas_call x1, Pallas kernels, wgrad_call(): call(functools.partial(wgrad_body, scale), [jax.ShapeDtypeStruct((27, o_o...  5.71 us
    ppermute x17, waiting for transfers between devices, hop(): lax.ppermute(x, axis, [(i, (i + offset) % count) for i in range(count)])  2.98 us
    ppermute x3, starting transfers between devices, swap(): return lax.ppermute(x, axis, [(i, i ^ bit) for i in range(count)])  2.94 us
    pallas_call x1, Pallas kernels, pack_call(): call(pack_body, outs, [HB] * 3, scratch, 1000000000.0, 1 << 18, 56)  1.94 us
  transfers between devices with their start and end apart: 20, of which 5 were waited for; matrix products, arithmetic and copies ran while one was open for 1% of the time, Pallas kernels for 24%

profile of v3, /device:TPU:1, one launch (start us, length us, event | category | flops | bytes accessed | tf_op | source)
XLA Modules:
  0.0 53.0 jit_solution(10088322914216896499)
XLA Ops:
  0.6 0.0 copy-start.6
  0.6 0.0 copy-start.5
  0.7 1.9 %shard_map.110 = (bf16[128,256]{1,0:T(8,128)(2,1)}, bf16[160,256]{1,0:T(8,128)(2,1)}, bf16[160,256]{1,0:T(8,128)(2,1)}, bf16[128,256]{1,0:T(8,128)(2,1)}, s32[4,8,512]{2,1,0:T(8,128)}) custom-call(s32[4,8,512]{2,1,0:T(8,128)} %labels.1, bf16[128,2,128]{2,1,0:T(2,128)(2,1)} %cells.1, bf16[128,2,128]{2,1,0:T(2,128)(2,1)} %cots.1), custom_call_target="tpu_custom_call" | custom-call | flops 1000000000 | bytes 262144 | tf_op jit(solution)/shard_map/pallas_call | solution.py:84
  2.6 0.0 copy-start
  2.6 0.0 copy-start.1
  2.6 0.0 copy-start.4
  2.6 0.0 copy-start.3
  2.7 3.2 %collective-permute-start.1 = (bf16[128,256]{1,0:T(8,128)(2,1)}, bf16[128,256]{1,0:T(8,128)(2,1)S(1)}, u32[]{:S(2)}, u32[]{:S(2)}) collective-permute-start(bf16[128,256]{1,0:T(8,128)(2,1)} %get-tuple-element.28.refs_1_), channel_id=1, source_target_pairs={{0,8},{4,12},{8,0},{12,4},{1,9},{5,13},{9,1},{13,5},{2,10},{6,14},... | collective-permute-start | bytes 196616 | tf_op jit(solution)/shard_map/ppermute | solution.py:460
  5.9 1.3 %collective-permute-start = (bf16[160,256]{1,0:T(8,128)(2,1)}, bf16[160,256]{1,0:T(8,128)(2,1)S(1)}, u32[]{:S(2)}, u32[]{:S(2)}) collective-permute-start(bf16[160,256]{1,0:T(8,128)(2,1)} %get-tuple-element.29), channel_id=1, source_target_pairs={{0,4},{4,8},{8,12},{12,0},{1,5},{5,9},{9,13},{13,1},{2,6},{6,10},{... | collective-permute-start | bytes 245768 | tf_op jit(solution)/shard_map/ppermute | solution.py:460
  7.2 2.0 %collective-permute-start.2 = (bf16[160,256]{1,0:T(8,128)(2,1)}, bf16[160,256]{1,0:T(8,128)(2,1)S(1)}, u32[]{:S(2)}, u32[]{:S(2)}) collective-permute-start(bf16[160,256]{1,0:T(8,128)(2,1)} %get-tuple-element.30), channel_id=1, source_target_pairs={{0,12},{4,0},{8,4},{12,8},{1,13},{5,1},{9,5},{13,9},{2,14},{6,2},{... | collective-permute-start | bytes 245768 | tf_op jit(solution)/shard_map/ppermute | solution.py:460
  9.1 0.0 copy-done.6
  9.1 0.2 copy.13
  9.3 0.2 copy.14
  9.5 0.1 reshape.20.taps
  9.6 0.0 copy-done.5
  9.6 0.8 %shard_map.111 = (bf16[384,480]{1,0:T(8,128)(2,1)S(1)}, bf16[128,128]{1,0:T(8,128)(2,1)S(1)}) custom-call(bf16[3,48,48]{2,1,0:T(8,128)(2,1)S(1)} %reshape.20.taps, bf16[16,1024]{1,0:T(8,128)(2,1)S(1)} %bitcast.16), custom_call_target="tpu_custom_call" | custom-call | flops 1200000000 | bytes 262144 | tf_op jit(solution)/shard_map/pallas_call | solution.py:138
  10.4 0.0 collective-permute-done.1.refs_3_
  10.5 0.8 %collective-permute-done.refs_2_ = bf16[160,256]{1,0:T(8,128)(2,1)S(1)} collective-permute-done((bf16[160,256]{1,0:T(8,128)(2,1)}, bf16[160,256]{1,0:T(8,128)(2,1)S(1)}, u32[]{:S(2)}, u32[]{:S(2)}) %collective-permute-start) | collective-permute-done | bytes 81952 | tf_op jit(solution)/shard_map/ppermute | solution.py:460
  11.3 0.7 %collective-permute-done.2.refs_4_ = bf16[160,256]{1,0:T(8,128)(2,1)S(1)} collective-permute-done((bf16[160,256]{1,0:T(8,128)(2,1)}, bf16[160,256]{1,0:T(8,128)(2,1)S(1)}, u32[]{:S(2)}, u32[]{:S(2)}) %collective-permute-start.2) | collective-permute-done | bytes 81952 | tf_op jit(solution)/shard_map/ppermute | solution.py:460
  11.9 0.0 copy-done
  11.9 0.0 copy-done.1
  12.0 2.0 %collective-permute-start.9 = (bf16[4,128,256]{2,1,0:T(8,128)(2,1)S(1)}, bf16[4,128,256]{2,1,0:T(8,128)(2,1)S(1)}, u32[]{:S(2)}, u32[]{:S(2)}) collective-permute-start(bf16[4,128,256]{2,1,0:T(8,128)(2,1)S(1)} %get-tuple-element.39.refs_5_), channel_id=1, source_target_pairs={{0,2},{1,3},{2,0},{3,1},{4,6},{5,7},{6,4},{7,5},{8,10},{9,11},{10,... | collective-permute-start | bytes 786440 | tf_op jit(solution)/shard_map/ppermute | solution.py:465
  14.0 1.8 %collective-permute-start.3 = (s32[6,512]{1,0:T(8,128)S(1)}, s32[6,512]{1,0:T(8,128)S(1)}, u32[]{:S(2)}, u32[]{:S(2)}) collective-permute-start(s32[6,512]{1,0:T(8,128)S(1)} %get-tuple-element.34), channel_id=1, source_target_pairs={{0,1},{1,2},{2,3},{3,0},{4,5},{5,6},{6,7},{7,4},{8,9},{9,10},{10,1... | collective-permute-start | bytes 36872 | tf_op jit(solution)/shard_map/ppermute | solution.py:460
  15.8 0.1 collective-permute-start.4
  15.9 0.0 copy-done.4
  15.9 2.8 %collective-permute-start.7 = (bf16[128,256]{1,0:T(8,128)(2,1)S(1)}, bf16[128,256]{1,0:T(8,128)(2,1)S(1)}, u32[]{:S(2)}, u32[]{:S(2)}) collective-permute-start(bf16[128,256]{1,0:T(8,128)(2,1)S(1)} %copy-done.4), channel_id=1, source_target_pairs={{0,12},{4,0},{8,4},{12,8},{1,13},{5,1},{9,5},{13,9},{2,14},{6,2},{... | collective-permute-start | bytes 196616 | tf_op jit(solution)/shard_map/ppermute | solution.py:460
  18.6 0.0 collective-permute-start.6
  18.6 0.0 collective-permute-done.3.left
  18.6 2.1 %collective-permute-start.5 = (bf16[128,256]{1,0:T(8,128)(2,1)S(1)}, bf16[128,256]{1,0:T(8,128)(2,1)S(1)}, u32[]{:S(2)}, u32[]{:S(2)}) collective-permute-start(bf16[128,256]{1,0:T(8,128)(2,1)S(1)} %copy-done.4), channel_id=1, source_target_pairs={{0,4},{4,8},{8,12},{12,0},{1,5},{5,9},{9,13},{13,1},{2,6},{6,10},{... | collective-permute-start | bytes 196616 | tf_op jit(solution)/shard_map/ppermute | solution.py:460
  20.7 0.4 collective-permute-done.4.right
  21.2 0.9 %collective-permute-start.8 = (bf16[4,128,256]{2,1,0:T(8,128)(2,1)S(1)}, bf16[4,128,256]{2,1,0:T(8,128)(2,1)S(1)}, u32[]{:S(2)}, u32[]{:S(2)}) collective-permute-start(bf16[4,128,256]{2,1,0:T(8,128)(2,1)S(1)} %get-tuple-element.39.refs_5_), channel_id=1, source_target_pairs={{0,1},{1,0},{2,3},{3,2},{4,5},{5,4},{6,7},{7,6},{8,9},{9,8},{10,11... | collective-permute-start | bytes 786440 | tf_op jit(solution)/shard_map/ppermute | solution.py:465
  22.1 0.0 collective-permute-done.9.refs_7_
  22.1 0.1 collective-permute-start.10
  22.1 0.0 copy-done.3
  22.1 0.0 copy-start.2
  22.1 6.4 %shard_map.113 = (bf16[16,4,8,512]{3,2,1,0:T(8,128)(2,1)}, f32[16,512]{1,0:T(8,128)S(1)}) custom-call(s32[4,8,512]{2,1,0:T(8,128)S(1)} %copy-done, s32[8,512]{1,0:T(8,128)S(1)} %get-tuple-element.32.below, s32[8,512]{1,0:T(8,128)S(1)} %get-tuple-element.33.above, s32[6,512]{1,0:T(8,128)S(1)} %collective-permute-done.3.left, ...), custom_call_target="tpu_custom_call" | custom-call | flops 7400000000 | bytes 4194304 | tf_op jit(solution)/shard_map/pallas_call | solution.py:244
  28.5 0.0 collective-permute-done.7.refs_4_
  28.5 0.5 collective-permute-start.13
  29.0 0.0 collective-permute-done.6.refs_3_
  29.0 1.6 %collective-permute-start.12 = (f32[16,512]{1,0:T(8,128)S(1)}, f32[16,512]{1,0:T(8,128)S(1)}, u32[]{:S(2)}, u32[]{:S(2)}) collective-permute-start(f32[16,512]{1,0:T(8,128)S(1)} %get-tuple-element.40.refs_9_), channel_id=1, source_target_pairs={{0,2},{1,3},{2,0},{3,1},{4,6},{5,7},{6,4},{7,5},{8,10},{9,11},{10,... | collective-permute-start | bytes 98312 | tf_op jit(solution)/shard_map/ppermute | solution.py:460
  30.6 0.0 collective-permute-done.5.refs_2_
  30.6 1.6 %collective-permute-start.11 = (f32[16,512]{1,0:T(8,128)S(1)}, f32[16,512]{1,0:T(8,128)S(1)}, u32[]{:S(2)}, u32[]{:S(2)}) collective-permute-start(f32[16,512]{1,0:T(8,128)S(1)} %get-tuple-element.40.refs_9_), channel_id=1, source_target_pairs={{0,1},{1,2},{2,3},{3,0},{4,5},{5,6},{6,7},{7,4},{8,9},{9,10},{10,1... | collective-permute-start | bytes 98312 | tf_op jit(solution)/shard_map/ppermute | solution.py:460
  32.2 0.1 collective-permute-done.13.refs_12_
  32.2 0.0 collective-permute-done.12.refs_11_
  32.3 1.0 %collective-permute-done.11.refs_10_ = f32[16,512]{1,0:T(8,128)S(1)} collective-permute-done((f32[16,512]{1,0:T(8,128)S(1)}, f32[16,512]{1,0:T(8,128)S(1)}, u32[]{:S(2)}, u32[]{:S(2)}) %collective-permute-start.11) | collective-permute-done | bytes 32800 | tf_op jit(solution)/shard_map/ppermute | solution.py:460
  33.2 0.0 collective-permute-done.8.refs_6_
  33.2 0.0 collective-permute-done.10.refs_8_
  33.2 0.0 copy-done.2
  33.2 5.8 %shard_map.114 = (bf16[128,2,128]{2,1,0:T(2,128)(2,1)}, f32[128,1280]{1,0:T(8,128)S(1)}, bf16[512,1280]{1,0:T(8,128)(2,1)S(1)}, bf16[4,256,128]{2,1,0:T(8,128)(2...) custom-call(bf16[3456,512]{1,0:T(8,128)(2,1)S(1)} %bitcast.15, bf16[128,256]{1,0:T(8,128)(2,1)S(1)} %copy-done.4, ...), custom_call_target="tpu_custom_call" | custom-call | flops 6600000000 | bytes 8388608 | tf_op jit(solution)/shard_map/pallas_call | solution.py:356
  39.0 1.5 %collective-permute-start.19 = (f32[16,512]{1,0:T(8,128)S(1)}, f32[16,512]{1,0:T(8,128)S(1)}, u32[]{:S(2)}, u32[]{:S(2)}) collective-permute-start(f32[16,512]{1,0:T(8,128)S(1)} %get-tuple-element.43.refs_4_), channel_id=1, source_target_pairs={{0,12},{4,0},{8,4},{12,8},{1,13},{5,1},{9,5},{13,9},{2,14},{6,2},{... | collective-permute-start | bytes 98312 | tf_op jit(solution)/shard_map/ppermute | solution.py:460
  40.5 0.4 collective-permute-start.18
  40.9 1.2 %collective-permute-start.17 = (f32[16,512]{1,0:T(8,128)S(1)}, f32[16,512]{1,0:T(8,128)S(1)}, u32[]{:S(2)}, u32[]{:S(2)}) collective-permute-start(f32[16,512]{1,0:T(8,128)S(1)} %get-tuple-element.43.refs_4_), channel_id=1, source_target_pairs={{0,4},{4,8},{8,12},{12,0},{1,5},{5,9},{9,13},{13,1},{2,6},{6,10},{... | collective-permute-start | bytes 98312 | tf_op jit(solution)/shard_map/ppermute | solution.py:460
  42.1 2.5 %collective-permute-start.16 = (bf16[256,128]{1,0:T(8,128)(2,1)S(1)}, bf16[256,128]{1,0:T(8,128)(2,1)S(1)}, u32[]{:S(2)}, u32[]{:S(2)}) collective-permute-start(bf16[256,128]{1,0:T(8,128)(2,1)S(1)} %get-tuple-element.49), channel_id=1, source_target_pairs={{0,3},{1,0},{2,1},{3,2},{4,7},{5,4},{6,5},{7,6},{8,11},{9,8},{10,9... | collective-permute-start | bytes 196616 | tf_op jit(solution)/shard_map/ppermute | solution.py:460
  44.6 0.8 %collective-permute-start.15 = (bf16[256,128]{1,0:T(8,128)(2,1)S(1)}, bf16[256,128]{1,0:T(8,128)(2,1)S(1)}, u32[]{:S(2)}, u32[]{:S(2)}) collective-permute-start(bf16[256,128]{1,0:T(8,128)(2,1)S(1)} %get-tuple-element.50), channel_id=1, source_target_pairs={{0,2},{1,3},{2,0},{3,1},{4,6},{5,7},{6,4},{7,5},{8,10},{9,11},{10,... | collective-permute-start | bytes 196616 | tf_op jit(solution)/shard_map/ppermute | solution.py:460
  45.5 0.0 collective-permute-done.19.refs_7_
  45.5 0.9 %collective-permute-start.14 = (bf16[256,128]{1,0:T(8,128)(2,1)S(1)}, bf16[256,128]{1,0:T(8,128)(2,1)S(1)}, u32[]{:S(2)}, u32[]{:S(2)}) collective-permute-start(bf16[256,128]{1,0:T(8,128)(2,1)S(1)} %get-tuple-element.51), channel_id=1, source_target_pairs={{0,1},{1,2},{2,3},{3,0},{4,5},{5,6},{6,7},{7,4},{8,9},{9,10},{10,1... | collective-permute-start | bytes 196616 | tf_op jit(solution)/shard_map/ppermute | solution.py:460
  46.3 5.7 %shard_map.116 = f32[27,128,512]{2,1,0:T(8,128)} custom-call(f32[128,1280]{1,0:T(8,128)S(1)} %get-tuple-element.47.delta, bf16[512,1280]{1,0:T(8,128)(2,1)S(1)} %get-tuple-element.48.full), custom_call_target="tpu_custom_call" | custom-call | flops 6600000000 | bytes 8388608 | tf_op jit(solution)/shard_map/pallas_call | solution.py:408
  52.0 0.0 collective-permute-done.18.refs_6_
  52.1 0.0 collective-permute-done.17.refs_5_
  52.1 0.0 collective-permute-done.16.refs_3_
  52.1 0.0 collective-permute-done.15.refs_2_
  52.1 0.0 collective-permute-done.14.refs_1_
  52.1 0.9 %shard_map.115 = (bf16[128,2,128]{2,1,0:T(2,128)(2,1)}, f32[16,16,27]{2,1,0:T(8,128)}) custom-call(f32[4,256,128]{2,1,0:T(8,128)S(1)} %get-tuple-element.41.refs_0_, bf16[256,128]{1,0:T(8,128)(2,1)S(1)} %collective-permute-done.14.refs_1_, bf16[256,128]{1,0:T(8,128)(2,1)S(1)} %collective-permute-done.15.refs_2_, ...), custom_call_target="tpu_custom_call" | custom-call | flops 131072 | bytes 393216 | tf_op jit(solution)/shard_map/pallas_call | solution.py:444
  (2 shorter events, 0.1 us)
Async XLA Ops:
  0.6 8.5 %copy-start.6 = (bf16[27,16,16]{0,2,1:T(8,128)(2,1)S(1)}, bf16[27,16,16]{0,2,1:T(8,128)(2,1)}, u32[]{:S(2)}) copy-start(bf16[27,16,16]{0,2,1:T(8,128)(2,1)} %param.9) | copy-start | bytes 41476
  0.6 9.0 %copy-start.5 = (bf16[1024,16]{0,1:T(8,128)(2,1)S(1)}, bf16[1024,16]{0,1:T(8,128)(2,1)}, u32[]{:S(2)}) copy-start(bf16[1024,16]{0,1:T(8,128)(2,1)} %param.8) | copy-start | bytes 98308
  2.6 9.3 %copy-start = (s32[4,8,512]{2,1,0:T(8,128)S(1)}, s32[4,8,512]{2,1,0:T(8,128)}, u32[]{:S(2)}) copy-start(s32[4,8,512]{2,1,0:T(8,128)} %get-tuple-element.27.refs_0_.own) | copy-start | bytes 196612
  2.6 9.3 %copy-start.1 = (bf16[128,256]{1,0:T(8,128)(2,1)S(1)}, bf16[128,256]{1,0:T(8,128)(2,1)}, u32[]{:S(2)}) copy-start(bf16[128,256]{1,0:T(8,128)(2,1)} %get-tuple-element.28.refs_1_) | copy-start | bytes 196612
  2.6 13.2 %copy-start.4 = (bf16[128,256]{1,0:T(8,128)(2,1)S(1)}, bf16[128,256]{1,0:T(8,128)(2,1)}, u32[]{:S(2)}) copy-start(bf16[128,256]{1,0:T(8,128)(2,1)} %get-tuple-element.38.refs_1_) | copy-start | bytes 196612
  2.6 19.5 %copy-start.3 = (bf16[16,4,8,512]{3,2,1,0:T(8,128)(2,1)S(1)}, bf16[16,4,8,512]{3,2,1,0:T(8,128)(2,1)}, u32[]{:S(2)}) copy-start(bf16[16,4,8,512]{3,2,1,0:T(8,128)(2,1)} %cot.1) | copy-start | bytes 1572868
  2.7 7.8 %collective-permute-start.1 = (bf16[128,256]{1,0:T(8,128)(2,1)}, bf16[128,256]{1,0:T(8,128)(2,1)S(1)}, u32[]{:S(2)}, u32[]{:S(2)}) collective-permute-start(bf16[128,256]{1,0:T(8,128)(2,1)} %get-tuple-element.28.refs_1_), channel_id=1, source_target_pairs={{0,8},{4,12},{8,0},{12,4},{1,9},{5,13},{9,1},{13,5},{2,10},{6,14},... | collective-permute-start | bytes 196616 | tf_op jit(solution)/shard_map/ppermute | solution.py:460
  5.9 5.4 %collective-permute-start = (bf16[160,256]{1,0:T(8,128)(2,1)}, bf16[160,256]{1,0:T(8,128)(2,1)S(1)}, u32[]{:S(2)}, u32[]{:S(2)}) collective-permute-start(bf16[160,256]{1,0:T(8,128)(2,1)} %get-tuple-element.29), channel_id=1, source_target_pairs={{0,4},{4,8},{8,12},{12,0},{1,5},{5,9},{9,13},{13,1},{2,6},{6,10},{... | collective-permute-start | bytes 245768 | tf_op jit(solution)/shard_map/ppermute | solution.py:460
  7.2 4.8 %collective-permute-start.2 = (bf16[160,256]{1,0:T(8,128)(2,1)}, bf16[160,256]{1,0:T(8,128)(2,1)S(1)}, u32[]{:S(2)}, u32[]{:S(2)}) collective-permute-start(bf16[160,256]{1,0:T(8,128)(2,1)} %get-tuple-element.30), channel_id=1, source_target_pairs={{0,12},{4,0},{8,4},{12,8},{1,13},{5,1},{9,5},{13,9},{2,14},{6,2},{... | collective-permute-start | bytes 245768 | tf_op jit(solution)/shard_map/ppermute | solution.py:460
  12.0 10.1 %collective-permute-start.9 = (bf16[4,128,256]{2,1,0:T(8,128)(2,1)S(1)}, bf16[4,128,256]{2,1,0:T(8,128)(2,1)S(1)}, u32[]{:S(2)}, u32[]{:S(2)}) collective-permute-start(bf16[4,128,256]{2,1,0:T(8,128)(2,1)S(1)} %get-tuple-element.39.refs_5_), channel_id=1, source_target_pairs={{0,2},{1,3},{2,0},{3,1},{4,6},{5,7},{6,4},{7,5},{8,10},{9,11},{10,... | collective-permute-start | bytes 786440 | tf_op jit(solution)/shard_map/ppermute | solution.py:465
  14.0 4.6 %collective-permute-start.3 = (s32[6,512]{1,0:T(8,128)S(1)}, s32[6,512]{1,0:T(8,128)S(1)}, u32[]{:S(2)}, u32[]{:S(2)}) collective-permute-start(s32[6,512]{1,0:T(8,128)S(1)} %get-tuple-element.34), channel_id=1, source_target_pairs={{0,1},{1,2},{2,3},{3,0},{4,5},{5,6},{6,7},{7,4},{8,9},{9,10},{10,1... | collective-permute-start | bytes 36872 | tf_op jit(solution)/shard_map/ppermute | solution.py:460
  15.8 5.4 %collective-permute-start.4 = (s32[6,512]{1,0:T(8,128)S(1)}, s32[6,512]{1,0:T(8,128)S(1)}, u32[]{:S(2)}, u32[]{:S(2)}) collective-permute-start(s32[6,512]{1,0:T(8,128)S(1)} %get-tuple-element.35), channel_id=1, source_target_pairs={{0,3},{1,0},{2,1},{3,2},{4,7},{5,4},{6,5},{7,6},{8,11},{9,8},{10,9... | collective-permute-start | bytes 36872 | tf_op jit(solution)/shard_map/ppermute | solution.py:460
  15.9 12.7 %collective-permute-start.7 = (bf16[128,256]{1,0:T(8,128)(2,1)S(1)}, bf16[128,256]{1,0:T(8,128)(2,1)S(1)}, u32[]{:S(2)}, u32[]{:S(2)}) collective-permute-start(bf16[128,256]{1,0:T(8,128)(2,1)S(1)} %copy-done.4), channel_id=1, source_target_pairs={{0,12},{4,0},{8,4},{12,8},{1,13},{5,1},{9,5},{13,9},{2,14},{6,2},{... | collective-permute-start | bytes 196616 | tf_op jit(solution)/shard_map/ppermute | solution.py:460
  18.6 10.4 %collective-permute-start.6 = (bf16[128,256]{1,0:T(8,128)(2,1)S(1)}, bf16[128,256]{1,0:T(8,128)(2,1)S(1)}, u32[]{:S(2)}, u32[]{:S(2)}) collective-permute-start(bf16[128,256]{1,0:T(8,128)(2,1)S(1)} %copy-done.4), channel_id=1, source_target_pairs={{0,8},{4,12},{8,0},{12,4},{1,9},{5,13},{9,1},{13,5},{2,10},{6,14},... | collective-permute-start | bytes 196616 | tf_op jit(solution)/shard_map/ppermute | solution.py:460
  18.6 12.0 %collective-permute-start.5 = (bf16[128,256]{1,0:T(8,128)(2,1)S(1)}, bf16[128,256]{1,0:T(8,128)(2,1)S(1)}, u32[]{:S(2)}, u32[]{:S(2)}) collective-permute-start(bf16[128,256]{1,0:T(8,128)(2,1)S(1)} %copy-done.4), channel_id=1, source_target_pairs={{0,4},{4,8},{8,12},{12,0},{1,5},{5,9},{9,13},{13,1},{2,6},{6,10},{... | collective-permute-start | bytes 196616 | tf_op jit(solution)/shard_map/ppermute | solution.py:460
  21.2 12.0 %collective-permute-start.8 = (bf16[4,128,256]{2,1,0:T(8,128)(2,1)S(1)}, bf16[4,128,256]{2,1,0:T(8,128)(2,1)S(1)}, u32[]{:S(2)}, u32[]{:S(2)}) collective-permute-start(bf16[4,128,256]{2,1,0:T(8,128)(2,1)S(1)} %get-tuple-element.39.refs_5_), channel_id=1, source_target_pairs={{0,1},{1,0},{2,3},{3,2},{4,5},{5,4},{6,7},{7,6},{8,9},{9,8},{10,11... | collective-permute-start | bytes 786440 | tf_op jit(solution)/shard_map/ppermute | solution.py:465
  22.1 11.1 %collective-permute-start.10 = (bf16[4,128,256]{2,1,0:T(8,128)(2,1)S(1)}, bf16[4,128,256]{2,1,0:T(8,128)(2,1)S(1)}, u32[]{:S(2)}, u32[]{:S(2)}) collective-permute-start(bf16[4,128,256]{2,1,0:T(8,128)(2,1)S(1)} %collective-permute-done.9.refs_7_), channel_id=1, source_target_pairs={{0,1},{1,0},{2,3},{3,2},{4,5},{5,4},{6,7},{7,6},{8,9},{9,8},{10,11... | collective-permute-start | bytes 786440 | tf_op jit(solution)/shard_map/ppermute | solution.py:465
  22.1 11.1 %copy-start.2 = (bf16[128,27,512]{2,0,1:T(8,128)(2,1)S(1)}, bf16[128,27,512]{2,0,1:T(8,128)(2,1)}, u32[]{:S(2)}) copy-start(bf16[128,27,512]{2,0,1:T(8,128)(2,1)} %param.12) | copy-start | bytes 10616836
  28.5 3.7 %collective-permute-start.13 = (f32[16,512]{1,0:T(8,128)S(1)}, f32[16,512]{1,0:T(8,128)S(1)}, u32[]{:S(2)}, u32[]{:S(2)}) collective-permute-start(f32[16,512]{1,0:T(8,128)S(1)} %get-tuple-element.40.refs_9_), channel_id=1, source_target_pairs={{0,3},{1,0},{2,1},{3,2},{4,7},{5,4},{6,5},{7,6},{8,11},{9,8},{10,9... | collective-permute-start | bytes 98312 | tf_op jit(solution)/shard_map/ppermute | solution.py:460
  29.0 3.2 %collective-permute-start.12 = (f32[16,512]{1,0:T(8,128)S(1)}, f32[16,512]{1,0:T(8,128)S(1)}, u32[]{:S(2)}, u32[]{:S(2)}) collective-permute-start(f32[16,512]{1,0:T(8,128)S(1)} %get-tuple-element.40.refs_9_), channel_id=1, source_target_pairs={{0,2},{1,3},{2,0},{3,1},{4,6},{5,7},{6,4},{7,5},{8,10},{9,11},{10,... | collective-permute-start | bytes 98312 | tf_op jit(solution)/shard_map/ppermute | solution.py:460
  30.6 2.6 %collective-permute-start.11 = (f32[16,512]{1,0:T(8,128)S(1)}, f32[16,512]{1,0:T(8,128)S(1)}, u32[]{:S(2)}, u32[]{:S(2)}) collective-permute-start(f32[16,512]{1,0:T(8,128)S(1)} %get-tuple-element.40.refs_9_), channel_id=1, source_target_pairs={{0,1},{1,2},{2,3},{3,0},{4,5},{5,6},{6,7},{7,4},{8,9},{9,10},{10,1... | collective-permute-start | bytes 98312 | tf_op jit(solution)/shard_map/ppermute | solution.py:460
  39.0 6.4 %collective-permute-start.19 = (f32[16,512]{1,0:T(8,128)S(1)}, f32[16,512]{1,0:T(8,128)S(1)}, u32[]{:S(2)}, u32[]{:S(2)}) collective-permute-start(f32[16,512]{1,0:T(8,128)S(1)} %get-tuple-element.43.refs_4_), channel_id=1, source_target_pairs={{0,12},{4,0},{8,4},{12,8},{1,13},{5,1},{9,5},{13,9},{2,14},{6,2},{... | collective-permute-start | bytes 98312 | tf_op jit(solution)/shard_map/ppermute | solution.py:460
  40.5 11.5 %collective-permute-start.18 = (f32[16,512]{1,0:T(8,128)S(1)}, f32[16,512]{1,0:T(8,128)S(1)}, u32[]{:S(2)}, u32[]{:S(2)}) collective-permute-start(f32[16,512]{1,0:T(8,128)S(1)} %get-tuple-element.43.refs_4_), channel_id=1, source_target_pairs={{0,8},{4,12},{8,0},{12,4},{1,9},{5,13},{9,1},{13,5},{2,10},{6,14},... | collective-permute-start | bytes 98312 | tf_op jit(solution)/shard_map/ppermute | solution.py:460
  40.9 11.1 %collective-permute-start.17 = (f32[16,512]{1,0:T(8,128)S(1)}, f32[16,512]{1,0:T(8,128)S(1)}, u32[]{:S(2)}, u32[]{:S(2)}) collective-permute-start(f32[16,512]{1,0:T(8,128)S(1)} %get-tuple-element.43.refs_4_), channel_id=1, source_target_pairs={{0,4},{4,8},{8,12},{12,0},{1,5},{5,9},{9,13},{13,1},{2,6},{6,10},{... | collective-permute-start | bytes 98312 | tf_op jit(solution)/shard_map/ppermute | solution.py:460
  42.1 9.9 %collective-permute-start.16 = (bf16[256,128]{1,0:T(8,128)(2,1)S(1)}, bf16[256,128]{1,0:T(8,128)(2,1)S(1)}, u32[]{:S(2)}, u32[]{:S(2)}) collective-permute-start(bf16[256,128]{1,0:T(8,128)(2,1)S(1)} %get-tuple-element.49), channel_id=1, source_target_pairs={{0,3},{1,0},{2,1},{3,2},{4,7},{5,4},{6,5},{7,6},{8,11},{9,8},{10,9... | collective-permute-start | bytes 196616 | tf_op jit(solution)/shard_map/ppermute | solution.py:460
  44.6 7.5 %collective-permute-start.15 = (bf16[256,128]{1,0:T(8,128)(2,1)S(1)}, bf16[256,128]{1,0:T(8,128)(2,1)S(1)}, u32[]{:S(2)}, u32[]{:S(2)}) collective-permute-start(bf16[256,128]{1,0:T(8,128)(2,1)S(1)} %get-tuple-element.50), channel_id=1, source_target_pairs={{0,2},{1,3},{2,0},{3,1},{4,6},{5,7},{6,4},{7,5},{8,10},{9,11},{10,... | collective-permute-start | bytes 196616 | tf_op jit(solution)/shard_map/ppermute | solution.py:460
  45.5 6.6 %collective-permute-start.14 = (bf16[256,128]{1,0:T(8,128)(2,1)S(1)}, bf16[256,128]{1,0:T(8,128)(2,1)S(1)}, u32[]{:S(2)}, u32[]{:S(2)}) collective-permute-start(bf16[256,128]{1,0:T(8,128)(2,1)S(1)} %get-tuple-element.51), channel_id=1, source_target_pairs={{0,1},{1,2},{2,3},{3,0},{4,5},{5,6},{6,7},{7,4},{8,9},{9,10},{10,1... | collective-permute-start | bytes 196616 | tf_op jit(solution)/shard_map/ppermute | solution.py:460

commit v4 on v3

--- a/solution.py
+++ b/solution.py
@@ -46,42 +46,57 @@
     return condition.astype(F32).astype(BF16)
 
 
-def pack_body(labels, cells, cots, slab, first, last, cot, ids, raw_cells, raw_cots, sems):
+def pick_rows(rows, count, which, turned=False):
+    shape = (rows * count, rows) if turned else (rows, rows * count)
+    far, near = (0, 1) if turned else (1, 0)
+    return hot(iota(shape, far) == count * iota(shape, near) + which)
+
+
+def apart(x, planes):
+    rows = x.shape[0] // planes
+    parts = [jnp.dot(pick_rows(rows, planes, p), x, preferred_element_type=F32) for p in range(planes)]
+    return jnp.concatenate(parts, axis=1).astype(BF16)
+
+
+def together(x, planes):
+    width = x.shape[1] // planes
+    x = x.astype(BF16)
+    parts = [
+        jnp.dot(pick_rows(x.shape[0], planes, p, True), x[:, p * width : (p + 1) * width], preferred_element_type=F32)
+        for p in range(planes)
+    ]
+    return sum(parts[1:], parts[0]).astype(BF16)
+
+
+def pack_body(planes, labels, cells, slab, first, last, ids, raw_cells, sems):
     copies = [
         pltpu.make_async_copy(cells, raw_cells, sems.at[0]),
         pltpu.make_async_copy(labels, ids, sems.at[1]),
-        pltpu.make_async_copy(cots, raw_cots, sems.at[2]),
     ]
     for copy in copies:
         copy.start()
-    cb, planes, width = cells.shape
-    lanes = planes * width
+    cb, lanes = slab.shape
     cols = labels.shape[2]
     copies[0].wait()
-    for p in range(planes):
-        block = raw_cells[:, p, :]
-        for to in (slab, first, last):
-            to[:cb, p * width : (p + 1) * width] = block
+    block = apart(raw_cells[...], planes)
+    for to in (slab, first, last):
+        to[:cb, :] = block
     copies[1].wait()
     for to, plane in ((first, ids[0]), (last, ids[labels.shape[0] - 1])):
         parts = [plane & 255, plane >> 8]
         rows = jnp.concatenate([part[:, i : i + lanes] for part in parts for i in range(0, cols, lanes)], axis=0)
         to[cb:, :] = rows.astype(F32).astype(BF16)
-    copies[2].wait()
-    for p in range(planes):
-        cot[:, p * width : (p + 1) * width] = raw_cots[:, p, :]
-
-
-def pack_call(labels, cells, cots):
+
+
+def pack_call(labels, cells, planes):
     depth, rows, cols = labels.shape
-    cb, planes, width = cells.shape
-    lanes = planes * width
+    cb, lanes = cells.shape[0] // planes, cells.shape[1] * planes
     more = 2 * rows * cols // lanes
     S = jax.ShapeDtypeStruct
     outs = [S((cb, lanes), BF16), S((cb + more, lanes), BF16), S((cb + more, lanes), BF16)]
-    outs += [S((cb, lanes), BF16), S(labels.shape, jnp.int32)]
-    scratch = [pltpu.VMEM(cells.shape, BF16), pltpu.VMEM(cots.shape, BF16), pltpu.SemaphoreType.DMA((3,))]
-    return call(pack_body, outs, [HB] * 3, scratch, 1e9, 1 << 18, 56)(labels, cells, cots)
+    outs += [S(labels.shape, jnp.int32)]
+    scratch = [pltpu.VMEM(cells.shape, BF16), pltpu.SemaphoreType.DMA((2,))]
+    return call(functools.partial(pack_body, planes), outs, [HB] * 2, scratch, 1e9, 1 << 18, 56)(labels, cells)
 
 
 def unpack_body(count, *refs):
@@ -154,14 +169,24 @@
     return high, (x - high.astype(F32)).astype(BF16)
 
 
-def fine_body(scale, own, below, above, left, right, table, kernel, cot, out, part, feats, grads):
+def fold_lanes(blocks, lanes):
+    return jnp.concatenate([b[:, i : i + lanes] for b in blocks for i in range(0, b.shape[1], lanes)], axis=0)
+
+
+def unfold_lanes(x, rows, wide):
+    count = wide // x.shape[1]
+    cut = [x[i * rows : (i + 1) * rows].astype(F32) for i in range(2 * count)]
+    return jnp.concatenate(cut[:count], axis=1) + jnp.concatenate(cut[count:], axis=1)
+
+
+def fine_body(scale, planes, own, below, above, left, right, table, kernel, cot, bott_cot, out, part, message, feats, grads):
     depth, rows, cols = own.shape
     ch = out.shape[0]
     place, count = lax.axis_index("space"), lax.axis_size("space")
     lane, lanes = lax.axis_index("chan"), lax.axis_size("chan")
     key = iota((LOW, cols), 0).astype(F32).astype(BF16)
     one, none = jnp.ones((), BF16), jnp.zeros((), BF16)
-    for x in range(depth + 2):
+    def find(x):
         for y in range(rows + 2):
             if y == 0:
                 ids = jnp.where(lane == 0, -1, left[x : x + 1])
@@ -187,11 +212,16 @@
                 bit -= 1
             at = (x * (rows + 2) + y) * ch
             feats[at : at + ch, :] = picked.astype(BF16)
+
     group = ch * rows
     step = (rows + 2) * ch
     w = lax.broadcasted_iota(jnp.int32, (1, cols), 1)
     first, last = w == 0, w == cols - 1
     for x in range(depth):
+        if x == 0:
+            find(0)
+            find(1)
+        find(x + 2)
         window = feats[x * step : (x + 3) * step, :]
         q = jnp.dot(kernel[...], window, preferred_element_type=F32)
         pre = q[group : 2 * group]
@@ -234,20 +264,26 @@
             both = jnp.concatenate(split(block[e * ch : (e + 1) * ch]), axis=0)
             moved = jnp.dot(both, hot(spot == 3 * b + e), preferred_element_type=F32)
             result = result + (moved[:ch] + moved[ch:])
-    part[...] = result * scale
-
-
-def fine_call(scale, own, below, above, left, right, table, kernel, cot):
+    result = result * scale
+    part[...] = result
+    o_own = bott_cot.shape[0] // planes
+    message[:o_own, :] = apart(bott_cot[...], planes)
+    message[o_own:, :] = fold_lanes(split(result), message.shape[1])
+
+
+def fine_call(scale, own, below, above, left, right, table, kernel, cot, bott_cot, planes):
     depth, rows, cols = own.shape
     ch = cot.shape[0]
-    body = functools.partial(fine_body, scale)
+    o_own, lanes = bott_cot.shape[0] // planes, bott_cot.shape[1] * planes
+    body = functools.partial(fine_body, scale, planes)
     return call(
         body,
         [
             jax.ShapeDtypeStruct((ch, depth, rows, cols), BF16),
             jax.ShapeDtypeStruct((ch, ch * TAPS), F32),
+            jax.ShapeDtypeStruct((o_own + 2 * ch * ch * TAPS // lanes, lanes), BF16),
         ],
-        [VM] * 8,
+        [VM] * 9,
         [
             pltpu.VMEM(((depth + 2) * (rows + 2) * ch, cols), BF16),
             pltpu.VMEM((3 * ch * rows, 3 * ch * (rows + 2)), F32),
@@ -255,7 +291,7 @@
         7.4e9,
         4 << 20,
         20,
-    )(own, below, above, left, right, table, kernel, cot)
+    )(own, below, above, left, right, table, kernel, cot, bott_cot)
 
 
 def shift_masks(width, sign):
@@ -268,22 +304,15 @@
     return masks
 
 
-def bott_body(pieces, slabs, planes, *refs):
-    weight, refs = refs[0], refs[1:]
-    cots, refs = refs[:slabs], refs[slabs:]
-    ins, refs = refs[:pieces], refs[pieces:]
-    parts, refs = refs[:pieces], refs[pieces:]
-    own_out, deltas, padded, share, mine, part_sum, acts, rows_t, cot_at = refs
+def bott_body(pieces, planes, *refs):
+    weight, ins, (pre_out, padded) = refs[0], refs[1 : 1 + pieces], refs[1 + pieces :]
     slabs, cb, lanes = ins[0].shape
     width = lanes // planes
     c_all = cb * pieces
-    o_own = own_out.shape[0]
+    o_own = pre_out.shape[0]
     total = slabs * planes
     place = lax.axis_index("space")
     chan = lax.axis_index("chan")
-    part_sum[...] = sum((part[...] for part in parts[1:]), parts[0][...])
-    for r in range(slabs):
-        cot_at[lax.rem(place - r + slabs, slabs)] = cots[r][...]
     padded[:, :width] = jnp.zeros((c_all, width), BF16)
     padded[:, (total + 1) * width :] = jnp.zeros((c_all, width), BF16)
     for j in range(pieces):
@@ -292,8 +321,6 @@
             slab = lax.rem(place - r + slabs, slabs)
             at = pl.multiple_of(slab * lanes + width, width)
             padded[pl.ds(row, cb), pl.ds(at, lanes)] = ins[j][r]
-    deltas[:, :width] = jnp.zeros((o_own, width), F32)
-    deltas[:, (total + 1) * width :] = jnp.zeros((o_own, width), F32)
     masks = shift_masks(width, 1)
     for n in range(slabs):
         base = n * lanes
@@ -310,15 +337,46 @@
                 if turn:
                     block = jnp.where(masks[k], pltpu.roll(block, turn, 1), 0.0)
                 pre[p] = pre[p] + block
-        cot = cot_at[n].astype(F32)
         for p in range(planes):
-            act, slope = silu_parts(pre[p])
-            acts[n, :, p * width : (p + 1) * width] = act
-            delta = (cot[:, p * width : (p + 1) * width] * slope).astype(BF16).astype(F32)
-            deltas[:, base + (p + 1) * width : base + (p + 2) * width] = delta
+            pre_out[:, base + p * width : base + (p + 1) * width] = pre[p]
+
+
+def bott_call(weight, ins, planes):
+    slabs, cb, lanes = ins[0].shape
+    pieces = len(ins)
+    o_own = weight.shape[0] // 27
+    S = jax.ShapeDtypeStruct
+    return call(
+        functools.partial(bott_body, pieces, planes),
+        [S((o_own, slabs * lanes), F32), S((pieces * cb, (slabs + 1) * lanes), BF16)],
+        [VM] * (1 + pieces),
+        [],
+        5e9,
+        1 << 20,
+        16,
+    )(weight, *ins)
+
+
+def back_body(slabs, planes, weight, pre, part, *refs):
+    messages, (own_out, deltas, share, mine, part_sum, rows_t) = refs[:slabs], refs[slabs:]
+    pieces, lanes, cb = mine.shape
+    o_own = deltas.shape[0]
+    width = lanes // planes
+    total = slabs * planes
+    place = lax.axis_index("space")
+    chan = lax.axis_index("chan")
+    deltas[:, :width] = jnp.zeros((o_own, width), F32)
+    deltas[:, (total + 1) * width :] = jnp.zeros((o_own, width), F32)
+    for r in range(slabs):
+        at = pl.multiple_of(lax.rem(place - r + slabs, slabs) * lanes, lanes)
+        act, slope = silu_parts(pre[:, pl.ds(at, lanes)])
+        delta = (messages[r][:o_own, :].astype(F32) * slope).astype(BF16).astype(F32)
+        deltas[:, pl.ds(pl.multiple_of(at + width, width), lanes)] = delta
+        if r == 0:
+            own_out[...] = together(act, planes)
     near = (planes + 2) * width
     turned = deltas[:, pl.ds(pl.multiple_of(place * lanes, width), near)].T
-    w = lax.broadcasted_iota(jnp.int32, (near, 1), 0) % BW
+    w = iota((near, 1), 0) % BW
     gap = width + 2 * BW
     for e in (-1, 0, 1):
         moved = turned
@@ -335,44 +393,44 @@
             starts = [(1 + p - a) * gap + BW - b * BW for p in range(planes)]
             blocks.append(jnp.concatenate([rows_t[e + 1, s : s + width, :] for s in starts], axis=0))
     back = jnp.dot(jnp.concatenate(blocks, axis=1), weight[...], preferred_element_type=F32)
+    grad = part[...]
+    for r in range(1, slabs):
+        grad = grad + unfold_lanes(messages[r][o_own:, :], *grad.shape)
+    part_sum[...] = grad
+    rest = fold_lanes(split(grad), cb)
     for j in range(pieces):
         block = back[:, j * cb : (j + 1) * cb]
         to = lax.rem(j - chan + pieces, pieces)
         mine[to] = block
-        share[to] = block.astype(BF16)
-    act = acts[place]
-    for p in range(planes):
-        own_out[:, p, :] = act[:, p * width : (p + 1) * width].astype(BF16)
-
-
-def bott_call(weight, cots, ins, parts, planes):
-    slabs, cb, lanes = ins[0].shape
-    pieces = len(ins)
-    o_own = cots[0].shape[0]
-    c_all = pieces * cb
+        share[to, :lanes, :] = block.astype(BF16)
+        share[j, lanes:, :] = rest
+
+
+def back_call(weight, pre, part, messages, pieces, planes):
+    slabs = len(messages)
+    o_own, length = pre.shape
+    lanes = length // slabs
     width = lanes // planes
-    total = slabs * planes
+    cb = weight.shape[1] // pieces
     S = jax.ShapeDtypeStruct
     return call(
-        functools.partial(bott_body, pieces, slabs, planes),
+        functools.partial(back_body, slabs, planes),
         [
-            S((o_own, planes, width), BF16),
-            S((o_own, (total + 2) * width), F32),
-            S((c_all, (total + 2) * width), BF16),
-            S((pieces, lanes, cb), BF16),
+            S((o_own * planes, width), BF16),
+            S((o_own, length + 2 * width), F32),
+            S((pieces, lanes + 2 * part.size // cb, cb), BF16),
             S((pieces, lanes, cb), F32),
-            S(parts[0].shape, F32),
+            S(part.shape, F32),
         ],
-        [VM] * (1 + slabs + 2 * pieces),
-        [
-            pltpu.VMEM((slabs, o_own, lanes), F32),
-            pltpu.VMEM((3, (planes + 2) * (width + 2 * BW), o_own), BF16),
-            pltpu.VMEM((slabs, o_own, lanes), BF16),
-        ],
-        6.6e9,
-        8 << 20,
-        24,
-    )(weight, *cots, *ins, *parts)
+        [VM] * (3 + slabs),
+        [pltpu.VMEM((3, (planes + 2) * (width + 2 * BW), o_own), BF16)],
+        2.3e9,
+        1 << 20,
+        16,
+    )(weight, pre, part, *messages)
+
+
+PLAN = ((0, 0, 4), (0, 4, 9), (1, 0, 9), (2, 0, 5), (2, 5, 9))
 
 
 def wgrad_body(scale, delta, full, out, shifted, stage, sems):
@@ -382,24 +440,37 @@
     masks = shift_masks(width, -1)
     shifted[:, :width] = jnp.zeros((9 * o_own, width), BF16)
     shifted[:, (total + 1) * width :] = jnp.zeros((9 * o_own, width), BF16)
-    for p in range(total):
-        block = delta[:, (p + 1) * width : (p + 2) * width]
-        for k, (b, e) in enumerate(STEPS):
+
+    def build(some):
+        for k in some:
+            b, e = STEPS[k]
             turn = (b * BW + e) % width
-            moved = jnp.where(masks[k], pltpu.roll(block, turn, 1), 0.0) if turn else block
-            shifted[k * o_own : (k + 1) * o_own, (p + 1) * width : (p + 2) * width] = moved.astype(BF16)
-    copies = []
-    for a in range(3):
-        if a >= 2:
-            copies[a - 2].wait()
-        left = shifted[:, (2 - a) * width : (2 - a) * width + length]
-        term = dot_nt(left, full[:, width : width + length]) * scale
-        stage[a % 2] = term.reshape(stage.shape[1:])
-        copy = pltpu.make_async_copy(stage.at[a % 2], out.at[a * 9 : (a + 1) * 9], sems.at[a % 2])
+            for p in range(total):
+                moved = delta[:, (p + 1) * width : (p + 2) * width]
+                if turn:
+                    moved = jnp.where(masks[k], pltpu.roll(moved, turn, 1), 0.0)
+                shifted[k * o_own : (k + 1) * o_own, (p + 1) * width : (p + 2) * width] = moved.astype(BF16)
+
+    busy = [[], []]
+    built = 0
+    right = full[:, width : width + length]
+    for a, low, high in PLAN:
+        build(range(built, max(built, high)))
+        built = max(built, high)
+        if low == 0:
+            for copy in busy[a % 2]:
+                copy.wait()
+            busy[a % 2] = []
+        left = shifted[low * o_own : high * o_own, (2 - a) * width : (2 - a) * width + length]
+        term = dot_nt(left, right) * scale
+        stage[a % 2, low:high] = term.reshape((high - low,) + stage.shape[2:])
+        to = out.at[a * 9 + low : a * 9 + high]
+        copy = pltpu.make_async_copy(stage.at[a % 2, low:high], to, sems.at[a % 2, low])
         copy.start()
-        copies.append(copy)
-    for copy in copies[1:]:
-        copy.wait()
+        busy[a % 2].append(copy)
+    for copies in busy:
+        for copy in copies:
+            copy.wait()
 
 
 def wgrad_call(scale, delta, full):
@@ -412,7 +483,7 @@
         [
             pltpu.VMEM((9 * o_own, length), BF16),
             pltpu.VMEM((2, 9, o_own, c_all), F32),
-            pltpu.SemaphoreType.DMA((2,)),
+            pltpu.SemaphoreType.DMA((2, 9)),
         ],
         6.6e9,
         8 << 20,
@@ -421,38 +492,34 @@
     )(delta, full)[0]
 
 
-def last_body(count, spaces, *refs):
-    mine, refs = refs[0], refs[1:]
-    others, refs = refs[:count], refs[count:]
-    parts, (out, taps) = refs[:spaces], refs[spaces:]
+def last_body(count, mine, part, *refs):
+    others, (out, taps) = refs[:count], refs[count:]
+    lanes = mine.shape[1]
     total = mine[0]
+    grad = part[...]
     for other in others:
-        total = total + other[...].astype(F32)
-    turned = total.T
-    planes = out.shape[1]
-    width = turned.shape[1] // planes
-    for p in range(planes):
-        out[:, p, :] = turned[:, p * width : (p + 1) * width].astype(BF16)
-    grad = sum((part[...] for part in parts[1:]), parts[0][...])
+        total = total + other[:lanes, :].astype(F32)
+        grad = grad + unfold_lanes(other[lanes:, :], *grad.shape)
+    out[...] = together(total.T, out.shape[0] // total.shape[1])
     for c in range(taps.shape[0]):
         taps[c] = grad[:, c * TAPS : c * TAPS + taps.shape[2]]
 
 
-def last_call(mine, others, parts, planes):
+def last_call(mine, part, others, planes):
     lanes, cb = mine.shape[1:]
-    ch = parts[0].shape[0]
+    ch = part.shape[0]
     return call(
-        functools.partial(last_body, len(others), len(parts)),
+        functools.partial(last_body, len(others)),
         [
-            jax.ShapeDtypeStruct((cb, planes, lanes // planes), BF16),
+            jax.ShapeDtypeStruct((cb * planes, lanes // planes), BF16),
             jax.ShapeDtypeStruct((ch, ch, 27), F32),
         ],
-        [VM] * (1 + len(others) + len(parts)),
+        [VM] * (2 + len(others)),
         [],
-        lanes * cb * 4,
-        lanes * cb * 12,
+        1e9,
+        1 << 18,
         12,
-    )(mine, *others, *parts)
+    )(mine, part, *others)
 
 
 def hop(x, axis, offset):
@@ -473,7 +540,7 @@
     lanes = planes * width
     o_own = bott_cot.shape[0]
 
-    slab, first, last, cot, ids = pack_call(labels, bott_in, bott_cot)
+    slab, first, last, ids = pack_call(labels, bott_in.reshape(cb * planes, width), planes)
     taps = fine_weight.reshape(3, 3, 3, ch, ch).transpose(1, 2, 4, 0, 3).reshape(3, 3 * ch, 3 * ch)
     kernel, lookup = prep_call(taps, table.T, rows)
     sends = [last] + [slab] * (spaces - 3) + [first]
@@ -481,24 +548,29 @@
     slabs, below, above, top, bottom = unpack_call(ids, slab, got, kernel)
     left = hop(bottom, "chan", 1)
     right = hop(top, "chan", chans - 1)
+    scale = (depth * spaces * rows * chans * cols) ** -0.5
+    cot = bott_cot.reshape(o_own * planes, width)
+    fine_out, part, message = fine_call(
+        scale, ids, below, above, left, right, lookup, kernel, fine_cot, cot, planes
+    )
+    messages = [message] + [hop(message, "space", r) for r in range(1, spaces)]
     pieces = {0: slabs}
     bits = [1 << i for i in range(chans.bit_length() - 1)]
     for bit in bits[1:] + bits[:1]:
-        pieces.update({j ^ bit: swap(x, "chan", bit) for j, x in list(pieces.items())})
+        for j, x in list(pieces.items()):
+            if bit == 1 and j:
+                x, part = lax.optimization_barrier((x, part))
+            pieces[j ^ bit] = swap(x, "chan", bit)
     ins = [pieces[j] for j in range(chans)]
-    cots = [cot] + [hop(cot, "space", r) for r in range(1, spaces)]
 
     weight = bott_weight.transpose(1, 0, 2).reshape(27 * o_own, cb * chans)
-    scale = (depth * spaces * rows * chans * cols) ** -0.5
-    fine_out, part = fine_call(scale, ids, below, above, left, right, lookup, kernel, fine_cot)
-    parts = [part] + [hop(part, "chan", r) for r in range(1, chans)]
-
-    bott_out, delta, full, share, mine, part = bott_call(weight, cots, ins, parts, planes)
+    pre, full = bott_call(weight, ins, planes)
+    bott_out, delta, share, mine, part = back_call(weight, pre, part, messages, chans, planes)
     others = [hop(share[r], "chan", r) for r in range(1, chans)]
-    parts = [part] + [hop(part, "space", r) for r in range(1, spaces)]
     bott_wgrad = wgrad_call((planes * spaces * width) ** -0.5, delta, full).transpose(1, 0, 2)
-    bott_dgrad, fine_wgrad = last_call(mine, others, parts, planes)
-    return fine_out, fine_wgrad.transpose(2, 0, 1), bott_out, bott_dgrad, bott_wgrad
+    bott_dgrad, fine_wgrad = last_call(mine, part, others, planes)
+    fine_wgrad = fine_wgrad.transpose(2, 0, 1)
+    return fine_out, fine_wgrad, bott_out.reshape(bott_cot.shape), bott_dgrad.reshape(bott_in.shape), bott_wgrad
 
 
 def solution(mesh):

time: 53.1 us -> 48.5 us (0.913)
  starting transfers between devices: 27.1 us -> 18.5 us
  waiting for transfers between devices: 2.99 us -> 6.53 us
    ppermute x17 -> x11, starting transfers between devices: 24.1 us -> 16.4 us  [hop(): lax.ppermute(x, axis, [(i, (i + offset) % count) for i in range(count)])]
    ppermute x17 -> x11, waiting for transfers between devices: 2.98 us -> 6.53 us  [hop(): lax.ppermute(x, axis, [(i, (i + offset) % count) for i in range(count)])]
    ppermute x3, starting transfers between devices: 2.94 us -> 2.14 us  [swap(): return lax.ppermute(x, axis, [(i, i ^ bit) for i in range(count)])]
    pallas_call x1, Pallas kernels: 6.38 us -> 7.11 us  [fine_call(): call(body, [jax.ShapeDtypeStruct((ch, depth, rows, cols), BF16), jax.Shap...]
    pallas_call x3 -> x4, Pallas kernels: 8.63 us -> 8.68 us  [the longest x1 4.07 us: bott_call(): call(functools.partial(bott_body, pieces, planes), [S((o_own, slabs * lan...]
  transfers between devices with their start and end apart: 20 -> 14, of which waited for: 5 -> 4; matrix products, arithmetic and copies ran while one was open for 1% -> 1% of each run, Pallas kernels for 24% -> 36%
where the time goes in v4:
time: 48.5 us; the launch traced here: 48.3 us
  Pallas kernels  21.9 us (45%)
  starting transfers between devices  18.5 us (38%)
  waiting for transfers between devices  6.53 us (13%)
  between operations  0.8 us (2%)
  local copies, waits for them, and re-layouts  0.52 us (1%)
    ppermute x11, starting transfers between devices, hop(): lax.ppermute(x, axis, [(i, (i + offset) % count) for i in range(count)])  16.4 us
    pallas_call x1, Pallas kernels, fine_call(): call(body, [jax.ShapeDtypeStruct((ch, depth, rows, cols), BF16), jax.Shap...  7.11 us
    ppermute x11, waiting for transfers between devices, hop(): lax.ppermute(x, axis, [(i, (i + offset) % count) for i in range(count)])  6.53 us
    pallas_call x1, Pallas kernels, wgrad_call(): call(functools.partial(wgrad_body, scale), [jax.ShapeDtypeStruct((27, o_o...  5.27 us
    pallas_call x1, Pallas kernels, bott_call(): call(functools.partial(bott_body, pieces, planes), [S((o_own, slabs * lan...  4.07 us
    ppermute x3, starting transfers between devices, swap(): return lax.ppermute(x, axis, [(i, i ^ bit) for i in range(count)])  2.14 us
    pallas_call x1, Pallas kernels, back_call(): call(functools.partial(back_body, slabs, planes), [S((o_own * planes, wid...  1.93 us
    pallas_call x1, Pallas kernels, pack_call(): call(functools.partial(pack_body, planes), outs, [HB] * 2, scratch, 10000...  1.77 us
  transfers between devices with their start and end apart: 14, of which 4 were waited for; matrix products, arithmetic and copies ran while one was open for 1% of the time, Pallas kernels for 36%

profile of v4, /device:TPU:1, one launch (start us, length us, event | category | flops | bytes accessed | tf_op | source)
XLA Modules:
  0.0 48.3 jit_solution(17249256409358234457)
XLA Ops:
  0.6 0.0 copy-start.6
  0.6 0.0 copy-start.5
  0.7 1.8 %shard_map.110 = (bf16[128,256]{1,0:T(8,128)(2,1)}, bf16[160,256]{1,0:T(8,128)(2,1)}, bf16[160,256]{1,0:T(8,128)(2,1)}, s32[4,8,512]{2,1,0:T(8,128)}) custom-call(s32[4,8,512]{2,1,0:T(8,128)} %labels.1, bf16[256,128]{1,0:T(8,128)(2,1)} %bitcast.24), custom_call_target="tpu_custom_call" | custom-call | flops 1000000000 | bytes 262144 | tf_op jit(solution)/shard_map/pallas_call | solution.py:99
  2.4 0.0 copy-start
  2.4 0.0 copy-start.1
  2.5 0.0 copy-start.3
  2.5 0.0 copy-start.4
  2.5 3.2 %collective-permute-start.1 = (bf16[128,256]{1,0:T(8,128)(2,1)}, bf16[128,256]{1,0:T(8,128)(2,1)S(1)}, u32[]{:S(2)}, u32[]{:S(2)}) collective-permute-start(bf16[128,256]{1,0:T(8,128)(2,1)} %get-tuple-element.31.refs_1_), channel_id=1, source_target_pairs={{0,8},{4,12},{8,0},{12,4},{1,9},{5,13},{9,1},{13,5},{2,10},{6,14},... | collective-permute-start | bytes 196616 | tf_op jit(solution)/shard_map/ppermute | solution.py:527
  5.7 1.3 %collective-permute-start = (bf16[160,256]{1,0:T(8,128)(2,1)}, bf16[160,256]{1,0:T(8,128)(2,1)S(1)}, u32[]{:S(2)}, u32[]{:S(2)}) collective-permute-start(bf16[160,256]{1,0:T(8,128)(2,1)} %get-tuple-element.32), channel_id=1, source_target_pairs={{0,4},{4,8},{8,12},{12,0},{1,5},{5,9},{9,13},{13,1},{2,6},{6,10},{... | collective-permute-start | bytes 245768 | tf_op jit(solution)/shard_map/ppermute | solution.py:527
  7.0 2.0 %collective-permute-start.2 = (bf16[160,256]{1,0:T(8,128)(2,1)}, bf16[160,256]{1,0:T(8,128)(2,1)S(1)}, u32[]{:S(2)}, u32[]{:S(2)}) collective-permute-start(bf16[160,256]{1,0:T(8,128)(2,1)} %get-tuple-element.33), channel_id=1, source_target_pairs={{0,12},{4,0},{8,4},{12,8},{1,13},{5,1},{9,5},{13,9},{2,14},{6,2},{... | collective-permute-start | bytes 245768 | tf_op jit(solution)/shard_map/ppermute | solution.py:527
  8.9 0.0 copy-done.6
  8.9 0.2 copy.13
  9.1 0.2 copy.14
  9.3 0.1 reshape.33.taps
  9.4 0.0 copy-done.5
  9.4 0.8 %shard_map.111 = (bf16[384,480]{1,0:T(8,128)(2,1)S(1)}, bf16[128,128]{1,0:T(8,128)(2,1)S(1)}) custom-call(bf16[3,48,48]{2,1,0:T(8,128)(2,1)S(1)} %reshape.33.taps, bf16[16,1024]{1,0:T(8,128)(2,1)S(1)} %bitcast.22), custom_call_target="tpu_custom_call" | custom-call | flops 1200000000 | bytes 262144 | tf_op jit(solution)/shard_map/pallas_call | solution.py:153
  10.3 0.0 collective-permute-done.1.refs_3_
  10.3 0.8 %collective-permute-done.refs_2_ = bf16[160,256]{1,0:T(8,128)(2,1)S(1)} collective-permute-done((bf16[160,256]{1,0:T(8,128)(2,1)}, bf16[160,256]{1,0:T(8,128)(2,1)S(1)}, u32[]{:S(2)}, u32[]{:S(2)}) %collective-permute-start) | collective-permute-done | bytes 81952 | tf_op jit(solution)/shard_map/ppermute | solution.py:527
  11.1 0.7 %collective-permute-done.2.refs_4_ = bf16[160,256]{1,0:T(8,128)(2,1)S(1)} collective-permute-done((bf16[160,256]{1,0:T(8,128)(2,1)}, bf16[160,256]{1,0:T(8,128)(2,1)S(1)}, u32[]{:S(2)}, u32[]{:S(2)}) %collective-permute-start.2) | collective-permute-done | bytes 81952 | tf_op jit(solution)/shard_map/ppermute | solution.py:527
  11.8 0.0 copy-done
  11.8 0.0 copy-done.1
  11.8 3.5 %collective-permute-start.3 = (s32[6,512]{1,0:T(8,128)S(1)}, s32[6,512]{1,0:T(8,128)S(1)}, u32[]{:S(2)}, u32[]{:S(2)}) collective-permute-start(s32[6,512]{1,0:T(8,128)S(1)} %get-tuple-element.37), channel_id=1, source_target_pairs={{0,1},{1,2},{2,3},{3,0},{4,5},{5,6},{6,7},{7,4},{8,9},{9,10},{10,1... | collective-permute-start | bytes 36872 | tf_op jit(solution)/shard_map/ppermute | solution.py:527
  15.3 0.0 collective-permute-start.4
  15.3 0.2 collective-permute-start.6
  15.4 2.0 %collective-permute-start.5 = (bf16[4,128,256]{2,1,0:T(8,128)(2,1)S(1)}, bf16[4,128,256]{2,1,0:T(8,128)(2,1)S(1)}, u32[]{:S(2)}, u32[]{:S(2)}) collective-permute-start(bf16[4,128,256]{2,1,0:T(8,128)(2,1)S(1)} %get-tuple-element.41.refs_1_), channel_id=1, source_target_pairs={{0,1},{1,0},{2,3},{3,2},{4,5},{5,4},{6,7},{7,6},{8,9},{9,8},{10,11... | collective-permute-start | bytes 786440 | tf_op jit(solution)/shard_map/ppermute | solution.py:532
  17.4 0.0 collective-permute-done.3.left
  17.4 1.1 %collective-permute-done.4.right = s32[6,512]{1,0:T(8,128)S(1)} collective-permute-done((s32[6,512]{1,0:T(8,128)S(1)}, s32[6,512]{1,0:T(8,128)S(1)}, u32[]{:S(2)}, u32[]{:S(2)}) %collective-permute-start.4) | collective-permute-done | bytes 12320 | tf_op jit(solution)/shard_map/ppermute | solution.py:527
  18.5 0.0 copy-done.3
  18.5 0.0 copy-done.4
  18.5 0.0 copy-start.2
  18.5 7.1 %shard_map.113 = (bf16[16,4,8,512]{3,2,1,0:T(8,128)(2,1)}, f32[16,512]{1,0:T(8,128)S(1)}, bf16[192,256]{1,0:T(8,128)(2,1)S(1)}) custom-call(s32[4,8,512]{2,1,0:T(8,128)S(1)} %copy-done, s32[8,512]{1,0:T(8,128)S(1)} %get-tuple-element.35.below, s32[8,512]{1,0:T(8,128)S(1)} %get-tuple-element.36.above, s32[6,512]{1,0:T(8,128)S(1)} %collective-permute-done.3.left, ...), custom_call_target="tpu_custom_call" | custom-call | flops 7400000000 | bytes 4194304 | tf_op jit(solution)/shard_map/pallas_call | solution.py:279
  25.7 0.0 collective-permute-done.6.refs_3_
  25.7 0.0 collective-permute-start.7
  25.7 2.6 %collective-permute-start.10 = (bf16[192,256]{1,0:T(8,128)(2,1)S(1)}, bf16[192,256]{1,0:T(8,128)(2,1)S(1)}, u32[]{:S(2)}, u32[]{:S(2)}) collective-permute-start(bf16[192,256]{1,0:T(8,128)(2,1)S(1)} %get-tuple-element.46.refs_0_), channel_id=1, source_target_pairs={{0,12},{4,0},{8,4},{12,8},{1,13},{5,1},{9,5},{13,9},{2,14},{6,2},{... | collective-permute-start | bytes 294920 | tf_op jit(solution)/shard_map/ppermute | solution.py:527
  28.3 0.0 collective-permute-start.9
  28.3 1.0 %collective-permute-start.8 = (bf16[192,256]{1,0:T(8,128)(2,1)S(1)}, bf16[192,256]{1,0:T(8,128)(2,1)S(1)}, u32[]{:S(2)}, u32[]{:S(2)}) collective-permute-start(bf16[192,256]{1,0:T(8,128)(2,1)S(1)} %get-tuple-element.46.refs_0_), channel_id=1, source_target_pairs={{0,4},{4,8},{8,12},{12,0},{1,5},{5,9},{9,13},{13,1},{2,6},{6,10},{... | collective-permute-start | bytes 294920 | tf_op jit(solution)/shard_map/ppermute | solution.py:527
  29.3 0.0 collective-permute-done.5.refs_2_
  29.3 0.0 collective-permute-done.7.refs_4_
  29.3 0.0 copy-done.2
  29.3 4.1 %shard_map.114 = (f32[128,1024]{1,0:T(8,128)S(1)}, bf16[512,1280]{1,0:T(8,128)(2,1)S(1)}) custom-call(bf16[3456,512]{1,0:T(8,128)(2,1)S(1)} %bitcast.19, bf16[4,128,256]{2,1,0:T(8,128)(2,1)S(1)} %get-tuple-element.41.refs_1_, bf16[4,128,256]{2,1,0:T(8,128)(2,1)S(1)} %collective-permute-done.5.refs_2_, ...), custom_call_target="tpu_custom_call" | custom-call | flops 5000000000 | bytes 1048576 | tf_op jit(solution)/shard_map/pallas_call | solution.py:349
  33.4 0.0 collective-permute-done.10.refs_3_
  33.4 3.9 %collective-permute-done.9.refs_2_ = bf16[192,256]{1,0:T(8,128)(2,1)S(1)} collective-permute-done((bf16[192,256]{1,0:T(8,128)(2,1)S(1)}, bf16[192,256]{1,0:T(8,128)(2,1)S(1)}, u32[]{:S(2)}, u32[]{:S(2)}) %collective-permute-start.9) | collective-permute-done | bytes 98336 | tf_op jit(solution)/shard_map/ppermute | solution.py:527
  37.3 0.0 collective-permute-done.8.refs_1_
  37.3 1.9 %shard_map.115 = (bf16[256,128]{1,0:T(8,128)(2,1)}, f32[128,1280]{1,0:T(8,128)S(1)}, bf16[4,384,128]{2,1,0:T(8,128)(2,1)S(1)}, f32[4,256,128]{2,1,0:T(8,128)S(1)}, f32[16,512]{1,0:T(8,128)S(1)}) custom-call(bf16[3456,512]{1,0:T(8,128)(2,1)S(1)} %bitcast.20, f32[128,1024]{1,0:T(8,128)S(1)} %get-tuple-element.44.pre, f32[16,512]{1,0:T(8,128)S(1)} %get-tuple-element.45.part, ...), custom_call_target="tpu_custom_call" | custom-call | flops 2300000000 | bytes 1048576 | tf_op jit(solution)/shard_map/pallas_call | solution.py:416
  39.3 1.1 %collective-permute-start.13 = (bf16[384,128]{1,0:T(8,128)(2,1)S(1)}, bf16[384,128]{1,0:T(8,128)(2,1)S(1)}, u32[]{:S(2)}, u32[]{:S(2)}) collective-permute-start(bf16[384,128]{1,0:T(8,128)(2,1)S(1)} %get-tuple-element.55), channel_id=1, source_target_pairs={{0,3},{1,0},{2,1},{3,2},{4,7},{5,4},{6,5},{7,6},{8,11},{9,8},{10,9... | collective-permute-start | bytes 294920 | tf_op jit(solution)/shard_map/ppermute | solution.py:527
  40.4 0.2 collective-permute-start.12
  40.6 1.5 %collective-permute-start.11 = (bf16[384,128]{1,0:T(8,128)(2,1)S(1)}, bf16[384,128]{1,0:T(8,128)(2,1)S(1)}, u32[]{:S(2)}, u32[]{:S(2)}) collective-permute-start(bf16[384,128]{1,0:T(8,128)(2,1)S(1)} %get-tuple-element.57), channel_id=1, source_target_pairs={{0,1},{1,2},{2,3},{3,0},{4,5},{5,6},{6,7},{7,4},{8,9},{9,10},{10,1... | collective-permute-start | bytes 294920 | tf_op jit(solution)/shard_map/ppermute | solution.py:527
  42.1 5.3 %shard_map.117 = f32[27,128,512]{2,1,0:T(8,128)} custom-call(f32[128,1280]{1,0:T(8,128)S(1)} %get-tuple-element.53.delta, bf16[512,1280]{1,0:T(8,128)(2,1)S(1)} %get-tuple-element.54.full), custom_call_target="tpu_custom_call" | custom-call | flops 6600000000 | bytes 8388608 | tf_op jit(solution)/shard_map/pallas_call | solution.py:479
  47.4 0.0 collective-permute-done.13.refs_2_
  47.4 0.0 collective-permute-done.12.refs_1_
  47.4 0.0 collective-permute-done.11.refs_0_
  47.4 0.9 %shard_map.116 = (bf16[256,128]{1,0:T(8,128)(2,1)}, f32[16,16,27]{2,1,0:T(8,128)}) custom-call(f32[4,256,128]{2,1,0:T(8,128)S(1)} %get-tuple-element.47.mine, f32[16,512]{1,0:T(8,128)S(1)} %get-tuple-element.48.part, bf16[384,128]{1,0:T(8,128)(2,1)S(1)} %collective-permute-done.11.refs_0_, bf16[384,128]{1,0:T(8,128)(2,1)S(1)} %collective-permute-done.12.refs_1_, ...), custom_call_target="tpu_custom_call" | custom-call | flops 1000000000 | bytes 262144 | tf_op jit(solution)/shard_map/pallas_call | solution.py:511
  (2 shorter events, 0.1 us)
Async XLA Ops:
  0.6 8.3 %copy-start.6 = (bf16[27,16,16]{0,2,1:T(8,128)(2,1)S(1)}, bf16[27,16,16]{0,2,1:T(8,128)(2,1)}, u32[]{:S(2)}) copy-start(bf16[27,16,16]{0,2,1:T(8,128)(2,1)} %param.9) | copy-start | bytes 41476
  0.6 8.8 %copy-start.5 = (bf16[1024,16]{0,1:T(8,128)(2,1)S(1)}, bf16[1024,16]{0,1:T(8,128)(2,1)}, u32[]{:S(2)}) copy-start(bf16[1024,16]{0,1:T(8,128)(2,1)} %param.8) | copy-start | bytes 98308
  2.4 9.3 %copy-start = (s32[4,8,512]{2,1,0:T(8,128)S(1)}, s32[4,8,512]{2,1,0:T(8,128)}, u32[]{:S(2)}) copy-start(s32[4,8,512]{2,1,0:T(8,128)} %get-tuple-element.30.refs_0_.own) | copy-start | bytes 196612
  2.4 9.3 %copy-start.1 = (bf16[128,256]{1,0:T(8,128)(2,1)S(1)}, bf16[128,256]{1,0:T(8,128)(2,1)}, u32[]{:S(2)}) copy-start(bf16[128,256]{1,0:T(8,128)(2,1)} %get-tuple-element.31.refs_1_) | copy-start | bytes 196612
  2.5 16.1 %copy-start.3 = (bf16[16,4,8,512]{3,2,1,0:T(8,128)(2,1)S(1)}, bf16[16,4,8,512]{3,2,1,0:T(8,128)(2,1)}, u32[]{:S(2)}) copy-start(bf16[16,4,8,512]{3,2,1,0:T(8,128)(2,1)} %cot.1) | copy-start | bytes 1572868
  2.5 16.1 %copy-start.4 = (bf16[128,2,128]{2,1,0:T(2,128)(2,1)S(1)}, bf16[128,2,128]{2,1,0:T(2,128)(2,1)}, u32[]{:S(2)}) copy-start(bf16[128,2,128]{2,1,0:T(2,128)(2,1)} %param.13) | copy-start | bytes 196612
  2.5 7.8 %collective-permute-start.1 = (bf16[128,256]{1,0:T(8,128)(2,1)}, bf16[128,256]{1,0:T(8,128)(2,1)S(1)}, u32[]{:S(2)}, u32[]{:S(2)}) collective-permute-start(bf16[128,256]{1,0:T(8,128)(2,1)} %get-tuple-element.31.refs_1_), channel_id=1, source_target_pairs={{0,8},{4,12},{8,0},{12,4},{1,9},{5,13},{9,1},{13,5},{2,10},{6,14},... | collective-permute-start | bytes 196616 | tf_op jit(solution)/shard_map/ppermute | solution.py:527
  5.7 5.4 %collective-permute-start = (bf16[160,256]{1,0:T(8,128)(2,1)}, bf16[160,256]{1,0:T(8,128)(2,1)S(1)}, u32[]{:S(2)}, u32[]{:S(2)}) collective-permute-start(bf16[160,256]{1,0:T(8,128)(2,1)} %get-tuple-element.32), channel_id=1, source_target_pairs={{0,4},{4,8},{8,12},{12,0},{1,5},{5,9},{9,13},{13,1},{2,6},{6,10},{... | collective-permute-start | bytes 245768 | tf_op jit(solution)/shard_map/ppermute | solution.py:527
  7.0 4.8 %collective-permute-start.2 = (bf16[160,256]{1,0:T(8,128)(2,1)}, bf16[160,256]{1,0:T(8,128)(2,1)S(1)}, u32[]{:S(2)}, u32[]{:S(2)}) collective-permute-start(bf16[160,256]{1,0:T(8,128)(2,1)} %get-tuple-element.33), channel_id=1, source_target_pairs={{0,12},{4,0},{8,4},{12,8},{1,13},{5,1},{9,5},{13,9},{2,14},{6,2},{... | collective-permute-start | bytes 245768 | tf_op jit(solution)/shard_map/ppermute | solution.py:527
  11.8 5.6 %collective-permute-start.3 = (s32[6,512]{1,0:T(8,128)S(1)}, s32[6,512]{1,0:T(8,128)S(1)}, u32[]{:S(2)}, u32[]{:S(2)}) collective-permute-start(s32[6,512]{1,0:T(8,128)S(1)} %get-tuple-element.37), channel_id=1, source_target_pairs={{0,1},{1,2},{2,3},{3,0},{4,5},{5,6},{6,7},{7,4},{8,9},{9,10},{10,1... | collective-permute-start | bytes 36872 | tf_op jit(solution)/shard_map/ppermute | solution.py:527
  15.3 3.3 %collective-permute-start.4 = (s32[6,512]{1,0:T(8,128)S(1)}, s32[6,512]{1,0:T(8,128)S(1)}, u32[]{:S(2)}, u32[]{:S(2)}) collective-permute-start(s32[6,512]{1,0:T(8,128)S(1)} %get-tuple-element.38), channel_id=1, source_target_pairs={{0,3},{1,0},{2,1},{3,2},{4,7},{5,4},{6,5},{7,6},{8,11},{9,8},{10,9... | collective-permute-start | bytes 36872 | tf_op jit(solution)/shard_map/ppermute | solution.py:527
  15.3 10.4 %collective-permute-start.6 = (bf16[4,128,256]{2,1,0:T(8,128)(2,1)S(1)}, bf16[4,128,256]{2,1,0:T(8,128)(2,1)S(1)}, u32[]{:S(2)}, u32[]{:S(2)}) collective-permute-start(bf16[4,128,256]{2,1,0:T(8,128)(2,1)S(1)} %get-tuple-element.41.refs_1_), channel_id=1, source_target_pairs={{0,2},{1,3},{2,0},{3,1},{4,6},{5,7},{6,4},{7,5},{8,10},{9,11},{10,... | collective-permute-start | bytes 786440 | tf_op jit(solution)/shard_map/ppermute | solution.py:532
  15.4 13.9 %collective-permute-start.5 = (bf16[4,128,256]{2,1,0:T(8,128)(2,1)S(1)}, bf16[4,128,256]{2,1,0:T(8,128)(2,1)S(1)}, u32[]{:S(2)}, u32[]{:S(2)}) collective-permute-start(bf16[4,128,256]{2,1,0:T(8,128)(2,1)S(1)} %get-tuple-element.41.refs_1_), channel_id=1, source_target_pairs={{0,1},{1,0},{2,3},{3,2},{4,5},{5,4},{6,7},{7,6},{8,9},{9,8},{10,11... | collective-permute-start | bytes 786440 | tf_op jit(solution)/shard_map/ppermute | solution.py:532
  18.5 10.8 %copy-start.2 = (bf16[128,27,512]{2,0,1:T(8,128)(2,1)S(1)}, bf16[128,27,512]{2,0,1:T(8,128)(2,1)}, u32[]{:S(2)}) copy-start(bf16[128,27,512]{2,0,1:T(8,128)(2,1)} %param.12) | copy-start | bytes 10616836
  25.7 3.6 %collective-permute-start.7 = (bf16[4,128,256]{2,1,0:T(8,128)(2,1)S(1)}, bf16[4,128,256]{2,1,0:T(8,128)(2,1)S(1)}, u32[]{:S(2)}, u32[]{:S(2)}) collective-permute-start(bf16[4,128,256]{2,1,0:T(8,128)(2,1)S(1)} %collective-permute-done.6.refs_3_), channel_id=1, source_target_pairs={{0,1},{1,0},{2,3},{3,2},{4,5},{5,4},{6,7},{7,6},{8,9},{9,8},{10,11... | collective-permute-start | bytes 786440 | tf_op jit(solution)/shard_map/ppermute | solution.py:532
  25.7 7.7 %collective-permute-start.10 = (bf16[192,256]{1,0:T(8,128)(2,1)S(1)}, bf16[192,256]{1,0:T(8,128)(2,1)S(1)}, u32[]{:S(2)}, u32[]{:S(2)}) collective-permute-start(bf16[192,256]{1,0:T(8,128)(2,1)S(1)} %get-tuple-element.46.refs_0_), channel_id=1, source_target_pairs={{0,12},{4,0},{8,4},{12,8},{1,13},{5,1},{9,5},{13,9},{2,14},{6,2},{... | collective-permute-start | bytes 294920 | tf_op jit(solution)/shard_map/ppermute | solution.py:527
  28.3 9.0 %collective-permute-start.9 = (bf16[192,256]{1,0:T(8,128)(2,1)S(1)}, bf16[192,256]{1,0:T(8,128)(2,1)S(1)}, u32[]{:S(2)}, u32[]{:S(2)}) collective-permute-start(bf16[192,256]{1,0:T(8,128)(2,1)S(1)} %get-tuple-element.46.refs_0_), channel_id=1, source_target_pairs={{0,8},{4,12},{8,0},{12,4},{1,9},{5,13},{9,1},{13,5},{2,10},{6,14},... | collective-permute-start | bytes 294920 | tf_op jit(solution)/shard_map/ppermute | solution.py:527
  28.3 9.0 %collective-permute-start.8 = (bf16[192,256]{1,0:T(8,128)(2,1)S(1)}, bf16[192,256]{1,0:T(8,128)(2,1)S(1)}, u32[]{:S(2)}, u32[]{:S(2)}) collective-permute-start(bf16[192,256]{1,0:T(8,128)(2,1)S(1)} %get-tuple-element.46.refs_0_), channel_id=1, source_target_pairs={{0,4},{4,8},{8,12},{12,0},{1,5},{5,9},{9,13},{13,1},{2,6},{6,10},{... | collective-permute-start | bytes 294920 | tf_op jit(solution)/shard_map/ppermute | solution.py:527
  39.3 8.1 %collective-permute-start.13 = (bf16[384,128]{1,0:T(8,128)(2,1)S(1)}, bf16[384,128]{1,0:T(8,128)(2,1)S(1)}, u32[]{:S(2)}, u32[]{:S(2)}) collective-permute-start(bf16[384,128]{1,0:T(8,128)(2,1)S(1)} %get-tuple-element.55), channel_id=1, source_target_pairs={{0,3},{1,0},{2,1},{3,2},{4,7},{5,4},{6,5},{7,6},{8,11},{9,8},{10,9... | collective-permute-start | bytes 294920 | tf_op jit(solution)/shard_map/ppermute | solution.py:527
  40.4 7.0 %collective-permute-start.12 = (bf16[384,128]{1,0:T(8,128)(2,1)S(1)}, bf16[384,128]{1,0:T(8,128)(2,1)S(1)}, u32[]{:S(2)}, u32[]{:S(2)}) collective-permute-start(bf16[384,128]{1,0:T(8,128)(2,1)S(1)} %get-tuple-element.56), channel_id=1, source_target_pairs={{0,2},{1,3},{2,0},{3,1},{4,6},{5,7},{6,4},{7,5},{8,10},{9,11},{10,... | collective-permute-start | bytes 294920 | tf_op jit(solution)/shard_map/ppermute | solution.py:527
  40.6 6.8 %collective-permute-start.11 = (bf16[384,128]{1,0:T(8,128)(2,1)S(1)}, bf16[384,128]{1,0:T(8,128)(2,1)S(1)}, u32[]{:S(2)}, u32[]{:S(2)}) collective-permute-start(bf16[384,128]{1,0:T(8,128)(2,1)S(1)} %get-tuple-element.57), channel_id=1, source_target_pairs={{0,1},{1,2},{2,3},{3,0},{4,5},{5,6},{6,7},{7,4},{8,9},{9,10},{10,1... | collective-permute-start | bytes 294920 | tf_op jit(solution)/shard_map/ppermute | solution.py:527

commit v5 on v4

--- a/solution.py
+++ b/solution.py
@@ -68,10 +68,12 @@
     return sum(parts[1:], parts[0]).astype(BF16)
 
 
-def pack_body(planes, labels, cells, slab, first, last, ids, raw_cells, sems):
+def pack_body(planes, labels, cells, cots, table, slab, first, last, cot, ids, near_table, raw_cells, raw_cots, sems):
     copies = [
         pltpu.make_async_copy(cells, raw_cells, sems.at[0]),
         pltpu.make_async_copy(labels, ids, sems.at[1]),
+        pltpu.make_async_copy(cots, raw_cots, sems.at[2]),
+        pltpu.make_async_copy(table, near_table, sems.at[3]),
     ]
     for copy in copies:
         copy.start()
@@ -86,17 +88,22 @@
         parts = [plane & 255, plane >> 8]
         rows = jnp.concatenate([part[:, i : i + lanes] for part in parts for i in range(0, cols, lanes)], axis=0)
         to[cb:, :] = rows.astype(F32).astype(BF16)
-
-
-def pack_call(labels, cells, planes):
+    copies[2].wait()
+    cot[...] = apart(raw_cots[...], planes)
+    copies[3].wait()
+
+
+def pack_call(labels, cells, cots, table, planes):
     depth, rows, cols = labels.shape
     cb, lanes = cells.shape[0] // planes, cells.shape[1] * planes
     more = 2 * rows * cols // lanes
     S = jax.ShapeDtypeStruct
     outs = [S((cb, lanes), BF16), S((cb + more, lanes), BF16), S((cb + more, lanes), BF16)]
-    outs += [S(labels.shape, jnp.int32)]
-    scratch = [pltpu.VMEM(cells.shape, BF16), pltpu.SemaphoreType.DMA((2,))]
-    return call(functools.partial(pack_body, planes), outs, [HB] * 2, scratch, 1e9, 1 << 18, 56)(labels, cells)
+    outs += [S((cots.shape[0] // planes, lanes), BF16), S(labels.shape, jnp.int32), S(table.shape, BF16)]
+    scratch = [pltpu.VMEM(cells.shape, BF16), pltpu.VMEM(cots.shape, BF16), pltpu.SemaphoreType.DMA((4,))]
+    body = functools.partial(pack_body, planes)
+    args = [pltpu.with_memory_space_constraint(x, pltpu.HBM) for x in (labels, cells, cots, table)]
+    return call(body, outs, [HB] * 4, scratch, 1e9, 1 << 18, 8)(*args)
 
 
 def unpack_body(count, *refs):
@@ -131,8 +138,22 @@
     return call(body, outs, [VM] * (3 + len(got)), [], 2e8, 1 << 18, 12)(labels, slab, *got, after)
 
 
-def prep_body(rows, taps, table, kernel, lookup):
+def find(lookup, ids, ch):
+    low = jnp.where(ids < 0, -1, ids & (LOW - 1)).astype(F32).astype(BF16)
+    key = iota((LOW, ids.shape[1]), 0).astype(F32).astype(BF16)
+    match = jnp.where(key == low, jnp.ones((), BF16), jnp.zeros((), BF16))
+    picked = jnp.dot(lookup[...], match, preferred_element_type=F32)
+    bit = 9
+    while picked.shape[0] > ch:
+        half = picked.shape[0] // 2
+        picked = jnp.where(((ids >> bit) & 1) == 1, picked[half:], picked[:half])
+        bit -= 1
+    return picked.astype(BF16)
+
+
+def prep_body(taps, table, ids, kernel, lookup, feats):
     ch = table.shape[0]
+    depth, rows, cols = ids.shape
     shape = kernel.shape
     step = (rows + 2) * ch
     spread = hot(iota((shape[0], 3 * ch), 0) // rows == iota((shape[0], 3 * ch), 1))
@@ -146,22 +167,28 @@
     kernel[...] = total.astype(BF16)
     for high in range(table.shape[1] // LOW):
         lookup[high * ch : (high + 1) * ch, :] = table[:, high * LOW : (high + 1) * LOW]
-
-
-def prep_call(taps, table, rows):
+    for x in range(depth):
+        for y in range(rows):
+            at = (x * rows + y) * ch
+            feats[at : at + ch, :] = find(lookup, ids[x, y : y + 1], ch)
+
+
+def prep_call(taps, table, ids):
     ch, grains = table.shape
+    depth, rows, cols = ids.shape
     return call(
-        functools.partial(prep_body, rows),
+        prep_body,
         [
             jax.ShapeDtypeStruct((3 * ch * rows, 3 * (rows + 2) * ch), BF16),
             jax.ShapeDtypeStruct((grains // LOW * ch, LOW), BF16),
+            jax.ShapeDtypeStruct((depth * rows * ch, cols), BF16),
         ],
-        [VM] * 2,
+        [VM] * 3,
         [],
-        1.2e9,
+        2.5e9,
         1 << 18,
         16,
-    )(taps, table)
+    )(taps, table, ids)
 
 
 def split(x):
@@ -175,43 +202,30 @@
 
 def unfold_lanes(x, rows, wide):
     count = wide // x.shape[1]
-    cut = [x[i * rows : (i + 1) * rows].astype(F32) for i in range(2 * count)]
-    return jnp.concatenate(cut[:count], axis=1) + jnp.concatenate(cut[count:], axis=1)
-
-
-def fine_body(scale, planes, own, below, above, left, right, table, kernel, cot, bott_cot, out, part, message, feats, grads):
-    depth, rows, cols = own.shape
-    ch = out.shape[0]
+    cut = [x[i * rows : (i + 1) * rows].astype(F32) for i in range(x.shape[0] // rows)]
+    wides = [jnp.concatenate(cut[i : i + count], axis=1) for i in range(0, len(cut), count)]
+    return sum(wides[1:], wides[0])
+
+
+def fine_body(scale, known, below, above, left, right, table, kernel, cot, bott_cot, after, *refs):
+    out, part, message, feats, grads, stage, sems = refs
+    ch, depth, rows, cols = out.shape
     place, count = lax.axis_index("space"), lax.axis_size("space")
     lane, lanes = lax.axis_index("chan"), lax.axis_size("chan")
-    key = iota((LOW, cols), 0).astype(F32).astype(BF16)
-    one, none = jnp.ones((), BF16), jnp.zeros((), BF16)
-    def find(x):
-        for y in range(rows + 2):
-            if y == 0:
-                ids = jnp.where(lane == 0, -1, left[x : x + 1])
-            elif y == rows + 1:
-                ids = jnp.where(lane == lanes - 1, -1, right[x : x + 1])
-            elif x == 0:
-                ids = below[y - 1 : y]
-            elif x == depth + 1:
-                ids = above[y - 1 : y]
-            else:
-                ids = own[x - 1, y - 1 : y]
-            if x == 0:
-                ids = jnp.where(place == 0, -1, ids)
-            if x == depth + 1:
-                ids = jnp.where(place == count - 1, -1, ids)
-            low = jnp.where(ids < 0, -1, ids & (LOW - 1))
-            match = jnp.where(key == low.astype(F32).astype(BF16), one, none)
-            picked = jnp.dot(table[...], match, preferred_element_type=F32)
-            bit = 9
-            while picked.shape[0] > ch:
-                half = picked.shape[0] // 2
-                picked = jnp.where(((ids >> bit) & 1) == 1, picked[half:], picked[:half])
-                bit -= 1
+
+    def fill(x):
+        outer = ((0, left, lane == 0), (rows + 1, right, lane == lanes - 1))
+        ids = [(y, jnp.where(off, -1, ref[x : x + 1])) for y, ref, off in outer]
+        if 0 < x <= depth:
+            at = (x * (rows + 2) + 1) * ch
+            feats[at : at + rows * ch, :] = known[(x - 1) * rows * ch : x * rows * ch, :]
+        else:
+            ref, off = (below, place == 0) if x == 0 else (above, place == count - 1)
+            ids = ids + [(y + 1, ref[y : y + 1]) for y in range(rows)]
+            ids = [(y, jnp.where(off, -1, row)) for y, row in ids]
+        for y, row in ids:
             at = (x * (rows + 2) + y) * ch
-            feats[at : at + ch, :] = picked.astype(BF16)
+            feats[at : at + ch, :] = find(table, row, ch)
 
     group = ch * rows
     step = (rows + 2) * ch
@@ -219,16 +233,17 @@
     first, last = w == 0, w == cols - 1
     for x in range(depth):
         if x == 0:
-            find(0)
-            find(1)
-        find(x + 2)
+            fill(0)
+            fill(1)
+        fill(x + 2)
         window = feats[x * step : (x + 3) * step, :]
         q = jnp.dot(kernel[...], window, preferred_element_type=F32)
         pre = q[group : 2 * group]
         pre = pre + jnp.where(first, 0.0, pltpu.roll(q[:group], 1, 1))
         pre = pre + jnp.where(last, 0.0, pltpu.roll(q[2 * group :], cols - 1, 1))
         act, slope = silu_parts(pre)
-        out[:, x] = act.reshape(ch, rows, cols).astype(BF16)
+        stage[:, x] = act.reshape(ch, rows, cols).astype(BF16)
+        pltpu.make_async_copy(stage.at[:, x], out.at[:, x], sems.at[x]).start()
         delta = cot[:, x].astype(F32).reshape(group, cols) * slope
         shifted = jnp.concatenate(
             [
@@ -266,32 +281,37 @@
             result = result + (moved[:ch] + moved[ch:])
     result = result * scale
     part[...] = result
-    o_own = bott_cot.shape[0] // planes
-    message[:o_own, :] = apart(bott_cot[...], planes)
-    message[o_own:, :] = fold_lanes(split(result), message.shape[1])
-
-
-def fine_call(scale, own, below, above, left, right, table, kernel, cot, bott_cot, planes):
-    depth, rows, cols = own.shape
-    ch = cot.shape[0]
-    o_own, lanes = bott_cot.shape[0] // planes, bott_cot.shape[1] * planes
-    body = functools.partial(fine_body, scale, planes)
+    o_own, wide = bott_cot.shape
+    message[:o_own, :] = bott_cot[...]
+    message[o_own:, :] = fold_lanes([result.astype(BF16)], wide)
+    for x in range(depth):
+        pltpu.make_async_copy(stage.at[:, x], out.at[:, x], sems.at[x]).wait()
+
+
+def fine_call(scale, known, below, above, left, right, table, kernel, cot, bott_cot, after):
+    ch, depth, rows, cols = cot.shape
+    o_own, lanes = bott_cot.shape
+    more = ch * ch * TAPS // lanes
+    S = jax.ShapeDtypeStruct
     return call(
-        body,
+        functools.partial(fine_body, scale),
         [
-            jax.ShapeDtypeStruct((ch, depth, rows, cols), BF16),
-            jax.ShapeDtypeStruct((ch, ch * TAPS), F32),
-            jax.ShapeDtypeStruct((o_own + 2 * ch * ch * TAPS // lanes, lanes), BF16),
+            S((ch, depth, rows, cols), BF16),
+            S((ch, ch * TAPS), F32),
+            S((o_own + more, lanes), BF16),
         ],
-        [VM] * 9,
+        [VM] * 10,
         [
             pltpu.VMEM(((depth + 2) * (rows + 2) * ch, cols), BF16),
             pltpu.VMEM((3 * ch * rows, 3 * ch * (rows + 2)), F32),
+            pltpu.VMEM((ch, depth, rows, cols), BF16),
+            pltpu.SemaphoreType.DMA((depth,)),
         ],
-        7.4e9,
+        6e9,
         4 << 20,
         20,
-    )(own, below, above, left, right, table, kernel, cot, bott_cot)
+        [HB, VM, VM],
+    )(known, below, above, left, right, table, kernel, cot, bott_cot, after)
 
 
 def shift_masks(width, sign):
@@ -358,7 +378,9 @@
 
 
 def back_body(slabs, planes, weight, pre, part, *refs):
-    messages, (own_out, deltas, share, mine, part_sum, rows_t) = refs[:slabs], refs[slabs:]
+    cots, refs = refs[:slabs], refs[slabs:]
+    own_out, deltas, share, mine, part_sum, rows_t, stage, sem = refs
+    send = pltpu.make_async_copy(stage, own_out, sem)
     pieces, lanes, cb = mine.shape
     o_own = deltas.shape[0]
     width = lanes // planes
@@ -370,10 +392,11 @@
     for r in range(slabs):
         at = pl.multiple_of(lax.rem(place - r + slabs, slabs) * lanes, lanes)
         act, slope = silu_parts(pre[:, pl.ds(at, lanes)])
-        delta = (messages[r][:o_own, :].astype(F32) * slope).astype(BF16).astype(F32)
+        delta = (cots[r][:o_own, :].astype(F32) * slope).astype(BF16).astype(F32)
         deltas[:, pl.ds(pl.multiple_of(at + width, width), lanes)] = delta
         if r == 0:
-            own_out[...] = together(act, planes)
+            stage[...] = together(act, planes)
+            send.start()
     near = (planes + 2) * width
     turned = deltas[:, pl.ds(pl.multiple_of(place * lanes, width), near)].T
     w = iota((near, 1), 0) % BW
@@ -395,19 +418,20 @@
     back = jnp.dot(jnp.concatenate(blocks, axis=1), weight[...], preferred_element_type=F32)
     grad = part[...]
     for r in range(1, slabs):
-        grad = grad + unfold_lanes(messages[r][o_own:, :], *grad.shape)
+        grad = grad + unfold_lanes(cots[r][o_own:, :], *grad.shape)
     part_sum[...] = grad
-    rest = fold_lanes(split(grad), cb)
+    rest = fold_lanes([grad.astype(BF16)], cb)
     for j in range(pieces):
         block = back[:, j * cb : (j + 1) * cb]
         to = lax.rem(j - chan + pieces, pieces)
         mine[to] = block
         share[to, :lanes, :] = block.astype(BF16)
         share[j, lanes:, :] = rest
-
-
-def back_call(weight, pre, part, messages, pieces, planes):
-    slabs = len(messages)
+    send.wait()
+
+
+def back_call(weight, pre, part, cots, pieces, planes):
+    slabs = len(cots)
     o_own, length = pre.shape
     lanes = length // slabs
     width = lanes // planes
@@ -418,19 +442,24 @@
         [
             S((o_own * planes, width), BF16),
             S((o_own, length + 2 * width), F32),
-            S((pieces, lanes + 2 * part.size // cb, cb), BF16),
+            S((pieces, lanes + part.size // cb, cb), BF16),
             S((pieces, lanes, cb), F32),
             S(part.shape, F32),
         ],
         [VM] * (3 + slabs),
-        [pltpu.VMEM((3, (planes + 2) * (width + 2 * BW), o_own), BF16)],
-        2.3e9,
+        [
+            pltpu.VMEM((3, (planes + 2) * (width + 2 * BW), o_own), BF16),
+            pltpu.VMEM((o_own * planes, width), BF16),
+            pltpu.SemaphoreType.DMA,
+        ],
+        1.8e9,
         1 << 20,
         16,
-    )(weight, pre, part, *messages)
-
-
-PLAN = ((0, 0, 4), (0, 4, 9), (1, 0, 9), (2, 0, 5), (2, 5, 9))
+        [HB, VM, VM, VM, VM],
+    )(weight, pre, part, *cots)
+
+
+PLAN = ((0, 0, 4), (0, 4, 9), (1, 0, 9), (2, 0, 4), (2, 4, 7), (2, 7, 9))
 
 
 def wgrad_body(scale, delta, full, out, shifted, stage, sems):
@@ -540,32 +569,33 @@
     lanes = planes * width
     o_own = bott_cot.shape[0]
 
-    slab, first, last, ids = pack_call(labels, bott_in.reshape(cb * planes, width), planes)
+    flat_in, flat_cot = bott_in.reshape(cb * planes, width), bott_cot.reshape(o_own * planes, width)
+    slab, first, last, cot, ids, near_table = pack_call(labels, flat_in, flat_cot, table.T, planes)
     taps = fine_weight.reshape(3, 3, 3, ch, ch).transpose(1, 2, 4, 0, 3).reshape(3, 3 * ch, 3 * ch)
-    kernel, lookup = prep_call(taps, table.T, rows)
+    kernel, lookup, known = prep_call(taps, near_table, ids)
     sends = [last] + [slab] * (spaces - 3) + [first]
     got = [hop(x, "space", r + 1) for r, x in enumerate(sends)]
     slabs, below, above, top, bottom = unpack_call(ids, slab, got, kernel)
     left = hop(bottom, "chan", 1)
     right = hop(top, "chan", chans - 1)
     scale = (depth * spaces * rows * chans * cols) ** -0.5
-    cot = bott_cot.reshape(o_own * planes, width)
+    mate = swap(slabs, "chan", 1)
     fine_out, part, message = fine_call(
-        scale, ids, below, above, left, right, lookup, kernel, fine_cot, cot, planes
+        scale, known, below, above, left, right, lookup, kernel, fine_cot, cot, mate
     )
-    messages = [message] + [hop(message, "space", r) for r in range(1, spaces)]
+    cots = [cot] + [hop(message, "space", r) for r in range(1, spaces)]
     pieces = {0: slabs}
     bits = [1 << i for i in range(chans.bit_length() - 1)]
     for bit in bits[1:] + bits[:1]:
         for j, x in list(pieces.items()):
             if bit == 1 and j:
                 x, part = lax.optimization_barrier((x, part))
-            pieces[j ^ bit] = swap(x, "chan", bit)
+            pieces[j ^ bit] = swap(x, "chan", bit) if j ^ bit > 1 else mate
     ins = [pieces[j] for j in range(chans)]
 
     weight = bott_weight.transpose(1, 0, 2).reshape(27 * o_own, cb * chans)
     pre, full = bott_call(weight, ins, planes)
-    bott_out, delta, share, mine, part = back_call(weight, pre, part, messages, chans, planes)
+    bott_out, delta, share, mine, part = back_call(weight, pre, part, cots, chans, planes)
     others = [hop(share[r], "chan", r) for r in range(1, chans)]
     bott_wgrad = wgrad_call((planes * spaces * width) ** -0.5, delta, full).transpose(1, 0, 2)
     bott_dgrad, fine_wgrad = last_call(mine, part, others, planes)

time: 48.5 us -> 45.2 us (0.932)
  starting transfers between devices: 18.5 us -> 17 us
  waiting for transfers between devices: 6.53 us -> 5.63 us
  Pallas kernels: 21.9 us -> 21.1 us
    ppermute x11, starting transfers between devices: 16.4 us -> 14.3 us  [hop(): lax.ppermute(x, axis, [(i, (i + offset) % count) for i in range(count)])]
    ppermute x11, waiting for transfers between devices: 6.53 us -> 5.62 us  [hop(): lax.ppermute(x, axis, [(i, (i + offset) % count) for i in range(count)])]
    ppermute x3, starting transfers between devices: 2.14 us -> 2.79 us  [swap(): return lax.ppermute(x, axis, [(i, i ^ bit) for i in range(count)])]
    pallas_call x3, Pallas kernels: 9.71 us -> 9.14 us  [the longest x1 5.89 us: fine_call(): call(functools.partial(fine_body, scale), [S((ch, depth, rows, cols), BF1...]
  transfers between devices with their start and end apart: 14 -> 14, of which waited for: 4 -> 4; matrix products, arithmetic and copies ran while one was open for 1% -> 1% of each run, Pallas kernels for 36% -> 38%
where the time goes in v5:
time: 45.2 us; the launch traced here: 45 us
  Pallas kernels  21.1 us (47%)
  starting transfers between devices  17 us (38%)
  waiting for transfers between devices  5.63 us (12%)
  between operations  0.8 us (2%)
  local copies, waits for them, and re-layouts  0.5 us (1%)
    ppermute x11, starting transfers between devices, hop(): lax.ppermute(x, axis, [(i, (i + offset) % count) for i in range(count)])  14.3 us
    pallas_call x1, Pallas kernels, fine_call(): call(functools.partial(fine_body, scale), [S((ch, depth, rows, cols), BF1...  5.89 us
    ppermute x11, waiting for transfers between devices, hop(): lax.ppermute(x, axis, [(i, (i + offset) % count) for i in range(count)])  5.62 us
    pallas_call x1, Pallas kernels, wgrad_call(): call(functools.partial(wgrad_body, scale), [jax.ShapeDtypeStruct((27, o_o...  5.08 us
    pallas_call x1, Pallas kernels, bott_call(): call(functools.partial(bott_body, pieces, planes), [S((o_own, slabs * lan...  4.08 us
    ppermute x3, starting transfers between devices, swap(): return lax.ppermute(x, axis, [(i, i ^ bit) for i in range(count)])  2.79 us
    pallas_call x1, Pallas kernels, prep_call(): call(prep_body, [jax.ShapeDtypeStruct((3 * ch * rows, 3 * (rows + 2) * ch...  1.98 us
    pallas_call x1, Pallas kernels, back_call(): call(functools.partial(back_body, slabs, planes), [S((o_own * planes, wid...  1.81 us
  transfers between devices with their start and end apart: 14, of which 4 were waited for; matrix products, arithmetic and copies ran while one was open for 1% of the time, Pallas kernels for 38%

profile of v5, /device:TPU:1, one launch (start us, length us, event | category | flops | bytes accessed | tf_op | source)
XLA Modules:
  0.0 45.0 jit_solution(15091069311395820914)
XLA Ops:
  0.6 0.0 copy-start.2
  0.6 1.3 %shard_map.110 = (bf16[128,256]{1,0:T(8,128)(2,1)S(1)}, bf16[160,256]{1,0:T(8,128)(2,1)S(1)}, bf16[160,256]{1,0:T(8,128)(2,1)S(1)}, bf16[128,256]{1,0:T(8,128)(2...) custom-call(s32[4,8,512]{2,1,0:T(8,128)} %labels.1, bf16[256,128]{1,0:T(8,128)(2,1)} %bitcast.22, ...), custom_call_target="tpu_custom_call" | custom-call | flops 1000000000 | bytes 262144 | tf_op jit(solution)/shard_map/pallas_call | solution.py:106
  1.9 3.2 %collective-permute-start.1 = (bf16[128,256]{1,0:T(8,128)(2,1)S(1)}, bf16[128,256]{1,0:T(8,128)(2,1)S(1)}, u32[]{:S(2)}, u32[]{:S(2)}) collective-permute-start(bf16[128,256]{1,0:T(8,128)(2,1)S(1)} %get-tuple-element.36.refs_1_), channel_id=1, source_target_pairs={{0,8},{4,12},{8,0},{12,4},{1,9},{5,13},{9,1},{13,5},{2,10},{6,14},... | collective-permute-start | bytes 196616 | tf_op jit(solution)/shard_map/ppermute | solution.py:556
  5.1 1.3 %collective-permute-start = (bf16[160,256]{1,0:T(8,128)(2,1)S(1)}, bf16[160,256]{1,0:T(8,128)(2,1)S(1)}, u32[]{:S(2)}, u32[]{:S(2)}) collective-permute-start(bf16[160,256]{1,0:T(8,128)(2,1)S(1)} %get-tuple-element.37), channel_id=1, source_target_pairs={{0,4},{4,8},{8,12},{12,0},{1,5},{5,9},{9,13},{13,1},{2,6},{6,10},{... | collective-permute-start | bytes 245768 | tf_op jit(solution)/shard_map/ppermute | solution.py:556
  6.4 2.0 %collective-permute-start.2 = (bf16[160,256]{1,0:T(8,128)(2,1)S(1)}, bf16[160,256]{1,0:T(8,128)(2,1)S(1)}, u32[]{:S(2)}, u32[]{:S(2)}) collective-permute-start(bf16[160,256]{1,0:T(8,128)(2,1)S(1)} %get-tuple-element.38), channel_id=1, source_target_pairs={{0,12},{4,0},{8,4},{12,8},{1,13},{5,1},{9,5},{13,9},{2,14},{6,2},{... | collective-permute-start | bytes 245768 | tf_op jit(solution)/shard_map/ppermute | solution.py:556
  8.4 0.0 copy-done.2
  8.4 0.2 copy.13
  8.6 0.2 copy.14
  8.7 0.1 reshape.32.taps
  8.9 0.0 copy-start.1
  8.9 2.0 %shard_map.111 = (bf16[384,480]{1,0:T(8,128)(2,1)S(1)}, bf16[128,128]{1,0:T(8,128)(2,1)S(1)}, bf16[512,512]{1,0:T(8,128)(2,1)S(1)}) custom-call(bf16[3,48,48]{2,1,0:T(8,128)(2,1)S(1)} %reshape.32.taps, bf16[16,1024]{1,0:T(8,128)(2,1)S(1)} %get-tuple-element.33.table, s32[4,8,512]{2,1,0:T(8,128)S(1)} %get-tuple-element.34.ids.refs_0_), custom_call_target="tpu_custom_call" | custom-call | flops 2500000000 | bytes 262144 | tf_op jit(solution)/shard_map/pallas_call | solution.py:179
  10.9 0.0 collective-permute-done.1.refs_3_
  10.9 0.0 collective-permute-done.refs_2_
  10.9 0.1 collective-permute-done.2.refs_4_
  11.0 2.2 %collective-permute-start.5 = (bf16[4,128,256]{2,1,0:T(8,128)(2,1)S(1)}, bf16[4,128,256]{2,1,0:T(8,128)(2,1)S(1)}, u32[]{:S(2)}, u32[]{:S(2)}) collective-permute-start(bf16[4,128,256]{2,1,0:T(8,128)(2,1)S(1)} %get-tuple-element.46.refs_1_), channel_id=1, source_target_pairs={{0,1},{1,0},{2,3},{3,2},{4,5},{5,4},{6,7},{7,6},{8,9},{9,8},{10,11... | collective-permute-start | bytes 786440 | tf_op jit(solution)/shard_map/ppermute | solution.py:561
  13.2 1.4 %collective-permute-start.3 = (s32[6,512]{1,0:T(8,128)S(1)}, s32[6,512]{1,0:T(8,128)S(1)}, u32[]{:S(2)}, u32[]{:S(2)}) collective-permute-start(s32[6,512]{1,0:T(8,128)S(1)} %get-tuple-element.42), channel_id=1, source_target_pairs={{0,1},{1,2},{2,3},{3,0},{4,5},{5,6},{6,7},{7,4},{8,9},{9,10},{10,1... | collective-permute-start | bytes 36872 | tf_op jit(solution)/shard_map/ppermute | solution.py:556
  14.6 0.0 collective-permute-start.4
  14.6 0.6 %collective-permute-start.6 = (bf16[4,128,256]{2,1,0:T(8,128)(2,1)S(1)}, bf16[4,128,256]{2,1,0:T(8,128)(2,1)S(1)}, u32[]{:S(2)}, u32[]{:S(2)}) collective-permute-start(bf16[4,128,256]{2,1,0:T(8,128)(2,1)S(1)} %get-tuple-element.46.refs_1_), channel_id=1, source_target_pairs={{0,2},{1,3},{2,0},{3,1},{4,6},{5,7},{6,4},{7,5},{8,10},{9,11},{10,... | collective-permute-start | bytes 786440 | tf_op jit(solution)/shard_map/ppermute | solution.py:561
  15.1 0.3 collective-permute-done.3.left
  15.4 2.4 %collective-permute-done.4.right = s32[6,512]{1,0:T(8,128)S(1)} collective-permute-done((s32[6,512]{1,0:T(8,128)S(1)}, s32[6,512]{1,0:T(8,128)S(1)}, u32[]{:S(2)}, u32[]{:S(2)}) %collective-permute-start.4) | collective-permute-done | bytes 12320 | tf_op jit(solution)/shard_map/ppermute | solution.py:556
  17.8 0.0 collective-permute-done.5.after.refs_2_
  17.8 0.0 copy-done.1
  17.8 0.0 copy-start
  17.9 5.9 %shard_map.113 = (bf16[16,4,8,512]{3,2,1,0:T(8,128)(2,1)}, f32[16,512]{1,0:T(8,128)S(1)}, bf16[160,256]{1,0:T(8,128)(2,1)S(1)}) custom-call(bf16[512,512]{1,0:T(8,128)(2,1)S(1)} %get-tuple-element.35.known, s32[8,512]{1,0:T(8,128)S(1)} %get-tuple-element.40.below, s32[8,512]{1,0:T(8,128)S(1)} %get-tuple-element.41.above, ...), custom_call_target="tpu_custom_call" | custom-call | flops 6000000000 | bytes 4194304 | tf_op jit(solution)/shard_map/pallas_call | solution.py:296
  23.7 0.0 collective-permute-done.6.refs_3_
  23.8 0.1 collective-permute-start.7
  23.8 2.7 %collective-permute-start.10 = (bf16[160,256]{1,0:T(8,128)(2,1)S(1)}, bf16[160,256]{1,0:T(8,128)(2,1)S(1)}, u32[]{:S(2)}, u32[]{:S(2)}) collective-permute-start(bf16[160,256]{1,0:T(8,128)(2,1)S(1)} %get-tuple-element.52), channel_id=1, source_target_pairs={{0,12},{4,0},{8,4},{12,8},{1,13},{5,1},{9,5},{13,9},{2,14},{6,2},{... | collective-permute-start | bytes 245768 | tf_op jit(solution)/shard_map/ppermute | solution.py:556
  26.5 0.0 collective-permute-start.9
  26.5 1.0 %collective-permute-start.8 = (bf16[160,256]{1,0:T(8,128)(2,1)S(1)}, bf16[160,256]{1,0:T(8,128)(2,1)S(1)}, u32[]{:S(2)}, u32[]{:S(2)}) collective-permute-start(bf16[160,256]{1,0:T(8,128)(2,1)S(1)} %get-tuple-element.52), channel_id=1, source_target_pairs={{0,4},{4,8},{8,12},{12,0},{1,5},{5,9},{9,13},{13,1},{2,6},{6,10},{... | collective-permute-start | bytes 245768 | tf_op jit(solution)/shard_map/ppermute | solution.py:556
  27.5 0.0 collective-permute-done.7.refs_4_
  27.5 0.0 copy-done
  27.5 4.1 %shard_map.114 = (f32[128,1024]{1,0:T(8,128)S(1)}, bf16[512,1280]{1,0:T(8,128)(2,1)S(1)}) custom-call(bf16[3456,512]{1,0:T(8,128)(2,1)S(1)} %bitcast.19, bf16[4,128,256]{2,1,0:T(8,128)(2,1)S(1)} %get-tuple-element.46.refs_1_, bf16[4,128,256]{2,1,0:T(8,128)(2,1)S(1)} %collective-permute-done.5.after.refs_2_, ...), custom_call_target="tpu_custom_call" | custom-call | flops 5000000000 | bytes 1048576 | tf_op jit(solution)/shard_map/pallas_call | solution.py:369
  31.6 0.0 collective-permute-done.10.refs_3_
  31.6 2.8 %collective-permute-done.9.refs_2_ = bf16[160,256]{1,0:T(8,128)(2,1)S(1)} collective-permute-done((bf16[160,256]{1,0:T(8,128)(2,1)S(1)}, bf16[160,256]{1,0:T(8,128)(2,1)S(1)}, u32[]{:S(2)}, u32[]{:S(2)}) %collective-permute-start.9) | collective-permute-done | bytes 81952 | tf_op jit(solution)/shard_map/ppermute | solution.py:556
  34.4 0.0 collective-permute-done.8.refs_1_
  34.4 1.8 %shard_map.115 = (bf16[256,128]{1,0:T(8,128)(2,1)}, f32[128,1280]{1,0:T(8,128)S(1)}, bf16[4,320,128]{2,1,0:T(8,128)(2,1)S(1)}, f32[4,256,128]{2,1,0:T(8,128)S(1)}, f32[16,512]{1,0:T(8,128)S(1)}) custom-call(bf16[3456,512]{1,0:T(8,128)(2,1)S(1)} %bitcast.20, f32[128,1024]{1,0:T(8,128)S(1)} %get-tuple-element.50.pre, f32[16,512]{1,0:T(8,128)S(1)} %get-tuple-element.51.part, ...), custom_call_target="tpu_custom_call" | custom-call | flops 1800000000 | bytes 1048576 | tf_op jit(solution)/shard_map/pallas_call | solution.py:440
  36.2 1.1 %collective-permute-start.13 = (bf16[320,128]{1,0:T(8,128)(2,1)S(1)}, bf16[320,128]{1,0:T(8,128)(2,1)S(1)}, u32[]{:S(2)}, u32[]{:S(2)}) collective-permute-start(bf16[320,128]{1,0:T(8,128)(2,1)S(1)} %get-tuple-element.61), channel_id=1, source_target_pairs={{0,3},{1,0},{2,1},{3,2},{4,7},{5,4},{6,5},{7,6},{8,11},{9,8},{10,9... | collective-permute-start | bytes 245768 | tf_op jit(solution)/shard_map/ppermute | solution.py:556
  37.3 0.3 collective-permute-start.12
  37.6 1.4 %collective-permute-start.11 = (bf16[320,128]{1,0:T(8,128)(2,1)S(1)}, bf16[320,128]{1,0:T(8,128)(2,1)S(1)}, u32[]{:S(2)}, u32[]{:S(2)}) collective-permute-start(bf16[320,128]{1,0:T(8,128)(2,1)S(1)} %get-tuple-element.63), channel_id=1, source_target_pairs={{0,1},{1,2},{2,3},{3,0},{4,5},{5,6},{6,7},{7,4},{8,9},{9,10},{10,1... | collective-permute-start | bytes 245768 | tf_op jit(solution)/shard_map/ppermute | solution.py:556
  39.0 5.1 %shard_map.117 = f32[27,128,512]{2,1,0:T(8,128)} custom-call(f32[128,1280]{1,0:T(8,128)S(1)} %get-tuple-element.59.delta, bf16[512,1280]{1,0:T(8,128)(2,1)S(1)} %get-tuple-element.60.full), custom_call_target="tpu_custom_call" | custom-call | flops 6600000000 | bytes 8388608 | tf_op jit(solution)/shard_map/pallas_call | solution.py:508
  44.1 0.0 collective-permute-done.13.refs_2_
  44.1 0.0 collective-permute-done.12.refs_1_
  44.1 0.0 collective-permute-done.11.refs_0_
  44.1 0.9 %shard_map.116 = (bf16[256,128]{1,0:T(8,128)(2,1)}, f32[16,16,27]{2,1,0:T(8,128)}) custom-call(f32[4,256,128]{2,1,0:T(8,128)S(1)} %get-tuple-element.53.mine, f32[16,512]{1,0:T(8,128)S(1)} %get-tuple-element.54.part, bf16[320,128]{1,0:T(8,128)(2,1)S(1)} %collective-permute-done.11.refs_0_, bf16[320,128]{1,0:T(8,128)(2,1)S(1)} %collective-permute-done.12.refs_1_, ...), custom_call_target="tpu_custom_call" | custom-call | flops 1000000000 | bytes 262144 | tf_op jit(solution)/shard_map/pallas_call | solution.py:540
  (2 shorter events, 0.1 us)
Async XLA Ops:
  0.6 7.8 %copy-start.2 = (bf16[27,16,16]{0,2,1:T(8,128)(2,1)S(1)}, bf16[27,16,16]{0,2,1:T(8,128)(2,1)}, u32[]{:S(2)}) copy-start(bf16[27,16,16]{0,2,1:T(8,128)(2,1)} %param.9) | copy-start | bytes 41476
  1.9 9.0 %collective-permute-start.1 = (bf16[128,256]{1,0:T(8,128)(2,1)S(1)}, bf16[128,256]{1,0:T(8,128)(2,1)S(1)}, u32[]{:S(2)}, u32[]{:S(2)}) collective-permute-start(bf16[128,256]{1,0:T(8,128)(2,1)S(1)} %get-tuple-element.36.refs_1_), channel_id=1, source_target_pairs={{0,8},{4,12},{8,0},{12,4},{1,9},{5,13},{9,1},{13,5},{2,10},{6,14},... | collective-permute-start | bytes 196616 | tf_op jit(solution)/shard_map/ppermute | solution.py:556
  5.1 5.8 %collective-permute-start = (bf16[160,256]{1,0:T(8,128)(2,1)S(1)}, bf16[160,256]{1,0:T(8,128)(2,1)S(1)}, u32[]{:S(2)}, u32[]{:S(2)}) collective-permute-start(bf16[160,256]{1,0:T(8,128)(2,1)S(1)} %get-tuple-element.37), channel_id=1, source_target_pairs={{0,4},{4,8},{8,12},{12,0},{1,5},{5,9},{9,13},{13,1},{2,6},{6,10},{... | collective-permute-start | bytes 245768 | tf_op jit(solution)/shard_map/ppermute | solution.py:556
  6.4 4.6 %collective-permute-start.2 = (bf16[160,256]{1,0:T(8,128)(2,1)S(1)}, bf16[160,256]{1,0:T(8,128)(2,1)S(1)}, u32[]{:S(2)}, u32[]{:S(2)}) collective-permute-start(bf16[160,256]{1,0:T(8,128)(2,1)S(1)} %get-tuple-element.38), channel_id=1, source_target_pairs={{0,12},{4,0},{8,4},{12,8},{1,13},{5,1},{9,5},{13,9},{2,14},{6,2},{... | collective-permute-start | bytes 245768 | tf_op jit(solution)/shard_map/ppermute | solution.py:556
  8.9 9.0 %copy-start.1 = (bf16[16,4,8,512]{3,2,1,0:T(8,128)(2,1)S(1)}, bf16[16,4,8,512]{3,2,1,0:T(8,128)(2,1)}, u32[]{:S(2)}) copy-start(bf16[16,4,8,512]{3,2,1,0:T(8,128)(2,1)} %cot.1) | copy-start | bytes 1572868
  11.0 6.8 %collective-permute-start.5 = (bf16[4,128,256]{2,1,0:T(8,128)(2,1)S(1)}, bf16[4,128,256]{2,1,0:T(8,128)(2,1)S(1)}, u32[]{:S(2)}, u32[]{:S(2)}) collective-permute-start(bf16[4,128,256]{2,1,0:T(8,128)(2,1)S(1)} %get-tuple-element.46.refs_1_), channel_id=1, source_target_pairs={{0,1},{1,0},{2,3},{3,2},{4,5},{5,4},{6,7},{7,6},{8,9},{9,8},{10,11... | collective-permute-start | bytes 786440 | tf_op jit(solution)/shard_map/ppermute | solution.py:561
  13.2 2.2 %collective-permute-start.3 = (s32[6,512]{1,0:T(8,128)S(1)}, s32[6,512]{1,0:T(8,128)S(1)}, u32[]{:S(2)}, u32[]{:S(2)}) collective-permute-start(s32[6,512]{1,0:T(8,128)S(1)} %get-tuple-element.42), channel_id=1, source_target_pairs={{0,1},{1,2},{2,3},{3,0},{4,5},{5,6},{6,7},{7,4},{8,9},{9,10},{10,1... | collective-permute-start | bytes 36872 | tf_op jit(solution)/shard_map/ppermute | solution.py:556
  14.6 3.3 %collective-permute-start.4 = (s32[6,512]{1,0:T(8,128)S(1)}, s32[6,512]{1,0:T(8,128)S(1)}, u32[]{:S(2)}, u32[]{:S(2)}) collective-permute-start(s32[6,512]{1,0:T(8,128)S(1)} %get-tuple-element.43), channel_id=1, source_target_pairs={{0,3},{1,0},{2,1},{3,2},{4,7},{5,4},{6,5},{7,6},{8,11},{9,8},{10,9... | collective-permute-start | bytes 36872 | tf_op jit(solution)/shard_map/ppermute | solution.py:556
  14.6 9.2 %collective-permute-start.6 = (bf16[4,128,256]{2,1,0:T(8,128)(2,1)S(1)}, bf16[4,128,256]{2,1,0:T(8,128)(2,1)S(1)}, u32[]{:S(2)}, u32[]{:S(2)}) collective-permute-start(bf16[4,128,256]{2,1,0:T(8,128)(2,1)S(1)} %get-tuple-element.46.refs_1_), channel_id=1, source_target_pairs={{0,2},{1,3},{2,0},{3,1},{4,6},{5,7},{6,4},{7,5},{8,10},{9,11},{10,... | collective-permute-start | bytes 786440 | tf_op jit(solution)/shard_map/ppermute | solution.py:561
  17.8 9.6 %copy-start = (bf16[128,27,512]{2,0,1:T(8,128)(2,1)S(1)}, bf16[128,27,512]{2,0,1:T(8,128)(2,1)}, u32[]{:S(2)}) copy-start(bf16[128,27,512]{2,0,1:T(8,128)(2,1)} %param.12) | copy-start | bytes 10616836
  23.8 3.7 %collective-permute-start.7 = (bf16[4,128,256]{2,1,0:T(8,128)(2,1)S(1)}, bf16[4,128,256]{2,1,0:T(8,128)(2,1)S(1)}, u32[]{:S(2)}, u32[]{:S(2)}) collective-permute-start(bf16[4,128,256]{2,1,0:T(8,128)(2,1)S(1)} %collective-permute-done.6.refs_3_), channel_id=1, source_target_pairs={{0,1},{1,0},{2,3},{3,2},{4,5},{5,4},{6,7},{7,6},{8,9},{9,8},{10,11... | collective-permute-start | bytes 786440 | tf_op jit(solution)/shard_map/ppermute | solution.py:561
  23.8 7.7 %collective-permute-start.10 = (bf16[160,256]{1,0:T(8,128)(2,1)S(1)}, bf16[160,256]{1,0:T(8,128)(2,1)S(1)}, u32[]{:S(2)}, u32[]{:S(2)}) collective-permute-start(bf16[160,256]{1,0:T(8,128)(2,1)S(1)} %get-tuple-element.52), channel_id=1, source_target_pairs={{0,12},{4,0},{8,4},{12,8},{1,13},{5,1},{9,5},{13,9},{2,14},{6,2},{... | collective-permute-start | bytes 245768 | tf_op jit(solution)/shard_map/ppermute | solution.py:556
  26.5 7.9 %collective-permute-start.9 = (bf16[160,256]{1,0:T(8,128)(2,1)S(1)}, bf16[160,256]{1,0:T(8,128)(2,1)S(1)}, u32[]{:S(2)}, u32[]{:S(2)}) collective-permute-start(bf16[160,256]{1,0:T(8,128)(2,1)S(1)} %get-tuple-element.52), channel_id=1, source_target_pairs={{0,8},{4,12},{8,0},{12,4},{1,9},{5,13},{9,1},{13,5},{2,10},{6,14},... | collective-permute-start | bytes 245768 | tf_op jit(solution)/shard_map/ppermute | solution.py:556
  26.5 7.9 %collective-permute-start.8 = (bf16[160,256]{1,0:T(8,128)(2,1)S(1)}, bf16[160,256]{1,0:T(8,128)(2,1)S(1)}, u32[]{:S(2)}, u32[]{:S(2)}) collective-permute-start(bf16[160,256]{1,0:T(8,128)(2,1)S(1)} %get-tuple-element.52), channel_id=1, source_target_pairs={{0,4},{4,8},{8,12},{12,0},{1,5},{5,9},{9,13},{13,1},{2,6},{6,10},{... | collective-permute-start | bytes 245768 | tf_op jit(solution)/shard_map/ppermute | solution.py:556
  36.2 7.9 %collective-permute-start.13 = (bf16[320,128]{1,0:T(8,128)(2,1)S(1)}, bf16[320,128]{1,0:T(8,128)(2,1)S(1)}, u32[]{:S(2)}, u32[]{:S(2)}) collective-permute-start(bf16[320,128]{1,0:T(8,128)(2,1)S(1)} %get-tuple-element.61), channel_id=1, source_target_pairs={{0,3},{1,0},{2,1},{3,2},{4,7},{5,4},{6,5},{7,6},{8,11},{9,8},{10,9... | collective-permute-start | bytes 245768 | tf_op jit(solution)/shard_map/ppermute | solution.py:556
  37.3 6.8 %collective-permute-start.12 = (bf16[320,128]{1,0:T(8,128)(2,1)S(1)}, bf16[320,128]{1,0:T(8,128)(2,1)S(1)}, u32[]{:S(2)}, u32[]{:S(2)}) collective-permute-start(bf16[320,128]{1,0:T(8,128)(2,1)S(1)} %get-tuple-element.62), channel_id=1, source_target_pairs={{0,2},{1,3},{2,0},{3,1},{4,6},{5,7},{6,4},{7,5},{8,10},{9,11},{10,... | collective-permute-start | bytes 245768 | tf_op jit(solution)/shard_map/ppermute | solution.py:556
  37.6 6.5 %collective-permute-start.11 = (bf16[320,128]{1,0:T(8,128)(2,1)S(1)}, bf16[320,128]{1,0:T(8,128)(2,1)S(1)}, u32[]{:S(2)}, u32[]{:S(2)}) collective-permute-start(bf16[320,128]{1,0:T(8,128)(2,1)S(1)} %get-tuple-element.63), channel_id=1, source_target_pairs={{0,1},{1,2},{2,3},{3,0},{4,5},{5,6},{6,7},{7,4},{8,9},{9,10},{10,1... | collective-permute-start | bytes 245768 | tf_op jit(solution)/shard_map/ppermute | solution.py:556

commit v6 on v5

--- a/solution.py
+++ b/solution.py
@@ -208,7 +208,7 @@
 
 
 def fine_body(scale, known, below, above, left, right, table, kernel, cot, bott_cot, after, *refs):
-    out, part, message, feats, grads, stage, sems = refs
+    out, part, message, feats, grads, stage, sems, pres, deltas, keeps = refs
     ch, depth, rows, cols = out.shape
     place, count = lax.axis_index("space"), lax.axis_size("space")
     lane, lanes = lax.axis_index("chan"), lax.axis_size("chan")
@@ -231,13 +231,26 @@
     step = (rows + 2) * ch
     w = lax.broadcasted_iota(jnp.int32, (1, cols), 1)
     first, last = w == 0, w == cols - 1
+
+    def forward(x):
+        pres[x % 2] = jnp.dot(kernel[...], feats[x * step : (x + 3) * step, :], preferred_element_type=F32)
+
+    def backward(x):
+        term = dot_nt(deltas[x % 2], feats[x * step : (x + 3) * step, :])
+        grads[...] = term if x == 0 else grads[...] + term
+
+    gap = (iota(grads.shape, 1) % step) // ch - iota(grads.shape, 0) % rows
+    for x in range(depth + 2):
+        fill(x)
+    for b in range(3):
+        keeps[b] = hot(gap == b)
+    forward(0)
     for x in range(depth):
-        if x == 0:
-            fill(0)
-            fill(1)
-        fill(x + 2)
-        window = feats[x * step : (x + 3) * step, :]
-        q = jnp.dot(kernel[...], window, preferred_element_type=F32)
+        if x + 1 < depth:
+            forward(x + 1)
+        if x > 0:
+            backward(x - 1)
+        q = pres[x % 2]
         pre = q[group : 2 * group]
         pre = pre + jnp.where(first, 0.0, pltpu.roll(q[:group], 1, 1))
         pre = pre + jnp.where(last, 0.0, pltpu.roll(q[2 * group :], cols - 1, 1))
@@ -245,29 +258,16 @@
         stage[:, x] = act.reshape(ch, rows, cols).astype(BF16)
         pltpu.make_async_copy(stage.at[:, x], out.at[:, x], sems.at[x]).start()
         delta = cot[:, x].astype(F32).reshape(group, cols) * slope
-        shifted = jnp.concatenate(
-            [
-                jnp.where(last, 0.0, pltpu.roll(delta, cols - 1, 1)).astype(BF16),
-                delta.astype(BF16),
-                jnp.where(first, 0.0, pltpu.roll(delta, 1, 1)).astype(BF16),
-            ],
-            axis=0,
-        )
-        term = dot_nt(shifted, window)
-        grads[...] = term if x == 0 else grads[...] + term
-    total = grads[...]
-    shape = total.shape
-    gap = (iota(shape, 1) % step) // ch - iota(shape, 0) % rows
+        deltas[x % 2, :group] = jnp.where(last, 0.0, pltpu.roll(delta, cols - 1, 1)).astype(BF16)
+        deltas[x % 2, group : 2 * group] = delta.astype(BF16)
+        deltas[x % 2, 2 * group :] = jnp.where(first, 0.0, pltpu.roll(delta, 1, 1)).astype(BF16)
+    backward(depth - 1)
+    shape = grads.shape
     gather = hot(iota((3 * ch, shape[0]), 0) == iota((3 * ch, shape[0]), 1) // rows)
     m, n = iota((shape[1], 3 * ch), 0), iota((shape[1], 3 * ch), 1)
     fold = hot((m // step == n // ch) & (m % ch == n % ch))
-    high, rest = split(total)
-    sums = []
-    for b in range(3):
-        keep = hot(gap == b)
-        kept = jnp.dot(gather, high * keep, preferred_element_type=F32)
-        kept = kept + jnp.dot(gather, rest * keep, preferred_element_type=F32)
-        sums.append(kept)
+    total = grads[...].astype(BF16)
+    sums = [jnp.dot(gather, total * keeps[b], preferred_element_type=F32) for b in range(3)]
     tall = jnp.concatenate([piece for b in range(3) for piece in split(sums[b])], axis=0)
     tall = jnp.dot(tall, fold, preferred_element_type=F32)
     m, n = iota((3 * ch, ch * TAPS), 0), iota((3 * ch, ch * TAPS), 1)
@@ -306,6 +306,9 @@
             pltpu.VMEM((3 * ch * rows, 3 * ch * (rows + 2)), F32),
             pltpu.VMEM((ch, depth, rows, cols), BF16),
             pltpu.SemaphoreType.DMA((depth,)),
+            pltpu.VMEM((2, 3 * ch * rows, cols), F32),
+            pltpu.VMEM((2, 3 * ch * rows, cols), BF16),
+            pltpu.VMEM((3, 3 * ch * rows, 3 * ch * (rows + 2)), BF16),
         ],
         6e9,
         4 << 20,
@@ -324,57 +327,90 @@
     return masks
 
 
-def bott_body(pieces, planes, *refs):
-    weight, ins, (pre_out, padded) = refs[0], refs[1 : 1 + pieces], refs[1 + pieces :]
-    slabs, cb, lanes = ins[0].shape
+def convolve(weight, padded, chunks, before, pre_out, slabs, planes):
+    o_own, lanes = pre_out.shape[0], pre_out.shape[1] // slabs
     width = lanes // planes
-    c_all = cb * pieces
-    o_own = pre_out.shape[0]
-    total = slabs * planes
-    place = lax.axis_index("space")
-    chan = lax.axis_index("chan")
-    padded[:, :width] = jnp.zeros((c_all, width), BF16)
-    padded[:, (total + 1) * width :] = jnp.zeros((c_all, width), BF16)
-    for j in range(pieces):
-        row = pl.multiple_of((chan ^ j) * cb, cb)
-        for r in range(slabs):
-            slab = lax.rem(place - r + slabs, slabs)
-            at = pl.multiple_of(slab * lanes + width, width)
-            padded[pl.ds(row, cb), pl.ds(at, lanes)] = ins[j][r]
     masks = shift_masks(width, 1)
     for n in range(slabs):
         base = n * lanes
-        pre = [jnp.zeros((o_own, width), F32) for _ in range(planes)]
+        at = [base + p * width for p in range(planes)]
+        pre = [jnp.zeros((o_own, width), F32) if before is None else before[:, i : i + width] for i in at]
         for k, (b, e) in enumerate(STEPS):
             term = jnp.zeros((o_own, lanes), F32)
             for a in range(3):
-                at = (a * 9 + k) * o_own
-                win = padded[:, base + a * width : base + a * width + lanes]
-                term = term + jnp.dot(weight[at : at + o_own, :], win, preferred_element_type=F32)
+                left = pl.ds((a * 9 + k) * o_own, o_own)
+                for rows, columns in chunks:
+                    win = padded[rows, base + a * width : base + a * width + lanes]
+                    term = term + jnp.dot(weight[left, columns], win, preferred_element_type=F32)
             turn = -(b * BW + e) % width
             for p in range(planes):
                 block = term[:, p * width : (p + 1) * width]
                 if turn:
                     block = jnp.where(masks[k], pltpu.roll(block, turn, 1), 0.0)
                 pre[p] = pre[p] + block
-        for p in range(planes):
-            pre_out[:, base + p * width : base + (p + 1) * width] = pre[p]
-
-
-def bott_call(weight, ins, planes):
+        for i, block in zip(at, pre):
+            pre_out[:, i : i + width] = block
+
+
+def lay(padded, row, piece, planes):
+    slabs, cb, lanes = piece.shape
+    width = lanes // planes
+    place = lax.axis_index("space")
+    rows = pl.ds(pl.multiple_of(row, cb), cb)
+    padded[rows, :width] = jnp.zeros((cb, width), BF16)
+    padded[rows, slabs * lanes + width :] = jnp.zeros((cb, width), BF16)
+    for r in range(slabs):
+        slab = lax.rem(place - r + slabs, slabs)
+        padded[rows, pl.ds(pl.multiple_of(slab * lanes + width, width), lanes)] = piece[r]
+
+
+def chip_body(planes, weight, after, mine, mate, pre_out, padded):
+    slabs, cb, lanes = mine.shape
+    chan = lax.axis_index("chan")
+    lay(padded, (chan & 1) * cb, mine, planes)
+    lay(padded, ((chan & 1) ^ 1) * cb, mate, planes)
+    columns = pl.ds(pl.multiple_of((chan >> 1) * 2 * cb, 2 * cb), 2 * cb)
+    convolve(weight, padded, [(pl.ds(0, 2 * cb), columns)], None, pre_out, slabs, planes)
+
+
+def chip_call(weight, after, mine, mate, planes):
+    slabs, cb, lanes = mine.shape
+    return call(
+        functools.partial(chip_body, planes),
+        [jax.ShapeDtypeStruct((weight.shape[0] // 27, slabs * lanes), F32)],
+        [VM] * 4,
+        [pltpu.VMEM((2 * cb, (slabs + 1) * lanes), BF16)],
+        2.5e9,
+        1 << 20,
+        16,
+    )(weight, after, mine, mate)[0]
+
+
+def bott_body(planes, weight, before, *refs):
+    ins, (pre_out, padded) = refs[:-2], refs[-2:]
     slabs, cb, lanes = ins[0].shape
-    pieces = len(ins)
-    o_own = weight.shape[0] // 27
+    chan = lax.axis_index("chan")
+    for j, piece in enumerate(ins):
+        lay(padded, (chan ^ j) * cb, piece, planes)
+    chunks = []
+    for other in range(1, len(ins) // 2):
+        at = pl.ds(pl.multiple_of(((chan >> 1) ^ other) * 2 * cb, 2 * cb), 2 * cb)
+        chunks.append((at, at))
+    convolve(weight, padded, chunks, before, pre_out, slabs, planes)
+
+
+def bott_call(weight, before, ins, planes):
+    slabs, cb, lanes = ins[0].shape
     S = jax.ShapeDtypeStruct
     return call(
-        functools.partial(bott_body, pieces, planes),
-        [S((o_own, slabs * lanes), F32), S((pieces * cb, (slabs + 1) * lanes), BF16)],
-        [VM] * (1 + pieces),
+        functools.partial(bott_body, planes),
+        [S(before.shape, F32), S((len(ins) * cb, (slabs + 1) * lanes), BF16)],
+        [VM] * (2 + len(ins)),
         [],
-        5e9,
+        2.5e9,
         1 << 20,
         16,
-    )(weight, *ins)
+    )(weight, before, *ins)
 
 
 def back_body(slabs, planes, weight, pre, part, *refs):
@@ -584,17 +620,11 @@
         scale, known, below, above, left, right, lookup, kernel, fine_cot, cot, mate
     )
     cots = [cot] + [hop(message, "space", r) for r in range(1, spaces)]
-    pieces = {0: slabs}
-    bits = [1 << i for i in range(chans.bit_length() - 1)]
-    for bit in bits[1:] + bits[:1]:
-        for j, x in list(pieces.items()):
-            if bit == 1 and j:
-                x, part = lax.optimization_barrier((x, part))
-            pieces[j ^ bit] = swap(x, "chan", bit) if j ^ bit > 1 else mate
-    ins = [pieces[j] for j in range(chans)]
+    ins = [slabs, mate] + [swap(slabs, "chan", j) for j in range(2, chans)]
 
     weight = bott_weight.transpose(1, 0, 2).reshape(27 * o_own, cb * chans)
-    pre, full = bott_call(weight, ins, planes)
+    pre = chip_call(weight, part, slabs, mate, planes)
+    pre, full = bott_call(weight, pre, ins, planes)
     bott_out, delta, share, mine, part = back_call(weight, pre, part, cots, chans, planes)
     others = [hop(share[r], "chan", r) for r in range(1, chans)]
     bott_wgrad = wgrad_call((planes * spaces * width) ** -0.5, delta, full).transpose(1, 0, 2)

time: 45.2 us -> 43.7 us (0.967)
  waiting for transfers between devices: 5.63 us -> 3.71 us
  starting transfers between devices: 17 us -> 18.5 us
  Pallas kernels: 21.1 us -> 20.1 us
    ppermute x11, waiting for transfers between devices: 5.62 us -> 3.68 us  [hop(): lax.ppermute(x, axis, [(i, (i + offset) % count) for i in range(count)])]
    pallas_call x1, Pallas kernels: 5.89 us -> 4.44 us  [fine_call(): call(functools.partial(fine_body, scale), [S((ch, depth, rows, cols), BF1...]
    ppermute x3, starting transfers between devices: 2.79 us -> 3.97 us  [swap(): return lax.ppermute(x, axis, [(i, i ^ bit) for i in range(count)])]
    pallas_call x1 -> x2, Pallas kernels: 4.08 us -> 4.53 us  [the longest x1 2.32 us: bott_call(): call(functools.partial(bott_body, planes), [S(before.shape, F32), S((len(...]
  transfers between devices with their start and end apart: 14 -> 14, of which waited for: 4 -> 3; matrix products, arithmetic and copies ran while one was open for 1% -> 1% of each run, Pallas kernels for 38% -> 37%
where the time goes in v6:
time: 43.7 us; the launch traced here: 43.5 us
  Pallas kernels  20.1 us (46%)
  starting transfers between devices  18.5 us (42%)
  waiting for transfers between devices  3.71 us (8%)
  between operations  0.8 us (2%)
  local copies, waits for them, and re-layouts  0.5 us (1%)
    ppermute x11, starting transfers between devices, hop(): lax.ppermute(x, axis, [(i, (i + offset) % count) for i in range(count)])  14.5 us
    pallas_call x1, Pallas kernels, wgrad_call(): call(functools.partial(wgrad_body, scale), [jax.ShapeDtypeStruct((27, o_o...  5.09 us
    pallas_call x1, Pallas kernels, fine_call(): call(functools.partial(fine_body, scale), [S((ch, depth, rows, cols), BF1...  4.44 us
    ppermute x3, starting transfers between devices, swap(): return lax.ppermute(x, axis, [(i, i ^ bit) for i in range(count)])  3.97 us
    ppermute x11, waiting for transfers between devices, hop(): lax.ppermute(x, axis, [(i, (i + offset) % count) for i in range(count)])  3.68 us
    pallas_call x1, Pallas kernels, bott_call(): call(functools.partial(bott_body, planes), [S(before.shape, F32), S((len(...  2.32 us
    pallas_call x1, Pallas kernels, chip_call(): call(functools.partial(chip_body, planes), [jax.ShapeDtypeStruct((weight....  2.21 us
    pallas_call x1, Pallas kernels, prep_call(): call(prep_body, [jax.ShapeDtypeStruct((3 * ch * rows, 3 * (rows + 2) * ch...  1.98 us
  transfers between devices with their start and end apart: 14, of which 3 were waited for; matrix products, arithmetic and copies ran while one was open for 1% of the time, Pallas kernels for 37%

profile of v6, /device:TPU:1, one launch (start us, length us, event | category | flops | bytes accessed | tf_op | source)
XLA Modules:
  0.0 43.5 jit_solution(7926162846555350303)
XLA Ops:
  0.6 0.0 copy-start.2
  0.6 1.3 %shard_map.110 = (bf16[128,256]{1,0:T(8,128)(2,1)S(1)}, bf16[160,256]{1,0:T(8,128)(2,1)S(1)}, bf16[160,256]{1,0:T(8,128)(2,1)S(1)}, bf16[128,256]{1,0:T(8,128)(2...) custom-call(s32[4,8,512]{2,1,0:T(8,128)} %labels.1, bf16[256,128]{1,0:T(8,128)(2,1)} %bitcast.23, ...), custom_call_target="tpu_custom_call" | custom-call | flops 1000000000 | bytes 262144 | tf_op jit(solution)/shard_map/pallas_call | solution.py:106
  1.9 3.2 %collective-permute-start.1 = (bf16[128,256]{1,0:T(8,128)(2,1)S(1)}, bf16[128,256]{1,0:T(8,128)(2,1)S(1)}, u32[]{:S(2)}, u32[]{:S(2)}) collective-permute-start(bf16[128,256]{1,0:T(8,128)(2,1)S(1)} %get-tuple-element.34.refs_1_), channel_id=1, source_target_pairs={{0,8},{4,12},{8,0},{12,4},{1,9},{5,13},{9,1},{13,5},{2,10},{6,14},... | collective-permute-start | bytes 196616 | tf_op jit(solution)/shard_map/ppermute | solution.py:592
  5.1 1.3 %collective-permute-start = (bf16[160,256]{1,0:T(8,128)(2,1)S(1)}, bf16[160,256]{1,0:T(8,128)(2,1)S(1)}, u32[]{:S(2)}, u32[]{:S(2)}) collective-permute-start(bf16[160,256]{1,0:T(8,128)(2,1)S(1)} %get-tuple-element.35), channel_id=1, source_target_pairs={{0,4},{4,8},{8,12},{12,0},{1,5},{5,9},{9,13},{13,1},{2,6},{6,10},{... | collective-permute-start | bytes 245768 | tf_op jit(solution)/shard_map/ppermute | solution.py:592
  6.4 2.0 %collective-permute-start.2 = (bf16[160,256]{1,0:T(8,128)(2,1)S(1)}, bf16[160,256]{1,0:T(8,128)(2,1)S(1)}, u32[]{:S(2)}, u32[]{:S(2)}) collective-permute-start(bf16[160,256]{1,0:T(8,128)(2,1)S(1)} %get-tuple-element.36), channel_id=1, source_target_pairs={{0,12},{4,0},{8,4},{12,8},{1,13},{5,1},{9,5},{13,9},{2,14},{6,2},{... | collective-permute-start | bytes 245768 | tf_op jit(solution)/shard_map/ppermute | solution.py:592
  8.4 0.0 copy-done.2
  8.4 0.2 copy.13
  8.6 0.2 copy.14
  8.7 0.1 reshape.32.taps
  8.9 0.0 copy-start.1
  8.9 2.0 %shard_map.111 = (bf16[384,480]{1,0:T(8,128)(2,1)S(1)}, bf16[128,128]{1,0:T(8,128)(2,1)S(1)}, bf16[512,512]{1,0:T(8,128)(2,1)S(1)}) custom-call(bf16[3,48,48]{2,1,0:T(8,128)(2,1)S(1)} %reshape.32.taps, bf16[16,1024]{1,0:T(8,128)(2,1)S(1)} %get-tuple-element.31.table, s32[4,8,512]{2,1,0:T(8,128)S(1)} %get-tuple-element.32.ids.refs_0_), custom_call_target="tpu_custom_call" | custom-call | flops 2500000000 | bytes 262144 | tf_op jit(solution)/shard_map/pallas_call | solution.py:179
  10.9 0.0 collective-permute-done.1.refs_3_
  10.9 0.0 collective-permute-done.refs_2_
  10.9 0.1 collective-permute-done.2.refs_4_
  11.0 2.2 %collective-permute-start.5 = (bf16[4,128,256]{2,1,0:T(8,128)(2,1)S(1)}, bf16[4,128,256]{2,1,0:T(8,128)(2,1)S(1)}, u32[]{:S(2)}, u32[]{:S(2)}) collective-permute-start(bf16[4,128,256]{2,1,0:T(8,128)(2,1)S(1)} %get-tuple-element.44.mine.refs_0_), channel_id=1, source_target_pairs={{0,1},{1,0},{2,3},{3,2},{4,5},{5,4},{6,7},{7,6},{8,9},{9,8},{10,11... | collective-permute-start | bytes 786440 | tf_op jit(solution)/shard_map/ppermute | solution.py:597
  13.2 1.4 %collective-permute-start.3 = (s32[6,512]{1,0:T(8,128)S(1)}, s32[6,512]{1,0:T(8,128)S(1)}, u32[]{:S(2)}, u32[]{:S(2)}) collective-permute-start(s32[6,512]{1,0:T(8,128)S(1)} %get-tuple-element.40), channel_id=1, source_target_pairs={{0,1},{1,2},{2,3},{3,0},{4,5},{5,6},{6,7},{7,4},{8,9},{9,10},{10,1... | collective-permute-start | bytes 36872 | tf_op jit(solution)/shard_map/ppermute | solution.py:592
  14.6 0.0 collective-permute-start.4
  14.6 1.7 %collective-permute-start.7 = (bf16[4,128,256]{2,1,0:T(8,128)(2,1)S(1)}, bf16[4,128,256]{2,1,0:T(8,128)(2,1)S(1)}, u32[]{:S(2)}, u32[]{:S(2)}) collective-permute-start(bf16[4,128,256]{2,1,0:T(8,128)(2,1)S(1)} %get-tuple-element.44.mine.refs_0_), channel_id=1, source_target_pairs={{0,3},{1,2},{2,1},{3,0},{4,7},{5,6},{6,5},{7,4},{8,11},{9,10},{10,... | collective-permute-start | bytes 786440 | tf_op jit(solution)/shard_map/ppermute | solution.py:597
  16.3 0.1 collective-permute-start.6
  16.4 0.0 collective-permute-done.3.left
  16.4 1.8 %collective-permute-done.4.right = s32[6,512]{1,0:T(8,128)S(1)} collective-permute-done((s32[6,512]{1,0:T(8,128)S(1)}, s32[6,512]{1,0:T(8,128)S(1)}, u32[]{:S(2)}, u32[]{:S(2)}) %collective-permute-start.4) | collective-permute-done | bytes 12320 | tf_op jit(solution)/shard_map/ppermute | solution.py:592
  18.2 0.0 collective-permute-done.5.after.mate.refs_1_
  18.2 0.0 copy-done.1
  18.2 0.0 copy-start
  18.2 4.4 %shard_map.113 = (bf16[16,4,8,512]{3,2,1,0:T(8,128)(2,1)}, f32[16,512]{1,0:T(8,128)S(1)}, bf16[160,256]{1,0:T(8,128)(2,1)S(1)}) custom-call(bf16[512,512]{1,0:T(8,128)(2,1)S(1)} %get-tuple-element.33.known, s32[8,512]{1,0:T(8,128)S(1)} %get-tuple-element.38.below, s32[8,512]{1,0:T(8,128)S(1)} %get-tuple-element.39.above, ...), custom_call_target="tpu_custom_call" | custom-call | flops 6000000000 | bytes 4194304 | tf_op jit(solution)/shard_map/pallas_call | solution.py:296
  22.7 2.7 %collective-permute-start.10 = (bf16[160,256]{1,0:T(8,128)(2,1)S(1)}, bf16[160,256]{1,0:T(8,128)(2,1)S(1)}, u32[]{:S(2)}, u32[]{:S(2)}) collective-permute-start(bf16[160,256]{1,0:T(8,128)(2,1)S(1)} %get-tuple-element.48), channel_id=1, source_target_pairs={{0,12},{4,0},{8,4},{12,8},{1,13},{5,1},{9,5},{13,9},{2,14},{6,2},{... | collective-permute-start | bytes 245768 | tf_op jit(solution)/shard_map/ppermute | solution.py:592
  25.3 0.0 collective-permute-start.9
  25.3 1.0 %collective-permute-start.8 = (bf16[160,256]{1,0:T(8,128)(2,1)S(1)}, bf16[160,256]{1,0:T(8,128)(2,1)S(1)}, u32[]{:S(2)}, u32[]{:S(2)}) collective-permute-start(bf16[160,256]{1,0:T(8,128)(2,1)S(1)} %get-tuple-element.48), channel_id=1, source_target_pairs={{0,4},{4,8},{8,12},{12,0},{1,5},{5,9},{9,13},{13,1},{2,6},{6,10},{... | collective-permute-start | bytes 245768 | tf_op jit(solution)/shard_map/ppermute | solution.py:592
  26.3 0.0 copy-done
  26.3 2.2 %shard_map.114.before = f32[128,1024]{1,0:T(8,128)S(1)} custom-call(bf16[3456,512]{1,0:T(8,128)(2,1)S(1)} %bitcast.19, f32[16,512]{1,0:T(8,128)S(1)} %get-tuple-element.46.after.part, bf16[4,128,256]{2,1,0:T(8,128)(2,1)S(1)} %get-tuple-element.44.mine.refs_0_, bf16[4,128,256]{2,1,0:T(8,128)(2,1)S(1)} %collective-permute-done.5.after.mate.refs_1_), custom_call_target="tpu_custom_call" | custom-call | flops 2500000000 | bytes 1048576 | tf_op jit(solution)/shard_map/pallas_call | solution.py:378
  28.6 0.0 collective-permute-done.7.refs_3_
  28.6 0.0 collective-permute-done.6.refs_2_
  28.6 2.3 %shard_map.115 = (f32[128,1024]{1,0:T(8,128)S(1)}, bf16[512,1280]{1,0:T(8,128)(2,1)S(1)}) custom-call(bf16[3456,512]{1,0:T(8,128)(2,1)S(1)} %bitcast.20, f32[128,1024]{1,0:T(8,128)S(1)} %shard_map.114.before, bf16[4,128,256]{2,1,0:T(8,128)(2,1)S(1)} %get-tuple-element.44.mine.refs_0_, bf16[4,128,256]{2,1,0:T(8,128)(2,1)S(1)} %collective-permute-done.5.after.mate.refs_1_, ...), custom_call_target="tpu_custom_call" | custom-call | flops 2500000000 | bytes 1048576 | tf_op jit(solution)/shard_map/pallas_call | solution.py:405
  30.9 0.0 collective-permute-done.10.refs_3_
  30.9 1.7 %collective-permute-done.9.refs_2_ = bf16[160,256]{1,0:T(8,128)(2,1)S(1)} collective-permute-done((bf16[160,256]{1,0:T(8,128)(2,1)S(1)}, bf16[160,256]{1,0:T(8,128)(2,1)S(1)}, u32[]{:S(2)}, u32[]{:S(2)}) %collective-permute-start.9) | collective-permute-done | bytes 81952 | tf_op jit(solution)/shard_map/ppermute | solution.py:592
  32.7 0.0 collective-permute-done.8.refs_1_
  32.7 1.8 %shard_map.116 = (bf16[256,128]{1,0:T(8,128)(2,1)}, f32[128,1280]{1,0:T(8,128)S(1)}, bf16[4,320,128]{2,1,0:T(8,128)(2,1)S(1)}, f32[4,256,128]{2,1,0:T(8,128)S(1)}, f32[16,512]{1,0:T(8,128)S(1)}) custom-call(bf16[3456,512]{1,0:T(8,128)(2,1)S(1)} %bitcast.21, f32[128,1024]{1,0:T(8,128)S(1)} %get-tuple-element.47.pre, ...), custom_call_target="tpu_custom_call" | custom-call | flops 1800000000 | bytes 1048576 | tf_op jit(solution)/shard_map/pallas_call | solution.py:476
  34.5 0.4 collective-permute-start.13
  34.9 1.2 %collective-permute-start.12 = (bf16[320,128]{1,0:T(8,128)(2,1)S(1)}, bf16[320,128]{1,0:T(8,128)(2,1)S(1)}, u32[]{:S(2)}, u32[]{:S(2)}) collective-permute-start(bf16[320,128]{1,0:T(8,128)(2,1)S(1)} %get-tuple-element.58), channel_id=1, source_target_pairs={{0,2},{1,3},{2,0},{3,1},{4,6},{5,7},{6,4},{7,5},{8,10},{9,11},{10,... | collective-permute-start | bytes 245768 | tf_op jit(solution)/shard_map/ppermute | solution.py:592
  36.2 1.3 %collective-permute-start.11 = (bf16[320,128]{1,0:T(8,128)(2,1)S(1)}, bf16[320,128]{1,0:T(8,128)(2,1)S(1)}, u32[]{:S(2)}, u32[]{:S(2)}) collective-permute-start(bf16[320,128]{1,0:T(8,128)(2,1)S(1)} %get-tuple-element.59), channel_id=1, source_target_pairs={{0,1},{1,2},{2,3},{3,0},{4,5},{5,6},{6,7},{7,4},{8,9},{9,10},{10,1... | collective-permute-start | bytes 245768 | tf_op jit(solution)/shard_map/ppermute | solution.py:592
  37.5 5.1 %shard_map.118 = f32[27,128,512]{2,1,0:T(8,128)} custom-call(f32[128,1280]{1,0:T(8,128)S(1)} %get-tuple-element.55.delta, bf16[512,1280]{1,0:T(8,128)(2,1)S(1)} %get-tuple-element.56.full), custom_call_target="tpu_custom_call" | custom-call | flops 6600000000 | bytes 8388608 | tf_op jit(solution)/shard_map/pallas_call | solution.py:544
  42.6 0.0 collective-permute-done.13.refs_2_
  42.6 0.0 collective-permute-done.12.refs_1_
  42.6 0.0 collective-permute-done.11.refs_0_
  42.6 0.9 %shard_map.117 = (bf16[256,128]{1,0:T(8,128)(2,1)}, f32[16,16,27]{2,1,0:T(8,128)}) custom-call(f32[4,256,128]{2,1,0:T(8,128)S(1)} %get-tuple-element.49.mine, f32[16,512]{1,0:T(8,128)S(1)} %get-tuple-element.50.part, bf16[320,128]{1,0:T(8,128)(2,1)S(1)} %collective-permute-done.11.refs_0_, bf16[320,128]{1,0:T(8,128)(2,1)S(1)} %collective-permute-done.12.refs_1_, ...), custom_call_target="tpu_custom_call" | custom-call | flops 1000000000 | bytes 262144 | tf_op jit(solution)/shard_map/pallas_call | solution.py:576
  (2 shorter events, 0.1 us)
Async XLA Ops:
  0.6 7.8 %copy-start.2 = (bf16[27,16,16]{0,2,1:T(8,128)(2,1)S(1)}, bf16[27,16,16]{0,2,1:T(8,128)(2,1)}, u32[]{:S(2)}) copy-start(bf16[27,16,16]{0,2,1:T(8,128)(2,1)} %param.9) | copy-start | bytes 41476
  1.9 9.0 %collective-permute-start.1 = (bf16[128,256]{1,0:T(8,128)(2,1)S(1)}, bf16[128,256]{1,0:T(8,128)(2,1)S(1)}, u32[]{:S(2)}, u32[]{:S(2)}) collective-permute-start(bf16[128,256]{1,0:T(8,128)(2,1)S(1)} %get-tuple-element.34.refs_1_), channel_id=1, source_target_pairs={{0,8},{4,12},{8,0},{12,4},{1,9},{5,13},{9,1},{13,5},{2,10},{6,14},... | collective-permute-start | bytes 196616 | tf_op jit(solution)/shard_map/ppermute | solution.py:592
  5.1 5.8 %collective-permute-start = (bf16[160,256]{1,0:T(8,128)(2,1)S(1)}, bf16[160,256]{1,0:T(8,128)(2,1)S(1)}, u32[]{:S(2)}, u32[]{:S(2)}) collective-permute-start(bf16[160,256]{1,0:T(8,128)(2,1)S(1)} %get-tuple-element.35), channel_id=1, source_target_pairs={{0,4},{4,8},{8,12},{12,0},{1,5},{5,9},{9,13},{13,1},{2,6},{6,10},{... | collective-permute-start | bytes 245768 | tf_op jit(solution)/shard_map/ppermute | solution.py:592
  6.4 4.6 %collective-permute-start.2 = (bf16[160,256]{1,0:T(8,128)(2,1)S(1)}, bf16[160,256]{1,0:T(8,128)(2,1)S(1)}, u32[]{:S(2)}, u32[]{:S(2)}) collective-permute-start(bf16[160,256]{1,0:T(8,128)(2,1)S(1)} %get-tuple-element.36), channel_id=1, source_target_pairs={{0,12},{4,0},{8,4},{12,8},{1,13},{5,1},{9,5},{13,9},{2,14},{6,2},{... | collective-permute-start | bytes 245768 | tf_op jit(solution)/shard_map/ppermute | solution.py:592
  8.9 9.3 %copy-start.1 = (bf16[16,4,8,512]{3,2,1,0:T(8,128)(2,1)S(1)}, bf16[16,4,8,512]{3,2,1,0:T(8,128)(2,1)}, u32[]{:S(2)}) copy-start(bf16[16,4,8,512]{3,2,1,0:T(8,128)(2,1)} %cot.1) | copy-start | bytes 1572868
  11.0 7.2 %collective-permute-start.5 = (bf16[4,128,256]{2,1,0:T(8,128)(2,1)S(1)}, bf16[4,128,256]{2,1,0:T(8,128)(2,1)S(1)}, u32[]{:S(2)}, u32[]{:S(2)}) collective-permute-start(bf16[4,128,256]{2,1,0:T(8,128)(2,1)S(1)} %get-tuple-element.44.mine.refs_0_), channel_id=1, source_target_pairs={{0,1},{1,0},{2,3},{3,2},{4,5},{5,4},{6,7},{7,6},{8,9},{9,8},{10,11... | collective-permute-start | bytes 786440 | tf_op jit(solution)/shard_map/ppermute | solution.py:597
  13.2 3.2 %collective-permute-start.3 = (s32[6,512]{1,0:T(8,128)S(1)}, s32[6,512]{1,0:T(8,128)S(1)}, u32[]{:S(2)}, u32[]{:S(2)}) collective-permute-start(s32[6,512]{1,0:T(8,128)S(1)} %get-tuple-element.40), channel_id=1, source_target_pairs={{0,1},{1,2},{2,3},{3,0},{4,5},{5,6},{6,7},{7,4},{8,9},{9,10},{10,1... | collective-permute-start | bytes 36872 | tf_op jit(solution)/shard_map/ppermute | solution.py:592
  14.6 3.6 %collective-permute-start.4 = (s32[6,512]{1,0:T(8,128)S(1)}, s32[6,512]{1,0:T(8,128)S(1)}, u32[]{:S(2)}, u32[]{:S(2)}) collective-permute-start(s32[6,512]{1,0:T(8,128)S(1)} %get-tuple-element.41), channel_id=1, source_target_pairs={{0,3},{1,0},{2,1},{3,2},{4,7},{5,4},{6,5},{7,6},{8,11},{9,8},{10,9... | collective-permute-start | bytes 36872 | tf_op jit(solution)/shard_map/ppermute | solution.py:592
  14.6 14.0 %collective-permute-start.7 = (bf16[4,128,256]{2,1,0:T(8,128)(2,1)S(1)}, bf16[4,128,256]{2,1,0:T(8,128)(2,1)S(1)}, u32[]{:S(2)}, u32[]{:S(2)}) collective-permute-start(bf16[4,128,256]{2,1,0:T(8,128)(2,1)S(1)} %get-tuple-element.44.mine.refs_0_), channel_id=1, source_target_pairs={{0,3},{1,2},{2,1},{3,0},{4,7},{5,6},{6,5},{7,4},{8,11},{9,10},{10,... | collective-permute-start | bytes 786440 | tf_op jit(solution)/shard_map/ppermute | solution.py:597
  16.3 12.3 %collective-permute-start.6 = (bf16[4,128,256]{2,1,0:T(8,128)(2,1)S(1)}, bf16[4,128,256]{2,1,0:T(8,128)(2,1)S(1)}, u32[]{:S(2)}, u32[]{:S(2)}) collective-permute-start(bf16[4,128,256]{2,1,0:T(8,128)(2,1)S(1)} %get-tuple-element.44.mine.refs_0_), channel_id=1, source_target_pairs={{0,2},{1,3},{2,0},{3,1},{4,6},{5,7},{6,4},{7,5},{8,10},{9,11},{10,... | collective-permute-start | bytes 786440 | tf_op jit(solution)/shard_map/ppermute | solution.py:597
  18.2 8.1 %copy-start = (bf16[128,27,512]{2,0,1:T(8,128)(2,1)S(1)}, bf16[128,27,512]{2,0,1:T(8,128)(2,1)}, u32[]{:S(2)}) copy-start(bf16[128,27,512]{2,0,1:T(8,128)(2,1)} %param.12) | copy-start | bytes 10616836
  22.7 8.3 %collective-permute-start.10 = (bf16[160,256]{1,0:T(8,128)(2,1)S(1)}, bf16[160,256]{1,0:T(8,128)(2,1)S(1)}, u32[]{:S(2)}, u32[]{:S(2)}) collective-permute-start(bf16[160,256]{1,0:T(8,128)(2,1)S(1)} %get-tuple-element.48), channel_id=1, source_target_pairs={{0,12},{4,0},{8,4},{12,8},{1,13},{5,1},{9,5},{13,9},{2,14},{6,2},{... | collective-permute-start | bytes 245768 | tf_op jit(solution)/shard_map/ppermute | solution.py:592
  25.3 7.3 %collective-permute-start.9 = (bf16[160,256]{1,0:T(8,128)(2,1)S(1)}, bf16[160,256]{1,0:T(8,128)(2,1)S(1)}, u32[]{:S(2)}, u32[]{:S(2)}) collective-permute-start(bf16[160,256]{1,0:T(8,128)(2,1)S(1)} %get-tuple-element.48), channel_id=1, source_target_pairs={{0,8},{4,12},{8,0},{12,4},{1,9},{5,13},{9,1},{13,5},{2,10},{6,14},... | collective-permute-start | bytes 245768 | tf_op jit(solution)/shard_map/ppermute | solution.py:592
  25.3 7.3 %collective-permute-start.8 = (bf16[160,256]{1,0:T(8,128)(2,1)S(1)}, bf16[160,256]{1,0:T(8,128)(2,1)S(1)}, u32[]{:S(2)}, u32[]{:S(2)}) collective-permute-start(bf16[160,256]{1,0:T(8,128)(2,1)S(1)} %get-tuple-element.48), channel_id=1, source_target_pairs={{0,4},{4,8},{8,12},{12,0},{1,5},{5,9},{9,13},{13,1},{2,6},{6,10},{... | collective-permute-start | bytes 245768 | tf_op jit(solution)/shard_map/ppermute | solution.py:592
  34.5 8.1 %collective-permute-start.13 = (bf16[320,128]{1,0:T(8,128)(2,1)S(1)}, bf16[320,128]{1,0:T(8,128)(2,1)S(1)}, u32[]{:S(2)}, u32[]{:S(2)}) collective-permute-start(bf16[320,128]{1,0:T(8,128)(2,1)S(1)} %get-tuple-element.57), channel_id=1, source_target_pairs={{0,3},{1,0},{2,1},{3,2},{4,7},{5,4},{6,5},{7,6},{8,11},{9,8},{10,9... | collective-permute-start | bytes 245768 | tf_op jit(solution)/shard_map/ppermute | solution.py:592
  34.9 7.7 %collective-permute-start.12 = (bf16[320,128]{1,0:T(8,128)(2,1)S(1)}, bf16[320,128]{1,0:T(8,128)(2,1)S(1)}, u32[]{:S(2)}, u32[]{:S(2)}) collective-permute-start(bf16[320,128]{1,0:T(8,128)(2,1)S(1)} %get-tuple-element.58), channel_id=1, source_target_pairs={{0,2},{1,3},{2,0},{3,1},{4,6},{5,7},{6,4},{7,5},{8,10},{9,11},{10,... | collective-permute-start | bytes 245768 | tf_op jit(solution)/shard_map/ppermute | solution.py:592
  36.2 6.4 %collective-permute-start.11 = (bf16[320,128]{1,0:T(8,128)(2,1)S(1)}, bf16[320,128]{1,0:T(8,128)(2,1)S(1)}, u32[]{:S(2)}, u32[]{:S(2)}) collective-permute-start(bf16[320,128]{1,0:T(8,128)(2,1)S(1)} %get-tuple-element.59), channel_id=1, source_target_pairs={{0,1},{1,2},{2,3},{3,0},{4,5},{5,6},{6,7},{7,4},{8,9},{9,10},{10,1... | collective-permute-start | bytes 245768 | tf_op jit(solution)/shard_map/ppermute | solution.py:592

commit v7 on v6

--- a/solution.py
+++ b/solution.py
@@ -113,7 +113,7 @@
     depth, rows, cols = labels.shape
     slabs[0] = slab[...]
     for r in range(count):
-        slabs[r + 1] = got[r][:cb, :]
+        slabs[r + 1] = got[r][:cb, :] if r in (0, count - 1) else apart(got[r][...], lanes // got[r].shape[1])
     planes = []
     for ref in (got[0], got[count - 1]):
         rest = ref[cb:, :].astype(F32)
@@ -208,7 +208,7 @@
 
 
 def fine_body(scale, known, below, above, left, right, table, kernel, cot, bott_cot, after, *refs):
-    out, part, message, feats, grads, stage, sems, pres, deltas, keeps = refs
+    out, part, message, feats, grads, stage, sems, pres, deltas, keeps, gather, fold, spread = refs
     ch, depth, rows, cols = out.shape
     place, count = lax.axis_index("space"), lax.axis_size("space")
     lane, lanes = lax.axis_index("chan"), lax.axis_size("chan")
@@ -244,6 +244,12 @@
         fill(x)
     for b in range(3):
         keeps[b] = hot(gap == b)
+    gather[...] = hot(iota(gather.shape, 0) == iota(gather.shape, 1) // rows)
+    m, n = iota(fold.shape, 0), iota(fold.shape, 1)
+    fold[...] = hot((m // step == n // ch) & (m % ch == n % ch))
+    m, n = iota(spread.shape, 0), iota(spread.shape, 1)
+    tap = 9 * (m % (3 * ch) // ch) + m // (3 * ch)
+    spread[...] = hot((m % ch == n // TAPS) & (tap == n % TAPS))
     forward(0)
     for x in range(depth):
         if x + 1 < depth:
@@ -262,23 +268,17 @@
         deltas[x % 2, group : 2 * group] = delta.astype(BF16)
         deltas[x % 2, 2 * group :] = jnp.where(first, 0.0, pltpu.roll(delta, 1, 1)).astype(BF16)
     backward(depth - 1)
-    shape = grads.shape
-    gather = hot(iota((3 * ch, shape[0]), 0) == iota((3 * ch, shape[0]), 1) // rows)
-    m, n = iota((shape[1], 3 * ch), 0), iota((shape[1], 3 * ch), 1)
-    fold = hot((m // step == n // ch) & (m % ch == n % ch))
     total = grads[...].astype(BF16)
-    sums = [jnp.dot(gather, total * keeps[b], preferred_element_type=F32) for b in range(3)]
+    sums = [jnp.dot(gather[...], total * keeps[b], preferred_element_type=F32) for b in range(3)]
     tall = jnp.concatenate([piece for b in range(3) for piece in split(sums[b])], axis=0)
-    tall = jnp.dot(tall, fold, preferred_element_type=F32)
-    m, n = iota((3 * ch, ch * TAPS), 0), iota((3 * ch, ch * TAPS), 1)
-    spot = jnp.where(m % ch == n // TAPS, n % TAPS - 9 * (m // ch), -1)
-    result = jnp.zeros((ch, ch * TAPS), F32)
+    tall = jnp.dot(tall, fold[...], preferred_element_type=F32)
+    blocks = []
     for b in range(3):
         block = tall[6 * b * ch : (6 * b + 3) * ch] + tall[(6 * b + 3) * ch : (6 * b + 6) * ch]
-        for e in range(3):
-            both = jnp.concatenate(split(block[e * ch : (e + 1) * ch]), axis=0)
-            moved = jnp.dot(both, hot(spot == 3 * b + e), preferred_element_type=F32)
-            result = result + (moved[:ch] + moved[ch:])
+        blocks += [block[e * ch : (e + 1) * ch] for e in range(3)]
+    both = jnp.concatenate(split(jnp.concatenate(blocks, axis=1)), axis=0)
+    moved = jnp.dot(both, spread[...], preferred_element_type=F32)
+    result = moved[:ch] + moved[ch:]
     result = result * scale
     part[...] = result
     o_own, wide = bott_cot.shape
@@ -309,6 +309,9 @@
             pltpu.VMEM((2, 3 * ch * rows, cols), F32),
             pltpu.VMEM((2, 3 * ch * rows, cols), BF16),
             pltpu.VMEM((3, 3 * ch * rows, 3 * ch * (rows + 2)), BF16),
+            pltpu.VMEM((3 * ch, 3 * ch * rows), BF16),
+            pltpu.VMEM((3 * ch * (rows + 2), 3 * ch), BF16),
+            pltpu.VMEM((27 * ch, ch * TAPS), BF16),
         ],
         6e9,
         4 << 20,
@@ -609,7 +612,7 @@
     slab, first, last, cot, ids, near_table = pack_call(labels, flat_in, flat_cot, table.T, planes)
     taps = fine_weight.reshape(3, 3, 3, ch, ch).transpose(1, 2, 4, 0, 3).reshape(3, 3 * ch, 3 * ch)
     kernel, lookup, known = prep_call(taps, near_table, ids)
-    sends = [last] + [slab] * (spaces - 3) + [first]
+    sends = [last] + [flat_in] * (spaces - 3) + [first]
     got = [hop(x, "space", r + 1) for r, x in enumerate(sends)]
     slabs, below, above, top, bottom = unpack_call(ids, slab, got, kernel)
     left = hop(bottom, "chan", 1)

time: 43.7 us -> 43.2 us (0.989)
  starting transfers between devices: 18.5 us -> 17.9 us
    ppermute x3, waiting for transfers between devices: 0.03 us -> 1.21 us  [swap(): return lax.ppermute(x, axis, [(i, i ^ bit) for i in range(count)])]
    ppermute x11, waiting for transfers between devices: 3.68 us -> 2.77 us  [hop(): lax.ppermute(x, axis, [(i, (i + offset) % count) for i in range(count)])]
    ppermute x11, starting transfers between devices: 14.5 us -> 13.7 us  [hop(): lax.ppermute(x, axis, [(i, (i + offset) % count) for i in range(count)])]
  transfers between devices with their start and end apart: 14 -> 14, of which waited for: 3 -> 3; matrix products, arithmetic and copies ran while one was open for 1% -> 1% of each run, Pallas kernels for 37% -> 39%
where the time goes in v7:
time: 43.2 us; the launch traced here: 43.1 us
  Pallas kernels  19.9 us (46%)
  starting transfers between devices  17.9 us (41%)
  waiting for transfers between devices  3.98 us (9%)
  between operations  0.81 us (2%)
  local copies, waits for them, and re-layouts  0.5 us (1%)
    ppermute x11, starting transfers between devices, hop(): lax.ppermute(x, axis, [(i, (i + offset) % count) for i in range(count)])  13.7 us
    pallas_call x1, Pallas kernels, wgrad_call(): call(functools.partial(wgrad_body, scale), [jax.ShapeDtypeStruct((27, o_o...  5.09 us
    ppermute x3, starting transfers between devices, swap(): return lax.ppermute(x, axis, [(i, i ^ bit) for i in range(count)])  4.19 us
    pallas_call x1, Pallas kernels, fine_call(): call(functools.partial(fine_body, scale), [S((ch, depth, rows, cols), BF1...  4.1 us
    ppermute x11, waiting for transfers between devices, hop(): lax.ppermute(x, axis, [(i, (i + offset) % count) for i in range(count)])  2.77 us
    pallas_call x1, Pallas kernels, bott_call(): call(functools.partial(bott_body, planes), [S(before.shape, F32), S((len(...  2.33 us
    pallas_call x1, Pallas kernels, chip_call(): call(functools.partial(chip_body, planes), [jax.ShapeDtypeStruct((weight....  2.21 us
    pallas_call x1, Pallas kernels, prep_call(): call(prep_body, [jax.ShapeDtypeStruct((3 * ch * rows, 3 * (rows + 2) * ch...  1.98 us
  transfers between devices with their start and end apart: 14, of which 3 were waited for; matrix products, arithmetic and copies ran while one was open for 1% of the time, Pallas kernels for 39%

profile of v7, /device:TPU:1, one launch (start us, length us, event | category | flops | bytes accessed | tf_op | source)
XLA Modules:
  0.0 43.1 jit_solution(8406022610669480194)
XLA Ops:
  0.6 0.0 copy-start.2
  0.6 3.2 %collective-permute-start.1 = (bf16[256,128]{1,0:T(8,128)(2,1)}, bf16[256,128]{1,0:T(8,128)(2,1)S(1)}, u32[]{:S(2)}, u32[]{:S(2)}) collective-permute-start(bf16[256,128]{1,0:T(8,128)(2,1)} %bitcast.24), channel_id=1, source_target_pairs={{0,8},{4,12},{8,0},{12,4},{1,9},{5,13},{9,1},{13,5},{2,10},{6,14},... | collective-permute-start | bytes 196616 | tf_op jit(solution)/shard_map/ppermute | solution.py:595
  3.8 1.3 %shard_map.110 = (bf16[128,256]{1,0:T(8,128)(2,1)S(1)}, bf16[160,256]{1,0:T(8,128)(2,1)S(1)}, bf16[160,256]{1,0:T(8,128)(2,1)S(1)}, bf16[128,256]{1,0:T(8,128)(2...) custom-call(s32[4,8,512]{2,1,0:T(8,128)} %labels.1, bf16[256,128]{1,0:T(8,128)(2,1)} %bitcast.25, ...), custom_call_target="tpu_custom_call" | custom-call | flops 1000000000 | bytes 262144 | tf_op jit(solution)/shard_map/pallas_call | solution.py:106
  5.1 1.3 %collective-permute-start = (bf16[160,256]{1,0:T(8,128)(2,1)S(1)}, bf16[160,256]{1,0:T(8,128)(2,1)S(1)}, u32[]{:S(2)}, u32[]{:S(2)}) collective-permute-start(bf16[160,256]{1,0:T(8,128)(2,1)S(1)} %get-tuple-element.35), channel_id=1, source_target_pairs={{0,4},{4,8},{8,12},{12,0},{1,5},{5,9},{9,13},{13,1},{2,6},{6,10},{... | collective-permute-start | bytes 245768 | tf_op jit(solution)/shard_map/ppermute | solution.py:595
  6.5 2.0 %collective-permute-start.2 = (bf16[160,256]{1,0:T(8,128)(2,1)S(1)}, bf16[160,256]{1,0:T(8,128)(2,1)S(1)}, u32[]{:S(2)}, u32[]{:S(2)}) collective-permute-start(bf16[160,256]{1,0:T(8,128)(2,1)S(1)} %get-tuple-element.36), channel_id=1, source_target_pairs={{0,12},{4,0},{8,4},{12,8},{1,13},{5,1},{9,5},{13,9},{2,14},{6,2},{... | collective-permute-start | bytes 245768 | tf_op jit(solution)/shard_map/ppermute | solution.py:595
  8.4 0.0 copy-done.2
  8.4 0.2 copy.13
  8.6 0.2 copy.14
  8.8 0.1 reshape.32.taps
  8.9 0.0 copy-start.1
  8.9 2.0 %shard_map.111 = (bf16[384,480]{1,0:T(8,128)(2,1)S(1)}, bf16[128,128]{1,0:T(8,128)(2,1)S(1)}, bf16[512,512]{1,0:T(8,128)(2,1)S(1)}) custom-call(bf16[3,48,48]{2,1,0:T(8,128)(2,1)S(1)} %reshape.32.taps, bf16[16,1024]{1,0:T(8,128)(2,1)S(1)} %get-tuple-element.31.table, s32[4,8,512]{2,1,0:T(8,128)S(1)} %get-tuple-element.32.ids.refs_0_), custom_call_target="tpu_custom_call" | custom-call | flops 2500000000 | bytes 262144 | tf_op jit(solution)/shard_map/pallas_call | solution.py:179
  10.9 0.0 collective-permute-done.1.refs_3_
  10.9 0.0 collective-permute-done.refs_2_
  10.9 0.0 collective-permute-done.2.refs_4_
  11.0 0.2 shard_map.112
  11.1 2.2 %collective-permute-start.5 = (bf16[4,128,256]{2,1,0:T(8,128)(2,1)S(1)}, bf16[4,128,256]{2,1,0:T(8,128)(2,1)S(1)}, u32[]{:S(2)}, u32[]{:S(2)}) collective-permute-start(bf16[4,128,256]{2,1,0:T(8,128)(2,1)S(1)} %get-tuple-element.44.mine.refs_0_), channel_id=1, source_target_pairs={{0,1},{1,0},{2,3},{3,2},{4,5},{5,4},{6,7},{7,6},{8,9},{9,8},{10,11... | collective-permute-start | bytes 786440 | tf_op jit(solution)/shard_map/ppermute | solution.py:600
  13.3 1.2 %collective-permute-start.3 = (s32[6,512]{1,0:T(8,128)S(1)}, s32[6,512]{1,0:T(8,128)S(1)}, u32[]{:S(2)}, u32[]{:S(2)}) collective-permute-start(s32[6,512]{1,0:T(8,128)S(1)} %get-tuple-element.40), channel_id=1, source_target_pairs={{0,1},{1,2},{2,3},{3,0},{4,5},{5,6},{6,7},{7,4},{8,9},{9,10},{10,1... | collective-permute-start | bytes 36872 | tf_op jit(solution)/shard_map/ppermute | solution.py:595
  14.5 0.0 collective-permute-start.4
  14.5 1.7 %collective-permute-start.7 = (bf16[4,128,256]{2,1,0:T(8,128)(2,1)S(1)}, bf16[4,128,256]{2,1,0:T(8,128)(2,1)S(1)}, u32[]{:S(2)}, u32[]{:S(2)}) collective-permute-start(bf16[4,128,256]{2,1,0:T(8,128)(2,1)S(1)} %get-tuple-element.44.mine.refs_0_), channel_id=1, source_target_pairs={{0,3},{1,2},{2,1},{3,0},{4,7},{5,6},{6,5},{7,4},{8,11},{9,10},{10,... | collective-permute-start | bytes 786440 | tf_op jit(solution)/shard_map/ppermute | solution.py:600
  16.2 0.3 collective-permute-start.6
  16.5 0.0 collective-permute-done.3.left
  16.5 1.6 %collective-permute-done.4.right = s32[6,512]{1,0:T(8,128)S(1)} collective-permute-done((s32[6,512]{1,0:T(8,128)S(1)}, s32[6,512]{1,0:T(8,128)S(1)}, u32[]{:S(2)}, u32[]{:S(2)}) %collective-permute-start.4) | collective-permute-done | bytes 12320 | tf_op jit(solution)/shard_map/ppermute | solution.py:595
  18.1 0.0 collective-permute-done.5.after.mate.refs_1_
  18.1 0.0 copy-done.1
  18.1 0.0 copy-start
  18.1 4.1 %shard_map.113 = (bf16[16,4,8,512]{3,2,1,0:T(8,128)(2,1)}, f32[16,512]{1,0:T(8,128)S(1)}, bf16[160,256]{1,0:T(8,128)(2,1)S(1)}) custom-call(bf16[512,512]{1,0:T(8,128)(2,1)S(1)} %get-tuple-element.33.known, s32[8,512]{1,0:T(8,128)S(1)} %get-tuple-element.38.below, s32[8,512]{1,0:T(8,128)S(1)} %get-tuple-element.39.above, ...), custom_call_target="tpu_custom_call" | custom-call | flops 6000000000 | bytes 4194304 | tf_op jit(solution)/shard_map/pallas_call | solution.py:296
  22.2 2.9 %collective-permute-start.10 = (bf16[160,256]{1,0:T(8,128)(2,1)S(1)}, bf16[160,256]{1,0:T(8,128)(2,1)S(1)}, u32[]{:S(2)}, u32[]{:S(2)}) collective-permute-start(bf16[160,256]{1,0:T(8,128)(2,1)S(1)} %get-tuple-element.48), channel_id=1, source_target_pairs={{0,12},{4,0},{8,4},{12,8},{1,13},{5,1},{9,5},{13,9},{2,14},{6,2},{... | collective-permute-start | bytes 245768 | tf_op jit(solution)/shard_map/ppermute | solution.py:595
  25.1 0.0 collective-permute-start.9
  25.1 0.4 collective-permute-start.8
  25.5 0.0 copy-done
  25.5 2.2 %shard_map.114.before = f32[128,1024]{1,0:T(8,128)S(1)} custom-call(bf16[3456,512]{1,0:T(8,128)(2,1)S(1)} %bitcast.19, f32[16,512]{1,0:T(8,128)S(1)} %get-tuple-element.46.after.part, bf16[4,128,256]{2,1,0:T(8,128)(2,1)S(1)} %get-tuple-element.44.mine.refs_0_, bf16[4,128,256]{2,1,0:T(8,128)(2,1)S(1)} %collective-permute-done.5.after.mate.refs_1_), custom_call_target="tpu_custom_call" | custom-call | flops 2500000000 | bytes 1048576 | tf_op jit(solution)/shard_map/pallas_call | solution.py:381
  27.7 0.0 collective-permute-done.7.refs_3_
  27.7 1.2 %collective-permute-done.6.refs_2_ = bf16[4,128,256]{2,1,0:T(8,128)(2,1)S(1)} collective-permute-done((bf16[4,128,256]{2,1,0:T(8,128)(2,1)S(1)}, bf16[4,128,256]{2,1,0:T(8,128)(2,1)S(1)}, u32[]{:S(2)}, u32[]{:S(2)}) %collective-permute-start.6) | collective-permute-done | bytes 262176 | tf_op jit(solution)/shard_map/ppermute | solution.py:600
  28.9 2.3 %shard_map.115 = (f32[128,1024]{1,0:T(8,128)S(1)}, bf16[512,1280]{1,0:T(8,128)(2,1)S(1)}) custom-call(bf16[3456,512]{1,0:T(8,128)(2,1)S(1)} %bitcast.20, f32[128,1024]{1,0:T(8,128)S(1)} %shard_map.114.before, bf16[4,128,256]{2,1,0:T(8,128)(2,1)S(1)} %get-tuple-element.44.mine.refs_0_, bf16[4,128,256]{2,1,0:T(8,128)(2,1)S(1)} %collective-permute-done.5.after.mate.refs_1_, ...), custom_call_target="tpu_custom_call" | custom-call | flops 2500000000 | bytes 1048576 | tf_op jit(solution)/shard_map/pallas_call | solution.py:408
  31.3 0.0 collective-permute-done.10.refs_3_
  31.3 1.1 %collective-permute-done.9.refs_2_ = bf16[160,256]{1,0:T(8,128)(2,1)S(1)} collective-permute-done((bf16[160,256]{1,0:T(8,128)(2,1)S(1)}, bf16[160,256]{1,0:T(8,128)(2,1)S(1)}, u32[]{:S(2)}, u32[]{:S(2)}) %collective-permute-start.9) | collective-permute-done | bytes 81952 | tf_op jit(solution)/shard_map/ppermute | solution.py:595
  32.4 0.0 collective-permute-done.8.refs_1_
  32.4 1.8 %shard_map.116 = (bf16[256,128]{1,0:T(8,128)(2,1)}, f32[128,1280]{1,0:T(8,128)S(1)}, bf16[4,320,128]{2,1,0:T(8,128)(2,1)S(1)}, f32[4,256,128]{2,1,0:T(8,128)S(1)}, f32[16,512]{1,0:T(8,128)S(1)}) custom-call(bf16[3456,512]{1,0:T(8,128)(2,1)S(1)} %bitcast.21, f32[128,1024]{1,0:T(8,128)S(1)} %get-tuple-element.47.pre, ...), custom_call_target="tpu_custom_call" | custom-call | flops 1800000000 | bytes 1048576 | tf_op jit(solution)/shard_map/pallas_call | solution.py:479
  34.3 0.4 %collective-permute-start.13 = (bf16[320,128]{1,0:T(8,128)(2,1)S(1)}, bf16[320,128]{1,0:T(8,128)(2,1)S(1)}, u32[]{:S(2)}, u32[]{:S(2)}) collective-permute-start(bf16[320,128]{1,0:T(8,128)(2,1)S(1)} %get-tuple-element.57), channel_id=1, source_target_pairs={{0,3},{1,0},{2,1},{3,2},{4,7},{5,4},{6,5},{7,6},{8,11},{9,8},{10,9... | collective-permute-start | bytes 245768 | tf_op jit(solution)/shard_map/ppermute | solution.py:595
  34.7 0.8 %collective-permute-start.12 = (bf16[320,128]{1,0:T(8,128)(2,1)S(1)}, bf16[320,128]{1,0:T(8,128)(2,1)S(1)}, u32[]{:S(2)}, u32[]{:S(2)}) collective-permute-start(bf16[320,128]{1,0:T(8,128)(2,1)S(1)} %get-tuple-element.58), channel_id=1, source_target_pairs={{0,2},{1,3},{2,0},{3,1},{4,6},{5,7},{6,4},{7,5},{8,10},{9,11},{10,... | collective-permute-start | bytes 245768 | tf_op jit(solution)/shard_map/ppermute | solution.py:595
  35.5 1.6 %collective-permute-start.11 = (bf16[320,128]{1,0:T(8,128)(2,1)S(1)}, bf16[320,128]{1,0:T(8,128)(2,1)S(1)}, u32[]{:S(2)}, u32[]{:S(2)}) collective-permute-start(bf16[320,128]{1,0:T(8,128)(2,1)S(1)} %get-tuple-element.59), channel_id=1, source_target_pairs={{0,1},{1,2},{2,3},{3,0},{4,5},{5,6},{6,7},{7,4},{8,9},{9,10},{10,1... | collective-permute-start | bytes 245768 | tf_op jit(solution)/shard_map/ppermute | solution.py:595
  37.0 5.1 %shard_map.118 = f32[27,128,512]{2,1,0:T(8,128)} custom-call(f32[128,1280]{1,0:T(8,128)S(1)} %get-tuple-element.55.delta, bf16[512,1280]{1,0:T(8,128)(2,1)S(1)} %get-tuple-element.56.full), custom_call_target="tpu_custom_call" | custom-call | flops 6600000000 | bytes 8388608 | tf_op jit(solution)/shard_map/pallas_call | solution.py:547
  42.1 0.0 collective-permute-done.13.refs_2_
  42.2 0.0 collective-permute-done.12.refs_1_
  42.2 0.0 collective-permute-done.11.refs_0_
  42.2 0.9 %shard_map.117 = (bf16[256,128]{1,0:T(8,128)(2,1)}, f32[16,16,27]{2,1,0:T(8,128)}) custom-call(f32[4,256,128]{2,1,0:T(8,128)S(1)} %get-tuple-element.49.mine, f32[16,512]{1,0:T(8,128)S(1)} %get-tuple-element.50.part, bf16[320,128]{1,0:T(8,128)(2,1)S(1)} %collective-permute-done.11.refs_0_, bf16[320,128]{1,0:T(8,128)(2,1)S(1)} %collective-permute-done.12.refs_1_, ...), custom_call_target="tpu_custom_call" | custom-call | flops 1000000000 | bytes 262144 | tf_op jit(solution)/shard_map/pallas_call | solution.py:579
  (1 shorter events, 0.0 us)
Async XLA Ops:
  0.6 7.8 %copy-start.2 = (bf16[27,16,16]{0,2,1:T(8,128)(2,1)S(1)}, bf16[27,16,16]{0,2,1:T(8,128)(2,1)}, u32[]{:S(2)}) copy-start(bf16[27,16,16]{0,2,1:T(8,128)(2,1)} %param.9) | copy-start | bytes 41476
  0.6 10.3 %collective-permute-start.1 = (bf16[256,128]{1,0:T(8,128)(2,1)}, bf16[256,128]{1,0:T(8,128)(2,1)S(1)}, u32[]{:S(2)}, u32[]{:S(2)}) collective-permute-start(bf16[256,128]{1,0:T(8,128)(2,1)} %bitcast.24), channel_id=1, source_target_pairs={{0,8},{4,12},{8,0},{12,4},{1,9},{5,13},{9,1},{13,5},{2,10},{6,14},... | collective-permute-start | bytes 196616 | tf_op jit(solution)/shard_map/ppermute | solution.py:595
  5.1 5.8 %collective-permute-start = (bf16[160,256]{1,0:T(8,128)(2,1)S(1)}, bf16[160,256]{1,0:T(8,128)(2,1)S(1)}, u32[]{:S(2)}, u32[]{:S(2)}) collective-permute-start(bf16[160,256]{1,0:T(8,128)(2,1)S(1)} %get-tuple-element.35), channel_id=1, source_target_pairs={{0,4},{4,8},{8,12},{12,0},{1,5},{5,9},{9,13},{13,1},{2,6},{6,10},{... | collective-permute-start | bytes 245768 | tf_op jit(solution)/shard_map/ppermute | solution.py:595
  6.5 4.5 %collective-permute-start.2 = (bf16[160,256]{1,0:T(8,128)(2,1)S(1)}, bf16[160,256]{1,0:T(8,128)(2,1)S(1)}, u32[]{:S(2)}, u32[]{:S(2)}) collective-permute-start(bf16[160,256]{1,0:T(8,128)(2,1)S(1)} %get-tuple-element.36), channel_id=1, source_target_pairs={{0,12},{4,0},{8,4},{12,8},{1,13},{5,1},{9,5},{13,9},{2,14},{6,2},{... | collective-permute-start | bytes 245768 | tf_op jit(solution)/shard_map/ppermute | solution.py:595
  8.9 9.2 %copy-start.1 = (bf16[16,4,8,512]{3,2,1,0:T(8,128)(2,1)S(1)}, bf16[16,4,8,512]{3,2,1,0:T(8,128)(2,1)}, u32[]{:S(2)}) copy-start(bf16[16,4,8,512]{3,2,1,0:T(8,128)(2,1)} %cot.1) | copy-start | bytes 1572868
  11.1 7.0 %collective-permute-start.5 = (bf16[4,128,256]{2,1,0:T(8,128)(2,1)S(1)}, bf16[4,128,256]{2,1,0:T(8,128)(2,1)S(1)}, u32[]{:S(2)}, u32[]{:S(2)}) collective-permute-start(bf16[4,128,256]{2,1,0:T(8,128)(2,1)S(1)} %get-tuple-element.44.mine.refs_0_), channel_id=1, source_target_pairs={{0,1},{1,0},{2,3},{3,2},{4,5},{5,4},{6,7},{7,6},{8,9},{9,8},{10,11... | collective-permute-start | bytes 786440 | tf_op jit(solution)/shard_map/ppermute | solution.py:600
  13.3 3.2 %collective-permute-start.3 = (s32[6,512]{1,0:T(8,128)S(1)}, s32[6,512]{1,0:T(8,128)S(1)}, u32[]{:S(2)}, u32[]{:S(2)}) collective-permute-start(s32[6,512]{1,0:T(8,128)S(1)} %get-tuple-element.40), channel_id=1, source_target_pairs={{0,1},{1,2},{2,3},{3,0},{4,5},{5,6},{6,7},{7,4},{8,9},{9,10},{10,1... | collective-permute-start | bytes 36872 | tf_op jit(solution)/shard_map/ppermute | solution.py:595
  14.5 3.6 %collective-permute-start.4 = (s32[6,512]{1,0:T(8,128)S(1)}, s32[6,512]{1,0:T(8,128)S(1)}, u32[]{:S(2)}, u32[]{:S(2)}) collective-permute-start(s32[6,512]{1,0:T(8,128)S(1)} %get-tuple-element.41), channel_id=1, source_target_pairs={{0,3},{1,0},{2,1},{3,2},{4,7},{5,4},{6,5},{7,6},{8,11},{9,8},{10,9... | collective-permute-start | bytes 36872 | tf_op jit(solution)/shard_map/ppermute | solution.py:595
  14.5 13.2 %collective-permute-start.7 = (bf16[4,128,256]{2,1,0:T(8,128)(2,1)S(1)}, bf16[4,128,256]{2,1,0:T(8,128)(2,1)S(1)}, u32[]{:S(2)}, u32[]{:S(2)}) collective-permute-start(bf16[4,128,256]{2,1,0:T(8,128)(2,1)S(1)} %get-tuple-element.44.mine.refs_0_), channel_id=1, source_target_pairs={{0,3},{1,2},{2,1},{3,0},{4,7},{5,6},{6,5},{7,4},{8,11},{9,10},{10,... | collective-permute-start | bytes 786440 | tf_op jit(solution)/shard_map/ppermute | solution.py:600
  16.2 12.7 %collective-permute-start.6 = (bf16[4,128,256]{2,1,0:T(8,128)(2,1)S(1)}, bf16[4,128,256]{2,1,0:T(8,128)(2,1)S(1)}, u32[]{:S(2)}, u32[]{:S(2)}) collective-permute-start(bf16[4,128,256]{2,1,0:T(8,128)(2,1)S(1)} %get-tuple-element.44.mine.refs_0_), channel_id=1, source_target_pairs={{0,2},{1,3},{2,0},{3,1},{4,6},{5,7},{6,4},{7,5},{8,10},{9,11},{10,... | collective-permute-start | bytes 786440 | tf_op jit(solution)/shard_map/ppermute | solution.py:600
  18.1 7.4 %copy-start = (bf16[128,27,512]{2,0,1:T(8,128)(2,1)S(1)}, bf16[128,27,512]{2,0,1:T(8,128)(2,1)}, u32[]{:S(2)}) copy-start(bf16[128,27,512]{2,0,1:T(8,128)(2,1)} %param.12) | copy-start | bytes 10616836
  22.2 9.0 %collective-permute-start.10 = (bf16[160,256]{1,0:T(8,128)(2,1)S(1)}, bf16[160,256]{1,0:T(8,128)(2,1)S(1)}, u32[]{:S(2)}, u32[]{:S(2)}) collective-permute-start(bf16[160,256]{1,0:T(8,128)(2,1)S(1)} %get-tuple-element.48), channel_id=1, source_target_pairs={{0,12},{4,0},{8,4},{12,8},{1,13},{5,1},{9,5},{13,9},{2,14},{6,2},{... | collective-permute-start | bytes 245768 | tf_op jit(solution)/shard_map/ppermute | solution.py:595
  25.1 7.3 %collective-permute-start.9 = (bf16[160,256]{1,0:T(8,128)(2,1)S(1)}, bf16[160,256]{1,0:T(8,128)(2,1)S(1)}, u32[]{:S(2)}, u32[]{:S(2)}) collective-permute-start(bf16[160,256]{1,0:T(8,128)(2,1)S(1)} %get-tuple-element.48), channel_id=1, source_target_pairs={{0,8},{4,12},{8,0},{12,4},{1,9},{5,13},{9,1},{13,5},{2,10},{6,14},... | collective-permute-start | bytes 245768 | tf_op jit(solution)/shard_map/ppermute | solution.py:595
  25.1 7.3 %collective-permute-start.8 = (bf16[160,256]{1,0:T(8,128)(2,1)S(1)}, bf16[160,256]{1,0:T(8,128)(2,1)S(1)}, u32[]{:S(2)}, u32[]{:S(2)}) collective-permute-start(bf16[160,256]{1,0:T(8,128)(2,1)S(1)} %get-tuple-element.48), channel_id=1, source_target_pairs={{0,4},{4,8},{8,12},{12,0},{1,5},{5,9},{9,13},{13,1},{2,6},{6,10},{... | collective-permute-start | bytes 245768 | tf_op jit(solution)/shard_map/ppermute | solution.py:595
  34.3 7.9 %collective-permute-start.13 = (bf16[320,128]{1,0:T(8,128)(2,1)S(1)}, bf16[320,128]{1,0:T(8,128)(2,1)S(1)}, u32[]{:S(2)}, u32[]{:S(2)}) collective-permute-start(bf16[320,128]{1,0:T(8,128)(2,1)S(1)} %get-tuple-element.57), channel_id=1, source_target_pairs={{0,3},{1,0},{2,1},{3,2},{4,7},{5,4},{6,5},{7,6},{8,11},{9,8},{10,9... | collective-permute-start | bytes 245768 | tf_op jit(solution)/shard_map/ppermute | solution.py:595
  34.7 7.5 %collective-permute-start.12 = (bf16[320,128]{1,0:T(8,128)(2,1)S(1)}, bf16[320,128]{1,0:T(8,128)(2,1)S(1)}, u32[]{:S(2)}, u32[]{:S(2)}) collective-permute-start(bf16[320,128]{1,0:T(8,128)(2,1)S(1)} %get-tuple-element.58), channel_id=1, source_target_pairs={{0,2},{1,3},{2,0},{3,1},{4,6},{5,7},{6,4},{7,5},{8,10},{9,11},{10,... | collective-permute-start | bytes 245768 | tf_op jit(solution)/shard_map/ppermute | solution.py:595
  35.5 6.7 %collective-permute-start.11 = (bf16[320,128]{1,0:T(8,128)(2,1)S(1)}, bf16[320,128]{1,0:T(8,128)(2,1)S(1)}, u32[]{:S(2)}, u32[]{:S(2)}) collective-permute-start(bf16[320,128]{1,0:T(8,128)(2,1)S(1)} %get-tuple-element.59), channel_id=1, source_target_pairs={{0,1},{1,2},{2,3},{3,0},{4,5},{5,6},{6,7},{7,4},{8,9},{9,10},{10,1... | collective-permute-start | bytes 245768 | tf_op jit(solution)/shard_map/ppermute | solution.py:595

commit v8 on v7

--- a/solution.py
+++ b/solution.py
@@ -416,10 +416,70 @@
     )(weight, before, *ins)
 
 
-def back_body(slabs, planes, weight, pre, part, *refs):
-    cots, refs = refs[:slabs], refs[slabs:]
-    own_out, deltas, share, mine, part_sum, rows_t, stage, sem = refs
+def spread_rows(rows_t, planes_of):
+    width = rows_t.shape[2] - 2 * BW
+    voxels = planes_of.T
+    w = iota((voxels.shape[0], 1), 0) % BW
+    none = jnp.zeros((BW, voxels.shape[1]), BF16)
+    for e in (-1, 0, 1):
+        moved = voxels
+        if e:
+            moved = jnp.where((w - e >= 0) & (w - e < BW), pltpu.roll(voxels, e % voxels.shape[0], 0), 0.0)
+        moved = moved.astype(BF16)
+        for p in range(voxels.shape[0] // width):
+            rows_t[e + 1, p, :BW, :] = none
+            rows_t[e + 1, p, BW : BW + width, :] = moved[p * width : (p + 1) * width]
+            rows_t[e + 1, p, BW + width :, :] = none
+
+
+def step_rows(rows_t, p, b, e):
+    width = rows_t.shape[2] - 2 * BW
+    return rows_t[e + 1, p, BW - b * BW : BW - b * BW + width, :]
+
+
+def own_body(planes, weight, pre, cot, own_out, back, rows_t, stage, sem):
     send = pltpu.make_async_copy(stage, own_out, sem)
+    o_own, lanes = cot.shape
+    width = lanes // planes
+    at = pl.multiple_of(lax.axis_index("space") * lanes, lanes)
+    act, slope = silu_parts(pre[:, pl.ds(at, lanes)])
+    stage[...] = together(act, planes)
+    send.start()
+    spread_rows(rows_t, (cot[...].astype(F32) * slope).astype(BF16).astype(F32))
+    blocks = []
+    for a in (-1, 0, 1):
+        for b, e in STEPS:
+            column = []
+            for p in range(planes):
+                inside = 0 <= p - a < planes
+                column.append(step_rows(rows_t, p - a, b, e) if inside else jnp.zeros((width, o_own), BF16))
+            blocks.append(jnp.concatenate(column, axis=0))
+    back[...] = jnp.dot(jnp.concatenate(blocks, axis=1), weight[...], preferred_element_type=F32)
+    send.wait()
+
+
+def own_call(weight, pre, cot, planes):
+    o_own, lanes = cot.shape
+    width = lanes // planes
+    S = jax.ShapeDtypeStruct
+    return call(
+        functools.partial(own_body, planes),
+        [S((o_own * planes, width), BF16), S((lanes, weight.shape[1]), F32)],
+        [VM] * 3,
+        [
+            pltpu.VMEM((3, planes, width + 2 * BW, o_own), BF16),
+            pltpu.VMEM((o_own * planes, width), BF16),
+            pltpu.SemaphoreType.DMA,
+        ],
+        1.6e9,
+        1 << 20,
+        16,
+        [HB, VM],
+    )(weight, pre, cot)
+
+
+def back_body(slabs, planes, weight, pre, part, before, *refs):
+    messages, (deltas, share, mine, part_sum, rows_t) = refs[:slabs], refs[slabs:]
     pieces, lanes, cb = mine.shape
     o_own = deltas.shape[0]
     width = lanes // planes
@@ -430,34 +490,22 @@
     deltas[:, (total + 1) * width :] = jnp.zeros((o_own, width), F32)
     for r in range(slabs):
         at = pl.multiple_of(lax.rem(place - r + slabs, slabs) * lanes, lanes)
-        act, slope = silu_parts(pre[:, pl.ds(at, lanes)])
-        delta = (cots[r][:o_own, :].astype(F32) * slope).astype(BF16).astype(F32)
+        slope = silu_parts(pre[:, pl.ds(at, lanes)])[1]
+        delta = (messages[r][:o_own, :].astype(F32) * slope).astype(BF16).astype(F32)
         deltas[:, pl.ds(pl.multiple_of(at + width, width), lanes)] = delta
-        if r == 0:
-            stage[...] = together(act, planes)
-            send.start()
-    near = (planes + 2) * width
-    turned = deltas[:, pl.ds(pl.multiple_of(place * lanes, width), near)].T
-    w = iota((near, 1), 0) % BW
-    gap = width + 2 * BW
-    for e in (-1, 0, 1):
-        moved = turned
-        if e:
-            moved = jnp.where((w - e >= 0) & (w - e < BW), pltpu.roll(turned, e % near, 0), 0.0)
-        moved = moved.astype(BF16)
-        for p in range(planes + 2):
-            rows_t[e + 1, p * gap : p * gap + BW, :] = jnp.zeros((BW, o_own), BF16)
-            rows_t[e + 1, p * gap + BW : p * gap + BW + width, :] = moved[p * width : (p + 1) * width]
-            rows_t[e + 1, p * gap + BW + width : (p + 1) * gap, :] = jnp.zeros((BW, o_own), BF16)
-    blocks = []
-    for a in (-1, 0, 1):
-        for b, e in STEPS:
-            starts = [(1 + p - a) * gap + BW - b * BW for p in range(planes)]
-            blocks.append(jnp.concatenate([rows_t[e + 1, s : s + width, :] for s in starts], axis=0))
-    back = jnp.dot(jnp.concatenate(blocks, axis=1), weight[...], preferred_element_type=F32)
+    base = place * lanes
+    sides = [deltas[:, pl.ds(pl.multiple_of(i, width), width)] for i in (base, base + lanes + width)]
+    spread_rows(rows_t, jnp.concatenate(sides, axis=1))
+    sides = [jnp.concatenate([step_rows(rows_t, p, b, e) for b, e in STEPS], axis=1) for p in (0, 1)]
+    first = jnp.dot(sides[0], weight[18 * o_own :, :], preferred_element_type=F32)
+    last = jnp.dot(sides[1], weight[: 9 * o_own, :], preferred_element_type=F32)
+    rows = [before[p * width : (p + 1) * width, :] for p in range(planes)]
+    rows[0] = rows[0] + first
+    rows[-1] = rows[-1] + last
+    back = jnp.concatenate(rows, axis=0)
     grad = part[...]
     for r in range(1, slabs):
-        grad = grad + unfold_lanes(cots[r][o_own:, :], *grad.shape)
+        grad = grad + unfold_lanes(messages[r][o_own:, :], *grad.shape)
     part_sum[...] = grad
     rest = fold_lanes([grad.astype(BF16)], cb)
     for j in range(pieces):
@@ -466,11 +514,10 @@
         mine[to] = block
         share[to, :lanes, :] = block.astype(BF16)
         share[j, lanes:, :] = rest
-    send.wait()
-
-
-def back_call(weight, pre, part, cots, pieces, planes):
-    slabs = len(cots)
+
+
+def back_call(weight, pre, part, before, messages, pieces, planes):
+    slabs = len(messages)
     o_own, length = pre.shape
     lanes = length // slabs
     width = lanes // planes
@@ -479,23 +526,17 @@
     return call(
         functools.partial(back_body, slabs, planes),
         [
-            S((o_own * planes, width), BF16),
             S((o_own, length + 2 * width), F32),
             S((pieces, lanes + part.size // cb, cb), BF16),
             S((pieces, lanes, cb), F32),
             S(part.shape, F32),
         ],
-        [VM] * (3 + slabs),
-        [
-            pltpu.VMEM((3, (planes + 2) * (width + 2 * BW), o_own), BF16),
-            pltpu.VMEM((o_own * planes, width), BF16),
-            pltpu.SemaphoreType.DMA,
-        ],
-        1.8e9,
+        [VM] * (4 + slabs),
+        [pltpu.VMEM((3, 2, width + 2 * BW, o_own), BF16)],
+        1.2e9,
         1 << 20,
         16,
-        [HB, VM, VM, VM, VM],
-    )(weight, pre, part, *cots)
+    )(weight, pre, part, before, *messages)
 
 
 PLAN = ((0, 0, 4), (0, 4, 9), (1, 0, 9), (2, 0, 4), (2, 4, 7), (2, 7, 9))
@@ -628,7 +669,8 @@
     weight = bott_weight.transpose(1, 0, 2).reshape(27 * o_own, cb * chans)
     pre = chip_call(weight, part, slabs, mate, planes)
     pre, full = bott_call(weight, pre, ins, planes)
-    bott_out, delta, share, mine, part = back_call(weight, pre, part, cots, chans, planes)
+    bott_out, before = own_call(weight, pre, cot, planes)
+    delta, share, mine, part = back_call(weight, pre, part, before, cots, chans, planes)
     others = [hop(share[r], "chan", r) for r in range(1, chans)]
     bott_wgrad = wgrad_call((planes * spaces * width) ** -0.5, delta, full).transpose(1, 0, 2)
     bott_dgrad, fine_wgrad = last_call(mine, part, others, planes)

time: 43.2 us -> 42.6 us (0.986)
  waiting for transfers between devices: 3.98 us -> 2.86 us
  Pallas kernels: 19.9 us -> 20.4 us
    ppermute x11, waiting for transfers between devices: 2.77 us -> 1.65 us  [hop(): lax.ppermute(x, axis, [(i, (i + offset) % count) for i in range(count)])]
    pallas_call x1 -> x2, Pallas kernels: 1.81 us -> 2.38 us  [the longest x1 1.61 us: own_call(): call(functools.partial(own_body, planes), [S((o_own * planes, width), BF1...]
  transfers between devices with their start and end apart: 14 -> 14, of which waited for: 3 -> 2; matrix products, arithmetic and copies ran while one was open for 1% -> 1% of each run, Pallas kernels for 39% -> 44%
where the time goes in v8:
time: 42.6 us; the launch traced here: 42.4 us
  Pallas kernels  20.4 us (48%)
  starting transfers between devices  17.8 us (42%)
  waiting for transfers between devices  2.86 us (7%)
  between operations  0.83 us (2%)
  local copies, waits for them, and re-layouts  0.5 us (1%)
    ppermute x11, starting transfers between devices, hop(): lax.ppermute(x, axis, [(i, (i + offset) % count) for i in range(count)])  13.6 us
    pallas_call x1, Pallas kernels, wgrad_call(): call(functools.partial(wgrad_body, scale), [jax.ShapeDtypeStruct((27, o_o...  5.07 us
    ppermute x3, starting transfers between devices, swap(): return lax.ppermute(x, axis, [(i, i ^ bit) for i in range(count)])  4.19 us
    pallas_call x1, Pallas kernels, fine_call(): call(functools.partial(fine_body, scale), [S((ch, depth, rows, cols), BF1...  4.1 us
    pallas_call x1, Pallas kernels, bott_call(): call(functools.partial(bott_body, planes), [S(before.shape, F32), S((len(...  2.33 us
    pallas_call x1, Pallas kernels, chip_call(): call(functools.partial(chip_body, planes), [jax.ShapeDtypeStruct((weight....  2.21 us
    pallas_call x1, Pallas kernels, prep_call(): call(prep_body, [jax.ShapeDtypeStruct((3 * ch * rows, 3 * (rows + 2) * ch...  1.98 us
    ppermute x11, waiting for transfers between devices, hop(): lax.ppermute(x, axis, [(i, (i + offset) % count) for i in range(count)])  1.65 us
  transfers between devices with their start and end apart: 14, of which 2 were waited for; matrix products, arithmetic and copies ran while one was open for 1% of the time, Pallas kernels for 44%

profile of v8, /device:TPU:1, one launch (start us, length us, event | category | flops | bytes accessed | tf_op | source)
XLA Modules:
  0.0 42.4 jit_solution(16828597654291300645)
XLA Ops:
  0.6 0.0 copy-start.2
  0.6 3.2 %collective-permute-start.1 = (bf16[256,128]{1,0:T(8,128)(2,1)}, bf16[256,128]{1,0:T(8,128)(2,1)S(1)}, u32[]{:S(2)}, u32[]{:S(2)}) collective-permute-start(bf16[256,128]{1,0:T(8,128)(2,1)} %bitcast.25), channel_id=1, source_target_pairs={{0,8},{4,12},{8,0},{12,4},{1,9},{5,13},{9,1},{13,5},{2,10},{6,14},... | collective-permute-start | bytes 196616 | tf_op jit(solution)/shard_map/ppermute | solution.py:636
  3.8 1.3 %shard_map.110 = (bf16[128,256]{1,0:T(8,128)(2,1)S(1)}, bf16[160,256]{1,0:T(8,128)(2,1)S(1)}, bf16[160,256]{1,0:T(8,128)(2,1)S(1)}, bf16[128,256]{1,0:T(8,128)(2...) custom-call(s32[4,8,512]{2,1,0:T(8,128)} %labels.1, bf16[256,128]{1,0:T(8,128)(2,1)} %bitcast.26, ...), custom_call_target="tpu_custom_call" | custom-call | flops 1000000000 | bytes 262144 | tf_op jit(solution)/shard_map/pallas_call | solution.py:106
  5.1 1.3 %collective-permute-start = (bf16[160,256]{1,0:T(8,128)(2,1)S(1)}, bf16[160,256]{1,0:T(8,128)(2,1)S(1)}, u32[]{:S(2)}, u32[]{:S(2)}) collective-permute-start(bf16[160,256]{1,0:T(8,128)(2,1)S(1)} %get-tuple-element.36), channel_id=1, source_target_pairs={{0,4},{4,8},{8,12},{12,0},{1,5},{5,9},{9,13},{13,1},{2,6},{6,10},{... | collective-permute-start | bytes 245768 | tf_op jit(solution)/shard_map/ppermute | solution.py:636
  6.5 2.0 %collective-permute-start.2 = (bf16[160,256]{1,0:T(8,128)(2,1)S(1)}, bf16[160,256]{1,0:T(8,128)(2,1)S(1)}, u32[]{:S(2)}, u32[]{:S(2)}) collective-permute-start(bf16[160,256]{1,0:T(8,128)(2,1)S(1)} %get-tuple-element.37), channel_id=1, source_target_pairs={{0,12},{4,0},{8,4},{12,8},{1,13},{5,1},{9,5},{13,9},{2,14},{6,2},{... | collective-permute-start | bytes 245768 | tf_op jit(solution)/shard_map/ppermute | solution.py:636
  8.4 0.0 copy-done.2
  8.4 0.2 copy.13
  8.6 0.2 copy.14
  8.8 0.1 reshape.32.taps
  8.9 0.0 copy-start.1
  8.9 2.0 %shard_map.111 = (bf16[384,480]{1,0:T(8,128)(2,1)S(1)}, bf16[128,128]{1,0:T(8,128)(2,1)S(1)}, bf16[512,512]{1,0:T(8,128)(2,1)S(1)}) custom-call(bf16[3,48,48]{2,1,0:T(8,128)(2,1)S(1)} %reshape.32.taps, bf16[16,1024]{1,0:T(8,128)(2,1)S(1)} %get-tuple-element.32.table, s32[4,8,512]{2,1,0:T(8,128)S(1)} %get-tuple-element.33.ids.refs_0_), custom_call_target="tpu_custom_call" | custom-call | flops 2500000000 | bytes 262144 | tf_op jit(solution)/shard_map/pallas_call | solution.py:179
  10.9 0.0 collective-permute-done.1.refs_3_
  10.9 0.0 collective-permute-done.refs_2_
  10.9 0.0 collective-permute-done.2.refs_4_
  11.0 0.2 shard_map.112
  11.1 2.2 %collective-permute-start.5 = (bf16[4,128,256]{2,1,0:T(8,128)(2,1)S(1)}, bf16[4,128,256]{2,1,0:T(8,128)(2,1)S(1)}, u32[]{:S(2)}, u32[]{:S(2)}) collective-permute-start(bf16[4,128,256]{2,1,0:T(8,128)(2,1)S(1)} %get-tuple-element.45.mine.refs_0_), channel_id=1, source_target_pairs={{0,1},{1,0},{2,3},{3,2},{4,5},{5,4},{6,7},{7,6},{8,9},{9,8},{10,11... | collective-permute-start | bytes 786440 | tf_op jit(solution)/shard_map/ppermute | solution.py:641
  13.3 1.2 %collective-permute-start.3 = (s32[6,512]{1,0:T(8,128)S(1)}, s32[6,512]{1,0:T(8,128)S(1)}, u32[]{:S(2)}, u32[]{:S(2)}) collective-permute-start(s32[6,512]{1,0:T(8,128)S(1)} %get-tuple-element.41), channel_id=1, source_target_pairs={{0,1},{1,2},{2,3},{3,0},{4,5},{5,6},{6,7},{7,4},{8,9},{9,10},{10,1... | collective-permute-start | bytes 36872 | tf_op jit(solution)/shard_map/ppermute | solution.py:636
  14.5 0.0 collective-permute-start.4
  14.5 1.7 %collective-permute-start.7 = (bf16[4,128,256]{2,1,0:T(8,128)(2,1)S(1)}, bf16[4,128,256]{2,1,0:T(8,128)(2,1)S(1)}, u32[]{:S(2)}, u32[]{:S(2)}) collective-permute-start(bf16[4,128,256]{2,1,0:T(8,128)(2,1)S(1)} %get-tuple-element.45.mine.refs_0_), channel_id=1, source_target_pairs={{0,3},{1,2},{2,1},{3,0},{4,7},{5,6},{6,5},{7,4},{8,11},{9,10},{10,... | collective-permute-start | bytes 786440 | tf_op jit(solution)/shard_map/ppermute | solution.py:641
  16.2 0.3 collective-permute-start.6
  16.5 0.0 collective-permute-done.3.left
  16.5 1.6 %collective-permute-done.4.right = s32[6,512]{1,0:T(8,128)S(1)} collective-permute-done((s32[6,512]{1,0:T(8,128)S(1)}, s32[6,512]{1,0:T(8,128)S(1)}, u32[]{:S(2)}, u32[]{:S(2)}) %collective-permute-start.4) | collective-permute-done | bytes 12320 | tf_op jit(solution)/shard_map/ppermute | solution.py:636
  18.1 0.0 collective-permute-done.5.after.mate.refs_1_
  18.1 0.0 copy-done.1
  18.1 0.0 copy-start
  18.1 4.1 %shard_map.113 = (bf16[16,4,8,512]{3,2,1,0:T(8,128)(2,1)}, f32[16,512]{1,0:T(8,128)S(1)}, bf16[160,256]{1,0:T(8,128)(2,1)S(1)}) custom-call(bf16[512,512]{1,0:T(8,128)(2,1)S(1)} %get-tuple-element.34.known, s32[8,512]{1,0:T(8,128)S(1)} %get-tuple-element.39.below, s32[8,512]{1,0:T(8,128)S(1)} %get-tuple-element.40.above, ...), custom_call_target="tpu_custom_call" | custom-call | flops 6000000000 | bytes 4194304 | tf_op jit(solution)/shard_map/pallas_call | solution.py:296
  22.2 2.9 %collective-permute-start.10 = (bf16[160,256]{1,0:T(8,128)(2,1)S(1)}, bf16[160,256]{1,0:T(8,128)(2,1)S(1)}, u32[]{:S(2)}, u32[]{:S(2)}) collective-permute-start(bf16[160,256]{1,0:T(8,128)(2,1)S(1)} %get-tuple-element.50), channel_id=1, source_target_pairs={{0,12},{4,0},{8,4},{12,8},{1,13},{5,1},{9,5},{13,9},{2,14},{6,2},{... | collective-permute-start | bytes 245768 | tf_op jit(solution)/shard_map/ppermute | solution.py:636
  25.1 0.0 collective-permute-start.9
  25.1 0.4 collective-permute-start.8
  25.5 0.0 copy-done
  25.5 2.2 %shard_map.114.before = f32[128,1024]{1,0:T(8,128)S(1)} custom-call(bf16[3456,512]{1,0:T(8,128)(2,1)S(1)} %bitcast.19, f32[16,512]{1,0:T(8,128)S(1)} %get-tuple-element.47.after.part, bf16[4,128,256]{2,1,0:T(8,128)(2,1)S(1)} %get-tuple-element.45.mine.refs_0_, bf16[4,128,256]{2,1,0:T(8,128)(2,1)S(1)} %collective-permute-done.5.after.mate.refs_1_), custom_call_target="tpu_custom_call" | custom-call | flops 2500000000 | bytes 1048576 | tf_op jit(solution)/shard_map/pallas_call | solution.py:381
  27.7 0.0 collective-permute-done.7.refs_3_
  27.7 1.2 %collective-permute-done.6.refs_2_ = bf16[4,128,256]{2,1,0:T(8,128)(2,1)S(1)} collective-permute-done((bf16[4,128,256]{2,1,0:T(8,128)(2,1)S(1)}, bf16[4,128,256]{2,1,0:T(8,128)(2,1)S(1)}, u32[]{:S(2)}, u32[]{:S(2)}) %collective-permute-start.6) | collective-permute-done | bytes 262176 | tf_op jit(solution)/shard_map/ppermute | solution.py:641
  28.9 2.3 %shard_map.115 = (f32[128,1024]{1,0:T(8,128)S(1)}, bf16[512,1280]{1,0:T(8,128)(2,1)S(1)}) custom-call(bf16[3456,512]{1,0:T(8,128)(2,1)S(1)} %bitcast.20, f32[128,1024]{1,0:T(8,128)S(1)} %shard_map.114.before, bf16[4,128,256]{2,1,0:T(8,128)(2,1)S(1)} %get-tuple-element.45.mine.refs_0_, bf16[4,128,256]{2,1,0:T(8,128)(2,1)S(1)} %collective-permute-done.5.after.mate.refs_1_, ...), custom_call_target="tpu_custom_call" | custom-call | flops 2500000000 | bytes 1048576 | tf_op jit(solution)/shard_map/pallas_call | solution.py:408
  31.3 1.6 %shard_map.116 = (bf16[256,128]{1,0:T(8,128)(2,1)}, f32[256,512]{1,0:T(8,128)S(1)}) custom-call(bf16[3456,512]{1,0:T(8,128)(2,1)S(1)} %bitcast.21, f32[128,1024]{1,0:T(8,128)S(1)} %get-tuple-element.48.pre, bf16[128,256]{1,0:T(8,128)(2,1)S(1)} %get-tuple-element.44.bott_cot.cot.refs_0_), custom_call_target="tpu_custom_call" | custom-call | flops 1600000000 | bytes 1048576 | tf_op jit(solution)/shard_map/pallas_call | solution.py:465
  32.9 0.0 collective-permute-done.10.refs_3_
  32.9 0.0 collective-permute-done.9.refs_2_
  32.9 0.0 collective-permute-done.8.refs_1_
  32.9 0.8 %shard_map.117 = (f32[128,1280]{1,0:T(8,128)S(1)}, bf16[4,320,128]{2,1,0:T(8,128)(2,1)S(1)}, f32[4,256,128]{2,1,0:T(8,128)S(1)}, f32[16,512]{1,0:T(8,128)S(1)}) custom-call(bf16[3456,512]{1,0:T(8,128)(2,1)S(1)} %bitcast.22, f32[128,1024]{1,0:T(8,128)S(1)} %get-tuple-element.48.pre, f32[16,512]{1,0:T(8,128)S(1)} %get-tuple-element.47.after.part, ...), custom_call_target="tpu_custom_call" | custom-call | flops 1200000000 | bytes 1048576 | tf_op jit(solution)/shard_map/pallas_call | solution.py:526
  33.7 0.7 %collective-permute-start.13 = (bf16[320,128]{1,0:T(8,128)(2,1)S(1)}, bf16[320,128]{1,0:T(8,128)(2,1)S(1)}, u32[]{:S(2)}, u32[]{:S(2)}) collective-permute-start(bf16[320,128]{1,0:T(8,128)(2,1)S(1)} %get-tuple-element.59), channel_id=1, source_target_pairs={{0,3},{1,0},{2,1},{3,2},{4,7},{5,4},{6,5},{7,6},{8,11},{9,8},{10,9... | collective-permute-start | bytes 245768 | tf_op jit(solution)/shard_map/ppermute | solution.py:636
  34.4 0.0 collective-permute-start.12
  34.4 1.9 %collective-permute-start.11 = (bf16[320,128]{1,0:T(8,128)(2,1)S(1)}, bf16[320,128]{1,0:T(8,128)(2,1)S(1)}, u32[]{:S(2)}, u32[]{:S(2)}) collective-permute-start(bf16[320,128]{1,0:T(8,128)(2,1)S(1)} %get-tuple-element.61), channel_id=1, source_target_pairs={{0,1},{1,2},{2,3},{3,0},{4,5},{5,6},{6,7},{7,4},{8,9},{9,10},{10,1... | collective-permute-start | bytes 245768 | tf_op jit(solution)/shard_map/ppermute | solution.py:636
  36.4 5.1 %shard_map.119 = f32[27,128,512]{2,1,0:T(8,128)} custom-call(f32[128,1280]{1,0:T(8,128)S(1)} %get-tuple-element.57.delta, bf16[512,1280]{1,0:T(8,128)(2,1)S(1)} %get-tuple-element.58.full), custom_call_target="tpu_custom_call" | custom-call | flops 6600000000 | bytes 8388608 | tf_op jit(solution)/shard_map/pallas_call | solution.py:588
  41.5 0.0 collective-permute-done.13.refs_2_
  41.5 0.0 collective-permute-done.12.refs_1_
  41.5 0.0 collective-permute-done.11.refs_0_
  41.5 0.9 %shard_map.118 = (bf16[256,128]{1,0:T(8,128)(2,1)}, f32[16,16,27]{2,1,0:T(8,128)}) custom-call(f32[4,256,128]{2,1,0:T(8,128)S(1)} %get-tuple-element.51.mine, f32[16,512]{1,0:T(8,128)S(1)} %get-tuple-element.52.part, bf16[320,128]{1,0:T(8,128)(2,1)S(1)} %collective-permute-done.11.refs_0_, bf16[320,128]{1,0:T(8,128)(2,1)S(1)} %collective-permute-done.12.refs_1_, ...), custom_call_target="tpu_custom_call" | custom-call | flops 1000000000 | bytes 262144 | tf_op jit(solution)/shard_map/pallas_call | solution.py:620
  (1 shorter events, 0.0 us)
Async XLA Ops:
  0.6 7.8 %copy-start.2 = (bf16[27,16,16]{0,2,1:T(8,128)(2,1)S(1)}, bf16[27,16,16]{0,2,1:T(8,128)(2,1)}, u32[]{:S(2)}) copy-start(bf16[27,16,16]{0,2,1:T(8,128)(2,1)} %param.9) | copy-start | bytes 41476
  0.6 10.3 %collective-permute-start.1 = (bf16[256,128]{1,0:T(8,128)(2,1)}, bf16[256,128]{1,0:T(8,128)(2,1)S(1)}, u32[]{:S(2)}, u32[]{:S(2)}) collective-permute-start(bf16[256,128]{1,0:T(8,128)(2,1)} %bitcast.25), channel_id=1, source_target_pairs={{0,8},{4,12},{8,0},{12,4},{1,9},{5,13},{9,1},{13,5},{2,10},{6,14},... | collective-permute-start | bytes 196616 | tf_op jit(solution)/shard_map/ppermute | solution.py:636
  5.1 5.8 %collective-permute-start = (bf16[160,256]{1,0:T(8,128)(2,1)S(1)}, bf16[160,256]{1,0:T(8,128)(2,1)S(1)}, u32[]{:S(2)}, u32[]{:S(2)}) collective-permute-start(bf16[160,256]{1,0:T(8,128)(2,1)S(1)} %get-tuple-element.36), channel_id=1, source_target_pairs={{0,4},{4,8},{8,12},{12,0},{1,5},{5,9},{9,13},{13,1},{2,6},{6,10},{... | collective-permute-start | bytes 245768 | tf_op jit(solution)/shard_map/ppermute | solution.py:636
  6.5 4.5 %collective-permute-start.2 = (bf16[160,256]{1,0:T(8,128)(2,1)S(1)}, bf16[160,256]{1,0:T(8,128)(2,1)S(1)}, u32[]{:S(2)}, u32[]{:S(2)}) collective-permute-start(bf16[160,256]{1,0:T(8,128)(2,1)S(1)} %get-tuple-element.37), channel_id=1, source_target_pairs={{0,12},{4,0},{8,4},{12,8},{1,13},{5,1},{9,5},{13,9},{2,14},{6,2},{... | collective-permute-start | bytes 245768 | tf_op jit(solution)/shard_map/ppermute | solution.py:636
  8.9 9.2 %copy-start.1 = (bf16[16,4,8,512]{3,2,1,0:T(8,128)(2,1)S(1)}, bf16[16,4,8,512]{3,2,1,0:T(8,128)(2,1)}, u32[]{:S(2)}) copy-start(bf16[16,4,8,512]{3,2,1,0:T(8,128)(2,1)} %cot.1) | copy-start | bytes 1572868
  11.1 7.0 %collective-permute-start.5 = (bf16[4,128,256]{2,1,0:T(8,128)(2,1)S(1)}, bf16[4,128,256]{2,1,0:T(8,128)(2,1)S(1)}, u32[]{:S(2)}, u32[]{:S(2)}) collective-permute-start(bf16[4,128,256]{2,1,0:T(8,128)(2,1)S(1)} %get-tuple-element.45.mine.refs_0_), channel_id=1, source_target_pairs={{0,1},{1,0},{2,3},{3,2},{4,5},{5,4},{6,7},{7,6},{8,9},{9,8},{10,11... | collective-permute-start | bytes 786440 | tf_op jit(solution)/shard_map/ppermute | solution.py:641
  13.3 3.2 %collective-permute-start.3 = (s32[6,512]{1,0:T(8,128)S(1)}, s32[6,512]{1,0:T(8,128)S(1)}, u32[]{:S(2)}, u32[]{:S(2)}) collective-permute-start(s32[6,512]{1,0:T(8,128)S(1)} %get-tuple-element.41), channel_id=1, source_target_pairs={{0,1},{1,2},{2,3},{3,0},{4,5},{5,6},{6,7},{7,4},{8,9},{9,10},{10,1... | collective-permute-start | bytes 36872 | tf_op jit(solution)/shard_map/ppermute | solution.py:636
  14.5 3.6 %collective-permute-start.4 = (s32[6,512]{1,0:T(8,128)S(1)}, s32[6,512]{1,0:T(8,128)S(1)}, u32[]{:S(2)}, u32[]{:S(2)}) collective-permute-start(s32[6,512]{1,0:T(8,128)S(1)} %get-tuple-element.42), channel_id=1, source_target_pairs={{0,3},{1,0},{2,1},{3,2},{4,7},{5,4},{6,5},{7,6},{8,11},{9,8},{10,9... | collective-permute-start | bytes 36872 | tf_op jit(solution)/shard_map/ppermute | solution.py:636
  14.5 13.2 %collective-permute-start.7 = (bf16[4,128,256]{2,1,0:T(8,128)(2,1)S(1)}, bf16[4,128,256]{2,1,0:T(8,128)(2,1)S(1)}, u32[]{:S(2)}, u32[]{:S(2)}) collective-permute-start(bf16[4,128,256]{2,1,0:T(8,128)(2,1)S(1)} %get-tuple-element.45.mine.refs_0_), channel_id=1, source_target_pairs={{0,3},{1,2},{2,1},{3,0},{4,7},{5,6},{6,5},{7,4},{8,11},{9,10},{10,... | collective-permute-start | bytes 786440 | tf_op jit(solution)/shard_map/ppermute | solution.py:641
  16.2 12.7 %collective-permute-start.6 = (bf16[4,128,256]{2,1,0:T(8,128)(2,1)S(1)}, bf16[4,128,256]{2,1,0:T(8,128)(2,1)S(1)}, u32[]{:S(2)}, u32[]{:S(2)}) collective-permute-start(bf16[4,128,256]{2,1,0:T(8,128)(2,1)S(1)} %get-tuple-element.45.mine.refs_0_), channel_id=1, source_target_pairs={{0,2},{1,3},{2,0},{3,1},{4,6},{5,7},{6,4},{7,5},{8,10},{9,11},{10,... | collective-permute-start | bytes 786440 | tf_op jit(solution)/shard_map/ppermute | solution.py:641
  18.1 7.4 %copy-start = (bf16[128,27,512]{2,0,1:T(8,128)(2,1)S(1)}, bf16[128,27,512]{2,0,1:T(8,128)(2,1)}, u32[]{:S(2)}) copy-start(bf16[128,27,512]{2,0,1:T(8,128)(2,1)} %param.12) | copy-start | bytes 10616836
  22.2 10.6 %collective-permute-start.10 = (bf16[160,256]{1,0:T(8,128)(2,1)S(1)}, bf16[160,256]{1,0:T(8,128)(2,1)S(1)}, u32[]{:S(2)}, u32[]{:S(2)}) collective-permute-start(bf16[160,256]{1,0:T(8,128)(2,1)S(1)} %get-tuple-element.50), channel_id=1, source_target_pairs={{0,12},{4,0},{8,4},{12,8},{1,13},{5,1},{9,5},{13,9},{2,14},{6,2},{... | collective-permute-start | bytes 245768 | tf_op jit(solution)/shard_map/ppermute | solution.py:636
  25.1 7.8 %collective-permute-start.9 = (bf16[160,256]{1,0:T(8,128)(2,1)S(1)}, bf16[160,256]{1,0:T(8,128)(2,1)S(1)}, u32[]{:S(2)}, u32[]{:S(2)}) collective-permute-start(bf16[160,256]{1,0:T(8,128)(2,1)S(1)} %get-tuple-element.50), channel_id=1, source_target_pairs={{0,8},{4,12},{8,0},{12,4},{1,9},{5,13},{9,1},{13,5},{2,10},{6,14},... | collective-permute-start | bytes 245768 | tf_op jit(solution)/shard_map/ppermute | solution.py:636
  25.1 7.8 %collective-permute-start.8 = (bf16[160,256]{1,0:T(8,128)(2,1)S(1)}, bf16[160,256]{1,0:T(8,128)(2,1)S(1)}, u32[]{:S(2)}, u32[]{:S(2)}) collective-permute-start(bf16[160,256]{1,0:T(8,128)(2,1)S(1)} %get-tuple-element.50), channel_id=1, source_target_pairs={{0,4},{4,8},{8,12},{12,0},{1,5},{5,9},{9,13},{13,1},{2,6},{6,10},{... | collective-permute-start | bytes 245768 | tf_op jit(solution)/shard_map/ppermute | solution.py:636
  33.7 7.7 %collective-permute-start.13 = (bf16[320,128]{1,0:T(8,128)(2,1)S(1)}, bf16[320,128]{1,0:T(8,128)(2,1)S(1)}, u32[]{:S(2)}, u32[]{:S(2)}) collective-permute-start(bf16[320,128]{1,0:T(8,128)(2,1)S(1)} %get-tuple-element.59), channel_id=1, source_target_pairs={{0,3},{1,0},{2,1},{3,2},{4,7},{5,4},{6,5},{7,6},{8,11},{9,8},{10,9... | collective-permute-start | bytes 245768 | tf_op jit(solution)/shard_map/ppermute | solution.py:636
  34.4 7.1 %collective-permute-start.12 = (bf16[320,128]{1,0:T(8,128)(2,1)S(1)}, bf16[320,128]{1,0:T(8,128)(2,1)S(1)}, u32[]{:S(2)}, u32[]{:S(2)}) collective-permute-start(bf16[320,128]{1,0:T(8,128)(2,1)S(1)} %get-tuple-element.60), channel_id=1, source_target_pairs={{0,2},{1,3},{2,0},{3,1},{4,6},{5,7},{6,4},{7,5},{8,10},{9,11},{10,... | collective-permute-start | bytes 245768 | tf_op jit(solution)/shard_map/ppermute | solution.py:636
  34.4 7.1 %collective-permute-start.11 = (bf16[320,128]{1,0:T(8,128)(2,1)S(1)}, bf16[320,128]{1,0:T(8,128)(2,1)S(1)}, u32[]{:S(2)}, u32[]{:S(2)}) collective-permute-start(bf16[320,128]{1,0:T(8,128)(2,1)S(1)} %get-tuple-element.61), channel_id=1, source_target_pairs={{0,1},{1,2},{2,3},{3,0},{4,5},{5,6},{6,7},{7,4},{8,9},{9,10},{10,1... | collective-permute-start | bytes 245768 | tf_op jit(solution)/shard_map/ppermute | solution.py:636

commit v9 on v8

--- a/solution.py
+++ b/solution.py
@@ -240,7 +240,7 @@
         grads[...] = term if x == 0 else grads[...] + term
 
     gap = (iota(grads.shape, 1) % step) // ch - iota(grads.shape, 0) % rows
-    for x in range(depth + 2):
+    for x in range(3):
         fill(x)
     for b in range(3):
         keeps[b] = hot(gap == b)
@@ -253,6 +253,7 @@
     forward(0)
     for x in range(depth):
         if x + 1 < depth:
+            fill(x + 3)
             forward(x + 1)
         if x > 0:
             backward(x - 1)

time: 42.6 us -> 42.6 us (level)
  no operation moved by 1% of the time
where the time goes in v9:
time: 42.6 us; the launch traced here: 42.4 us
  Pallas kernels  20.7 us (49%)
  starting transfers between devices  17.8 us (42%)
  waiting for transfers between devices  2.6 us (6%)
  between operations  0.83 us (2%)
  local copies, waits for them, and re-layouts  0.5 us (1%)
    ppermute x11, starting transfers between devices, hop(): lax.ppermute(x, axis, [(i, (i + offset) % count) for i in range(count)])  13.6 us
    pallas_call x1, Pallas kernels, wgrad_call(): call(functools.partial(wgrad_body, scale), [jax.ShapeDtypeStruct((27, o_o...  5.07 us
    pallas_call x1, Pallas kernels, fine_call(): call(functools.partial(fine_body, scale), [S((ch, depth, rows, cols), BF1...  4.38 us
    ppermute x3, starting transfers between devices, swap(): return lax.ppermute(x, axis, [(i, i ^ bit) for i in range(count)])  4.19 us
    pallas_call x1, Pallas kernels, bott_call(): call(functools.partial(bott_body, planes), [S(before.shape, F32), S((len(...  2.33 us
    pallas_call x1, Pallas kernels, chip_call(): call(functools.partial(chip_body, planes), [jax.ShapeDtypeStruct((weight....  2.21 us
    pallas_call x1, Pallas kernels, prep_call(): call(prep_body, [jax.ShapeDtypeStruct((3 * ch * rows, 3 * (rows + 2) * ch...  1.98 us
    ppermute x11, waiting for transfers between devices, hop(): lax.ppermute(x, axis, [(i, (i + offset) % count) for i in range(count)])  1.65 us
  transfers between devices with their start and end apart: 14, of which 2 were waited for; matrix products, arithmetic and copies ran while one was open for 1% of the time, Pallas kernels for 44%

profile of v9, /device:TPU:1, one launch (start us, length us, event | category | flops | bytes accessed | tf_op | source)
XLA Modules:
  0.0 42.4 jit_solution(5372263431140247138)
XLA Ops:
  0.6 0.0 copy-start.2
  0.6 3.2 %collective-permute-start.1 = (bf16[256,128]{1,0:T(8,128)(2,1)}, bf16[256,128]{1,0:T(8,128)(2,1)S(1)}, u32[]{:S(2)}, u32[]{:S(2)}) collective-permute-start(bf16[256,128]{1,0:T(8,128)(2,1)} %bitcast.25), channel_id=1, source_target_pairs={{0,8},{4,12},{8,0},{12,4},{1,9},{5,13},{9,1},{13,5},{2,10},{6,14},... | collective-permute-start | bytes 196616 | tf_op jit(solution)/shard_map/ppermute | solution.py:637
  3.8 1.3 %shard_map.110 = (bf16[128,256]{1,0:T(8,128)(2,1)S(1)}, bf16[160,256]{1,0:T(8,128)(2,1)S(1)}, bf16[160,256]{1,0:T(8,128)(2,1)S(1)}, bf16[128,256]{1,0:T(8,128)(2...) custom-call(s32[4,8,512]{2,1,0:T(8,128)} %labels.1, bf16[256,128]{1,0:T(8,128)(2,1)} %bitcast.26, ...), custom_call_target="tpu_custom_call" | custom-call | flops 1000000000 | bytes 262144 | tf_op jit(solution)/shard_map/pallas_call | solution.py:106
  5.1 1.3 %collective-permute-start = (bf16[160,256]{1,0:T(8,128)(2,1)S(1)}, bf16[160,256]{1,0:T(8,128)(2,1)S(1)}, u32[]{:S(2)}, u32[]{:S(2)}) collective-permute-start(bf16[160,256]{1,0:T(8,128)(2,1)S(1)} %get-tuple-element.36), channel_id=1, source_target_pairs={{0,4},{4,8},{8,12},{12,0},{1,5},{5,9},{9,13},{13,1},{2,6},{6,10},{... | collective-permute-start | bytes 245768 | tf_op jit(solution)/shard_map/ppermute | solution.py:637
  6.5 2.0 %collective-permute-start.2 = (bf16[160,256]{1,0:T(8,128)(2,1)S(1)}, bf16[160,256]{1,0:T(8,128)(2,1)S(1)}, u32[]{:S(2)}, u32[]{:S(2)}) collective-permute-start(bf16[160,256]{1,0:T(8,128)(2,1)S(1)} %get-tuple-element.37), channel_id=1, source_target_pairs={{0,12},{4,0},{8,4},{12,8},{1,13},{5,1},{9,5},{13,9},{2,14},{6,2},{... | collective-permute-start | bytes 245768 | tf_op jit(solution)/shard_map/ppermute | solution.py:637
  8.4 0.0 copy-done.2
  8.4 0.2 copy.13
  8.6 0.2 copy.14
  8.8 0.1 reshape.32.taps
  8.9 0.0 copy-start.1
  8.9 2.0 %shard_map.111 = (bf16[384,480]{1,0:T(8,128)(2,1)S(1)}, bf16[128,128]{1,0:T(8,128)(2,1)S(1)}, bf16[512,512]{1,0:T(8,128)(2,1)S(1)}) custom-call(bf16[3,48,48]{2,1,0:T(8,128)(2,1)S(1)} %reshape.32.taps, bf16[16,1024]{1,0:T(8,128)(2,1)S(1)} %get-tuple-element.32.table, s32[4,8,512]{2,1,0:T(8,128)S(1)} %get-tuple-element.33.ids.refs_0_), custom_call_target="tpu_custom_call" | custom-call | flops 2500000000 | bytes 262144 | tf_op jit(solution)/shard_map/pallas_call | solution.py:179
  10.9 0.0 collective-permute-done.1.refs_3_
  10.9 0.0 collective-permute-done.refs_2_
  10.9 0.0 collective-permute-done.2.refs_4_
  11.0 0.2 shard_map.112
  11.1 2.2 %collective-permute-start.5 = (bf16[4,128,256]{2,1,0:T(8,128)(2,1)S(1)}, bf16[4,128,256]{2,1,0:T(8,128)(2,1)S(1)}, u32[]{:S(2)}, u32[]{:S(2)}) collective-permute-start(bf16[4,128,256]{2,1,0:T(8,128)(2,1)S(1)} %get-tuple-element.45.mine.refs_0_), channel_id=1, source_target_pairs={{0,1},{1,0},{2,3},{3,2},{4,5},{5,4},{6,7},{7,6},{8,9},{9,8},{10,11... | collective-permute-start | bytes 786440 | tf_op jit(solution)/shard_map/ppermute | solution.py:642
  13.3 1.2 %collective-permute-start.3 = (s32[6,512]{1,0:T(8,128)S(1)}, s32[6,512]{1,0:T(8,128)S(1)}, u32[]{:S(2)}, u32[]{:S(2)}) collective-permute-start(s32[6,512]{1,0:T(8,128)S(1)} %get-tuple-element.41), channel_id=1, source_target_pairs={{0,1},{1,2},{2,3},{3,0},{4,5},{5,6},{6,7},{7,4},{8,9},{9,10},{10,1... | collective-permute-start | bytes 36872 | tf_op jit(solution)/shard_map/ppermute | solution.py:637
  14.5 0.0 collective-permute-start.4
  14.5 1.7 %collective-permute-start.7 = (bf16[4,128,256]{2,1,0:T(8,128)(2,1)S(1)}, bf16[4,128,256]{2,1,0:T(8,128)(2,1)S(1)}, u32[]{:S(2)}, u32[]{:S(2)}) collective-permute-start(bf16[4,128,256]{2,1,0:T(8,128)(2,1)S(1)} %get-tuple-element.45.mine.refs_0_), channel_id=1, source_target_pairs={{0,3},{1,2},{2,1},{3,0},{4,7},{5,6},{6,5},{7,4},{8,11},{9,10},{10,... | collective-permute-start | bytes 786440 | tf_op jit(solution)/shard_map/ppermute | solution.py:642
  16.2 0.3 collective-permute-start.6
  16.5 0.0 collective-permute-done.3.left
  16.5 1.6 %collective-permute-done.4.right = s32[6,512]{1,0:T(8,128)S(1)} collective-permute-done((s32[6,512]{1,0:T(8,128)S(1)}, s32[6,512]{1,0:T(8,128)S(1)}, u32[]{:S(2)}, u32[]{:S(2)}) %collective-permute-start.4) | collective-permute-done | bytes 12320 | tf_op jit(solution)/shard_map/ppermute | solution.py:637
  18.1 0.0 collective-permute-done.5.after.mate.refs_1_
  18.1 0.0 copy-done.1
  18.1 0.0 copy-start
  18.1 4.4 %shard_map.113 = (bf16[16,4,8,512]{3,2,1,0:T(8,128)(2,1)}, f32[16,512]{1,0:T(8,128)S(1)}, bf16[160,256]{1,0:T(8,128)(2,1)S(1)}) custom-call(bf16[512,512]{1,0:T(8,128)(2,1)S(1)} %get-tuple-element.34.known, s32[8,512]{1,0:T(8,128)S(1)} %get-tuple-element.39.below, s32[8,512]{1,0:T(8,128)S(1)} %get-tuple-element.40.above, ...), custom_call_target="tpu_custom_call" | custom-call | flops 6000000000 | bytes 4194304 | tf_op jit(solution)/shard_map/pallas_call | solution.py:297
  22.5 2.9 %collective-permute-start.10 = (bf16[160,256]{1,0:T(8,128)(2,1)S(1)}, bf16[160,256]{1,0:T(8,128)(2,1)S(1)}, u32[]{:S(2)}, u32[]{:S(2)}) collective-permute-start(bf16[160,256]{1,0:T(8,128)(2,1)S(1)} %get-tuple-element.50), channel_id=1, source_target_pairs={{0,12},{4,0},{8,4},{12,8},{1,13},{5,1},{9,5},{13,9},{2,14},{6,2},{... | collective-permute-start | bytes 245768 | tf_op jit(solution)/shard_map/ppermute | solution.py:637
  25.4 0.0 collective-permute-start.9
  25.4 0.4 collective-permute-start.8
  25.8 0.0 copy-done
  25.8 2.2 %shard_map.114.before = f32[128,1024]{1,0:T(8,128)S(1)} custom-call(bf16[3456,512]{1,0:T(8,128)(2,1)S(1)} %bitcast.19, f32[16,512]{1,0:T(8,128)S(1)} %get-tuple-element.47.after.part, bf16[4,128,256]{2,1,0:T(8,128)(2,1)S(1)} %get-tuple-element.45.mine.refs_0_, bf16[4,128,256]{2,1,0:T(8,128)(2,1)S(1)} %collective-permute-done.5.after.mate.refs_1_), custom_call_target="tpu_custom_call" | custom-call | flops 2500000000 | bytes 1048576 | tf_op jit(solution)/shard_map/pallas_call | solution.py:382
  28.0 0.0 collective-permute-done.7.refs_3_
  28.0 0.9 %collective-permute-done.6.refs_2_ = bf16[4,128,256]{2,1,0:T(8,128)(2,1)S(1)} collective-permute-done((bf16[4,128,256]{2,1,0:T(8,128)(2,1)S(1)}, bf16[4,128,256]{2,1,0:T(8,128)(2,1)S(1)}, u32[]{:S(2)}, u32[]{:S(2)}) %collective-permute-start.6) | collective-permute-done | bytes 262176 | tf_op jit(solution)/shard_map/ppermute | solution.py:642
  28.9 2.3 %shard_map.115 = (f32[128,1024]{1,0:T(8,128)S(1)}, bf16[512,1280]{1,0:T(8,128)(2,1)S(1)}) custom-call(bf16[3456,512]{1,0:T(8,128)(2,1)S(1)} %bitcast.20, f32[128,1024]{1,0:T(8,128)S(1)} %shard_map.114.before, bf16[4,128,256]{2,1,0:T(8,128)(2,1)S(1)} %get-tuple-element.45.mine.refs_0_, bf16[4,128,256]{2,1,0:T(8,128)(2,1)S(1)} %collective-permute-done.5.after.mate.refs_1_, ...), custom_call_target="tpu_custom_call" | custom-call | flops 2500000000 | bytes 1048576 | tf_op jit(solution)/shard_map/pallas_call | solution.py:409
  31.3 1.6 %shard_map.116 = (bf16[256,128]{1,0:T(8,128)(2,1)}, f32[256,512]{1,0:T(8,128)S(1)}) custom-call(bf16[3456,512]{1,0:T(8,128)(2,1)S(1)} %bitcast.21, f32[128,1024]{1,0:T(8,128)S(1)} %get-tuple-element.48.pre, bf16[128,256]{1,0:T(8,128)(2,1)S(1)} %get-tuple-element.44.bott_cot.cot.refs_0_), custom_call_target="tpu_custom_call" | custom-call | flops 1600000000 | bytes 1048576 | tf_op jit(solution)/shard_map/pallas_call | solution.py:466
  32.9 0.0 collective-permute-done.10.refs_3_
  32.9 0.0 collective-permute-done.9.refs_2_
  32.9 0.0 collective-permute-done.8.refs_1_
  32.9 0.8 %shard_map.117 = (f32[128,1280]{1,0:T(8,128)S(1)}, bf16[4,320,128]{2,1,0:T(8,128)(2,1)S(1)}, f32[4,256,128]{2,1,0:T(8,128)S(1)}, f32[16,512]{1,0:T(8,128)S(1)}) custom-call(bf16[3456,512]{1,0:T(8,128)(2,1)S(1)} %bitcast.22, f32[128,1024]{1,0:T(8,128)S(1)} %get-tuple-element.48.pre, f32[16,512]{1,0:T(8,128)S(1)} %get-tuple-element.47.after.part, ...), custom_call_target="tpu_custom_call" | custom-call | flops 1200000000 | bytes 1048576 | tf_op jit(solution)/shard_map/pallas_call | solution.py:527
  33.7 0.7 %collective-permute-start.13 = (bf16[320,128]{1,0:T(8,128)(2,1)S(1)}, bf16[320,128]{1,0:T(8,128)(2,1)S(1)}, u32[]{:S(2)}, u32[]{:S(2)}) collective-permute-start(bf16[320,128]{1,0:T(8,128)(2,1)S(1)} %get-tuple-element.59), channel_id=1, source_target_pairs={{0,3},{1,0},{2,1},{3,2},{4,7},{5,4},{6,5},{7,6},{8,11},{9,8},{10,9... | collective-permute-start | bytes 245768 | tf_op jit(solution)/shard_map/ppermute | solution.py:637
  34.4 0.3 collective-permute-start.12
  34.7 1.7 %collective-permute-start.11 = (bf16[320,128]{1,0:T(8,128)(2,1)S(1)}, bf16[320,128]{1,0:T(8,128)(2,1)S(1)}, u32[]{:S(2)}, u32[]{:S(2)}) collective-permute-start(bf16[320,128]{1,0:T(8,128)(2,1)S(1)} %get-tuple-element.61), channel_id=1, source_target_pairs={{0,1},{1,2},{2,3},{3,0},{4,5},{5,6},{6,7},{7,4},{8,9},{9,10},{10,1... | collective-permute-start | bytes 245768 | tf_op jit(solution)/shard_map/ppermute | solution.py:637
  36.4 5.1 %shard_map.119 = f32[27,128,512]{2,1,0:T(8,128)} custom-call(f32[128,1280]{1,0:T(8,128)S(1)} %get-tuple-element.57.delta, bf16[512,1280]{1,0:T(8,128)(2,1)S(1)} %get-tuple-element.58.full), custom_call_target="tpu_custom_call" | custom-call | flops 6600000000 | bytes 8388608 | tf_op jit(solution)/shard_map/pallas_call | solution.py:589
  41.5 0.0 collective-permute-done.13.refs_2_
  41.5 0.0 collective-permute-done.12.refs_1_
  41.5 0.0 collective-permute-done.11.refs_0_
  41.5 0.9 %shard_map.118 = (bf16[256,128]{1,0:T(8,128)(2,1)}, f32[16,16,27]{2,1,0:T(8,128)}) custom-call(f32[4,256,128]{2,1,0:T(8,128)S(1)} %get-tuple-element.51.mine, f32[16,512]{1,0:T(8,128)S(1)} %get-tuple-element.52.part, bf16[320,128]{1,0:T(8,128)(2,1)S(1)} %collective-permute-done.11.refs_0_, bf16[320,128]{1,0:T(8,128)(2,1)S(1)} %collective-permute-done.12.refs_1_, ...), custom_call_target="tpu_custom_call" | custom-call | flops 1000000000 | bytes 262144 | tf_op jit(solution)/shard_map/pallas_call | solution.py:621
  (1 shorter events, 0.0 us)
Async XLA Ops:
  0.6 7.8 %copy-start.2 = (bf16[27,16,16]{0,2,1:T(8,128)(2,1)S(1)}, bf16[27,16,16]{0,2,1:T(8,128)(2,1)}, u32[]{:S(2)}) copy-start(bf16[27,16,16]{0,2,1:T(8,128)(2,1)} %param.9) | copy-start | bytes 41476
  0.6 10.3 %collective-permute-start.1 = (bf16[256,128]{1,0:T(8,128)(2,1)}, bf16[256,128]{1,0:T(8,128)(2,1)S(1)}, u32[]{:S(2)}, u32[]{:S(2)}) collective-permute-start(bf16[256,128]{1,0:T(8,128)(2,1)} %bitcast.25), channel_id=1, source_target_pairs={{0,8},{4,12},{8,0},{12,4},{1,9},{5,13},{9,1},{13,5},{2,10},{6,14},... | collective-permute-start | bytes 196616 | tf_op jit(solution)/shard_map/ppermute | solution.py:637
  5.1 5.8 %collective-permute-start = (bf16[160,256]{1,0:T(8,128)(2,1)S(1)}, bf16[160,256]{1,0:T(8,128)(2,1)S(1)}, u32[]{:S(2)}, u32[]{:S(2)}) collective-permute-start(bf16[160,256]{1,0:T(8,128)(2,1)S(1)} %get-tuple-element.36), channel_id=1, source_target_pairs={{0,4},{4,8},{8,12},{12,0},{1,5},{5,9},{9,13},{13,1},{2,6},{6,10},{... | collective-permute-start | bytes 245768 | tf_op jit(solution)/shard_map/ppermute | solution.py:637
  6.5 4.5 %collective-permute-start.2 = (bf16[160,256]{1,0:T(8,128)(2,1)S(1)}, bf16[160,256]{1,0:T(8,128)(2,1)S(1)}, u32[]{:S(2)}, u32[]{:S(2)}) collective-permute-start(bf16[160,256]{1,0:T(8,128)(2,1)S(1)} %get-tuple-element.37), channel_id=1, source_target_pairs={{0,12},{4,0},{8,4},{12,8},{1,13},{5,1},{9,5},{13,9},{2,14},{6,2},{... | collective-permute-start | bytes 245768 | tf_op jit(solution)/shard_map/ppermute | solution.py:637
  8.9 9.2 %copy-start.1 = (bf16[16,4,8,512]{3,2,1,0:T(8,128)(2,1)S(1)}, bf16[16,4,8,512]{3,2,1,0:T(8,128)(2,1)}, u32[]{:S(2)}) copy-start(bf16[16,4,8,512]{3,2,1,0:T(8,128)(2,1)} %cot.1) | copy-start | bytes 1572868
  11.1 7.0 %collective-permute-start.5 = (bf16[4,128,256]{2,1,0:T(8,128)(2,1)S(1)}, bf16[4,128,256]{2,1,0:T(8,128)(2,1)S(1)}, u32[]{:S(2)}, u32[]{:S(2)}) collective-permute-start(bf16[4,128,256]{2,1,0:T(8,128)(2,1)S(1)} %get-tuple-element.45.mine.refs_0_), channel_id=1, source_target_pairs={{0,1},{1,0},{2,3},{3,2},{4,5},{5,4},{6,7},{7,6},{8,9},{9,8},{10,11... | collective-permute-start | bytes 786440 | tf_op jit(solution)/shard_map/ppermute | solution.py:642
  13.3 3.2 %collective-permute-start.3 = (s32[6,512]{1,0:T(8,128)S(1)}, s32[6,512]{1,0:T(8,128)S(1)}, u32[]{:S(2)}, u32[]{:S(2)}) collective-permute-start(s32[6,512]{1,0:T(8,128)S(1)} %get-tuple-element.41), channel_id=1, source_target_pairs={{0,1},{1,2},{2,3},{3,0},{4,5},{5,6},{6,7},{7,4},{8,9},{9,10},{10,1... | collective-permute-start | bytes 36872 | tf_op jit(solution)/shard_map/ppermute | solution.py:637
  14.5 3.6 %collective-permute-start.4 = (s32[6,512]{1,0:T(8,128)S(1)}, s32[6,512]{1,0:T(8,128)S(1)}, u32[]{:S(2)}, u32[]{:S(2)}) collective-permute-start(s32[6,512]{1,0:T(8,128)S(1)} %get-tuple-element.42), channel_id=1, source_target_pairs={{0,3},{1,0},{2,1},{3,2},{4,7},{5,4},{6,5},{7,6},{8,11},{9,8},{10,9... | collective-permute-start | bytes 36872 | tf_op jit(solution)/shard_map/ppermute | solution.py:637
  14.5 13.5 %collective-permute-start.7 = (bf16[4,128,256]{2,1,0:T(8,128)(2,1)S(1)}, bf16[4,128,256]{2,1,0:T(8,128)(2,1)S(1)}, u32[]{:S(2)}, u32[]{:S(2)}) collective-permute-start(bf16[4,128,256]{2,1,0:T(8,128)(2,1)S(1)} %get-tuple-element.45.mine.refs_0_), channel_id=1, source_target_pairs={{0,3},{1,2},{2,1},{3,0},{4,7},{5,6},{6,5},{7,4},{8,11},{9,10},{10,... | collective-permute-start | bytes 786440 | tf_op jit(solution)/shard_map/ppermute | solution.py:642
  16.2 12.7 %collective-permute-start.6 = (bf16[4,128,256]{2,1,0:T(8,128)(2,1)S(1)}, bf16[4,128,256]{2,1,0:T(8,128)(2,1)S(1)}, u32[]{:S(2)}, u32[]{:S(2)}) collective-permute-start(bf16[4,128,256]{2,1,0:T(8,128)(2,1)S(1)} %get-tuple-element.45.mine.refs_0_), channel_id=1, source_target_pairs={{0,2},{1,3},{2,0},{3,1},{4,6},{5,7},{6,4},{7,5},{8,10},{9,11},{10,... | collective-permute-start | bytes 786440 | tf_op jit(solution)/shard_map/ppermute | solution.py:642
  18.1 7.6 %copy-start = (bf16[128,27,512]{2,0,1:T(8,128)(2,1)S(1)}, bf16[128,27,512]{2,0,1:T(8,128)(2,1)}, u32[]{:S(2)}) copy-start(bf16[128,27,512]{2,0,1:T(8,128)(2,1)} %param.12) | copy-start | bytes 10616836
  22.5 10.4 %collective-permute-start.10 = (bf16[160,256]{1,0:T(8,128)(2,1)S(1)}, bf16[160,256]{1,0:T(8,128)(2,1)S(1)}, u32[]{:S(2)}, u32[]{:S(2)}) collective-permute-start(bf16[160,256]{1,0:T(8,128)(2,1)S(1)} %get-tuple-element.50), channel_id=1, source_target_pairs={{0,12},{4,0},{8,4},{12,8},{1,13},{5,1},{9,5},{13,9},{2,14},{6,2},{... | collective-permute-start | bytes 245768 | tf_op jit(solution)/shard_map/ppermute | solution.py:637
  25.4 7.5 %collective-permute-start.9 = (bf16[160,256]{1,0:T(8,128)(2,1)S(1)}, bf16[160,256]{1,0:T(8,128)(2,1)S(1)}, u32[]{:S(2)}, u32[]{:S(2)}) collective-permute-start(bf16[160,256]{1,0:T(8,128)(2,1)S(1)} %get-tuple-element.50), channel_id=1, source_target_pairs={{0,8},{4,12},{8,0},{12,4},{1,9},{5,13},{9,1},{13,5},{2,10},{6,14},... | collective-permute-start | bytes 245768 | tf_op jit(solution)/shard_map/ppermute | solution.py:637
  25.4 7.5 %collective-permute-start.8 = (bf16[160,256]{1,0:T(8,128)(2,1)S(1)}, bf16[160,256]{1,0:T(8,128)(2,1)S(1)}, u32[]{:S(2)}, u32[]{:S(2)}) collective-permute-start(bf16[160,256]{1,0:T(8,128)(2,1)S(1)} %get-tuple-element.50), channel_id=1, source_target_pairs={{0,4},{4,8},{8,12},{12,0},{1,5},{5,9},{9,13},{13,1},{2,6},{6,10},{... | collective-permute-start | bytes 245768 | tf_op jit(solution)/shard_map/ppermute | solution.py:637
  33.7 7.7 %collective-permute-start.13 = (bf16[320,128]{1,0:T(8,128)(2,1)S(1)}, bf16[320,128]{1,0:T(8,128)(2,1)S(1)}, u32[]{:S(2)}, u32[]{:S(2)}) collective-permute-start(bf16[320,128]{1,0:T(8,128)(2,1)S(1)} %get-tuple-element.59), channel_id=1, source_target_pairs={{0,3},{1,0},{2,1},{3,2},{4,7},{5,4},{6,5},{7,6},{8,11},{9,8},{10,9... | collective-permute-start | bytes 245768 | tf_op jit(solution)/shard_map/ppermute | solution.py:637
  34.4 7.1 %collective-permute-start.12 = (bf16[320,128]{1,0:T(8,128)(2,1)S(1)}, bf16[320,128]{1,0:T(8,128)(2,1)S(1)}, u32[]{:S(2)}, u32[]{:S(2)}) collective-permute-start(bf16[320,128]{1,0:T(8,128)(2,1)S(1)} %get-tuple-element.60), channel_id=1, source_target_pairs={{0,2},{1,3},{2,0},{3,1},{4,6},{5,7},{6,4},{7,5},{8,10},{9,11},{10,... | collective-permute-start | bytes 245768 | tf_op jit(solution)/shard_map/ppermute | solution.py:637
  34.7 6.8 %collective-permute-start.11 = (bf16[320,128]{1,0:T(8,128)(2,1)S(1)}, bf16[320,128]{1,0:T(8,128)(2,1)S(1)}, u32[]{:S(2)}, u32[]{:S(2)}) collective-permute-start(bf16[320,128]{1,0:T(8,128)(2,1)S(1)} %get-tuple-element.61), channel_id=1, source_target_pairs={{0,1},{1,2},{2,3},{3,0},{4,5},{5,6},{6,7},{7,4},{8,9},{9,10},{10,1... | collective-permute-start | bytes 245768 | tf_op jit(solution)/shard_map/ppermute | solution.py:637

commit v10 on v8

--- a/solution.py
+++ b/solution.py
@@ -85,8 +85,8 @@
         to[:cb, :] = block
     copies[1].wait()
     for to, plane in ((first, ids[0]), (last, ids[labels.shape[0] - 1])):
-        parts = [plane & 255, plane >> 8]
-        rows = jnp.concatenate([part[:, i : i + lanes] for part in parts for i in range(0, cols, lanes)], axis=0)
+        coded = ((plane & 127) + 128) << (plane >> 7)
+        rows = jnp.concatenate([coded[:, i : i + lanes] for i in range(0, cols, lanes)], axis=0)
         to[cb:, :] = rows.astype(F32).astype(BF16)
     copies[2].wait()
     cot[...] = apart(raw_cots[...], planes)
@@ -96,7 +96,7 @@
 def pack_call(labels, cells, cots, table, planes):
     depth, rows, cols = labels.shape
     cb, lanes = cells.shape[0] // planes, cells.shape[1] * planes
-    more = 2 * rows * cols // lanes
+    more = rows * cols // lanes
     S = jax.ShapeDtypeStruct
     outs = [S((cb, lanes), BF16), S((cb + more, lanes), BF16), S((cb + more, lanes), BF16)]
     outs += [S((cots.shape[0] // planes, lanes), BF16), S(labels.shape, jnp.int32), S(table.shape, BF16)]
@@ -118,9 +118,9 @@
     for ref in (got[0], got[count - 1]):
         rest = ref[cb:, :].astype(F32)
         pieces = [rest[i * rows : (i + 1) * rows] for i in range(rest.shape[0] // rows)]
-        half = len(pieces) // 2
-        low, high = (jnp.concatenate(part, axis=1) for part in (pieces[:half], pieces[half:]))
-        planes.append((low + 256.0 * high).astype(jnp.int32))
+        coded = jnp.concatenate(pieces, axis=1).astype(jnp.int32)
+        high = sum((coded >= (128 << t)).astype(jnp.int32) for t in range(1, 8))
+        planes.append(high * 128 + (coded >> high) - 128)
     below[...] = planes[0]
     above[...] = planes[1]
     all_planes = [planes[0]] + [labels[x] for x in range(depth)] + [planes[1]]

time: 42.6 us -> 42.3 us (level)
  no operation moved by 1% of the time
where the time goes in v10:
time: 42.3 us; the launch traced here: 42.2 us
  Pallas kernels  20.4 us (48%)
  starting transfers between devices  17.7 us (42%)
  waiting for transfers between devices  2.71 us (6%)
  between operations  0.83 us (2%)
  local copies, waits for them, and re-layouts  0.5 us (1%)
    ppermute x11, starting transfers between devices, hop(): lax.ppermute(x, axis, [(i, (i + offset) % count) for i in range(count)])  13.7 us
    pallas_call x1, Pallas kernels, wgrad_call(): call(functools.partial(wgrad_body, scale), [jax.ShapeDtypeStruct((27, o_o...  5.07 us
    pallas_call x1, Pallas kernels, fine_call(): call(functools.partial(fine_body, scale), [S((ch, depth, rows, cols), BF1...  4.1 us
    ppermute x3, starting transfers between devices, swap(): return lax.ppermute(x, axis, [(i, i ^ bit) for i in range(count)])  3.96 us
    pallas_call x1, Pallas kernels, bott_call(): call(functools.partial(bott_body, planes), [S(before.shape, F32), S((len(...  2.33 us
    pallas_call x1, Pallas kernels, chip_call(): call(functools.partial(chip_body, planes), [jax.ShapeDtypeStruct((weight....  2.21 us
    pallas_call x1, Pallas kernels, prep_call(): call(prep_body, [jax.ShapeDtypeStruct((3 * ch * rows, 3 * (rows + 2) * ch...  1.98 us
    ppermute x11, waiting for transfers between devices, hop(): lax.ppermute(x, axis, [(i, (i + offset) % count) for i in range(count)])  1.65 us
  transfers between devices with their start and end apart: 14, of which 2 were waited for; matrix products, arithmetic and copies ran while one was open for 1% of the time, Pallas kernels for 44%

profile of v10, /device:TPU:1, one launch (start us, length us, event | category | flops | bytes accessed | tf_op | source)
XLA Modules:
  0.0 42.2 jit_solution(2139475308860296925)
XLA Ops:
  0.6 0.0 copy-start.2
  0.6 3.2 %collective-permute-start.1 = (bf16[256,128]{1,0:T(8,128)(2,1)}, bf16[256,128]{1,0:T(8,128)(2,1)S(1)}, u32[]{:S(2)}, u32[]{:S(2)}) collective-permute-start(bf16[256,128]{1,0:T(8,128)(2,1)} %bitcast.25), channel_id=1, source_target_pairs={{0,8},{4,12},{8,0},{12,4},{1,9},{5,13},{9,1},{13,5},{2,10},{6,14},... | collective-permute-start | bytes 196616 | tf_op jit(solution)/shard_map/ppermute | solution.py:636
  3.8 1.3 %shard_map.110 = (bf16[128,256]{1,0:T(8,128)(2,1)S(1)}, bf16[144,256]{1,0:T(8,128)(2,1)S(1)}, bf16[144,256]{1,0:T(8,128)(2,1)S(1)}, bf16[128,256]{1,0:T(8,128)(2...) custom-call(s32[4,8,512]{2,1,0:T(8,128)} %labels.1, bf16[256,128]{1,0:T(8,128)(2,1)} %bitcast.26, ...), custom_call_target="tpu_custom_call" | custom-call | flops 1000000000 | bytes 262144 | tf_op jit(solution)/shard_map/pallas_call | solution.py:106
  5.1 1.3 %collective-permute-start = (bf16[144,256]{1,0:T(8,128)(2,1)S(1)}, bf16[144,256]{1,0:T(8,128)(2,1)S(1)}, u32[]{:S(2)}, u32[]{:S(2)}) collective-permute-start(bf16[144,256]{1,0:T(8,128)(2,1)S(1)} %get-tuple-element.36), channel_id=1, source_target_pairs={{0,4},{4,8},{8,12},{12,0},{1,5},{5,9},{9,13},{13,1},{2,6},{6,10},{... | collective-permute-start | bytes 221192 | tf_op jit(solution)/shard_map/ppermute | solution.py:636
  6.5 2.0 %collective-permute-start.2 = (bf16[144,256]{1,0:T(8,128)(2,1)S(1)}, bf16[144,256]{1,0:T(8,128)(2,1)S(1)}, u32[]{:S(2)}, u32[]{:S(2)}) collective-permute-start(bf16[144,256]{1,0:T(8,128)(2,1)S(1)} %get-tuple-element.37), channel_id=1, source_target_pairs={{0,12},{4,0},{8,4},{12,8},{1,13},{5,1},{9,5},{13,9},{2,14},{6,2},{... | collective-permute-start | bytes 221192 | tf_op jit(solution)/shard_map/ppermute | solution.py:636
  8.4 0.0 copy-done.2
  8.4 0.2 copy.13
  8.6 0.2 copy.14
  8.8 0.1 reshape.32.taps
  8.9 0.0 copy-start.1
  8.9 2.0 %shard_map.111 = (bf16[384,480]{1,0:T(8,128)(2,1)S(1)}, bf16[128,128]{1,0:T(8,128)(2,1)S(1)}, bf16[512,512]{1,0:T(8,128)(2,1)S(1)}) custom-call(bf16[3,48,48]{2,1,0:T(8,128)(2,1)S(1)} %reshape.32.taps, bf16[16,1024]{1,0:T(8,128)(2,1)S(1)} %get-tuple-element.32.table, s32[4,8,512]{2,1,0:T(8,128)S(1)} %get-tuple-element.33.ids.refs_0_), custom_call_target="tpu_custom_call" | custom-call | flops 2500000000 | bytes 262144 | tf_op jit(solution)/shard_map/pallas_call | solution.py:179
  10.9 0.0 collective-permute-done.1.refs_3_
  10.9 0.0 collective-permute-done.refs_2_
  10.9 0.0 collective-permute-done.2.refs_4_
  11.0 0.2 shard_map.112
  11.1 2.0 %collective-permute-start.5 = (bf16[4,128,256]{2,1,0:T(8,128)(2,1)S(1)}, bf16[4,128,256]{2,1,0:T(8,128)(2,1)S(1)}, u32[]{:S(2)}, u32[]{:S(2)}) collective-permute-start(bf16[4,128,256]{2,1,0:T(8,128)(2,1)S(1)} %get-tuple-element.45.mine.refs_0_), channel_id=1, source_target_pairs={{0,1},{1,0},{2,3},{3,2},{4,5},{5,4},{6,7},{7,6},{8,9},{9,8},{10,11... | collective-permute-start | bytes 786440 | tf_op jit(solution)/shard_map/ppermute | solution.py:641
  13.1 1.2 %collective-permute-start.3 = (s32[6,512]{1,0:T(8,128)S(1)}, s32[6,512]{1,0:T(8,128)S(1)}, u32[]{:S(2)}, u32[]{:S(2)}) collective-permute-start(s32[6,512]{1,0:T(8,128)S(1)} %get-tuple-element.41), channel_id=1, source_target_pairs={{0,1},{1,2},{2,3},{3,0},{4,5},{5,6},{6,7},{7,4},{8,9},{9,10},{10,1... | collective-permute-start | bytes 36872 | tf_op jit(solution)/shard_map/ppermute | solution.py:636
  14.3 0.0 collective-permute-start.4
  14.3 1.7 %collective-permute-start.7 = (bf16[4,128,256]{2,1,0:T(8,128)(2,1)S(1)}, bf16[4,128,256]{2,1,0:T(8,128)(2,1)S(1)}, u32[]{:S(2)}, u32[]{:S(2)}) collective-permute-start(bf16[4,128,256]{2,1,0:T(8,128)(2,1)S(1)} %get-tuple-element.45.mine.refs_0_), channel_id=1, source_target_pairs={{0,3},{1,2},{2,1},{3,0},{4,7},{5,6},{6,5},{7,4},{8,11},{9,10},{10,... | collective-permute-start | bytes 786440 | tf_op jit(solution)/shard_map/ppermute | solution.py:641
  16.0 0.3 collective-permute-start.6
  16.3 0.0 collective-permute-done.3.left
  16.3 1.6 %collective-permute-done.4.right = s32[6,512]{1,0:T(8,128)S(1)} collective-permute-done((s32[6,512]{1,0:T(8,128)S(1)}, s32[6,512]{1,0:T(8,128)S(1)}, u32[]{:S(2)}, u32[]{:S(2)}) %collective-permute-start.4) | collective-permute-done | bytes 12320 | tf_op jit(solution)/shard_map/ppermute | solution.py:636
  17.9 0.0 collective-permute-done.5.after.mate.refs_1_
  17.9 0.0 copy-done.1
  17.9 0.0 copy-start
  17.9 4.1 %shard_map.113 = (bf16[16,4,8,512]{3,2,1,0:T(8,128)(2,1)}, f32[16,512]{1,0:T(8,128)S(1)}, bf16[160,256]{1,0:T(8,128)(2,1)S(1)}) custom-call(bf16[512,512]{1,0:T(8,128)(2,1)S(1)} %get-tuple-element.34.known, s32[8,512]{1,0:T(8,128)S(1)} %get-tuple-element.39.below, s32[8,512]{1,0:T(8,128)S(1)} %get-tuple-element.40.above, ...), custom_call_target="tpu_custom_call" | custom-call | flops 6000000000 | bytes 4194304 | tf_op jit(solution)/shard_map/pallas_call | solution.py:296
  22.0 3.0 %collective-permute-start.10 = (bf16[160,256]{1,0:T(8,128)(2,1)S(1)}, bf16[160,256]{1,0:T(8,128)(2,1)S(1)}, u32[]{:S(2)}, u32[]{:S(2)}) collective-permute-start(bf16[160,256]{1,0:T(8,128)(2,1)S(1)} %get-tuple-element.50), channel_id=1, source_target_pairs={{0,12},{4,0},{8,4},{12,8},{1,13},{5,1},{9,5},{13,9},{2,14},{6,2},{... | collective-permute-start | bytes 245768 | tf_op jit(solution)/shard_map/ppermute | solution.py:636
  25.0 0.0 collective-permute-start.9
  25.0 0.4 collective-permute-start.8
  25.4 0.0 copy-done
  25.4 2.2 %shard_map.114.before = f32[128,1024]{1,0:T(8,128)S(1)} custom-call(bf16[3456,512]{1,0:T(8,128)(2,1)S(1)} %bitcast.19, f32[16,512]{1,0:T(8,128)S(1)} %get-tuple-element.47.after.part, bf16[4,128,256]{2,1,0:T(8,128)(2,1)S(1)} %get-tuple-element.45.mine.refs_0_, bf16[4,128,256]{2,1,0:T(8,128)(2,1)S(1)} %collective-permute-done.5.after.mate.refs_1_), custom_call_target="tpu_custom_call" | custom-call | flops 2500000000 | bytes 1048576 | tf_op jit(solution)/shard_map/pallas_call | solution.py:381
  27.6 0.0 collective-permute-done.7.refs_3_
  27.6 1.1 %collective-permute-done.6.refs_2_ = bf16[4,128,256]{2,1,0:T(8,128)(2,1)S(1)} collective-permute-done((bf16[4,128,256]{2,1,0:T(8,128)(2,1)S(1)}, bf16[4,128,256]{2,1,0:T(8,128)(2,1)S(1)}, u32[]{:S(2)}, u32[]{:S(2)}) %collective-permute-start.6) | collective-permute-done | bytes 262176 | tf_op jit(solution)/shard_map/ppermute | solution.py:641
  28.7 2.3 %shard_map.115 = (f32[128,1024]{1,0:T(8,128)S(1)}, bf16[512,1280]{1,0:T(8,128)(2,1)S(1)}) custom-call(bf16[3456,512]{1,0:T(8,128)(2,1)S(1)} %bitcast.20, f32[128,1024]{1,0:T(8,128)S(1)} %shard_map.114.before, bf16[4,128,256]{2,1,0:T(8,128)(2,1)S(1)} %get-tuple-element.45.mine.refs_0_, bf16[4,128,256]{2,1,0:T(8,128)(2,1)S(1)} %collective-permute-done.5.after.mate.refs_1_, ...), custom_call_target="tpu_custom_call" | custom-call | flops 2500000000 | bytes 1048576 | tf_op jit(solution)/shard_map/pallas_call | solution.py:408
  31.0 1.6 %shard_map.116 = (bf16[256,128]{1,0:T(8,128)(2,1)}, f32[256,512]{1,0:T(8,128)S(1)}) custom-call(bf16[3456,512]{1,0:T(8,128)(2,1)S(1)} %bitcast.21, f32[128,1024]{1,0:T(8,128)S(1)} %get-tuple-element.48.pre, bf16[128,256]{1,0:T(8,128)(2,1)S(1)} %get-tuple-element.44.bott_cot.cot.refs_0_), custom_call_target="tpu_custom_call" | custom-call | flops 1600000000 | bytes 1048576 | tf_op jit(solution)/shard_map/pallas_call | solution.py:465
  32.7 0.0 collective-permute-done.10.refs_3_
  32.7 0.0 collective-permute-done.9.refs_2_
  32.7 0.0 collective-permute-done.8.refs_1_
  32.7 0.8 %shard_map.117 = (f32[128,1280]{1,0:T(8,128)S(1)}, bf16[4,320,128]{2,1,0:T(8,128)(2,1)S(1)}, f32[4,256,128]{2,1,0:T(8,128)S(1)}, f32[16,512]{1,0:T(8,128)S(1)}) custom-call(bf16[3456,512]{1,0:T(8,128)(2,1)S(1)} %bitcast.22, f32[128,1024]{1,0:T(8,128)S(1)} %get-tuple-element.48.pre, f32[16,512]{1,0:T(8,128)S(1)} %get-tuple-element.47.after.part, ...), custom_call_target="tpu_custom_call" | custom-call | flops 1200000000 | bytes 1048576 | tf_op jit(solution)/shard_map/pallas_call | solution.py:526
  33.5 0.7 %collective-permute-start.13 = (bf16[320,128]{1,0:T(8,128)(2,1)S(1)}, bf16[320,128]{1,0:T(8,128)(2,1)S(1)}, u32[]{:S(2)}, u32[]{:S(2)}) collective-permute-start(bf16[320,128]{1,0:T(8,128)(2,1)S(1)} %get-tuple-element.59), channel_id=1, source_target_pairs={{0,3},{1,0},{2,1},{3,2},{4,7},{5,4},{6,5},{7,6},{8,11},{9,8},{10,9... | collective-permute-start | bytes 245768 | tf_op jit(solution)/shard_map/ppermute | solution.py:636
  34.2 0.2 collective-permute-start.12
  34.3 1.8 %collective-permute-start.11 = (bf16[320,128]{1,0:T(8,128)(2,1)S(1)}, bf16[320,128]{1,0:T(8,128)(2,1)S(1)}, u32[]{:S(2)}, u32[]{:S(2)}) collective-permute-start(bf16[320,128]{1,0:T(8,128)(2,1)S(1)} %get-tuple-element.61), channel_id=1, source_target_pairs={{0,1},{1,2},{2,3},{3,0},{4,5},{5,6},{6,7},{7,4},{8,9},{9,10},{10,1... | collective-permute-start | bytes 245768 | tf_op jit(solution)/shard_map/ppermute | solution.py:636
  36.1 5.1 %shard_map.119 = f32[27,128,512]{2,1,0:T(8,128)} custom-call(f32[128,1280]{1,0:T(8,128)S(1)} %get-tuple-element.57.delta, bf16[512,1280]{1,0:T(8,128)(2,1)S(1)} %get-tuple-element.58.full), custom_call_target="tpu_custom_call" | custom-call | flops 6600000000 | bytes 8388608 | tf_op jit(solution)/shard_map/pallas_call | solution.py:588
  41.2 0.0 collective-permute-done.13.refs_2_
  41.2 0.0 collective-permute-done.12.refs_1_
  41.3 0.0 collective-permute-done.11.refs_0_
  41.3 0.9 %shard_map.118 = (bf16[256,128]{1,0:T(8,128)(2,1)}, f32[16,16,27]{2,1,0:T(8,128)}) custom-call(f32[4,256,128]{2,1,0:T(8,128)S(1)} %get-tuple-element.51.mine, f32[16,512]{1,0:T(8,128)S(1)} %get-tuple-element.52.part, bf16[320,128]{1,0:T(8,128)(2,1)S(1)} %collective-permute-done.11.refs_0_, bf16[320,128]{1,0:T(8,128)(2,1)S(1)} %collective-permute-done.12.refs_1_, ...), custom_call_target="tpu_custom_call" | custom-call | flops 1000000000 | bytes 262144 | tf_op jit(solution)/shard_map/pallas_call | solution.py:620
  (1 shorter events, 0.0 us)
Async XLA Ops:
  0.6 7.8 %copy-start.2 = (bf16[27,16,16]{0,2,1:T(8,128)(2,1)S(1)}, bf16[27,16,16]{0,2,1:T(8,128)(2,1)}, u32[]{:S(2)}) copy-start(bf16[27,16,16]{0,2,1:T(8,128)(2,1)} %param.9) | copy-start | bytes 41476
  0.6 10.3 %collective-permute-start.1 = (bf16[256,128]{1,0:T(8,128)(2,1)}, bf16[256,128]{1,0:T(8,128)(2,1)S(1)}, u32[]{:S(2)}, u32[]{:S(2)}) collective-permute-start(bf16[256,128]{1,0:T(8,128)(2,1)} %bitcast.25), channel_id=1, source_target_pairs={{0,8},{4,12},{8,0},{12,4},{1,9},{5,13},{9,1},{13,5},{2,10},{6,14},... | collective-permute-start | bytes 196616 | tf_op jit(solution)/shard_map/ppermute | solution.py:636
  5.1 5.8 %collective-permute-start = (bf16[144,256]{1,0:T(8,128)(2,1)S(1)}, bf16[144,256]{1,0:T(8,128)(2,1)S(1)}, u32[]{:S(2)}, u32[]{:S(2)}) collective-permute-start(bf16[144,256]{1,0:T(8,128)(2,1)S(1)} %get-tuple-element.36), channel_id=1, source_target_pairs={{0,4},{4,8},{8,12},{12,0},{1,5},{5,9},{9,13},{13,1},{2,6},{6,10},{... | collective-permute-start | bytes 221192 | tf_op jit(solution)/shard_map/ppermute | solution.py:636
  6.5 4.5 %collective-permute-start.2 = (bf16[144,256]{1,0:T(8,128)(2,1)S(1)}, bf16[144,256]{1,0:T(8,128)(2,1)S(1)}, u32[]{:S(2)}, u32[]{:S(2)}) collective-permute-start(bf16[144,256]{1,0:T(8,128)(2,1)S(1)} %get-tuple-element.37), channel_id=1, source_target_pairs={{0,12},{4,0},{8,4},{12,8},{1,13},{5,1},{9,5},{13,9},{2,14},{6,2},{... | collective-permute-start | bytes 221192 | tf_op jit(solution)/shard_map/ppermute | solution.py:636
  8.9 9.0 %copy-start.1 = (bf16[16,4,8,512]{3,2,1,0:T(8,128)(2,1)S(1)}, bf16[16,4,8,512]{3,2,1,0:T(8,128)(2,1)}, u32[]{:S(2)}) copy-start(bf16[16,4,8,512]{3,2,1,0:T(8,128)(2,1)} %cot.1) | copy-start | bytes 1572868
  11.1 6.8 %collective-permute-start.5 = (bf16[4,128,256]{2,1,0:T(8,128)(2,1)S(1)}, bf16[4,128,256]{2,1,0:T(8,128)(2,1)S(1)}, u32[]{:S(2)}, u32[]{:S(2)}) collective-permute-start(bf16[4,128,256]{2,1,0:T(8,128)(2,1)S(1)} %get-tuple-element.45.mine.refs_0_), channel_id=1, source_target_pairs={{0,1},{1,0},{2,3},{3,2},{4,5},{5,4},{6,7},{7,6},{8,9},{9,8},{10,11... | collective-permute-start | bytes 786440 | tf_op jit(solution)/shard_map/ppermute | solution.py:641
  13.1 3.2 %collective-permute-start.3 = (s32[6,512]{1,0:T(8,128)S(1)}, s32[6,512]{1,0:T(8,128)S(1)}, u32[]{:S(2)}, u32[]{:S(2)}) collective-permute-start(s32[6,512]{1,0:T(8,128)S(1)} %get-tuple-element.41), channel_id=1, source_target_pairs={{0,1},{1,2},{2,3},{3,0},{4,5},{5,6},{6,7},{7,4},{8,9},{9,10},{10,1... | collective-permute-start | bytes 36872 | tf_op jit(solution)/shard_map/ppermute | solution.py:636
  14.3 3.6 %collective-permute-start.4 = (s32[6,512]{1,0:T(8,128)S(1)}, s32[6,512]{1,0:T(8,128)S(1)}, u32[]{:S(2)}, u32[]{:S(2)}) collective-permute-start(s32[6,512]{1,0:T(8,128)S(1)} %get-tuple-element.42), channel_id=1, source_target_pairs={{0,3},{1,0},{2,1},{3,2},{4,7},{5,4},{6,5},{7,6},{8,11},{9,8},{10,9... | collective-permute-start | bytes 36872 | tf_op jit(solution)/shard_map/ppermute | solution.py:636
  14.3 13.4 %collective-permute-start.7 = (bf16[4,128,256]{2,1,0:T(8,128)(2,1)S(1)}, bf16[4,128,256]{2,1,0:T(8,128)(2,1)S(1)}, u32[]{:S(2)}, u32[]{:S(2)}) collective-permute-start(bf16[4,128,256]{2,1,0:T(8,128)(2,1)S(1)} %get-tuple-element.45.mine.refs_0_), channel_id=1, source_target_pairs={{0,3},{1,2},{2,1},{3,0},{4,7},{5,6},{6,5},{7,4},{8,11},{9,10},{10,... | collective-permute-start | bytes 786440 | tf_op jit(solution)/shard_map/ppermute | solution.py:641
  16.0 12.7 %collective-permute-start.6 = (bf16[4,128,256]{2,1,0:T(8,128)(2,1)S(1)}, bf16[4,128,256]{2,1,0:T(8,128)(2,1)S(1)}, u32[]{:S(2)}, u32[]{:S(2)}) collective-permute-start(bf16[4,128,256]{2,1,0:T(8,128)(2,1)S(1)} %get-tuple-element.45.mine.refs_0_), channel_id=1, source_target_pairs={{0,2},{1,3},{2,0},{3,1},{4,6},{5,7},{6,4},{7,5},{8,10},{9,11},{10,... | collective-permute-start | bytes 786440 | tf_op jit(solution)/shard_map/ppermute | solution.py:641
  17.9 7.5 %copy-start = (bf16[128,27,512]{2,0,1:T(8,128)(2,1)S(1)}, bf16[128,27,512]{2,0,1:T(8,128)(2,1)}, u32[]{:S(2)}) copy-start(bf16[128,27,512]{2,0,1:T(8,128)(2,1)} %param.12) | copy-start | bytes 10616836
  22.0 10.6 %collective-permute-start.10 = (bf16[160,256]{1,0:T(8,128)(2,1)S(1)}, bf16[160,256]{1,0:T(8,128)(2,1)S(1)}, u32[]{:S(2)}, u32[]{:S(2)}) collective-permute-start(bf16[160,256]{1,0:T(8,128)(2,1)S(1)} %get-tuple-element.50), channel_id=1, source_target_pairs={{0,12},{4,0},{8,4},{12,8},{1,13},{5,1},{9,5},{13,9},{2,14},{6,2},{... | collective-permute-start | bytes 245768 | tf_op jit(solution)/shard_map/ppermute | solution.py:636
  25.0 7.6 %collective-permute-start.9 = (bf16[160,256]{1,0:T(8,128)(2,1)S(1)}, bf16[160,256]{1,0:T(8,128)(2,1)S(1)}, u32[]{:S(2)}, u32[]{:S(2)}) collective-permute-start(bf16[160,256]{1,0:T(8,128)(2,1)S(1)} %get-tuple-element.50), channel_id=1, source_target_pairs={{0,8},{4,12},{8,0},{12,4},{1,9},{5,13},{9,1},{13,5},{2,10},{6,14},... | collective-permute-start | bytes 245768 | tf_op jit(solution)/shard_map/ppermute | solution.py:636
  25.0 7.6 %collective-permute-start.8 = (bf16[160,256]{1,0:T(8,128)(2,1)S(1)}, bf16[160,256]{1,0:T(8,128)(2,1)S(1)}, u32[]{:S(2)}, u32[]{:S(2)}) collective-permute-start(bf16[160,256]{1,0:T(8,128)(2,1)S(1)} %get-tuple-element.50), channel_id=1, source_target_pairs={{0,4},{4,8},{8,12},{12,0},{1,5},{5,9},{9,13},{13,1},{2,6},{6,10},{... | collective-permute-start | bytes 245768 | tf_op jit(solution)/shard_map/ppermute | solution.py:636
  33.5 7.7 %collective-permute-start.13 = (bf16[320,128]{1,0:T(8,128)(2,1)S(1)}, bf16[320,128]{1,0:T(8,128)(2,1)S(1)}, u32[]{:S(2)}, u32[]{:S(2)}) collective-permute-start(bf16[320,128]{1,0:T(8,128)(2,1)S(1)} %get-tuple-element.59), channel_id=1, source_target_pairs={{0,3},{1,0},{2,1},{3,2},{4,7},{5,4},{6,5},{7,6},{8,11},{9,8},{10,9... | collective-permute-start | bytes 245768 | tf_op jit(solution)/shard_map/ppermute | solution.py:636
  34.2 7.1 %collective-permute-start.12 = (bf16[320,128]{1,0:T(8,128)(2,1)S(1)}, bf16[320,128]{1,0:T(8,128)(2,1)S(1)}, u32[]{:S(2)}, u32[]{:S(2)}) collective-permute-start(bf16[320,128]{1,0:T(8,128)(2,1)S(1)} %get-tuple-element.60), channel_id=1, source_target_pairs={{0,2},{1,3},{2,0},{3,1},{4,6},{5,7},{6,4},{7,5},{8,10},{9,11},{10,... | collective-permute-start | bytes 245768 | tf_op jit(solution)/shard_map/ppermute | solution.py:636
  34.3 6.9 %collective-permute-start.11 = (bf16[320,128]{1,0:T(8,128)(2,1)S(1)}, bf16[320,128]{1,0:T(8,128)(2,1)S(1)}, u32[]{:S(2)}, u32[]{:S(2)}) collective-permute-start(bf16[320,128]{1,0:T(8,128)(2,1)S(1)} %get-tuple-element.61), channel_id=1, source_target_pairs={{0,1},{1,2},{2,3},{3,0},{4,5},{5,6},{6,7},{7,4},{8,9},{9,10},{10,1... | collective-permute-start | bytes 245768 | tf_op jit(solution)/shard_map/ppermute | solution.py:636
